TPU v7x, 128 devices: a whole 4x4x4 slice. The times are simulated.
128 devices in a mesh: ctx: 8 (over x, core), ch: 16 (over z, y).
Axes of the slice: x: 4, y: 4, z: 4, core: 2. Of those that a mesh axis runs over, the one named last changes fastest.
Arguments:
- mr_query: bfloat16 [16384, 8192], P(('ctx', 'ch')), may hold values from -6 to 6
- mr_key: bfloat16 [16384, 8192], P(('ctx', 'ch')), may hold values from -6 to 6
- mr_value: bfloat16 [16384, 8192], P(('ctx', 'ch')), may hold values from -6 to 6
- li_query: bfloat16 [16384, 8192], P(('ctx', 'ch')), may hold values from -6 to 6
- li_key: bfloat16 [16384, 8192], P(('ctx', 'ch')), may hold values from -6 to 6
- out_cotangent: bfloat16 [16384, 8192], P(('ctx', 'ch')), may hold values from -6 to 6
- mr_short: bfloat16 [3, 3, 8192], replicated, may hold values from -3.5 to 3.5
- li_short: bfloat16 [3, 3, 8192], replicated, may hold values from -3.5 to 3.5
- mr_filter: bfloat16 [128, 512], replicated, may hold values from -0.5 to 0.5
- li_rate: float32 [512, 16], replicated, may hold values from 0 to 1, as said below
- li_residue: float32 [512, 16], replicated, may hold values from -1 to 1, as said below
- li_skip: float32 [8192], replicated, may hold values from -4 to 4
Outputs:
- output: bfloat16 [16384, 8192], P(('ctx', 'ch'))
- grad_mr_query: bfloat16 [16384, 8192], P(('ctx', 'ch'))
- grad_mr_key: bfloat16 [16384, 8192], P(('ctx', 'ch'))
- grad_mr_value: bfloat16 [16384, 8192], P(('ctx', 'ch'))
- grad_li_query: bfloat16 [16384, 8192], P(('ctx', 'ch'))
- grad_li_key: bfloat16 [16384, 8192], P(('ctx', 'ch'))
Inputs may be any that keep to these rules, and one draw needn't show every extreme that they name: `li_rate`: positive decay rates, one for each of a group's 16 modes. `li_residue`: real residues, one for each of a group's 16 modes.
All inputs are finite; a program needn't handle non-finite values.
Results may differ from a plain program's by a relative error of at most 0.011.
Values may be sent and summed in bfloat16 or wider, within the bound.
No kernel may reach another device: no remote copies, remote signals or barrier semaphores. Data moves between devices by JAX's collectives and lax.ppermute only.
A program may use at most 576 MiB of HBM per device.

v0:
```python
import jax
import jax.numpy as jnp
from jax import lax
from jax.sharding import PartitionSpec as P

GROUP = 16
SHORT = 3
MR_TAPS = 128


HIGHEST = lax.Precision.HIGHEST


def passed_along(array, axis, by):
    size = lax.axis_size(axis)
    pairs = [(i, i + by) for i in range(size) if 0 <= i + by < size]
    return lax.ppermute(array, axis, pairs)


def prefix(value, axis, join, neutral, backward):
    count, mine = (lax.axis_size(axis), lax.axis_index(axis))
    pieces = jax.tree.map(lambda part: lax.all_gather(part, axis), value)
    if backward:
        pieces = jax.tree.map(lambda part: part[::-1], pieces)
        mine = count - 1 - mine
    subtotal = jax.tree.map(
        lambda part, zero: jnp.full_like(part, 0) + jnp.asarray(zero, part.dtype), value, neutral
    )

    def hop(position, subtotal):
        longer = join(subtotal, jax.tree.map(lambda part: part[position], pieces))
        return jax.tree.map(lambda new, old: jnp.where(position < mine, new, old), longer, subtotal)

    return lax.fori_loop(0, count - 1, hop, subtotal)


def contract(pattern, first_operand, second_operand):
    return jnp.einsum(pattern, first_operand, second_operand, precision=HIGHEST)


def lag_tables():
    steps_in = jnp.arange(MR_TAPS, dtype=jnp.int32)
    lagged = steps_in[:, None] - steps_in[None, :]
    tap_index = steps_in[:, None, None]
    lower_table = (lagged[None, :, :] == tap_index).astype(jnp.float32)
    upper_table = (lagged[None, :, :] + MR_TAPS == tap_index).astype(jnp.float32)
    return (lower_table, upper_table)


def toeplitz(filters, table):
    return contract("kg,kij->gij", filters, table)


def short_forward(signal, margin, filter_taps):
    count_rows = signal.shape[0]
    extended = jnp.concatenate([margin.astype(jnp.float32), signal.astype(jnp.float32)], 0)
    result = jnp.zeros((count_rows, signal.shape[1]), jnp.float32)
    for offset in range(SHORT):
        first_row = SHORT - 1 - offset
        result = (
            result
            + filter_taps[offset].astype(jnp.float32) * extended[first_row : first_row + count_rows]
        )
    return result


def short_backward(signal, margin, filter_taps):
    count_rows = signal.shape[0]
    extended = jnp.concatenate([signal, margin], 0)
    result = jnp.zeros((count_rows, signal.shape[1]), jnp.float32)
    for offset in range(SHORT):
        result = (
            result
            + filter_taps[offset].astype(jnp.float32) * extended[offset : offset + count_rows]
        )
    return result


def split_blocks(signal, groups):
    count_rows, channels = signal.shape
    return signal.reshape(count_rows // MR_TAPS, MR_TAPS, groups, channels // groups)


def causal_medium(signal, near_toeplitz, far_toeplitz, before_block):
    groups = near_toeplitz.shape[0]
    blocks = split_blocks(signal, groups)
    prior_blocks = jnp.concatenate([split_blocks(before_block, groups), blocks[:-1]], 0)
    result = contract("gij,bjgc->bigc", near_toeplitz, blocks) + contract(
        "gij,bjgc->bigc", far_toeplitz, prior_blocks
    )
    return result.reshape(signal.shape)


def anticausal_medium(signal, near_toeplitz, far_toeplitz, after_block):
    groups = near_toeplitz.shape[0]
    blocks = split_blocks(signal, groups)
    later_blocks = jnp.concatenate([blocks[1:], split_blocks(after_block, groups)], 0)
    result = contract("gij,bigc->bjgc", near_toeplitz, blocks) + contract(
        "gij,bigc->bjgc", far_toeplitz, later_blocks
    )
    return result.reshape(signal.shape)


def modal_tables(li_rate, li_residue, lower_table):
    positions = jnp.arange(MR_TAPS, dtype=jnp.float32)
    powers = jnp.exp(-li_rate[:, :, None] * positions)
    impulse = contract("gn,gnk->kg", li_residue, powers)
    near_long = toeplitz(impulse, lower_table)
    emit_table = li_residue[:, :, None] * jnp.exp(-li_rate[:, :, None] * (positions + 1.0))
    absorb_table = jnp.exp(-li_rate[:, :, None] * (MR_TAPS - 1.0 - positions))
    emit_back = li_residue[:, :, None] * jnp.exp(-li_rate[:, :, None] * (MR_TAPS - positions))
    return (near_long, emit_table, absorb_table, emit_back, powers)


def long_forward(signal, near_long, emit_table, end_states, block_decay, incoming):
    groups = near_long.shape[0]
    blocks = split_blocks(signal, groups)

    def advance(carried, end_state):
        return (block_decay[:, :, None] * carried + end_state, carried)

    unused, start_states = lax.scan(advance, incoming, end_states)
    result = contract("gij,bjgc->bigc", near_long, blocks) + contract(
        "gni,bgnc->bigc", emit_table, start_states
    )
    return result.reshape(signal.shape)


def long_backward(signal, near_long, emit_back, owned_states, block_decay, incoming):
    groups = near_long.shape[0]
    blocks = split_blocks(signal, groups)

    def retreat(carried, own_state):
        return (own_state + block_decay[:, :, None] * carried, carried)

    unused, closing_states = lax.scan(retreat, incoming, owned_states, reverse=True)
    result = contract("gij,bigc->bjgc", near_long, blocks) + contract(
        "gnj,bgnc->bjgc", emit_back, closing_states
    )
    return result.reshape(signal.shape)


def chain_states(earlier, later):
    return (earlier[0] * later[0], later[0] * earlier[1] + later[1])


def prev_rows_ctx(stacked):
    return passed_along(stacked, "ctx", 1)


def prev_products_ctx(tail_rows):
    return passed_along(tail_rows, "ctx", 1)


def next_rows_ctx(head_rows):
    return passed_along(head_rows, "ctx", -1)


def carry_ctx(device_decay, device_state):
    return prefix(
        (device_decay, device_state),
        "ctx",
        chain_states,
        (jnp.ones_like(device_decay), jnp.zeros_like(device_state)),
        False,
    )[1]


def carry_back_ctx(device_decay, device_state):
    return prefix(
        (device_decay, device_state),
        "ctx",
        chain_states,
        (jnp.ones_like(device_decay), jnp.zeros_like(device_state)),
        True,
    )[1]


def operator_pair(inputs, weights, neighbour_links):
    mr_query, mr_key, mr_value, li_query, li_key, out_cotangent = inputs
    mr_short, li_short, mr_filter, li_rate, li_residue, li_skip = weights
    prev_rows, prev_products, next_rows, carry_forward, carry_backward = neighbour_links
    count_rows, channels = mr_query.shape
    groups = channels // GROUP
    blocks_count = count_rows // MR_TAPS
    edge_rows = SHORT - 1
    lower_table, upper_table = lag_tables()
    near_medium = toeplitz(mr_filter.astype(jnp.float32), lower_table)
    far_medium = toeplitz(mr_filter.astype(jnp.float32), upper_table)
    tail_start = count_rows - edge_rows
    margin_one = prev_rows(
        jnp.stack([mr_query[tail_start:], mr_key[tail_start:], mr_value[tail_start:]])
    )
    query_one = short_forward(mr_query, margin_one[0], mr_short[0])
    keys_one = short_forward(mr_key, margin_one[1], mr_short[1])
    value_one = short_forward(mr_value, margin_one[2], mr_short[2])
    prod_one = keys_one * value_one
    tail_rows = prev_products(prod_one[count_rows - MR_TAPS + 1 :])
    before_block = jnp.concatenate([jnp.zeros((1, channels), jnp.float32), tail_rows], 0)
    conv_one = causal_medium(prod_one, near_medium, far_medium, before_block)
    mixed_one = (query_one * conv_one).astype(jnp.bfloat16)
    margin_two = prev_rows(
        jnp.stack([li_query[tail_start:], li_key[tail_start:], mixed_one[tail_start:]])
    )
    query_two = short_forward(li_query, margin_two[0], li_short[0])
    keys_two = short_forward(li_key, margin_two[1], li_short[1])
    value_two = short_forward(mixed_one, margin_two[2], li_short[2])
    prod_two = keys_two * value_two
    near_long, emit_table, absorb_table, emit_back, absorb_back = modal_tables(
        li_rate, li_residue, lower_table
    )
    block_decay = jnp.exp(-li_rate * MR_TAPS)
    block_order = jnp.arange(blocks_count, dtype=jnp.float32)
    device_decay = jnp.exp(-li_rate * count_rows)[:, :, None]
    end_states = contract("gnj,bjgc->bgnc", absorb_table, split_blocks(prod_two, groups))
    toward_end = jnp.exp(
        -li_rate[None, :, :] * (MR_TAPS * (blocks_count - 1.0 - block_order))[:, None, None]
    )
    device_state = contract("bgn,bgnc->gnc", toward_end, end_states)
    incoming = carry_forward(device_decay, device_state)
    conv_two = (
        long_forward(prod_two, near_long, emit_table, end_states, block_decay, incoming)
        + li_skip * prod_two
    )
    output = (query_two * conv_two).astype(jnp.bfloat16)
    upstream = out_cotangent.astype(jnp.float32)
    query_two_grad = upstream * conv_two
    conv_two_grad = upstream * query_two
    owned_states = contract("gnj,bjgc->bgnc", absorb_back, split_blocks(conv_two_grad, groups))
    toward_start = jnp.exp(-li_rate[None, :, :] * (MR_TAPS * block_order)[:, None, None])
    device_back = contract("bgn,bgnc->gnc", toward_start, owned_states)
    incoming_back = carry_backward(device_decay, device_back)
    prod_two_grad = (
        long_backward(conv_two_grad, near_long, emit_back, owned_states, block_decay, incoming_back)
        + li_skip * conv_two_grad
    )
    keys_two_grad = prod_two_grad * value_two
    value_two_grad = prod_two_grad * keys_two
    margin_three = next_rows(
        jnp.stack(
            [query_two_grad[:edge_rows], keys_two_grad[:edge_rows], value_two_grad[:edge_rows]]
        )
    )
    grad_li_query = short_backward(query_two_grad, margin_three[0], li_short[0]).astype(
        jnp.bfloat16
    )
    grad_li_key = short_backward(keys_two_grad, margin_three[1], li_short[1]).astype(jnp.bfloat16)
    mixed_grad = short_backward(value_two_grad, margin_three[2], li_short[2])
    query_one_grad = mixed_grad * conv_one
    conv_one_grad = mixed_grad * query_one
    head_rows = next_rows(conv_one_grad[: MR_TAPS - 1])
    after_block = jnp.concatenate([head_rows, jnp.zeros((1, channels), jnp.float32)], 0)
    prod_one_grad = anticausal_medium(conv_one_grad, near_medium, far_medium, after_block)
    keys_one_grad = prod_one_grad * value_one
    value_one_grad = prod_one_grad * keys_one
    margin_four = next_rows(
        jnp.stack(
            [query_one_grad[:edge_rows], keys_one_grad[:edge_rows], value_one_grad[:edge_rows]]
        )
    )
    grad_mr_query = short_backward(query_one_grad, margin_four[0], mr_short[0]).astype(jnp.bfloat16)
    grad_mr_key = short_backward(keys_one_grad, margin_four[1], mr_short[1]).astype(jnp.bfloat16)
    grad_mr_value = short_backward(value_one_grad, margin_four[2], mr_short[2]).astype(jnp.bfloat16)
    return (output, grad_mr_query, grad_mr_key, grad_mr_value, grad_li_query, grad_li_key)


def per_device(
    mr_query,
    mr_key,
    mr_value,
    li_query,
    li_key,
    out_cotangent,
    mr_short,
    li_short,
    mr_filter,
    li_rate,
    li_residue,
    li_skip,
):
    mr_inputs = (
        lax.all_to_all(mr_query, "ch", split_axis=1, concat_axis=0, tiled=True),
        lax.all_to_all(mr_key, "ch", split_axis=1, concat_axis=0, tiled=True),
        lax.all_to_all(mr_value, "ch", split_axis=1, concat_axis=0, tiled=True),
    )
    li_inputs = (
        lax.all_to_all(li_query, "ch", split_axis=1, concat_axis=0, tiled=True),
        lax.all_to_all(li_key, "ch", split_axis=1, concat_axis=0, tiled=True),
    )
    upstream = lax.all_to_all(out_cotangent, "ch", split_axis=1, concat_axis=0, tiled=True)
    channels = upstream.shape[1]
    local_groups = channels // GROUP
    position = lax.axis_index("ch")
    column_start = position * channels
    group_start = position * local_groups
    local_weights = (
        lax.dynamic_slice_in_dim(mr_short, column_start, channels, 2),
        lax.dynamic_slice_in_dim(li_short, column_start, channels, 2),
        lax.dynamic_slice_in_dim(mr_filter, group_start, local_groups, 1),
        lax.dynamic_slice_in_dim(li_rate, group_start, local_groups, 0),
        lax.dynamic_slice_in_dim(li_residue, group_start, local_groups, 0),
        lax.dynamic_slice_in_dim(li_skip, column_start, channels, 0),
    )
    neighbour_links = (prev_rows_ctx, prev_products_ctx, next_rows_ctx, carry_ctx, carry_back_ctx)
    results = operator_pair(
        (mr_inputs[0], mr_inputs[1], mr_inputs[2], li_inputs[0], li_inputs[1], upstream),
        local_weights,
        neighbour_links,
    )
    output = lax.all_to_all(results[0], "ch", split_axis=0, concat_axis=1, tiled=True)
    gradients = (
        lax.all_to_all(results[1], "ch", split_axis=0, concat_axis=1, tiled=True),
        lax.all_to_all(results[2], "ch", split_axis=0, concat_axis=1, tiled=True),
        lax.all_to_all(results[3], "ch", split_axis=0, concat_axis=1, tiled=True),
        lax.all_to_all(results[4], "ch", split_axis=0, concat_axis=1, tiled=True),
        lax.all_to_all(results[5], "ch", split_axis=0, concat_axis=1, tiled=True),
    )
    return (output, gradients[0], gradients[1], gradients[2], gradients[3], gradients[4])


def solution(mesh):
    placed = (
        P(("ctx", "ch"), None),
        P(("ctx", "ch"), None),
        P(("ctx", "ch"), None),
        P(("ctx", "ch"), None),
        P(("ctx", "ch"), None),
        P(("ctx", "ch"), None),
        P(),
        P(),
        P(),
        P(),
        P(),
        P(),
    )
    return jax.shard_map(
        per_device,
        mesh=mesh,
        in_specs=placed,
        out_specs=(
            P(("ctx", "ch"), None),
            P(("ctx", "ch"), None),
            P(("ctx", "ch"), None),
            P(("ctx", "ch"), None),
            P(("ctx", "ch"), None),
            P(("ctx", "ch"), None),
        ),
        check_vma=False,
    )
```

profile of v0, /device:TPU:1, one launch (start us, length us, event | category | flops | bytes accessed | tf_op | source)
XLA Modules:
  0.0 732.6 jit_solution(6454637891330733651)
XLA Ops:
  17.4 26.4 %all-to-all-done.3 = bf16[128,16,512]{0,2,1:T(8,128)(2,1)S(1)} async-done(((bf16[128,16,512]{0,2,1:T(8,128)(2,1)}), bf16[128,16,512]{0,2,1:T(8,128)(2,1)S(1)}, u32[]{:S(2)}, u32[]{:S(2)}) %all-to-all-start.3) | async-done | bytes 2097184 | tf_op jit(solution)/shard_map/all_to_all | solution.py:283
  53.5 24.7 %all-to-all-done.4 = bf16[128,16,512]{0,2,1:T(8,128)(2,1)S(1)} async-done(((bf16[128,16,512]{0,2,1:T(8,128)(2,1)}), bf16[128,16,512]{0,2,1:T(8,128)(2,1)S(1)}, u32[]{:S(2)}, u32[]{:S(2)}) %all-to-all-start.4) | async-done | bytes 2097184 | tf_op jit(solution)/shard_map/all_to_all | solution.py:284
  90.8 20.4 %all-to-all-done.2 = bf16[128,16,512]{0,2,1:T(8,128)(2,1)} async-done(((bf16[128,16,512]{0,2,1:T(8,128)(2,1)}), bf16[128,16,512]{0,2,1:T(8,128)(2,1)}, u32[]{:S(2)}, u32[]{:S(2)}) %all-to-all-start.2) | async-done | bytes 2097184 | tf_op jit(solution)/shard_map/all_to_all | solution.py:282
  126.3 15.3 %all-gather.3 = f32[8,32,16]{1,2,0:T(8,128)S(1)} all-gather(f32[1,32,16]{1,2,0:T(8,128)S(1)} %exponential_bitcast_fusion.2), channel_id=2, replica_groups=mesh['ctx'=8,'ch'=16] {'ctx'}, dimensions={0}, use_global_device_ids=true | all-gather | bytes 18432 | tf_op jit(solution)/shard_map/all_gather | solution.py:22
  180.3 16.6 %all-to-all-done = bf16[128,16,512]{0,2,1:T(8,128)(2,1)} async-done(((bf16[128,16,512]{0,2,1:T(8,128)(2,1)}), bf16[128,16,512]{0,2,1:T(8,128)(2,1)}, u32[]{:S(2)}, u32[]{:S(2)}) %all-to-all-start) | async-done | bytes 2097184 | tf_op jit(solution)/shard_map/all_to_all | solution.py:287
  278.6 18.3 %all-gather.2 = f32[256,16,16]{2,1,0:T(8,128)} all-gather(f32[32,16,16]{2,1,0:T(8,128)S(1)} %copy.254), channel_id=4, replica_groups=mesh['ctx'=8,'ch'=16] {'ctx'}, dimensions={0}, use_global_device_ids=true | all-gather | bytes 294912 | tf_op jit(solution)/shard_map/all_gather | solution.py:22
  300.5 15.0 %while.59 = (s32[]{:T(128)}, f32[32,16,16]{0,2,1:T(8,128)S(1)}, s32[]{:T(128)}, f32[8,32,16,1]{1,2,3,0:T(8,128)}, f32[8,32,16,16]{1,0,3,2:T(8,128)}, /*index=5*/s32[]{:T(128)}, s32[]{:T(128)}) while((s32[]{:T(128)}, f32[32,16,16]{0,2,1:T(8,128)S(1)}, s32[]{:T(128)}, f32[8,32,16,1]{1,2,3,0:T(8,128)}, f32[8,32,16,16]{1,0,3,2:T(8,128)}, ...), condition=%wide.region_5.6_spmd.clone, body=%wide.region_4.5_spmd.clone.sunk | while | flops 32772 | bytes 170089 | solution.py:34
  322.1 26.3 %while.57 = (s32[]{:T(128)}, f32[32,16,16]{0,2,1:T(8,128)S(1)}, f32[16,32,16,16]{1,3,2,0:T(8,128)}, f32[16,32,16,16]{1,3,2,0:T(8,128)}, f32[32,16]{0,1:T(8,128)S(1)}, /*index=5*/s32[]{:T(128)}, s32[]{:T(128)}) while((s32[]{:T(128)}, f32[32,16,16]{0,2,1:T(8,128)S(1)}, f32[16,32,16,16]{1,3,2,0:T(8,128)}, f32[16,32,16,16]{1,3,2,0:T(8,128)}, ...), condition=%wide.region_7.8_spmd, body=%wide.region_6.7_spmd.sunk | while | flops 16387 | bytes 264289 | solution.py:136
  370.9 11.9 %fusion.174 = (f32[2048,512]{0,1:T(8,128)}, f32[2048,512]{0,1:T(8,128)S(1)}, f32[2048,512]{0,1:T(8,128)S(1)}) fusion(f32[2048,512]{0,1:T(8,128)S(1)} %copy-done.2, f32[512]{0:T(512)S(1)} %dynamic_slice.64, f32[64,8,16,128]{3,2,1,0:T(8,128)} %bitcast.372, f32[2048,512]{0,1:T(8,128)} %get-tuple-element.504, f32[2,512]{0,1:T(8,128)S(1)} %copy-done.37, ...), kind=kLoop, calls=%fused_computation.295 | loop fusion | flops 12582912 | bytes 27275264 | tf_op jit(solution)/shard_map/mul | solution.py:237
  382.9 9.1 %fusion.176 = (f32[2048,512]{0,1:T(8,128)}, f32[2048,512]{0,1:T(8,128)S(1)}) fusion(f32[2048,512]{0,1:T(8,128)S(1)} %get-tuple-element.496, f32[2048,512]{0,1:T(8,128)} %get-tuple-element.512, f32[2,512]{0,1:T(8,128)S(1)} %copy-done.36, f32[512]{0:T(512)S(1)} %bitcast.414, f32[512]{0:T(512)S(1)} %bitcast.412, f32[512]{0:T(512)S(1)} %bitcast.416), kind=kLoop, calls=%fused_computation.296 | loop fusion | flops 8388608 | bytes 16787456 | tf_op jit(solution)/shard_map/mul | solution.py:238
  401.1 16.2 %all-gather.1 = f32[256,16,16]{2,1,0:T(8,128)S(1)} all-gather(f32[32,16,16]{2,1,0:T(8,128)S(1)} %copy.243), channel_id=3, replica_groups=mesh['ctx'=8,'ch'=16] {'ctx'}, dimensions={0}, use_global_device_ids=true | all-gather | bytes 294912 | tf_op jit(solution)/shard_map/all_gather | solution.py:22
  428.7 16.0 %while.56 = (s32[]{:T(128)}, f32[32,16,16]{0,2,1:T(8,128)S(1)}, f32[16,32,16,16]{1,3,2,0:T(8,128)S(1)}, f32[32,16]{0,1:T(8,128)S(1)}, f32[16,32,16,16]{1,3,2,0:T(8,128)}, /*index=5*/s32[]{:T(128)}) while((s32[]{:T(128)}, f32[32,16,16]{0,2,1:T(8,128)S(1)}, f32[16,32,16,16]{1,3,2,0:T(8,128)S(1)}, f32[32,16]{0,1:T(8,128)S(1)}, ...), condition=%wide.region_3.4_spmd, body=%wide.region_2.3_spmd.sunk | while | flops 16386 | bytes 362573 | solution.py:122
  465.3 10.5 %bitcast_multiply_fusion.4 = (f32[2048,512]{0,1:T(8,128)}, f32[2048,512]{0,1:T(8,128)}) fusion(f32[2048,512]{0,1:T(8,128)} %copy-done.6, f32[2048,512]{0,1:T(8,128)S(1)} %copy-done.5, f32[512]{0:T(512)S(1)} %dynamic_slice.64, f32[64,8,16,128]{3,2,1,0:T(8,128)} %bitcast.377, bf16[128,16,512]{0,2,1:T(8,128)(2,1)} %copy-done.16), kind=kLoop, calls=%fused_computation.99 | loop fusion | flops 5242880 | bytes 23070720 | tf_op jit(solution)/shard_map/mul | solution.py:227
  496.2 9.2 %copy_bitcast_fusion.5 = bf16[16,128,512]{1,2,0:T(8,128)(2,1)} fusion(f32[2,512]{0,1:T(8,128)S(1)} %bitcast.388, f32[2048,512]{0,1:T(8,128)} %get-tuple-element.495, f32[512]{0:T(512)S(1)} %bitcast.415, f32[512]{0:T(512)S(1)} %bitcast.413, f32[512]{0:T(512)S(1)} %bitcast.417), kind=kLoop, calls=%fused_computation.164 | loop fusion | flops 8388608 | bytes 6301696 | tf_op jit(solution)/shard_map/all_to_all | solution.py:316
  505.4 14.8 %all-to-all-done.5 = bf16[16,128,512]{1,2,0:T(8,128)(2,1)S(1)} async-done(((bf16[16,128,512]{1,2,0:T(8,128)(2,1)}), bf16[16,128,512]{1,2,0:T(8,128)(2,1)S(1)}, u32[]{:S(2)}, u32[]{:S(2)}) %all-to-all-start.5) | async-done | bytes 2097184 | tf_op jit(solution)/shard_map/all_to_all | solution.py:310
  524.7 11.0 %bitcast_multiply_fusion.2 = (f32[2048,512]{0,1:T(8,128)}, f32[2048,512]{0,1:T(8,128)S(1)}) fusion(f32[64,8,16,128]{3,2,1,0:T(8,128)} %bitcast.369, f32[2,512]{0,1:T(8,128)S(1)} %bitcast.386, f32[2048,512]{0,1:T(8,128)} %get-tuple-element.498, f32[512]{0:T(512)S(1)} %bitcast.407, f32[512]{0:T(512)S(1)} %bitcast.411, f32[512]{0:T(512)S(1)} %bitcast.409), kind=kLoop, calls=%fused_computation.96 | loop fusion | flops 8388608 | bytes 16787456 | tf_op jit(solution)/shard_map/mul | solution.py:249
  558.5 9.5 %copy_bitcast_fusion.6 = bf16[16,128,512]{1,2,0:T(8,128)(2,1)} fusion(f32[2,512]{0,1:T(8,128)S(1)} %bitcast.387, f32[2048,512]{0,1:T(8,128)} %get-tuple-element.493, f32[512]{0:T(512)S(1)} %bitcast.405, f32[512]{0:T(512)S(1)} %bitcast.403, f32[512]{0:T(512)S(1)} %bitcast.401), kind=kLoop, calls=%fused_computation.165 | loop fusion | flops 8388608 | bytes 6301696 | tf_op jit(solution)/shard_map/all_to_all | solution.py:315
  590.2 9.3 %bitcast_multiply_fusion.1 = (f32[2048,512]{0,1:T(8,128)S(1)}, f32[2048,512]{0,1:T(8,128)}) fusion(f32[2048,512]{0,1:T(8,128)} %get-tuple-element.508, f32[64,8,16,128]{3,2,1,0:T(8,128)} %bitcast.371, f32[2048,512]{0,1:T(8,128)} %get-tuple-element.509), kind=kLoop, calls=%fused_computation.93 | loop fusion | flops 2097152 | bytes 20971520 | tf_op jit(solution)/shard_map/mul | solution.py:254
  608.3 9.5 %copy_bitcast_fusion.7 = bf16[16,128,512]{1,2,0:T(8,128)(2,1)} fusion(f32[2,512]{0,1:T(8,128)S(1)} %bitcast.389, f32[2048,512]{0,1:T(8,128)} %get-tuple-element.511, f32[512]{0:T(512)S(1)} %bitcast.429, f32[512]{0:T(512)S(1)} %bitcast.425, f32[512]{0:T(512)S(1)} %bitcast.427), kind=kLoop, calls=%fused_computation.166 | loop fusion | flops 8388608 | bytes 6301696 | tf_op jit(solution)/shard_map/all_to_all | solution.py:314
  629.3 9.3 %copy_bitcast_fusion.8 = bf16[16,128,512]{1,2,0:T(8,128)(2,1)} fusion(f32[2,512]{0,1:T(8,128)S(1)} %bitcast.390, f32[2048,512]{0,1:T(8,128)} %copy-done.23, f32[512]{0:T(512)S(1)} %bitcast.419, f32[512]{0:T(512)S(1)} %bitcast.421, f32[512]{0:T(512)S(1)} %bitcast.423), kind=kLoop, calls=%fused_computation.167 | loop fusion | flops 8388608 | bytes 6301696 | tf_op jit(solution)/shard_map/all_to_all | solution.py:313
  638.6 23.1 %all-to-all-done.9 = bf16[16,128,512]{1,2,0:T(8,128)(2,1)} async-done(((bf16[16,128,512]{1,2,0:T(8,128)(2,1)}), bf16[16,128,512]{1,2,0:T(8,128)(2,1)}, u32[]{:S(2)}, u32[]{:S(2)}) %all-to-all-start.9) | async-done | bytes 2097184 | tf_op jit(solution)/shard_map/all_to_all | solution.py:314
  666.3 9.4 %copy_bitcast_fusion.9 = bf16[16,128,512]{1,2,0:T(8,128)(2,1)} fusion(f32[2,512]{0,1:T(8,128)S(1)} %bitcast.391, f32[2048,512]{0,1:T(8,128)} %get-tuple-element.491, f32[512]{0:T(512)S(1)} %bitcast.397, f32[512]{0:T(512)S(1)} %bitcast.399, f32[512]{0:T(512)S(1)} %bitcast.395), kind=kLoop, calls=%fused_computation.168 | loop fusion | flops 8388608 | bytes 6301696 | tf_op jit(solution)/shard_map/all_to_all | solution.py:312
  675.7 19.8 %all-to-all-done.8 = bf16[16,128,512]{1,2,0:T(8,128)(2,1)} async-done(((bf16[16,128,512]{1,2,0:T(8,128)(2,1)}), bf16[16,128,512]{1,2,0:T(8,128)(2,1)}, u32[]{:S(2)}, u32[]{:S(2)}) %all-to-all-start.8) | async-done | bytes 2097184 | tf_op jit(solution)/shard_map/all_to_all | solution.py:313
  718.7 9.4 %all-to-all-done.7 = bf16[16,128,512]{1,2,0:T(8,128)(2,1)} async-done(((bf16[16,128,512]{1,2,0:T(8,128)(2,1)}), bf16[16,128,512]{1,2,0:T(8,128)(2,1)}, u32[]{:S(2)}, u32[]{:S(2)}) %all-to-all-start.7) | async-done | bytes 2097184 | tf_op jit(solution)/shard_map/all_to_all | solution.py:312
  (399 shorter events, 431.3 us)
Async XLA Ops:
  0.6 141.7 %copy-start = (bf16[128,512]{1,0:T(8,128)(2,1)S(1)}, bf16[128,512]{1,0:T(8,128)(2,1)}, u32[]{:S(2)}) copy-start(bf16[128,512]{1,0:T(8,128)(2,1)} %param.28) | copy-start | bytes 393220
  4.8 39.1 %all-to-all-start.3 = ((bf16[128,16,512]{0,2,1:T(8,128)(2,1)}), bf16[128,16,512]{0,2,1:T(8,128)(2,1)S(1)}, u32[]{:S(2)}, u32[]{:S(2)}) async-start(bf16[128,16,512]{0,2,1:T(8,128)(2,1)} %bitcast.21), calls=%async_computation.3 | async-start | bytes 4194304 | tf_op jit(solution)/shard_map/all_to_all | solution.py:283
  45.2 33.0 %all-to-all-start.4 = ((bf16[128,16,512]{0,2,1:T(8,128)(2,1)}), bf16[128,16,512]{0,2,1:T(8,128)(2,1)S(1)}, u32[]{:S(2)}, u32[]{:S(2)}) async-start(bf16[128,16,512]{0,2,1:T(8,128)(2,1)} %bitcast.24), calls=%async_computation.4 | async-start | bytes 4194304 | tf_op jit(solution)/shard_map/all_to_all | solution.py:284
  78.2 33.0 %all-to-all-start.2 = ((bf16[128,16,512]{0,2,1:T(8,128)(2,1)}), bf16[128,16,512]{0,2,1:T(8,128)(2,1)}, u32[]{:S(2)}, u32[]{:S(2)}) async-start(bf16[128,16,512]{0,2,1:T(8,128)(2,1)} %bitcast.17), calls=%async_computation.2 | async-start | bytes 4194304 | tf_op jit(solution)/shard_map/all_to_all | solution.py:282
  111.1 45.8 %all-to-all-start.1 = ((bf16[128,16,512]{0,2,1:T(8,128)(2,1)}), bf16[128,16,512]{0,2,1:T(8,128)(2,1)}, u32[]{:S(2)}, u32[]{:S(2)}) async-start(bf16[128,16,512]{0,2,1:T(8,128)(2,1)} %bitcast.13), calls=%async_computation.1 | async-start | bytes 4194304 | tf_op jit(solution)/shard_map/all_to_all | solution.py:288
  118.1 35.3 %copy-start.39 = (f32[32,16]{1,0:T(8,128)}, f32[32,16]{1,0:T(8,128)S(1)}, u32[]{:S(2)}) copy-start(f32[32,16]{1,0:T(8,128)S(1)} %copy.178) | copy-start | bytes 6148
  157.0 39.9 %all-to-all-start = ((bf16[128,16,512]{0,2,1:T(8,128)(2,1)}), bf16[128,16,512]{0,2,1:T(8,128)(2,1)}, u32[]{:S(2)}, u32[]{:S(2)}) async-start(bf16[128,16,512]{0,2,1:T(8,128)(2,1)} %bitcast.9), calls=%async_computation | async-start | bytes 4194304 | tf_op jit(solution)/shard_map/all_to_all | solution.py:287
  172.2 34.8 %collective-permute-start = (bf16[3,2,512]{1,2,0:T(8,128)(2,1)S(1)}, bf16[3,2,512]{1,2,0:T(8,128)(2,1)}, u32[]{:S(2)}, u32[]{:S(2)}) collective-permute-start(bf16[3,2,512]{1,2,0:T(8,128)(2,1)S(1)} %pad_maximum_fusion.12), channel_id=1, source_target_pairs={{0,16},{16,32},{32,48},{48,64},{64,80},{80,96},{96,112},{1,17},{17... | collective-permute-start | bytes 18440 | tf_op jit(solution)/shard_map/ppermute | solution.py:17
  196.9 66.1 %all-to-all-start.6 = ((bf16[128,16,512]{0,2,1:T(8,128)(2,1)}), bf16[128,16,512]{0,2,1:T(8,128)(2,1)S(1)}, u32[]{:S(2)}, u32[]{:S(2)}) async-start(bf16[128,16,512]{0,2,1:T(8,128)(2,1)} %bitcast.382), calls=%async_computation.6 | async-start | bytes 4194304 | tf_op jit(solution)/shard_map/all_to_all | solution.py:290
  228.1 11.3 %collective-permute-start.1 = (f32[127,512]{0,1:T(8,128)S(1)}, f32[127,512]{0,1:T(8,128)S(1)}, u32[]{:S(2)}, u32[]{:S(2)}) collective-permute-start(f32[127,512]{0,1:T(8,128)S(1)} %slice.368), channel_id=1, source_target_pairs={{0,16},{16,32},{32,48},{48,64},{64,80},{80,96},{96,112},{1,17},{17... | collective-permute-start | bytes 780296 | tf_op jit(solution)/shard_map/ppermute | solution.py:17
  254.2 6.9 collective-permute-start.2
  263.0 107.9 %copy-start.16 = (bf16[128,16,512]{0,2,1:T(8,128)(2,1)}, bf16[128,16,512]{0,2,1:T(8,128)(2,1)S(1)}, u32[]{:S(2)}) copy-start(bf16[128,16,512]{0,2,1:T(8,128)(2,1)S(1)} %all-to-all-done.6) | copy-start | bytes 6291460
  480.0 40.2 %all-to-all-start.5 = ((bf16[16,128,512]{1,2,0:T(8,128)(2,1)}), bf16[16,128,512]{1,2,0:T(8,128)(2,1)S(1)}, u32[]{:S(2)}, u32[]{:S(2)}) async-start(bf16[16,128,512]{1,2,0:T(8,128)(2,1)} %copy_bitcast_fusion.10), calls=%async_computation.5 | async-start | bytes 4194304 | tf_op jit(solution)/shard_map/all_to_all | solution.py:310
  490.6 5.3 collective-permute-start.3
  520.2 63.1 %all-to-all-start.11 = ((bf16[16,128,512]{1,2,0:T(8,128)(2,1)}), bf16[16,128,512]{1,2,0:T(8,128)(2,1)}, u32[]{:S(2)}, u32[]{:S(2)}) async-start(bf16[16,128,512]{1,2,0:T(8,128)(2,1)} %copy_bitcast_fusion.5), calls=%async_computation.11 | async-start | bytes 4194304 | tf_op jit(solution)/shard_map/all_to_all | solution.py:316
  554.1 20.3 %collective-permute-start.4 = (f32[127,512]{0,1:T(8,128)S(1)}, f32[127,512]{0,1:T(8,128)S(1)}, u32[]{:S(2)}, u32[]{:S(2)}) collective-permute-start(f32[127,512]{0,1:T(8,128)S(1)} %slice.388), channel_id=1, source_target_pairs={{16,0},{32,16},{48,32},{64,48},{80,64},{96,80},{112,96},{17,1},{33... | collective-permute-start | bytes 780296 | tf_op jit(solution)/shard_map/ppermute | solution.py:17
  583.3 41.3 %all-to-all-start.10 = ((bf16[16,128,512]{1,2,0:T(8,128)(2,1)}), bf16[16,128,512]{1,2,0:T(8,128)(2,1)S(1)}, u32[]{:S(2)}, u32[]{:S(2)}) async-start(bf16[16,128,512]{1,2,0:T(8,128)(2,1)} %copy_bitcast_fusion.6), calls=%async_computation.10 | async-start | bytes 4194304 | tf_op jit(solution)/shard_map/all_to_all | solution.py:315
  602.8 5.3 collective-permute-start.5
  624.6 37.1 %all-to-all-start.9 = ((bf16[16,128,512]{1,2,0:T(8,128)(2,1)}), bf16[16,128,512]{1,2,0:T(8,128)(2,1)}, u32[]{:S(2)}, u32[]{:S(2)}) async-start(bf16[16,128,512]{1,2,0:T(8,128)(2,1)} %copy_bitcast_fusion.7), calls=%async_computation.9 | async-start | bytes 4194304 | tf_op jit(solution)/shard_map/all_to_all | solution.py:314
  629.2 37.1 %copy-start.46 = (f32[1,1,512]{2,1,0:T(1,128)S(1)}, f32[1,1,512]{2,1,0:T(1,128)}, u32[]{:S(2)}) copy-start(f32[1,1,512]{2,1,0:T(1,128)} %get-tuple-element.537) | copy-start | bytes 6148
  629.3 37.1 %copy-start.48 = (f32[1,1,512]{2,1,0:T(1,128)S(1)}, f32[1,1,512]{2,1,0:T(1,128)}, u32[]{:S(2)}) copy-start(f32[1,1,512]{2,1,0:T(1,128)} %get-tuple-element.543) | copy-start | bytes 6148
  629.3 37.1 %copy-start.50 = (f32[1,1,512]{2,1,0:T(1,128)S(1)}, f32[1,1,512]{2,1,0:T(1,128)}, u32[]{:S(2)}) copy-start(f32[1,1,512]{2,1,0:T(1,128)} %get-tuple-element.544) | copy-start | bytes 6148
  661.7 33.8 %all-to-all-start.8 = ((bf16[16,128,512]{1,2,0:T(8,128)(2,1)}), bf16[16,128,512]{1,2,0:T(8,128)(2,1)}, u32[]{:S(2)}, u32[]{:S(2)}) async-start(bf16[16,128,512]{1,2,0:T(8,128)(2,1)} %copy_bitcast_fusion.8), calls=%async_computation.8 | async-start | bytes 4194304 | tf_op jit(solution)/shard_map/all_to_all | solution.py:313
  695.5 32.7 %all-to-all-start.7 = ((bf16[16,128,512]{1,2,0:T(8,128)(2,1)}), bf16[16,128,512]{1,2,0:T(8,128)(2,1)}, u32[]{:S(2)}, u32[]{:S(2)}) async-start(bf16[16,128,512]{1,2,0:T(8,128)(2,1)} %copy_bitcast_fusion.9), calls=%async_computation.7 | async-start | bytes 4194304 | tf_op jit(solution)/shard_map/all_to_all | solution.py:312
  (72 other events, 696.8 us)
where the time goes:
time: 747 us; the launch traced here: 733 us
  other arithmetic  186 us (25%)
  waiting for transfers between devices  170 us (23%)
  local copies, waits for them, and re-layouts  166 us (22%)
  starting transfers between devices  85.2 us (11%)
  matrix products  72 us (10%)
  blocking collectives  49.7 us (7%)
    dot_general x14, matrix products, contract(): return jnp.einsum(pattern, first_operand, second_operand, precision=HIGHEST)  72 us
    unnamed x182, local copies, waits for them, and re-layouts  62.2 us
    all_gather x3, blocking collectives, prefix(): pieces = jax.tree.map(lambda part: lax.all_gather(part, axis), value)  49.7 us
    all_to_all x1, waiting for transfers between devices, per_device(): lax.all_to_all(mr_key, 'ch', split_axis=1, concat_axis=0, tiled=True)  26.4 us
    all_to_all x1, waiting for transfers between devices, per_device(): lax.all_to_all(mr_value, 'ch', split_axis=1, concat_axis=0, tiled=True)  24.7 us
    all_to_all x1, waiting for transfers between devices, per_device(): lax.all_to_all(results[3], 'ch', split_axis=0, concat_axis=1, tiled=True)  23.1 us
    all_to_all x1, waiting for transfers between devices, per_device(): lax.all_to_all(mr_query, 'ch', split_axis=1, concat_axis=0, tiled=True)  20.4 us
    all_to_all x1, waiting for transfers between devices, per_device(): lax.all_to_all(results[2], 'ch', split_axis=0, concat_axis=1, tiled=True)  19.8 us
  transfers between devices with their start and end apart: 18, of which 12 were waited for; matrix products, arithmetic and copies ran while one was open for 31% of the time, Pallas kernels for 0%

commit v1 on v0

v1 whole, which is shorter than its diff:
```python
import functools

import jax
import jax.numpy as jnp
from jax import lax
from jax.experimental import pallas as pl
from jax.experimental.pallas import tpu as pltpu
from jax.sharding import PartitionSpec as P

GROUP = 16
SHORT = 3
MR_TAPS = 128
MODES = 16
ROWS = 128
LANES = 128
TILE_GROUPS = LANES // GROUP
AXES = ("ctx", "ch")
BF16 = jnp.bfloat16
F32 = jnp.float32

MR_Q, MR_K, MR_V, LI_Q, LI_K, LI_V, SKIP, LAST_TAP, IMPULSE_0, IMPULSE_1 = 0, 3, 6, 9, 12, 15, 18, 19, 20, 21
TABLE_ROWS = 24


def lane_call(body, name, width, ins, outs, scratch, flops):
    channels = next(a.shape[1] for a, kind in ins if kind == "r")
    width = min(width, channels)
    tiles = width // LANES

    def spec(shape, kind):
        if kind == "r":
            return pl.BlockSpec((shape[0], width), lambda i: (0, i))
        if kind == "g":
            return pl.BlockSpec((width // GROUP, shape[1]), lambda i: (i, 0))
        return pl.BlockSpec((2 * tiles, 8, LANES), lambda i: (i, 0, 0))

    def view(ref, kind, t):
        if kind == "r":
            return ref.at[:, pl.ds(pl.multiple_of(t * LANES, LANES), LANES)]
        if kind == "g":
            return ref.at[pl.ds(pl.multiple_of(t * TILE_GROUPS, TILE_GROUPS), TILE_GROUPS), :]
        return ref.at[pl.ds(2 * t, 2)]

    kinds = [kind for _, kind in ins] + [kind for _, _, kind in outs]

    def kernel(*refs):
        arrays, extra = refs[: len(kinds)], refs[len(kinds) :]

        def step(t, unused):
            body(*[view(ref, kind, t) for ref, kind in zip(arrays, kinds)], *extra)
            return unused

        lax.fori_loop(0, tiles, step, 0)

    moved = sum(a.size * a.dtype.itemsize for a, _ in ins)
    out_shape = [jax.ShapeDtypeStruct(shape, dtype) for shape, dtype, _ in outs]
    moved += sum(s.size * s.dtype.itemsize for s in out_shape)
    return pl.pallas_call(
        kernel,
        name=name,
        grid=(channels // width,),
        in_specs=[spec(a.shape, kind) for a, kind in ins],
        out_specs=[spec(shape, kind) for shape, _, kind in outs],
        out_shape=out_shape,
        scratch_shapes=scratch,
        compiler_params=pltpu.CompilerParams(vmem_limit_bytes=32 * 1024 * 1024),
        cost_estimate=pl.CostEstimate(flops=flops, bytes_accessed=moved, transcendentals=0),
    )(*[a for a, _ in ins])


EXT = pltpu.VMEM((ROWS + 16, LANES), F32)


def turned(x, by):
    return pltpu.roll(x, by, 0) if by else x


def fill(ext, value, prev8=None, next8=None):
    ext[8 : 8 + ROWS, :] = value
    if prev8 is not None:
        ext[0:8, :] = prev8
    if next8 is not None:
        ext[8 + ROWS :, :] = next8


def taps(table, first):
    return [table[first + j : first + j + 1, :] for j in range(SHORT)]


def short_forward(ext, weights, rows=ROWS):
    return (
        weights[0] * ext[8 : 8 + rows, :]
        + weights[1] * ext[7 : 7 + rows, :]
        + weights[2] * ext[6 : 6 + rows, :]
    )


def short_backward(ext, weights):
    return (
        weights[0] * ext[8 : 8 + ROWS, :]
        + weights[1] * ext[9 : 9 + ROWS, :]
        + weights[2] * ext[10 : 10 + ROWS, :]
    )


def iota(shape, dim):
    return lax.broadcasted_iota(jnp.int32, shape, dim)


def circulant(base, g):
    row = jnp.broadcast_to(base[g : g + 1, :], (ROWS, LANES))
    return pltpu.roll(row, 0, 1, stride=1, stride_axis=0)


def paired(signal):
    odd = ((iota((ROWS, LANES), 1) // GROUP) % 2).astype(F32)
    upper = signal * (1.0 - odd).astype(signal.dtype)
    lower = signal * odd.astype(signal.dtype)
    return jnp.concatenate([upper, lower], 0)


def pick_pairs(products, rows):
    pair = iota((rows, LANES), 1) // (2 * GROUP)
    total = products[0:rows]
    for p in range(1, TILE_GROUPS // 2):
        total = jnp.where(pair == p, products[p * rows : (p + 1) * rows], total)
    return total


def toeplitz_product(base_ref, keep, signal, tables):
    base = base_ref[...]
    for g in range(TILE_GROUPS):
        p, half = g // 2, g % 2
        table = jnp.where(keep, circulant(base, g), 0.0).astype(BF16)
        tables[p * ROWS : (p + 1) * ROWS, half * LANES : (half + 1) * LANES] = table
    products = jnp.dot(tables[...], paired(signal), preferred_element_type=F32)
    return pick_pairs(products, ROWS)


def own_group():
    return (iota((LANES, LANES), 0) // MODES == iota((LANES, LANES), 1) // GROUP).astype(F32)


def spread(state):
    return (jnp.concatenate([state] * TILE_GROUPS, 0) * own_group()).astype(BF16)


def absorb(powers, signal):
    every = lax.dot_general(
        powers.astype(BF16), signal, (((0,), (0,)), ((), ())), preferred_element_type=F32
    )
    return (every * own_group()).reshape(TILE_GROUPS, MODES, LANES).sum(0)


def store_state(ref, state):
    ref[...] = state.reshape(2, 8, LANES)


def load_state(ref):
    return ref[...].reshape(MODES, LANES)


def product_one_body(key, value, prev_kv, table, out, ext_k, ext_v):
    weights = table[...]
    margin = prev_kv[...].astype(F32)
    fill(ext_k, key[...].astype(F32), turned(margin, 4))
    fill(ext_v, value[...].astype(F32), margin)
    keys_one = short_forward(ext_k, taps(weights, MR_K))
    value_one = short_forward(ext_v, taps(weights, MR_V))
    out[...] = (keys_one * value_one).astype(BF16)


def upstream_body(li_query, upstream, prev_rest, table, rate, cotangent, state, ext):
    weights = table[...]
    margin = prev_rest[...].astype(F32)
    fill(ext, li_query[...].astype(F32), turned(margin, 2))
    query_two = short_forward(ext, taps(weights, LI_Q))
    rounded = (upstream[...].astype(F32) * query_two).astype(BF16)
    cotangent[...] = rounded
    position = iota((ROWS, LANES), 0).astype(F32)
    store_state(state, absorb(jnp.exp(-rate[...] * position), rounded))


def long_back_near_body(cotangent, table, base, out, tables):
    keep = iota((ROWS, LANES), 1) >= iota((ROWS, LANES), 0)
    signal = cotangent[...]
    near = toeplitz_product(base, keep, signal, tables)
    out[...] = near + table[SKIP : SKIP + 1, :] * signal.astype(F32)


def medium_near_body(
    signal, query, prev_kv, prev_rest, table, base, out, tail, ext, tables
):
    weights = table[...]
    keep = iota((ROWS, LANES), 1) <= iota((ROWS, LANES), 0)
    near = toeplitz_product(base, keep, signal[...], tables)
    out[...] = near
    margin = prev_kv[...].astype(F32)
    w_k, w_v = taps(weights, MR_K), taps(weights, MR_V)
    key_before = w_k[0] * margin[3:4] + w_k[1] * margin[2:3] + w_k[2] * margin[1:2]
    value_before = w_v[0] * margin[7:8] + w_v[1] * margin[6:7] + w_v[2] * margin[5:6]
    before = (key_before * value_before).astype(BF16).astype(F32)
    far = weights[LAST_TAP : LAST_TAP + 1] * before
    fill(ext, query[...].astype(F32), turned(prev_rest[...].astype(F32), 4))
    query_one = short_forward(ext, taps(weights, MR_Q))
    first = query_one[ROWS - 2 : ROWS - 1] * (near[ROWS - 2 : ROWS - 1] + far)
    second = query_one[ROWS - 1 :] * near[ROWS - 1 :]
    tail[0:1, :] = first.astype(BF16).astype(F32)
    tail[1:2, :] = second.astype(BF16).astype(F32)


def long_back_body(
    near, closing, cotangent, li_query, li_key, query, prev_rest, next_rest, table, rate, residue,
    grad_two, grad_two_after, mixed_grad, out, mixed_head, out_head,
    ext_q, ext_k, ext_g, ext_o,
):
    weights = table[...]
    before = prev_rest[...].astype(F32)
    after = next_rest[...].astype(F32)[0:8]
    fill(ext_q, li_query[...].astype(F32), None, after)
    w = taps(weights, LI_Q)
    base = 8 + ROWS
    query_after = w[0] * ext_q[base : base + 8, :] + w[1] * ext_q[base - 1 : base + 7, :] + w[2] * ext_q[base - 2 : base + 6, :]
    cot_after = turned(after, 4) * query_after
    state = load_state(closing)
    distance = (ROWS - iota((ROWS + 16, LANES), 0)).astype(F32)
    emit = (residue[...] * jnp.exp(-rate[...] * distance)).astype(BF16)
    emitted = jnp.dot(emit, spread(state), preferred_element_type=F32)
    later = jnp.dot(emit[ROWS:], spread(state - cot_after[0:1]), preferred_element_type=F32)
    skip = weights[SKIP : SKIP + 1]
    own = near[...] + emitted[0:ROWS]
    at_row = iota((8, LANES), 0)
    past = jnp.where(at_row == 0, emitted[ROWS : ROWS + 8], later[0:8]) + skip * cot_after
    past = jnp.where(at_row < 2, past, 0.0)
    grad_two[...] = own.astype(BF16)
    grad_two_after[...] = past
    fill(ext_k, li_key[...].astype(F32), before, turned(after, 6))
    keys_two = short_forward(ext_k, taps(weights, LI_K), ROWS + 8)
    fill(ext_g, own * keys_two[0:ROWS], None, past * keys_two[ROWS:])
    mixed = short_backward(ext_g, taps(weights, LI_V))
    fill(ext_o, query[...].astype(F32), turned(before, 4))
    conv_grad = mixed * short_forward(ext_o, taps(weights, MR_Q))
    mixed_grad[...] = mixed.astype(BF16)
    mixed_head[...] = mixed[0:2]
    out[...] = conv_grad.astype(BF16)
    out_head[...] = conv_grad[0:1]


def medium_far_body(
    before, near, query, li_key, prev_rest, prev_tail, table, base, rate,
    conv_one, value_two, prod_two, state, head, ext_q, ext_k, ext_m, tables,
):
    weights = table[...]
    keep = iota((ROWS, LANES), 1) > iota((ROWS, LANES), 0)
    conv = near[...] + toeplitz_product(base, keep, before[...], tables)
    margin = prev_rest[...].astype(F32)
    fill(ext_q, query[...].astype(F32), turned(margin, 4))
    query_one = short_forward(ext_q, taps(weights, MR_Q))
    fill(ext_m, (query_one * conv).astype(BF16).astype(F32))
    ext_m[6:8, :] = prev_tail[...]
    value = short_forward(ext_m, taps(weights, LI_V))
    fill(ext_k, li_key[...].astype(F32), margin)
    keys_two = short_forward(ext_k, taps(weights, LI_K))
    product = (keys_two * value).astype(BF16)
    conv_one[...] = conv.astype(BF16)
    value_two[...] = value.astype(BF16)
    prod_two[...] = product
    head[0:2, :] = product[0:16].astype(F32)[0:2]
    head[2:4, :] = value[0:2]
    head[4:6, :] = conv[0:2]
    position = (ROWS - 1 - iota((ROWS, LANES), 0)).astype(F32)
    store_state(state, absorb(jnp.exp(-rate[...] * position), product))


def long_near_body(
    prod_two, grad_two, grad_two_after, value_two, mixed_grad, mixed_after, conv_one, next_head,
    table, base, near, grad_li_key, grad_mr_query, ext_k, ext_q, tables,
):
    weights = table[...]
    keep = iota((ROWS, LANES), 1) <= iota((ROWS, LANES), 0)
    signal = prod_two[...]
    product = toeplitz_product(base, keep, signal, tables)
    near[...] = product + weights[SKIP : SKIP + 1] * signal.astype(F32)
    fill(ext_k, grad_two[...].astype(F32) * value_two[...].astype(F32))
    ext_k[8 + ROWS : 10 + ROWS, :] = grad_two_after[0:2, :] * next_head[2:4, :]
    grad_li_key[...] = short_backward(ext_k, taps(weights, LI_K)).astype(BF16)
    fill(ext_q, mixed_grad[...].astype(F32) * conv_one[...].astype(F32))
    ext_q[8 + ROWS : 10 + ROWS, :] = mixed_after[...] * next_head[4:6, :]
    grad_mr_query[...] = short_backward(ext_q, taps(weights, MR_Q)).astype(BF16)


def long_body(
    near, start, end, li_query, upstream, prev_rest, next_rest, next_head, table, rate, residue,
    out, grad_li_query, ext_q, ext_g,
):
    weights = table[...]
    distance = (iota((ROWS + 16, LANES), 0) + 1).astype(F32)
    emit = (residue[...] * jnp.exp(-rate[...] * distance)).astype(BF16)
    emitted = jnp.dot(emit, spread(load_state(start)), preferred_element_type=F32)
    conv = near[...] + emitted[0:ROWS]
    margin = prev_rest[...].astype(F32)
    fill(ext_q, li_query[...].astype(F32), turned(margin, 2))
    query_two = short_forward(ext_q, taps(weights, LI_Q))
    out[...] = (query_two * conv).astype(BF16)
    ended = jnp.dot(emit[0:16], spread(load_state(end)), preferred_element_type=F32)
    at_once = weights[IMPULSE_0 : IMPULSE_0 + 1] + weights[SKIP : SKIP + 1]
    first, second = next_head[0:1, :], next_head[1:2, :]
    past = emitted[ROWS : ROWS + 8] + ended[0:8]
    past_first = past[0:1] + at_once * first
    past_second = past[1:2] + weights[IMPULSE_1 : IMPULSE_1 + 1] * first + at_once * second
    after = turned(next_rest[...].astype(F32)[0:8], 4)
    fill(ext_g, upstream[...].astype(F32) * conv)
    ext_g[8 + ROWS : 9 + ROWS, :] = after[0:1] * past_first
    ext_g[9 + ROWS : 10 + ROWS, :] = after[1:2] * past_second
    grad_li_query[...] = short_backward(ext_g, taps(weights, LI_Q)).astype(BF16)


def medium_back_near_body(cotangent, base, out, tables):
    keep = iota((ROWS, LANES), 1) >= iota((ROWS, LANES), 0)
    out[...] = toeplitz_product(base, keep, cotangent[...], tables)


def medium_back_body(
    near, after, after_next, key, value, prev_kv, next_rest, table, base_ref,
    grad_key, grad_value, ext_k, ext_v, ext_gk, ext_gv, tables,
):
    weights = table[...]
    base = base_ref[...]
    row, lane = iota((ROWS, LANES), 0), iota((ROWS, LANES), 1)
    rows = ROWS + 16
    for g in range(TILE_GROUPS):
        p, half = g // 2, g % 2
        whole = circulant(base, g)
        at = slice(half * LANES, (half + 1) * LANES)
        tables[p * rows : p * rows + ROWS, at] = jnp.where(lane < row, whole, 0.0).astype(BF16)
        tables[p * rows + ROWS : (p + 1) * rows, at] = jnp.where(
            lane[0:16] >= row[0:16], whole[0:16], 0.0
        ).astype(BF16)
    products = pick_pairs(
        jnp.dot(tables[...], paired(after[...]), preferred_element_type=F32), rows
    )
    grad = near[...] + products[0:ROWS]
    beyond = weights[LAST_TAP : LAST_TAP + 1] * after_next[...].astype(BF16).astype(F32)
    at_row = iota((8, LANES), 0)
    past = products[ROWS : ROWS + 8] + jnp.where(at_row == 1, beyond, 0.0)
    before = prev_kv[...].astype(F32)
    following = next_rest[...].astype(F32)
    fill(ext_k, key[...].astype(F32), turned(before, 4), turned(following[0:8], 2))
    fill(ext_v, value[...].astype(F32), before, following[8:16])
    keys_one = short_forward(ext_k, taps(weights, MR_K), ROWS + 8)
    value_one = short_forward(ext_v, taps(weights, MR_V), ROWS + 8)
    fill(ext_gk, grad * value_one[0:ROWS], None, past * value_one[ROWS:])
    fill(ext_gv, grad * keys_one[0:ROWS], None, past * keys_one[ROWS:])
    grad_key[...] = short_backward(ext_gk, taps(weights, MR_K)).astype(BF16)
    grad_value[...] = short_backward(ext_gv, taps(weights, MR_V)).astype(BF16)


def scan_states(states, rates, backward):
    count = states.shape[0]

    def kernel(states_ref, rates_ref, out_ref):
        decay = jnp.exp(rates_ref[...] * (-float(ROWS)))

        def step(k, carried):
            b = count - 1 - k if backward else k
            out_ref[b] = carried
            return decay * carried + states_ref[b]

        lax.fori_loop(0, count, step, jnp.zeros((8, LANES), F32), unroll=8)

    return pl.pallas_call(
        kernel,
        name="scan_back" if backward else "scan_forward",
        out_shape=jax.ShapeDtypeStruct(states.shape, F32),
        in_specs=[pl.BlockSpec(memory_space=pltpu.VMEM)] * 2,
        out_specs=pl.BlockSpec(memory_space=pltpu.VMEM),
        cost_estimate=pl.CostEstimate(flops=0, bytes_accessed=8 * states.size, transcendentals=0),
    )(states, rates)


def sent(array, by):
    size = lax.axis_size(AXES)
    pairs = [(i, i + by) for i in range(size) if 0 <= i + by < size]
    return lax.ppermute(array, AXES, pairs)


def exchanged(array):
    return lax.all_to_all(array, AXES, split_axis=0, concat_axis=0, tiled=True)


def by_channel(per_group):
    return jnp.repeat(per_group, GROUP)[None, :]


def reversed_base(base):
    return jnp.concatenate([base[:, :1], base[:, :0:-1]], 1)


def per_device(
    mr_query, mr_key, mr_value, li_query, li_key, upstream,
    mr_short, li_short, mr_filter, li_rate, li_residue, li_skip,
):
    channels = mr_query.shape[1]
    tiles = channels // LANES
    devices = lax.axis_size(AXES)
    assert mr_query.shape[0] == ROWS and devices == 2 * tiles
    rows = (ROWS, channels)
    states = (2 * tiles, 8, LANES)

    prev_kv = sent(jnp.concatenate([mr_key[ROWS - 4 :], mr_value[ROWS - 4 :]], 0), 1)
    prev_rest = sent(
        jnp.concatenate([mr_query[ROWS - 4 :], li_query[ROWS - 2 :], li_key[ROWS - 2 :]], 0), 1
    )
    next_rest = sent(
        jnp.concatenate(
            [li_query[:2], li_key[:2], upstream[:2], mr_key[:2], mr_value[:2],
             jnp.zeros((6, channels), BF16)], 0
        ),
        -1,
    )

    positions = jnp.arange(MR_TAPS, dtype=F32)
    impulse = jnp.sum(
        li_residue[:, :, None] * jnp.exp(-li_rate[:, :, None] * positions), axis=1
    )
    taps_by_group = mr_filter.astype(F32).T
    base_medium_back = taps_by_group
    base_medium = reversed_base(taps_by_group)
    base_long_back = impulse
    base_long = reversed_base(impulse)
    table = jnp.concatenate(
        [
            mr_short.reshape(9, channels).astype(F32),
            li_short.reshape(9, channels).astype(F32),
            li_skip[None, :],
            by_channel(taps_by_group[:, MR_TAPS - 1]),
            by_channel(impulse[:, 0]),
            by_channel(impulse[:, 1]),
            jnp.zeros((TABLE_ROWS - 22, channels), F32),
        ],
        0,
    )
    rate = li_rate.reshape(1, channels)
    residue = li_residue.reshape(1, channels)
    me = lax.axis_index(AXES)
    my_rates = lax.dynamic_slice(
        li_rate, ((me // 2) * TILE_GROUPS, (me % 2) * 8), (TILE_GROUPS, 8)
    )
    my_rates = jnp.repeat(my_rates.T, GROUP, axis=1)

    wide = pltpu.VMEM((TILE_GROUPS // 2 * ROWS, 2 * LANES), BF16)
    wider = pltpu.VMEM((TILE_GROUPS // 2 * (ROWS + 16), 2 * LANES), BF16)
    heavy = 2 * 512 * 128 * 256 * 128 * 2
    call = functools.partial(lane_call)

    (signal_one,) = call(
        product_one_body, "product_one", 1024,
        [(mr_key, "r"), (mr_value, "r"), (prev_kv, "r"), (table, "r")],
        [(rows, BF16, "r")], [EXT, EXT], 0,
    )
    before_one = sent(signal_one, 1)

    cotangent, state_back = call(
        upstream_body, "upstream", 1024,
        [(li_query, "r"), (upstream, "r"), (prev_rest, "r"), (table, "r"), (rate, "r")],
        [(rows, BF16, "r"), (states, F32, "s")], [EXT], 0,
    )
    gathered_back = exchanged(state_back)

    (near_back,) = call(
        long_back_near_body, "long_back_near", 1024,
        [(cotangent, "r"), (table, "r"), (base_long_back, "g")],
        [(rows, F32, "r")], [wide], heavy,
    )
    near_one, tail = call(
        medium_near_body, "medium_near", 1024,
        [(signal_one, "r"), (mr_query, "r"), (prev_kv, "r"), (prev_rest, "r"), (table, "r"),
         (base_medium, "g")],
        [(rows, F32, "r"), ((2, channels), F32, "r")], [EXT, wide], heavy,
    )
    prev_tail = sent(tail, 1)

    closing = exchanged(scan_states(gathered_back, my_rates, True))

    grad_two, grad_two_after, mixed_grad, conv_grad, mixed_head, conv_head = call(
        long_back_body, "long_back", 1024,
        [(near_back, "r"), (closing, "s"), (cotangent, "r"), (li_query, "r"), (li_key, "r"),
         (mr_query, "r"), (prev_rest, "r"), (next_rest, "r"), (table, "r"), (rate, "r"),
         (residue, "r")],
        [(rows, BF16, "r"), ((8, channels), F32, "r"), (rows, BF16, "r"), (rows, BF16, "r"),
         ((2, channels), F32, "r"), ((1, channels), F32, "r")],
        [EXT, EXT, EXT, EXT], 0,
    )
    after_one = sent(conv_grad, -1)
    mixed_after = sent(mixed_head, -1)
    after_next = sent(conv_head, -2)

    conv_one, value_two, prod_two, state, head = call(
        medium_far_body, "medium_far", 1024,
        [(before_one, "r"), (near_one, "r"), (mr_query, "r"), (li_key, "r"), (prev_rest, "r"),
         (prev_tail, "r"), (table, "r"), (base_medium, "g"), (rate, "r")],
        [(rows, BF16, "r"), (rows, BF16, "r"), (rows, BF16, "r"), (states, F32, "s"),
         ((6, channels), F32, "r")],
        [EXT, EXT, EXT, wide], heavy,
    )
    next_head = sent(head, -1)
    gathered = exchanged(state)

    near_two, grad_li_key, grad_mr_query = call(
        long_near_body, "long_near", 1024,
        [(prod_two, "r"), (grad_two, "r"), (grad_two_after, "r"), (value_two, "r"),
         (mixed_grad, "r"), (mixed_after, "r"), (conv_one, "r"), (next_head, "r"), (table, "r"),
         (base_long, "g")],
        [(rows, F32, "r"), (rows, BF16, "r"), (rows, BF16, "r")], [EXT, EXT, wide], heavy,
    )
    (near_grad,) = call(
        medium_back_near_body, "medium_back_near", 1024,
        [(conv_grad, "r"), (base_medium_back, "g")],
        [(rows, F32, "r")], [wide], heavy,
    )

    start = exchanged(scan_states(gathered, my_rates, False))

    output, grad_li_query = call(
        long_body, "long_forward", 1024,
        [(near_two, "r"), (start, "s"), (state, "s"), (li_query, "r"), (upstream, "r"),
         (prev_rest, "r"), (next_rest, "r"), (next_head, "r"), (table, "r"), (rate, "r"),
         (residue, "r")],
        [(rows, BF16, "r"), (rows, BF16, "r")], [EXT, EXT], 0,
    )
    grad_mr_key, grad_mr_value = call(
        medium_back_body, "medium_back", 1024,
        [(near_grad, "r"), (after_one, "r"), (after_next, "r"), (mr_key, "r"), (mr_value, "r"),
         (prev_kv, "r"), (next_rest, "r"), (table, "r"), (base_medium_back, "g")],
        [(rows, BF16, "r"), (rows, BF16, "r")], [EXT, EXT, EXT, EXT, wider], heavy,
    )
    return (output, grad_mr_query, grad_mr_key, grad_mr_value, grad_li_query, grad_li_key)


def solution(mesh):
    split = P(("ctx", "ch"), None)
    return jax.shard_map(
        per_device,
        mesh=mesh,
        in_specs=(split,) * 6 + (P(),) * 6,
        out_specs=(split,) * 6,
        check_vma=False,
    )
```

time: 747 us -> 390 us (0.52); the launches traced: 733 us -> 388 us
  Pallas kernels: 0 us -> 199 us
  other arithmetic: 186 us -> 11.2 us
  waiting for transfers between devices: 170 us -> 18 us
  local copies, waits for them, and re-layouts: 166 us -> 82.5 us
  matrix products: 72 us -> 0 us
  blocking collectives: 49.7 us -> 0 us
  starting transfers between devices: 85.2 us -> 75.5 us
    pallas_call x0 -> x12, Pallas kernels: none -> 199 us  [the longest x10 195 us: lane_call(): pl.pallas_call(kernel, name=name, grid=(channels // width,), in_specs=[sp...]
    all_to_all x12 -> x4, waiting for transfers between devices: 162 us -> 0.01 us  [exchanged(): return lax.all_to_all(array, AXES, split_axis=0, concat_axis=0, tiled=True)]
    dot_general x14 -> x0, matrix products: 72 us -> none  [contract(): return jnp.einsum(pattern, first_operand, second_operand, precision=HIGHEST)]
    mul x8 -> x0, other arithmetic: 59.6 us -> none  [the longest x1 11.9 us: operator_pair(): keys_two_grad = prod_two_grad * value_two]
    all_to_all x8 -> x0, other arithmetic: 58.3 us -> none  [the longest x1 9.53 us: per_device(): lax.all_to_all(results[3], 'ch', split_axis=0, concat_axis=1, tiled=True)]
    all_gather x3 -> x0, blocking collectives: 49.7 us -> none  [prefix(): pieces = jax.tree.map(lambda part: lax.all_gather(part, axis), value)]
    all_to_all x12 -> x4, starting transfers between devices: 68.1 us -> 35.3 us  [exchanged(): return lax.all_to_all(array, AXES, split_axis=0, concat_axis=0, tiled=True)]
    add x34 -> x0, other arithmetic: 31.3 us -> none  [the longest x16 15.4 us: advance(): return (block_decay[:, :, None] * carried + end_state, carried)]
  transfers between devices with their start and end apart: 18 -> 13, of which waited for: 12 -> 1; matrix products, arithmetic and copies ran while one was open for 31% -> 11% of each run, Pallas kernels for 0% -> 44%
where the time goes in v1:
time: 390 us; the launch traced here: 388 us
  Pallas kernels  199 us (51%)
  local copies, waits for them, and re-layouts  82.5 us (21%)
  starting transfers between devices  75.5 us (19%)
  waiting for transfers between devices  18 us (5%)
  other arithmetic  11.2 us (3%)
    pallas_call x10, Pallas kernels, lane_call(): pl.pallas_call(kernel, name=name, grid=(channels // width,), in_specs=[sp...  195 us
    unnamed x97, local copies, waits for them, and re-layouts  49.7 us
    ppermute x9, starting transfers between devices, sent(): return lax.ppermute(array, AXES, pairs)  40.2 us
    all_to_all x4, starting transfers between devices, exchanged(): return lax.all_to_all(array, AXES, split_axis=0, concat_axis=0, tiled=True)  35.3 us
    ppermute x9, waiting for transfers between devices, sent(): return lax.ppermute(array, AXES, pairs)  18 us
  transfers between devices with their start and end apart: 13, of which 1 were waited for; matrix products, arithmetic and copies ran while one was open for 11% of the time, Pallas kernels for 44%

profile of v1, /device:TPU:1, one launch (start us, length us, event | category | flops | bytes accessed | tf_op | source)
XLA Modules:
  0.0 387.6 jit_solution(14347394793448612079)
XLA Ops:
  3.3 4.0 %collective-permute-start = (bf16[8,8192]{1,0:T(8,128)(2,1)}, bf16[8,8192]{1,0:T(8,128)(2,1)}, u32[]{:S(2)}, u32[]{:S(2)}) collective-permute-start(bf16[8,8192]{1,0:T(8,128)(2,1)} %pad_maximum_fusion.2), channel_id=1, source_target_pairs={{0,1},{1,2},{2,3},{3,4},{4,5},{5,6},{6,7},{7,8},{8,9},{9,10},{10,1... | collective-permute-start | bytes 393224 | tf_op jit(solution)/shard_map/ppermute | solution.py:384
  13.5 6.0 %multiply_reduce_fusion.refs_2_ = f32[512,128]{1,0:T(8,128)S(1)} fusion(f32[512,16]{1,0:T(8,128)S(1)} %copy.30, f32[512,16]{1,0:T(8,128)S(1)} %copy.29), kind=kLoop, calls=%fused_computation | loop fusion | flops 3080192 | bytes 327680 | tf_op jit(solution)/shard_map/reduce_sum | solution.py:423
  25.4 5.2 %concatenate.19.refs_3_.refs_4_.refs_6_.refs_1_.refs_8_.refs_7_ = f32[24,8192]{1,0:T(8,128)S(1)} concatenate(f32[9,8192]{1,0:T(8,128)} %reshape.33, f32[9,8192]{1,0:T(8,128)} %reshape.34, f32[1,8192]{1,0:T(1,128)} %bitcast.5, f32[1,8192]{1,0:T(1,128)S(1)} %broadcast_in_dim_reshape.9, f32[1,8192]{1,0:T(1,128)} %broadcast_in_dim_reshape.10, f32[1,8192]{1,0:T(1,128)} %broadcast_in_dim_reshape.11, ...), dimensions={0} | concatenate | bytes 1572864 | tf_op jit(solution)/shard_map/concatenate | solution.py:431
  33.8 6.4 %product_one.1.refs_0_ = bf16[128,8192]{1,0:T(8,128)(2,1)} custom-call(bf16[128,8192]{1,0:T(8,128)(2,1)S(1)} %copy-done.7, bf16[128,8192]{1,0:T(8,128)(2,1)S(1)} %copy-done.9, bf16[8,8192]{1,0:T(8,128)(2,1)} %collective-permute-done.refs_2_.refs_5_, f32[24,8192]{1,0:T(8,128)S(1)} %concatenate.19.refs_3_.refs_4_.refs_6_.refs_1_.refs_8_.refs_7_), custom_call_target="tpu_custom_call" | custom-call | bytes 7208960 | tf_op jit(solution)/shard_map/product_one/pallas_call | solution.py:58
  40.2 3.2 collective-permute-start.1
  47.8 3.2 concatenate.22
  51.0 6.0 %collective-permute-start.4 = (bf16[16,8192]{1,0:T(8,128)(2,1)}, bf16[16,8192]{1,0:T(8,128)(2,1)}, u32[]{:S(2)}, u32[]{:S(2)}) collective-permute-start(bf16[16,8192]{1,0:T(8,128)(2,1)} %concatenate.22), channel_id=1, source_target_pairs={{1,0},{2,1},{3,2},{4,3},{5,4},{6,5},{7,6},{8,7},{9,8},{10,9},{11,1... | collective-permute-start | bytes 786440 | tf_op jit(solution)/shard_map/ppermute | solution.py:384
  72.5 18.0 %collective-permute-done.2.refs_3_.refs_4_.refs_2_.refs_6_.refs_5_ = bf16[8,8192]{1,0:T(8,128)(2,1)} collective-permute-done((bf16[8,8192]{1,0:T(8,128)(2,1)}, bf16[8,8192]{1,0:T(8,128)(2,1)}, u32[]{:S(2)}, u32[]{:S(2)}) %collective-permute-start.2) | collective-permute-done | bytes 131104 | tf_op jit(solution)/shard_map/ppermute | solution.py:384
  92.1 14.6 %upstream.1 = (bf16[128,8192]{1,0:T(8,128)(2,1)S(1)}, f32[128,8,128]{2,1,0:T(8,128)S(1)}) custom-call(bf16[128,8192]{1,0:T(8,128)(2,1)S(1)} %copy-done, bf16[128,8192]{1,0:T(8,128)(2,1)S(1)} %copy-done.1, bf16[8,8192]{1,0:T(8,128)(2,1)} %collective-permute-done.2.refs_3_.refs_4_.refs_2_.refs_6_.refs_5_, ...), custom_call_target="tpu_custom_call" | custom-call | bytes 7766016 | tf_op jit(solution)/shard_map/upstream/pallas_call | solution.py:58
  108.8 12.9 %all-to-all-start = ((f32[128,8,128]{2,1,0:T(8,128)}), f32[128,8,128]{2,1,0:T(8,128)}, u32[]{:S(2)}, u32[]{:S(2)}) async-start(f32[128,8,128]{2,1,0:T(8,128)} %copy-done.21), calls=%async_computation | async-start | bytes 1048576 | tf_op jit(solution)/shard_map/all_to_all | solution.py:388
  124.3 21.9 %medium_near.1 = (f32[128,8192]{1,0:T(8,128)S(1)}, f32[2,8192]{1,0:T(2,128)}) custom-call(bf16[128,8192]{1,0:T(8,128)(2,1)} %product_one.1.refs_0_, bf16[128,8192]{1,0:T(8,128)(2,1)S(1)} %copy-done.11, bf16[8,8192]{1,0:T(8,128)(2,1)} %collective-permute-done.refs_2_.refs_5_, bf16[8,8192]{1,0:T(8,128)(2,1)} %collective-permute-done.2.refs_3_.refs_4_.refs_2_.refs_6_.refs_5_, ...), custom_call_target="tpu_custom_call" | custom-call | flops 8589934592 | bytes 9764864 | tf_op jit(solution)/shard_map/medium_near/pallas_call | solution.py:58
  148.2 3.3 collective-permute-start.3
  153.6 10.1 %all-to-all-start.1 = ((f32[128,8,128]{2,1,0:T(8,128)}), f32[128,8,128]{2,1,0:T(8,128)}, u32[]{:S(2)}, u32[]{:S(2)}) async-start(f32[128,8,128]{2,1,0:T(8,128)} %scan_back.1), calls=%async_computation.1 | async-start | bytes 1048576 | tf_op jit(solution)/shard_map/all_to_all | solution.py:388
  165.3 19.9 %long_back_near.1.refs_0_ = f32[128,8192]{1,0:T(8,128)S(1)} custom-call(bf16[128,8192]{1,0:T(8,128)(2,1)S(1)} %copy-done.17, f32[24,8192]{1,0:T(8,128)S(1)} %concatenate.19.refs_3_.refs_4_.refs_6_.refs_1_.refs_8_.refs_7_, f32[512,128]{1,0:T(8,128)S(1)} %multiply_reduce_fusion.refs_2_), custom_call_target="tpu_custom_call" | custom-call | flops 8589934592 | bytes 7340032 | tf_op jit(solution)/shard_map/long_back_near/pallas_call | solution.py:58
  194.2 16.3 %long_back.1 = (bf16[128,8192]{1,0:T(8,128)(2,1)S(1)}, f32[8,8192]{1,0:T(8,128)S(1)}, bf16[128,8192]{1,0:T(8,128)(2,1)S(1)}, bf16[128,8192]{1,0:T(8,128)(2,1)}, f32[2,8192]{1,0:T(2,128)}, /*index=5*/f32[1,8192]{1,0:T(1,128)}) custom-call(f32[128,8192]{1,0:T(8,128)S(1)} %copy-done.4, f32[128,8,128]{2,1,0:T(8,128)} %all-to-all-done.1.refs_1_, ...), custom_call_target="tpu_custom_call" | custom-call | bytes 21004288 | tf_op jit(solution)/shard_map/long_back/pallas_call | solution.py:58
  213.8 7.7 %collective-permute-start.5 = (f32[2,8192]{1,0:T(2,128)}, f32[2,8192]{1,0:T(2,128)S(1)}, u32[]{:S(2)}, u32[]{:S(2)}) collective-permute-start(f32[2,8192]{1,0:T(2,128)} %get-tuple-element.37), channel_id=1, source_target_pairs={{1,0},{2,1},{3,2},{4,3},{5,4},{6,5},{7,6},{8,7},{9,8},{10,9},{11,1... | collective-permute-start | bytes 196616 | tf_op jit(solution)/shard_map/ppermute | solution.py:384
  224.3 32.6 %medium_far.1 = (bf16[128,8192]{1,0:T(8,128)(2,1)S(1)}, bf16[128,8192]{1,0:T(8,128)(2,1)S(1)}, bf16[128,8192]{1,0:T(8,128)(2,1)S(1)}, f32[128,8,128]{2,1,0:T(8,128)S(1)}, f32[6,8192]{1,0:T(8,128)}) custom-call(bf16[128,8192]{1,0:T(8,128)(2,1)} %collective-permute-done.1.refs_0_, f32[128,8192]{1,0:T(8,128)S(1)} %copy-done.34, ...), custom_call_target="tpu_custom_call" | custom-call | flops 8589934592 | bytes 18776064 | tf_op jit(solution)/shard_map/medium_far/pallas_call | solution.py:58
  264.1 7.0 %all-to-all-start.2 = ((f32[128,8,128]{2,1,0:T(8,128)}), f32[128,8,128]{2,1,0:T(8,128)}, u32[]{:S(2)}, u32[]{:S(2)}) async-start(f32[128,8,128]{2,1,0:T(8,128)} %copy-done.19), calls=%async_computation.2 | async-start | bytes 1048576 | tf_op jit(solution)/shard_map/all_to_all | solution.py:388
  271.1 20.5 %medium_back_near.1.refs_0_ = f32[128,8192]{1,0:T(8,128)S(1)} custom-call(bf16[128,8192]{1,0:T(8,128)(2,1)} %get-tuple-element.44.refs_0_, f32[512,128]{1,0:T(8,128)S(1)} %convert_bitcast_fusion.refs_1_.refs_8_), custom_call_target="tpu_custom_call" | custom-call | flops 8589934592 | bytes 6553600 | tf_op jit(solution)/shard_map/medium_back_near/pallas_call | solution.py:58
  293.6 8.1 %collective-permute-start.8 = (f32[1,8192]{1,0:T(1,128)}, f32[1,8192]{1,0:T(1,128)}, u32[]{:S(2)}, u32[]{:S(2)}) collective-permute-start(f32[1,8192]{1,0:T(1,128)} %get-tuple-element.45), channel_id=1, source_target_pairs={{2,0},{3,1},{4,2},{5,3},{6,4},{7,5},{8,6},{9,7},{10,8},{11,9},{12,... | collective-permute-start | bytes 98312 | tf_op jit(solution)/shard_map/ppermute | solution.py:384
  303.8 5.3 %all-to-all-start.3 = ((f32[128,8,128]{2,1,0:T(8,128)}), f32[128,8,128]{2,1,0:T(8,128)}, u32[]{:S(2)}, u32[]{:S(2)}) async-start(f32[128,8,128]{2,1,0:T(8,128)} %scan_forward.1), calls=%async_computation.3 | async-start | bytes 1048576 | tf_op jit(solution)/shard_map/all_to_all | solution.py:388
  318.0 23.7 %long_near.1 = (f32[128,8192]{1,0:T(8,128)S(1)}, bf16[128,8192]{1,0:T(8,128)(2,1)}, bf16[128,8192]{1,0:T(8,128)(2,1)}) custom-call(bf16[128,8192]{1,0:T(8,128)(2,1)S(1)} %copy-done.40, bf16[128,8192]{1,0:T(8,128)(2,1)S(1)} %copy-done.26, f32[8,8192]{1,0:T(8,128)S(1)} %copy-done.30, bf16[128,8192]{1,0:T(8,128)(2,1)S(1)} %copy-done.38, ...), custom_call_target="tpu_custom_call" | custom-call | flops 8589934592 | bytes 20447232 | tf_op jit(solution)/shard_map/long_near/pallas_call | solution.py:58
  348.6 15.1 %long_forward.1 = (bf16[128,8192]{1,0:T(8,128)(2,1)}, bf16[128,8192]{1,0:T(8,128)(2,1)}) custom-call(f32[128,8192]{1,0:T(8,128)S(1)} %copy-done.6, f32[128,8,128]{2,1,0:T(8,128)} %all-to-all-done.3.refs_1_, f32[128,8,128]{2,1,0:T(8,128)S(1)} %copy-done.20, bf16[128,8192]{1,0:T(8,128)(2,1)S(1)} %copy-done, bf16[128,8192]{1,0:T(8,128)(2,1)S(1)} %copy-done.2, ...), custom_call_target="tpu_custom_call" | custom-call | bytes 15073280 | tf_op jit(solution)/shard_map/long_forward/pallas_call | solution.py:58
  363.7 23.9 %medium_back.1 = (bf16[128,8192]{1,0:T(8,128)(2,1)}, bf16[128,8192]{1,0:T(8,128)(2,1)}) custom-call(f32[128,8192]{1,0:T(8,128)S(1)} %copy-done.32, bf16[128,8192]{1,0:T(8,128)(2,1)} %collective-permute-done.7.refs_1_, f32[1,8192]{1,0:T(1,128)} %collective-permute-done.8.refs_2_, bf16[128,8192]{1,0:T(8,128)(2,1)S(1)} %copy-done.8, ...), custom_call_target="tpu_custom_call" | custom-call | flops 8589934592 | bytes 16154624 | tf_op jit(solution)/shard_map/medium_back/pallas_call | solution.py:58
  (152 shorter events, 91.5 us)
Async XLA Ops:
  3.3 27.3 %collective-permute-start = (bf16[8,8192]{1,0:T(8,128)(2,1)}, bf16[8,8192]{1,0:T(8,128)(2,1)}, u32[]{:S(2)}, u32[]{:S(2)}) collective-permute-start(bf16[8,8192]{1,0:T(8,128)(2,1)} %pad_maximum_fusion.2), channel_id=1, source_target_pairs={{0,1},{1,2},{2,3},{3,4},{4,5},{5,6},{6,7},{7,8},{8,9},{9,10},{10,1... | collective-permute-start | bytes 393224 | tf_op jit(solution)/shard_map/ppermute | solution.py:384
  30.6 17.2 %slice-start = ((bf16[128,8192]{1,0:T(8,128)(2,1)}), bf16[2,8192]{1,0:T(2,128)(2,1)S(1)}, s32[]{:S(2)}) async-start(bf16[128,8192]{1,0:T(8,128)(2,1)} %refs_4_.4), calls=%async_computation.4 | async-start | bytes 65536 | tf_op jit(solution)/shard_map/slice | solution.py:416
  33.8 14.0 %slice-start.1 = ((bf16[128,8192]{1,0:T(8,128)(2,1)}), bf16[2,8192]{1,0:T(2,128)(2,1)S(1)}, s32[]{:S(2)}) async-start(bf16[128,8192]{1,0:T(8,128)(2,1)} %refs_3_.7), calls=%async_computation.5 | async-start | bytes 65536 | tf_op jit(solution)/shard_map/slice | solution.py:416
  33.8 14.0 %slice-start.2 = ((bf16[128,8192]{1,0:T(8,128)(2,1)}), bf16[2,8192]{1,0:T(2,128)(2,1)S(1)}, s32[]{:S(2)}) async-start(bf16[128,8192]{1,0:T(8,128)(2,1)} %refs_4_.5), calls=%async_computation.6 | async-start | bytes 65536 | tf_op jit(solution)/shard_map/slice | solution.py:416
  40.2 184.0 %collective-permute-start.1 = (bf16[128,8192]{1,0:T(8,128)(2,1)}, bf16[128,8192]{1,0:T(8,128)(2,1)}, u32[]{:S(2)}, u32[]{:S(2)}) collective-permute-start(bf16[128,8192]{1,0:T(8,128)(2,1)} %product_one.1.refs_0_), channel_id=1, source_target_pairs={{0,1},{1,2},{2,3},{3,4},{4,5},{5,6},{6,7},{7,8},{8,9},{9,10},{10,1... | collective-permute-start | bytes 6291464 | tf_op jit(solution)/shard_map/ppermute | solution.py:384
  44.2 46.3 %collective-permute-start.2 = (bf16[8,8192]{1,0:T(8,128)(2,1)}, bf16[8,8192]{1,0:T(8,128)(2,1)}, u32[]{:S(2)}, u32[]{:S(2)}) collective-permute-start(bf16[8,8192]{1,0:T(8,128)(2,1)} %pad_maximum_fusion.3), channel_id=1, source_target_pairs={{0,1},{1,2},{2,3},{3,4},{4,5},{5,6},{6,7},{7,8},{8,9},{9,10},{10,1... | collective-permute-start | bytes 393224 | tf_op jit(solution)/shard_map/ppermute | solution.py:384
  51.0 136.1 %collective-permute-start.4 = (bf16[16,8192]{1,0:T(8,128)(2,1)}, bf16[16,8192]{1,0:T(8,128)(2,1)}, u32[]{:S(2)}, u32[]{:S(2)}) collective-permute-start(bf16[16,8192]{1,0:T(8,128)(2,1)} %concatenate.22), channel_id=1, source_target_pairs={{1,0},{2,1},{3,2},{4,3},{5,4},{6,5},{7,6},{8,7},{9,8},{10,9},{11,1... | collective-permute-start | bytes 786440 | tf_op jit(solution)/shard_map/ppermute | solution.py:384
  108.8 42.6 %all-to-all-start = ((f32[128,8,128]{2,1,0:T(8,128)}), f32[128,8,128]{2,1,0:T(8,128)}, u32[]{:S(2)}, u32[]{:S(2)}) async-start(f32[128,8,128]{2,1,0:T(8,128)} %copy-done.21), calls=%async_computation | async-start | bytes 1048576 | tf_op jit(solution)/shard_map/all_to_all | solution.py:388
  148.2 76.1 %collective-permute-start.3 = (f32[2,8192]{1,0:T(2,128)}, f32[2,8192]{1,0:T(2,128)}, u32[]{:S(2)}, u32[]{:S(2)}) collective-permute-start(f32[2,8192]{1,0:T(2,128)} %get-tuple-element.29), channel_id=1, source_target_pairs={{0,1},{1,2},{2,3},{3,4},{4,5},{5,6},{6,7},{7,8},{8,9},{9,10},{10,1... | collective-permute-start | bytes 196616 | tf_op jit(solution)/shard_map/ppermute | solution.py:384
  153.6 33.6 %all-to-all-start.1 = ((f32[128,8,128]{2,1,0:T(8,128)}), f32[128,8,128]{2,1,0:T(8,128)}, u32[]{:S(2)}, u32[]{:S(2)}) async-start(f32[128,8,128]{2,1,0:T(8,128)} %scan_back.1), calls=%async_computation.1 | async-start | bytes 1048576 | tf_op jit(solution)/shard_map/all_to_all | solution.py:388
  194.1 30.1 %copy-start.13 = (bf16[128,8192]{1,0:T(8,128)(2,1)S(1)}, bf16[128,8192]{1,0:T(8,128)(2,1)}, u32[]{:S(2)}) copy-start(bf16[128,8192]{1,0:T(8,128)(2,1)} %refs_5_.1) | copy-start | bytes 6291460
  194.1 30.1 %copy-start.15 = (bf16[128,8192]{1,0:T(8,128)(2,1)S(1)}, bf16[128,8192]{1,0:T(8,128)(2,1)}, u32[]{:S(2)}) copy-start(bf16[128,8192]{1,0:T(8,128)(2,1)} %refs_4_.3) | copy-start | bytes 6291460
  194.1 30.1 %copy-start.24 = (f32[512,128]{1,0:T(8,128)S(1)}, f32[512,128]{1,0:T(8,128)}, u32[]{:S(2)}) copy-start(f32[512,128]{1,0:T(8,128)} %pad_maximum_fusion.refs_5_.refs_7_) | copy-start | bytes 786436
  194.1 30.1 %copy-start.34 = (f32[128,8192]{1,0:T(8,128)S(1)}, f32[128,8192]{1,0:T(8,128)}, u32[]{:S(2)}) copy-start(f32[128,8192]{1,0:T(8,128)} %copy-done.33) | copy-start | bytes 12582916
  213.8 95.3 %collective-permute-start.5 = (f32[2,8192]{1,0:T(2,128)}, f32[2,8192]{1,0:T(2,128)S(1)}, u32[]{:S(2)}, u32[]{:S(2)}) collective-permute-start(f32[2,8192]{1,0:T(2,128)} %get-tuple-element.37), channel_id=1, source_target_pairs={{1,0},{2,1},{3,2},{4,3},{5,4},{6,5},{7,6},{8,7},{9,8},{10,9},{11,1... | collective-permute-start | bytes 196616 | tf_op jit(solution)/shard_map/ppermute | solution.py:384
  221.5 142.1 %collective-permute-start.7 = (bf16[128,8192]{1,0:T(8,128)(2,1)}, bf16[128,8192]{1,0:T(8,128)(2,1)}, u32[]{:S(2)}, u32[]{:S(2)}) collective-permute-start(bf16[128,8192]{1,0:T(8,128)(2,1)} %get-tuple-element.44.refs_0_), channel_id=1, source_target_pairs={{1,0},{2,1},{3,2},{4,3},{5,4},{6,5},{7,6},{8,7},{9,8},{10,9},{11,1... | collective-permute-start | bytes 6291464 | tf_op jit(solution)/shard_map/ppermute | solution.py:384
  261.7 47.4 %collective-permute-start.6 = (f32[6,8192]{1,0:T(8,128)}, f32[6,8192]{1,0:T(8,128)}, u32[]{:S(2)}, u32[]{:S(2)}) collective-permute-start(f32[6,8192]{1,0:T(8,128)} %get-tuple-element.39), channel_id=1, source_target_pairs={{1,0},{2,1},{3,2},{4,3},{5,4},{6,5},{7,6},{8,7},{9,8},{10,9},{11,1... | collective-permute-start | bytes 589832 | tf_op jit(solution)/shard_map/ppermute | solution.py:384
  264.1 37.6 %all-to-all-start.2 = ((f32[128,8,128]{2,1,0:T(8,128)}), f32[128,8,128]{2,1,0:T(8,128)}, u32[]{:S(2)}, u32[]{:S(2)}) async-start(f32[128,8,128]{2,1,0:T(8,128)} %copy-done.19), calls=%async_computation.2 | async-start | bytes 1048576 | tf_op jit(solution)/shard_map/all_to_all | solution.py:388
  293.6 15.5 %copy-start.22 = (f32[512,128]{1,0:T(8,128)S(1)}, f32[512,128]{1,0:T(8,128)}, u32[]{:S(2)}) copy-start(f32[512,128]{1,0:T(8,128)} %pad_maximum_fusion.1.refs_9_) | copy-start | bytes 786436
  293.6 70.1 %collective-permute-start.8 = (f32[1,8192]{1,0:T(1,128)}, f32[1,8192]{1,0:T(1,128)}, u32[]{:S(2)}, u32[]{:S(2)}) collective-permute-start(f32[1,8192]{1,0:T(1,128)} %get-tuple-element.45), channel_id=1, source_target_pairs={{2,0},{3,1},{4,2},{5,3},{6,4},{7,5},{8,6},{9,7},{10,8},{11,9},{12,... | collective-permute-start | bytes 98312 | tf_op jit(solution)/shard_map/ppermute | solution.py:384
  303.8 39.9 %all-to-all-start.3 = ((f32[128,8,128]{2,1,0:T(8,128)}), f32[128,8,128]{2,1,0:T(8,128)}, u32[]{:S(2)}, u32[]{:S(2)}) async-start(f32[128,8,128]{2,1,0:T(8,128)} %scan_forward.1), calls=%async_computation.3 | async-start | bytes 1048576 | tf_op jit(solution)/shard_map/all_to_all | solution.py:388
  348.6 15.1 %copy-start.8 = (bf16[128,8192]{1,0:T(8,128)(2,1)S(1)}, bf16[128,8192]{1,0:T(8,128)(2,1)}, u32[]{:S(2)}) copy-start(bf16[128,8192]{1,0:T(8,128)(2,1)} %refs_3_.7) | copy-start | bytes 6291460
  348.6 15.1 %copy-start.10 = (bf16[128,8192]{1,0:T(8,128)(2,1)S(1)}, bf16[128,8192]{1,0:T(8,128)(2,1)}, u32[]{:S(2)}) copy-start(bf16[128,8192]{1,0:T(8,128)(2,1)} %refs_4_.5) | copy-start | bytes 6291460
  348.6 15.1 %copy-start.32 = (f32[128,8192]{1,0:T(8,128)S(1)}, f32[128,8192]{1,0:T(8,128)}, u32[]{:S(2)}) copy-start(f32[128,8192]{1,0:T(8,128)} %copy-done.31) | copy-start | bytes 12582916
  (39 other events, 120.3 us)

commit v2 on v1

v2 whole, which is shorter than its diff:
```python
import jax
import jax.numpy as jnp
from jax import lax
from jax.experimental import pallas as pl
from jax.experimental.pallas import tpu as pltpu
from jax.sharding import PartitionSpec as P

GROUP = 16
SHORT = 3
MR_TAPS = 128
MODES = 16
ROWS = 128
LANES = 128
STRIP = 32
STRIPS = ROWS // STRIP
TILE_GROUPS = LANES // GROUP
AXES = ("ctx", "ch")
BF16 = jnp.bfloat16
F32 = jnp.float32
VMEM_LIMIT = 56 * 1024 * 1024

MR_Q, MR_K, MR_V, LI_Q, LI_K, LI_V, SKIP = 0, 3, 6, 9, 12, 15, 18
TABLE_ROWS = 24


def cost(microseconds):
    return pl.CostEstimate(
        flops=0, bytes_accessed=int(microseconds * 3.6e6), transcendentals=0
    )


def lane_call(body, name, channels, ins, outs, scratch, us, part=(0, 1), into=None, width=1024, unroll=2):
    span = channels // part[1]
    width = min(width, span)
    tiles = width // LANES
    blocks = span // width
    into = into or {}

    def spec(shape, kind):
        whole = {"r": shape[-1], "g": shape[0] * GROUP, "s": shape[0] * (LANES // 2)}[kind] == channels
        first = part[0] * blocks if whole else 0
        if kind == "r":
            return pl.BlockSpec((shape[0], width), lambda i: (0, first + i))
        if kind == "g":
            return pl.BlockSpec((width // GROUP, shape[1]), lambda i: (first + i, 0))
        return pl.BlockSpec((2 * tiles, 8, LANES), lambda i: (first + i, 0, 0))

    def view(ref, kind, t):
        if kind == "r":
            return ref.at[:, pl.ds(pl.multiple_of(t * LANES, LANES), LANES)]
        if kind == "g":
            return ref.at[pl.ds(pl.multiple_of(t * TILE_GROUPS, TILE_GROUPS), TILE_GROUPS), :]
        return ref.at[pl.ds(2 * t, 2)]

    kinds = [kind for _, kind in ins] + [kind for _, _, kind in outs]
    count_in, count_out = len(ins), len(outs)

    def kernel(*refs):
        arrays = refs[:count_in] + refs[count_in + len(into) : count_in + len(into) + count_out]
        extra = refs[count_in + len(into) + count_out :]

        def step(k, unused):
            for u in range(unroll):
                t = k * unroll + u
                body(
                    *[view(ref, kind, t) for ref, kind in zip(arrays, kinds)],
                    *[ref.at[u] for ref in extra],
                )
            return unused

        lax.fori_loop(0, tiles // unroll, step, 0)

    return pl.pallas_call(
        kernel,
        name=name,
        grid=(blocks,),
        in_specs=[spec(a.shape, kind) for a, kind in ins]
        + [pl.BlockSpec(memory_space=pl.ANY)] * len(into),
        out_specs=[spec(shape, kind) for shape, _, kind in outs],
        out_shape=[jax.ShapeDtypeStruct(shape, dtype) for shape, dtype, _ in outs],
        scratch_shapes=[pltpu.VMEM((unroll, *shape), dtype) for shape, dtype in scratch],
        input_output_aliases={count_in + n: at for n, at in enumerate(into)},
        compiler_params=pltpu.CompilerParams(vmem_limit_bytes=VMEM_LIMIT),
        cost_estimate=cost(us),
    )(*[a for a, _ in ins], *into.values())


EXT = ((ROWS + 16, LANES), F32)


def turned(x, by):
    return pltpu.roll(x, by, 0) if by else x


def fill(ext, value, prev8=None, next8=None):
    ext[8 : 8 + ROWS, :] = value
    if prev8 is not None:
        ext[0:8, :] = prev8
    if next8 is not None:
        ext[8 + ROWS :, :] = next8


def taps(table, first):
    return [table[first + j : first + j + 1, :] for j in range(SHORT)]


def short_forward(ext, weights, rows=ROWS):
    return (
        weights[0] * ext[8 : 8 + rows, :]
        + weights[1] * ext[7 : 7 + rows, :]
        + weights[2] * ext[6 : 6 + rows, :]
    )


def short_backward(ext, weights):
    return (
        weights[0] * ext[8 : 8 + ROWS, :]
        + weights[1] * ext[9 : 9 + ROWS, :]
        + weights[2] * ext[10 : 10 + ROWS, :]
    )


def iota(shape, dim):
    return lax.broadcasted_iota(jnp.int32, shape, dim)


def circulant(base, g, rows, shift=0):
    row = jnp.broadcast_to(base[g : g + 1, :], (rows, LANES))
    return pltpu.roll(row, shift, 1, stride=1, stride_axis=0)


def pick(products, rows, count):
    columns = LANES // count
    owner = iota((rows, LANES), 1) // columns
    picked = []
    for q in range(products.shape[1] // LANES):
        at = slice(q * LANES, (q + 1) * LANES)
        total = products[0:rows, at]
        for p in range(1, count):
            total = jnp.where(owner == p, products[p * rows : (p + 1) * rows, at], total)
        picked.append(total)
    return jnp.concatenate(picked, 0)


def windows(signal, first, length):
    count = signal.shape[0]
    parts = []
    for q in range(STRIPS):
        low, high = STRIP * q + first, STRIP * q + first + length
        inside = signal[max(low, 0) : min(high, count)]
        pieces = [inside]
        if low < 0:
            pieces.insert(0, jnp.zeros((-low, LANES), signal.dtype))
        if high > count:
            pieces.append(jnp.zeros((high - count, LANES), signal.dtype))
        parts.append(jnp.concatenate(pieces, 0) if len(pieces) > 1 else inside)
    return jnp.concatenate(parts, 1)


def split_groups(signal):
    odd = ((iota(signal.shape, 1) // GROUP) % 2).astype(F32)
    return signal * (1.0 - odd).astype(signal.dtype), signal * odd.astype(signal.dtype)


def long_product(base_ref, signal, tables, backward):
    base = base_ref[...]
    row, lane = iota((STRIP, LANES), 0), iota((STRIP, LANES), 1)
    first = 0 if backward else STRIP - LANES
    keep = lane >= row if backward else lane + first <= row
    for g in range(TILE_GROUPS):
        p, half = g // 2, g % 2
        table = jnp.where(keep, circulant(base, g, STRIP, -first), 0.0).astype(BF16)
        tables[p * STRIP : (p + 1) * STRIP, half * LANES : (half + 1) * LANES] = table
    even, odd = split_groups(signal)
    right = jnp.concatenate([windows(even, first, LANES), windows(odd, first, LANES)], 0)
    return pick(jnp.dot(tables[...], right, preferred_element_type=F32), STRIP, TILE_GROUPS // 2)


def medium_product(base_ref, pair, tables, backward):
    base = base_ref[...]
    row, lane = iota((STRIP, LANES), 0), iota((STRIP, LANES), 1)
    for g in range(TILE_GROUPS):
        whole = circulant(base, g, STRIP)
        keep = lane >= row if backward else lane > row
        rows = slice(g * STRIP, (g + 1) * STRIP)
        tables[rows, 0:LANES] = jnp.where(keep, whole, 0.0).astype(BF16)
        tables[rows, LANES:] = jnp.where(keep, 0.0, whole).astype(BF16)
    products = jnp.dot(tables[...], windows(pair, 0, 2 * LANES), preferred_element_type=F32)
    return pick(products, STRIP, TILE_GROUPS)


def on_channels(base, column):
    own = iota((TILE_GROUPS, LANES), 0) == iota((TILE_GROUPS, LANES), 1) // GROUP
    return jnp.where(own, base[:, column : column + 1], 0.0).sum(0, keepdims=True)


def own_group():
    return (iota((LANES, LANES), 0) // MODES == iota((LANES, LANES), 1) // GROUP).astype(F32)


def spread(state):
    return (jnp.concatenate([state] * TILE_GROUPS, 0) * own_group()).astype(BF16)


def absorb(powers, signal):
    every = lax.dot_general(
        powers.astype(BF16), signal, (((0,), (0,)), ((), ())), preferred_element_type=F32
    )
    return (every * own_group()).reshape(TILE_GROUPS, MODES, LANES).sum(0)


def store_state(ref, state):
    ref[...] = state.reshape(2, 8, LANES)


def load_state(ref):
    return ref[...].reshape(MODES, LANES)


def margins_before(ref):
    rows = ref[...].astype(F32)
    return rows[0:8], rows[8:16]


def margins_after(ref):
    rows = ref[...].astype(F32)
    return rows[0:8], rows[8:16]


def edges(mr_query, mr_key, mr_value, li_query, li_key, upstream):
    channels = mr_query.shape[1]
    width = min(2048, channels)

    def kernel(q_end, k_end, v_end, lq_end, lk_end, lq, lk, g, k, v, last, first, last_kv, a, b):
        a[0:4, :] = k_end[...].astype(F32)[12:16]
        a[4:8, :] = v_end[...].astype(F32)[12:16]
        a[8:12, :] = q_end[...].astype(F32)[12:16]
        a[12:14, :] = lq_end[...].astype(F32)[14:16]
        a[14:16, :] = lk_end[...].astype(F32)[14:16]
        for n, ref in enumerate((lq, lk, g, k, v)):
            b[2 * n : 2 * n + 2, :] = ref[...].astype(F32)[0:2]
        b[10:16, :] = jnp.zeros((6, width), F32)
        last[...] = a[...].astype(BF16)
        first[...] = b[...].astype(BF16)
        last_kv[...] = a[0:8, :].astype(BF16)

    low = pl.BlockSpec((16, width), lambda i: (ROWS // 16 - 1, i))
    high = pl.BlockSpec((16, width), lambda i: (0, i))
    small = jax.ShapeDtypeStruct((16, channels), BF16)
    return pl.pallas_call(
        kernel,
        name="edges",
        grid=(channels // width,),
        in_specs=[low] * 5 + [high] * 5,
        out_specs=[high, high, pl.BlockSpec((8, width), lambda i: (0, i))],
        out_shape=[small, small, jax.ShapeDtypeStruct((8, channels), BF16)],
        scratch_shapes=[pltpu.VMEM((16, width), F32)] * 2,
        compiler_params=pltpu.CompilerParams(vmem_limit_bytes=VMEM_LIMIT),
        cost_estimate=cost(3.5),
    )(mr_query, mr_key, mr_value, li_query, li_key, li_query, li_key, upstream, mr_key, mr_value)


def make_tables(mr_short, li_short, li_skip, mr_filter, li_rate, li_residue):
    groups = mr_filter.shape[1]
    channels = groups * GROUP
    block = min(128, groups)
    width = block * GROUP

    def kernel(mr, li, skip, filters, rate, residue, table, medium, medium_back, long, long_back):
        for n in range(3):
            table[3 * n : 3 * n + 3, :] = mr[n].astype(F32)
            table[9 + 3 * n : 12 + 3 * n, :] = li[n].astype(F32)
        table[SKIP : SKIP + 1, :] = skip[...]
        table[SKIP + 1 :, :] = jnp.zeros((TABLE_ROWS - SKIP - 1, width), F32)
        row, lane = iota((LANES, LANES), 0), iota((LANES, LANES), 1)
        same = (row == lane).astype(F32).astype(BF16)
        turn = (row == (LANES - lane) % LANES).astype(F32).astype(BF16)
        by_rows = (((0,), (0,)), ((), ()))
        medium[...] = lax.dot_general(filters[...], turn, by_rows, preferred_element_type=F32)
        medium_back[...] = lax.dot_general(filters[...], same, by_rows, preferred_element_type=F32)
        position = iota((block, LANES), 1).astype(F32)
        impulse = jnp.zeros((block, LANES), F32)
        for n in range(MODES):
            impulse += residue[:, n : n + 1] * jnp.exp(-rate[:, n : n + 1] * position)
        long_back[...] = impulse
        long[...] = jnp.dot(impulse.astype(BF16), turn, preferred_element_type=F32)

    shorts = pl.BlockSpec((3, 3, width), lambda i: (0, 0, i))
    modes = pl.BlockSpec((block, MODES), lambda i: (i, 0))
    by_tap = pl.BlockSpec((block, LANES), lambda i: (i, 0))
    shapes = [jax.ShapeDtypeStruct((TABLE_ROWS, channels), F32)]
    shapes += [jax.ShapeDtypeStruct((groups, LANES), F32)] * 4
    return pl.pallas_call(
        kernel,
        name="tables",
        grid=(groups // block,),
        in_specs=[
            shorts, shorts, pl.BlockSpec((1, width), lambda i: (0, i)),
            pl.BlockSpec((MR_TAPS, block), lambda i: (0, i)), modes, modes,
        ],
        out_specs=[pl.BlockSpec((TABLE_ROWS, width), lambda i: (0, i))] + [by_tap] * 4,
        out_shape=shapes,
        compiler_params=pltpu.CompilerParams(vmem_limit_bytes=VMEM_LIMIT),
        cost_estimate=cost(5),
    )(mr_short, li_short, li_skip, mr_filter, li_rate, li_residue)


def product_one_body(key, value, prev, table, out, ext_k, ext_v):
    weights = table[...]
    margin, _ = margins_before(prev)
    fill(ext_k, key[...].astype(F32), turned(margin, 4))
    fill(ext_v, value[...].astype(F32), margin)
    keys_one = short_forward(ext_k, taps(weights, MR_K))
    value_one = short_forward(ext_v, taps(weights, MR_V))
    out[...] = (keys_one * value_one).astype(BF16)


def upstream_body(li_query, upstream, prev, table, rate, cotangent, state, ext):
    weights = table[...]
    _, margin = margins_before(prev)
    fill(ext, li_query[...].astype(F32), turned(margin, 2))
    query_two = short_forward(ext, taps(weights, LI_Q))
    rounded = (upstream[...].astype(F32) * query_two).astype(BF16)
    position = iota((ROWS, LANES), 0).astype(F32)
    store_state(state, absorb(jnp.exp(-rate[...] * position), rounded))
    cotangent[...] = rounded


def long_back_near_body(cotangent, table, base, near, tables):
    signal = cotangent[...]
    product = long_product(base, signal, tables, True)
    near[...] = product + table[SKIP : SKIP + 1, :] * signal.astype(F32)


def long_back_body(
    near, closing, li_query, li_key, query, prev, following, table, rate, residue,
    grad_two, grad_two_after, mixed_grad, mixed_head, out_head, out,
    ext_q, ext_k, ext_g, ext_o,
):
    weights = table[...]
    _, before = margins_before(prev)
    after, _ = margins_after(following)
    fill(ext_q, li_query[...].astype(F32), None, after)
    w = taps(weights, LI_Q)
    base = 8 + ROWS
    query_after = (
        w[0] * ext_q[base : base + 8, :]
        + w[1] * ext_q[base - 1 : base + 7, :]
        + w[2] * ext_q[base - 2 : base + 6, :]
    )
    cot_after = turned(after, 4) * query_after
    state = load_state(closing)
    distance = (ROWS - iota((ROWS + 16, LANES), 0)).astype(F32)
    emit = (residue[...] * jnp.exp(-rate[...] * distance)).astype(BF16)
    emitted = jnp.dot(emit, spread(state), preferred_element_type=F32)
    later = jnp.dot(emit[ROWS:], spread(state - cot_after[0:1]), preferred_element_type=F32)
    skip = weights[SKIP : SKIP + 1]
    own = near[...] + emitted[0:ROWS]
    at_row = iota((8, LANES), 0)
    past = jnp.where(at_row == 0, emitted[ROWS : ROWS + 8], later[0:8]) + skip * cot_after
    past = jnp.where(at_row < 2, past, 0.0)
    grad_two[...] = own.astype(BF16)
    grad_two_after[...] = past[0:2]
    fill(ext_k, li_key[...].astype(F32), before, turned(after, 6))
    keys_two = short_forward(ext_k, taps(weights, LI_K), ROWS + 8)
    fill(ext_g, own * keys_two[0:ROWS], None, past * keys_two[ROWS:])
    mixed = short_backward(ext_g, taps(weights, LI_V))
    fill(ext_o, query[...].astype(F32), turned(before, 4))
    conv_grad = mixed * short_forward(ext_o, taps(weights, MR_Q))
    mixed_grad[...] = mixed.astype(BF16)
    mixed_head[...] = mixed[0:2]
    out[...] = conv_grad.astype(BF16)
    out_head[...] = conv_grad[0:1]


def forward_body(
    before, before_kv, signal, query, li_key, prev, table, base_ref, base_long, rate,
    conv_one, value_two, near, state, head, ext_q, ext_k, ext_m, tables, tables_edge, tables_long,
):
    weights = table[...]
    earlier = before[...]
    pair = jnp.concatenate([earlier, signal[...]], 0)
    conv = medium_product(base_ref, pair, tables, False)
    base = base_ref[...]
    row, lane = iota((16, LANES), 0), iota((16, LANES), 1)
    for g in range(TILE_GROUPS):
        whole = circulant(base, g, 16, ROWS - 16)
        tables_edge[g * 16 : (g + 1) * 16, :] = jnp.where(
            lane <= row + (ROWS - 16), whole, 0.0
        ).astype(BF16)
    edge = pick(jnp.dot(tables_edge[...], earlier, preferred_element_type=F32), 16, TILE_GROUPS)
    raw = before_kv[...].astype(F32)
    w_k, w_v = taps(weights, MR_K), taps(weights, MR_V)
    key_last = w_k[0] * raw[3:4] + w_k[1] * raw[2:3] + w_k[2] * raw[1:2]
    value_last = w_v[0] * raw[7:8] + w_v[1] * raw[6:7] + w_v[2] * raw[5:6]
    far = on_channels(base, 1) * (key_last * value_last).astype(BF16).astype(F32)
    conv_before = edge[8:16] + jnp.where(iota((8, LANES), 0) == 6, far, 0.0)
    _, margin = margins_before(prev)
    fill(ext_q, query[...].astype(F32), turned(margin, 4))
    w = taps(weights, MR_Q)
    query_one = short_forward(ext_q, w)
    query_before = w[0] * margin[0:8] + w[1] * turned(margin, 1) + w[2] * turned(margin, 2)
    mixed_before = turned(query_before, 4) * conv_before
    fill(
        ext_m,
        (query_one * conv).astype(BF16).astype(F32),
        mixed_before.astype(BF16).astype(F32),
    )
    value = short_forward(ext_m, taps(weights, LI_V))
    fill(ext_k, li_key[...].astype(F32), margin)
    keys_two = short_forward(ext_k, taps(weights, LI_K))
    product = keys_two * value
    rounded = product.astype(BF16)
    position = (ROWS - 1 - iota((ROWS, LANES), 0)).astype(F32)
    store_state(state, absorb(jnp.exp(-rate[...] * position), rounded))
    conv_one[...] = conv.astype(BF16)
    value_two[...] = value.astype(BF16)
    near[...] = (
        long_product(base_long, rounded, tables_long, False) + weights[SKIP : SKIP + 1] * product
    )
    head[0:2, :] = product[0:2]
    head[2:4, :] = value[0:2]
    head[4:6, :] = conv[0:2]


def long_body(
    near, start, end, li_query, upstream, prev, following, next_head, grad_two, grad_two_after,
    value_two, table, rate, residue, base_back,
    out, grad_li_query, grad_li_key, ext_q, ext_g, ext_k,
):
    weights = table[...]
    distance = (iota((ROWS + 16, LANES), 0) + 1).astype(F32)
    emit = (residue[...] * jnp.exp(-rate[...] * distance)).astype(BF16)
    emitted = jnp.dot(emit, spread(load_state(start)), preferred_element_type=F32)
    conv = near[...] + emitted[0:ROWS]
    _, margin = margins_before(prev)
    fill(ext_q, li_query[...].astype(F32), turned(margin, 2))
    query_two = short_forward(ext_q, taps(weights, LI_Q))
    out[...] = (query_two * conv).astype(BF16)
    ended = jnp.dot(emit[0:16], spread(load_state(end)), preferred_element_type=F32)
    impulse = base_back[...]
    at_once = on_channels(impulse, 0) + weights[SKIP : SKIP + 1]
    first, second = next_head[0:1, :], next_head[1:2, :]
    past = emitted[ROWS : ROWS + 8] + ended[0:8]
    past_first = past[0:1] + at_once * first
    past_second = past[1:2] + on_channels(impulse, 1) * first + at_once * second
    after, _ = margins_after(following)
    fill(ext_g, upstream[...].astype(F32) * conv)
    ext_g[8 + ROWS : 9 + ROWS, :] = after[4:5] * past_first
    ext_g[9 + ROWS : 10 + ROWS, :] = after[5:6] * past_second
    grad_li_query[...] = short_backward(ext_g, taps(weights, LI_Q)).astype(BF16)
    fill(ext_k, grad_two[...].astype(F32) * value_two[...].astype(F32))
    ext_k[8 + ROWS : 10 + ROWS, :] = grad_two_after[...] * next_head[2:4, :]
    grad_li_key[...] = short_backward(ext_k, taps(weights, LI_K)).astype(BF16)


def medium_back_body(
    conv_grad, after, after_next, key, value, prev, following, mixed_grad, mixed_after,
    conv_one, next_head, table, base_ref,
    grad_query, grad_key, grad_value, ext_k, ext_v, ext_gk, ext_gv, ext_q, tables,
):
    weights = table[...]
    later = after[...]
    pair = jnp.concatenate([conv_grad[...], later], 0)
    grad = medium_product(base_ref, pair, tables, True)
    left = jnp.concatenate(
        [tables[g * STRIP : g * STRIP + 16, 0:LANES] for g in range(TILE_GROUPS)], 0
    )
    edge = pick(jnp.dot(left, later, preferred_element_type=F32), 16, TILE_GROUPS)
    far = on_channels(base_ref[...], MR_TAPS - 1) * after_next[...].astype(BF16).astype(F32)
    past = edge[0:8] + jnp.where(iota((8, LANES), 0) == 1, far, 0.0)
    before, _ = margins_before(prev)
    next_a, next_b = margins_after(following)
    fill(ext_k, key[...].astype(F32), turned(before, 4), turned(next_a, 2))
    fill(ext_v, value[...].astype(F32), before, next_b)
    keys_one = short_forward(ext_k, taps(weights, MR_K), ROWS + 8)
    value_one = short_forward(ext_v, taps(weights, MR_V), ROWS + 8)
    fill(ext_gk, grad * value_one[0:ROWS], None, past * value_one[ROWS:])
    fill(ext_gv, grad * keys_one[0:ROWS], None, past * keys_one[ROWS:])
    grad_key[...] = short_backward(ext_gk, taps(weights, MR_K)).astype(BF16)
    grad_value[...] = short_backward(ext_gv, taps(weights, MR_V)).astype(BF16)
    fill(ext_q, mixed_grad[...].astype(F32) * conv_one[...].astype(F32))
    ext_q[8 + ROWS : 10 + ROWS, :] = mixed_after[...] * next_head[4:6, :]
    grad_query[...] = short_backward(ext_q, taps(weights, MR_Q)).astype(BF16)


def scan_states(states, rates, backward):
    count = states.shape[0]

    def kernel(states_ref, rates_ref, out_ref):
        decay = jnp.exp(rates_ref[...] * (-float(ROWS)))

        def step(k, carried):
            b = count - 1 - k if backward else k
            out_ref[b] = carried
            return decay * carried + states_ref[b]

        lax.fori_loop(0, count, step, jnp.zeros((8, LANES), F32), unroll=8)

    out_shape = jax.ShapeDtypeStruct(states.shape, F32)
    return pl.pallas_call(
        kernel,
        name="scan_back" if backward else "scan_forward",
        out_shape=out_shape,
        in_specs=[pl.BlockSpec(memory_space=pltpu.VMEM)] * 2,
        out_specs=pl.BlockSpec(memory_space=pltpu.VMEM),
        cost_estimate=cost(2),
    )(states, rates)


def sent(array, by):
    size = lax.axis_size(AXES)
    pairs = [(i, i + by) for i in range(size) if 0 <= i + by < size]
    return lax.ppermute(array, AXES, pairs)


def exchanged(array):
    return lax.all_to_all(array, AXES, split_axis=0, concat_axis=0, tiled=True)


def after(array, *others):
    return lax.optimization_barrier((array, *others))[0]


def per_device(
    mr_query, mr_key, mr_value, li_query, li_key, upstream,
    mr_short, li_short, mr_filter, li_rate, li_residue, li_skip,
):
    channels = mr_query.shape[1]
    tiles = channels // LANES
    assert mr_query.shape[0] == ROWS and lax.axis_size(AXES) == 2 * tiles
    rows = (ROWS, channels)
    full, full32 = (rows, BF16, "r"), (rows, F32, "r")
    half = ((ROWS, channels // 2), BF16, "r")
    state_out = ((2 * tiles, 8, LANES), F32, "s")
    halves = ((0, 2), (1, 2))

    def few(n):
        return ((n, channels), F32, "r")

    last_rows, first_rows, last_kv = edges(mr_query, mr_key, mr_value, li_query, li_key, upstream)
    prev = sent(last_rows, 1)
    following = sent(first_rows, -1)
    before_kv = sent(last_kv, 2)

    table, medium, medium_turned, long, long_turned = make_tables(
        mr_short, li_short, li_skip[None, :], mr_filter, li_rate, li_residue
    )
    rate = li_rate.reshape(1, channels)
    residue = li_residue.reshape(1, channels)
    me = lax.axis_index(AXES)
    my_rates = lax.dynamic_slice(
        li_rate, ((me // 2) * TILE_GROUPS, (me % 2) * 8), (TILE_GROUPS, 8)
    )
    my_rates = jnp.repeat(my_rates.T, GROUP, axis=1)

    tables_long = ((TILE_GROUPS // 2 * STRIP, 2 * LANES), BF16)
    tables_medium = ((TILE_GROUPS * STRIP, 2 * LANES), BF16)
    tables_edge = ((TILE_GROUPS * 16, LANES), BF16)

    cotangent, state_back = lane_call(
        upstream_body, "upstream", channels,
        [(li_query, "r"), (upstream, "r"), (prev, "r"), (table, "r"), (rate, "r")],
        [full, state_out], [EXT], 7,
    )
    gathered_back = after(exchanged(state_back), following, before_kv)
    signal_one = [
        lane_call(
            product_one_body, "product_one", channels,
            [(mr_key, "r"), (mr_value, "r"), (prev, "r"), (table, "r")],
            [half], [EXT, EXT], 4, part,
        )[0]
        for part in halves
    ]
    (near_back,) = lane_call(
        long_back_near_body, "long_back_near", channels,
        [(cotangent, "r"), (table, "r"), (long_turned, "g")],
        [full32], [tables_long], 6,
    )
    closing = exchanged(scan_states(gathered_back, my_rates, True))
    before_one = [sent(after(signal, closing), 1) for signal in signal_one]

    outs = [full, few(2), full, few(2), few(1), half]
    into = {}
    conv_grad = []
    for part in halves:
        got = lane_call(
            long_back_body, "long_back", channels,
            [(near_back, "r"), (closing, "s"), (li_query, "r"), (li_key, "r"), (mr_query, "r"),
             (prev, "r"), (following, "r"), (table, "r"), (rate, "r"), (residue, "r")],
            outs, [EXT, EXT, EXT, EXT], 6.5, part, into,
        )
        conv_grad.append(got[5])
        into = dict(enumerate(got[:5]))
    grad_two, grad_two_after, mixed_grad, mixed_head, conv_head, _ = got
    after_one = [sent(signal, -1) for signal in conv_grad]
    mixed_after = sent(mixed_head, -1)
    after_next = sent(conv_head, -2)

    into = {}
    for n, part in enumerate(halves):
        got = lane_call(
            forward_body, "forward", channels,
            [(before_one[n], "r"), (before_kv, "r"), (signal_one[n], "r"), (mr_query, "r"),
             (li_key, "r"), (prev, "r"), (table, "r"), (medium, "g"), (long, "g"), (rate, "r")],
            [full, full, full32, state_out, few(6)],
            [EXT, EXT, EXT, tables_medium, tables_edge, tables_long], 15, part, into,
        )
        into = dict(enumerate(got))
    conv_one, value_two, near, state, head = got
    next_head = sent(head, -1)
    start = exchanged(scan_states(exchanged(state), my_rates, False))

    output, grad_li_query, grad_li_key = lane_call(
        long_body, "long_forward", channels,
        [(near, "r"), (start, "s"), (state, "s"), (li_query, "r"), (upstream, "r"), (prev, "r"),
         (following, "r"), (next_head, "r"), (grad_two, "r"), (grad_two_after, "r"),
         (value_two, "r"), (table, "r"), (rate, "r"), (residue, "r"), (long_turned, "g")],
        [full, full, full], [EXT, EXT, EXT], 14,
    )
    into = {}
    for n, part in enumerate(halves):
        got = lane_call(
            medium_back_body, "medium_back", channels,
            [(conv_grad[n], "r"), (after_one[n], "r"), (after_next, "r"), (mr_key, "r"),
             (mr_value, "r"), (prev, "r"), (following, "r"), (mixed_grad, "r"),
             (mixed_after, "r"), (conv_one, "r"), (next_head, "r"), (table, "r"),
             (medium_turned, "g")],
            [full, full, full], [EXT, EXT, EXT, EXT, EXT, tables_medium], 8.5, part, into,
        )
        into = dict(enumerate(got))
    grad_mr_query, grad_mr_key, grad_mr_value = got
    return (output, grad_mr_query, grad_mr_key, grad_mr_value, grad_li_query, grad_li_key)


def solution(mesh):
    split = P(("ctx", "ch"), None)
    return jax.shard_map(
        per_device,
        mesh=mesh,
        in_specs=(split,) * 6 + (P(),) * 6,
        out_specs=(split,) * 6,
        check_vma=False,
    )
```

time: 390 us -> 233 us (0.60)
  Pallas kernels: 199 us -> 123 us
  local copies, waits for them, and re-layouts: 82.5 us -> 7.73 us
  blocking collectives: 0 us -> 17.8 us
  starting transfers between devices: 75.5 us -> 61.7 us
  other arithmetic: 11.2 us -> 0 us
    pallas_call x10 -> x13, Pallas kernels: 195 us -> 119 us  [the longest x11 110 us: lane_call(): pl.pallas_call(kernel, name=name, grid=(blocks,), in_specs=[spec(a.shape,...]
    unnamed x97 -> x44, local copies, waits for them, and re-layouts: 49.7 us -> 5.38 us
    all_to_all x0 -> x1, blocking collectives: none -> 17.8 us  [exchanged(): return lax.all_to_all(array, AXES, split_axis=0, concat_axis=0, tiled=True)]
    all_to_all x4 -> x3, starting transfers between devices: 35.3 us -> 20.4 us  [exchanged(): return lax.all_to_all(array, AXES, split_axis=0, concat_axis=0, tiled=True)]
    slice x14 -> x0, local copies, waits for them, and re-layouts: 8.55 us -> none  [the longest x3 2.52 us: reversed_base(): return jnp.concatenate([base[:, :1], base[:, :0:-1]], 1)]
    concatenate x2 -> x0, local copies, waits for them, and re-layouts: 8.42 us -> none  [the longest x1 5.19 us: per_device(): jnp.concatenate([mr_short.reshape(9, channels).astype(F32), li_short.resh...]
    rev x2 -> x0, local copies, waits for them, and re-layouts: 6.22 us -> none  [reversed_base(): return jnp.concatenate([base[:, :1], base[:, :0:-1]], 1)]
    reduce_sum x1 -> x0, other arithmetic: 5.97 us -> none  [per_device(): jnp.sum(li_residue[:, :, None] * jnp.exp(-li_rate[:, :, None] * positions...]
  transfers between devices with their start and end apart: 13 -> 13, of which waited for: 1 -> 4; matrix products, arithmetic and copies ran while one was open for 11% -> 1% of each run, Pallas kernels for 44% -> 41%
where the time goes in v2:
time: 233 us; the launch traced here: 231 us
  Pallas kernels  123 us (53%)
  starting transfers between devices  61.7 us (26%)
  waiting for transfers between devices  18.9 us (8%)
  blocking collectives  17.8 us (8%)
  local copies, waits for them, and re-layouts  7.73 us (3%)
    pallas_call x11, Pallas kernels, lane_call(): pl.pallas_call(kernel, name=name, grid=(blocks,), in_specs=[spec(a.shape,...  110 us
    ppermute x10, starting transfers between devices, sent(): return lax.ppermute(array, AXES, pairs)  41.3 us
    all_to_all x3, starting transfers between devices, exchanged(): return lax.all_to_all(array, AXES, split_axis=0, concat_axis=0, tiled=True)  20.4 us
    all_to_all x1, blocking collectives, exchanged(): return lax.all_to_all(array, AXES, split_axis=0, concat_axis=0, tiled=True)  17.8 us
    ppermute x10, waiting for transfers between devices, sent(): return lax.ppermute(array, AXES, pairs)  13.7 us
    unnamed x44, local copies, waits for them, and re-layouts  5.38 us
    pallas_call x1, Pallas kernels, make_tables(): pl.pallas_call(kernel, name='tables', grid=(groups // block,), in_specs=[...  5.15 us
    all_to_all x3, waiting for transfers between devices, exchanged(): return lax.all_to_all(array, AXES, split_axis=0, concat_axis=0, tiled=True)  5.13 us
  transfers between devices with their start and end apart: 13, of which 4 were waited for; matrix products, arithmetic and copies ran while one was open for 1% of the time, Pallas kernels for 41%

profile of v2, /device:TPU:1, one launch (start us, length us, event | category | flops | bytes accessed | tf_op | source)
XLA Modules:
  0.0 230.6 jit_solution(13538549381268389304)
XLA Ops:
  0.7 3.6 %edges.1 = (bf16[16,8192]{1,0:T(8,128)(2,1)}, bf16[16,8192]{1,0:T(8,128)(2,1)}, bf16[8,8192]{1,0:T(8,128)(2,1)}) custom-call(bf16[128,8192]{1,0:T(8,128)(2,1)} %refs_4_.10, bf16[128,8192]{1,0:T(8,128)(2,1)} %refs_3_.13, bf16[128,8192]{1,0:T(8,128)(2,1)} %refs_4_.13, bf16[128,8192]{1,0:T(8,128)(2,1)} %refs_3_.11, bf16[128,8192]{1,0:T(8,128)(2,1)} %refs_3_.10, ...), custom_call_target="tpu_custom_call" | custom-call | bytes 12600000 | tf_op jit(solution)/shard_map/edges/pallas_call | solution.py:250
  4.3 4.0 %collective-permute-start = (bf16[16,8192]{1,0:T(8,128)(2,1)}, bf16[16,8192]{1,0:T(8,128)(2,1)S(1)}, u32[]{:S(2)}, u32[]{:S(2)}) collective-permute-start(bf16[16,8192]{1,0:T(8,128)(2,1)} %get-tuple-element.50), channel_id=1, source_target_pairs={{0,1},{1,2},{2,3},{3,4},{4,5},{5,6},{6,7},{7,8},{8,9},{9,10},{10,1... | collective-permute-start | bytes 786440 | tf_op jit(solution)/shard_map/ppermute | solution.py:514
  10.1 5.2 %tables.1 = (f32[24,8192]{1,0:T(8,128)}, f32[512,128]{1,0:T(8,128)}, f32[512,128]{1,0:T(8,128)}, f32[512,128]{1,0:T(8,128)}, f32[512,128]{1,0:T(8,128)}) custom-call(bf16[3,3,8192]{2,1,0:T(4,128)(2,1)} %mr.1, bf16[3,3,8192]{2,1,0:T(4,128)(2,1)} %li.1, f32[1,8192]{1,0:T(1,128)} %bitcast.3, bf16[128,512]{1,0:T(8,128)(2,1)} %filters.1, f32[512,16]{1,0:T(8,128)} %copy-done.6, ...), custom_call_target="tpu_custom_call" | custom-call | bytes 18000000 | tf_op jit(solution)/shard_map/tables/pallas_call | solution.py:293
  18.8 10.2 %upstream.1 = (bf16[128,8192]{1,0:T(8,128)(2,1)}, f32[128,8,128]{2,1,0:T(8,128)}) custom-call(bf16[128,8192]{1,0:T(8,128)(2,1)} %refs_3_.11, bf16[128,8192]{1,0:T(8,128)(2,1)} %refs_4_.11, bf16[16,8192]{1,0:T(8,128)(2,1)} %copy-done, f32[24,8192]{1,0:T(8,128)} %get-tuple-element.51.refs_3_.refs_6_.refs_1_.refs_7_.refs_11_, ...), custom_call_target="tpu_custom_call" | custom-call | bytes 25200000 | tf_op jit(solution)/shard_map/upstream/pallas_call | solution.py:73
  29.0 7.9 %all-to-all-start = ((f32[128,8,128]{2,1,0:T(8,128)}), f32[128,8,128]{2,1,0:T(8,128)S(1)}, u32[]{:S(2)}, u32[]{:S(2)}) async-start(f32[128,8,128]{2,1,0:T(8,128)} %get-tuple-element.52), calls=%async_computation | async-start | bytes 1048576 | tf_op jit(solution)/shard_map/all_to_all | solution.py:518
  36.9 7.7 %collective-permute-start.1 = (bf16[16,8192]{1,0:T(8,128)(2,1)S(1)}, bf16[16,8192]{1,0:T(8,128)(2,1)S(1)}, u32[]{:S(2)}, u32[]{:S(2)}) collective-permute-start(bf16[16,8192]{1,0:T(8,128)(2,1)S(1)} %copy-done.19), channel_id=1, source_target_pairs={{1,0},{2,1},{3,2},{4,3},{5,4},{6,5},{7,6},{8,7},{9,8},{10,9},{11,1... | collective-permute-start | bytes 786440 | tf_op jit(solution)/shard_map/ppermute | solution.py:514
  47.4 7.1 %collective-permute-done.2.refs_1_ = bf16[8,8192]{1,0:T(8,128)(2,1)S(1)} collective-permute-done((bf16[8,8192]{1,0:T(8,128)(2,1)S(1)}, bf16[8,8192]{1,0:T(8,128)(2,1)S(1)}, u32[]{:S(2)}, u32[]{:S(2)}) %collective-permute-start.2) | collective-permute-done | bytes 131104 | tf_op jit(solution)/shard_map/ppermute | solution.py:514
  57.5 8.5 %all-to-all-start.1 = ((f32[128,8,128]{2,1,0:T(8,128)}), f32[128,8,128]{2,1,0:T(8,128)S(1)}, u32[]{:S(2)}, u32[]{:S(2)}) async-start(f32[128,8,128]{2,1,0:T(8,128)} %scan_back.1), calls=%async_computation.1 | async-start | bytes 1048576 | tf_op jit(solution)/shard_map/all_to_all | solution.py:518
  66.0 4.4 %product_one.2.refs_2_ = bf16[128,4096]{1,0:T(8,128)(2,1)} custom-call(bf16[128,8192]{1,0:T(8,128)(2,1)} %refs_3_.13, bf16[128,8192]{1,0:T(8,128)(2,1)} %refs_4_.13, bf16[16,8192]{1,0:T(8,128)(2,1)} %copy-done, f32[24,8192]{1,0:T(8,128)} %get-tuple-element.51.refs_3_.refs_6_.refs_1_.refs_7_.refs_11_), custom_call_target="tpu_custom_call" | custom-call | bytes 14400000 | tf_op jit(solution)/shard_map/product_one/pallas_call | solution.py:73
  70.4 4.5 %product_one.3.refs_2_ = bf16[128,4096]{1,0:T(8,128)(2,1)} custom-call(bf16[128,8192]{1,0:T(8,128)(2,1)} %refs_3_.13, bf16[128,8192]{1,0:T(8,128)(2,1)} %refs_4_.13, bf16[16,8192]{1,0:T(8,128)(2,1)} %copy-done, f32[24,8192]{1,0:T(8,128)} %get-tuple-element.51.refs_3_.refs_6_.refs_1_.refs_7_.refs_11_), custom_call_target="tpu_custom_call" | custom-call | bytes 14400000 | tf_op jit(solution)/shard_map/product_one/pallas_call | solution.py:73
  75.0 5.1 %all-to-all-done.1.refs_1_ = f32[128,8,128]{2,1,0:T(8,128)S(1)} async-done(((f32[128,8,128]{2,1,0:T(8,128)}), f32[128,8,128]{2,1,0:T(8,128)S(1)}, u32[]{:S(2)}, u32[]{:S(2)}) %all-to-all-start.1) | async-done | bytes 524320 | tf_op jit(solution)/shard_map/all_to_all | solution.py:518
  85.2 11.2 %long_back_near.1.refs_0_ = f32[128,8192]{1,0:T(8,128)} custom-call(bf16[128,8192]{1,0:T(8,128)(2,1)} %get-tuple-element.68.refs_0_, f32[24,8192]{1,0:T(8,128)} %get-tuple-element.51.refs_3_.refs_6_.refs_1_.refs_7_.refs_11_, f32[512,128]{1,0:T(8,128)} %get-tuple-element.69.refs_2_.refs_14_), custom_call_target="tpu_custom_call" | custom-call | bytes 21600000 | tf_op jit(solution)/shard_map/long_back_near/pallas_call | solution.py:73
  96.5 7.2 %long_back.2 = (bf16[128,8192]{1,0:T(8,128)(2,1)}, f32[2,8192]{1,0:T(2,128)}, bf16[128,8192]{1,0:T(8,128)(2,1)}, f32[2,8192]{1,0:T(2,128)}, f32[1,8192]{1,0:T(1,128)}, /*index=5*/bf16[128,4096]{1,0:T(8,128)(2,1)}) custom-call(f32[128,8192]{1,0:T(8,128)} %long_back_near.1.refs_0_, f32[128,8,128]{2,1,0:T(8,128)} %copy-done.2, bf16[128,8192]{1,0:T(8,128)(2,1)} %refs_3_.11, ...), custom_call_target="tpu_custom_call" | custom-call | bytes 23400000 | tf_op jit(solution)/shard_map/long_back/pallas_call | solution.py:73
  103.7 6.8 %collective-permute-start.9 = (bf16[128,4096]{1,0:T(8,128)(2,1)}, bf16[128,4096]{1,0:T(8,128)(2,1)S(1)}, u32[]{:S(2)}, u32[]{:S(2)}) collective-permute-start(bf16[128,4096]{1,0:T(8,128)(2,1)} %get-tuple-element.85.refs_0_), channel_id=1, source_target_pairs={{1,0},{2,1},{3,2},{4,3},{5,4},{6,5},{7,6},{8,7},{9,8},{10,9},{11,1... | collective-permute-start | bytes 3145736 | tf_op jit(solution)/shard_map/ppermute | solution.py:514
  110.5 7.3 %long_back.3 = (bf16[128,8192]{1,0:T(8,128)(2,1)}, f32[2,8192]{1,0:T(2,128)}, bf16[128,8192]{1,0:T(8,128)(2,1)}, f32[2,8192]{1,0:T(2,128)}, f32[1,8192]{1,0:T(1,128)}, /*index=5*/bf16[128,4096]{1,0:T(8,128)(2,1)}) custom-call(f32[128,8192]{1,0:T(8,128)} %long_back_near.1.refs_0_, ...), custom_call_target="tpu_custom_call", output_to_operand_aliasing={{0}: (10, {}), {1}: (11, {}), {2}: (12, {}), {3}: (13, {}),... | custom-call | bytes 23400000 | tf_op jit(solution)/shard_map/long_back/pallas_call | solution.py:73
  121.4 16.0 %forward.2 = (bf16[128,8192]{1,0:T(8,128)(2,1)}, bf16[128,8192]{1,0:T(8,128)(2,1)}, f32[128,8192]{1,0:T(8,128)}, f32[128,8,128]{2,1,0:T(8,128)}, f32[6,8192]{1,0:T(8,128)}) custom-call(bf16[128,4096]{1,0:T(8,128)(2,1)} %collective-permute-done.4.refs_0_, bf16[8,8192]{1,0:T(8,128)(2,1)} %copy-done.11, bf16[128,4096]{1,0:T(8,128)(2,1)} %product_one.3.refs_2_, ...), custom_call_target="tpu_custom_call" | custom-call | bytes 54000000 | tf_op jit(solution)/shard_map/forward/pallas_call | solution.py:73
  137.4 16.1 %forward.3 = (bf16[128,8192]{1,0:T(8,128)(2,1)}, bf16[128,8192]{1,0:T(8,128)(2,1)}, f32[128,8192]{1,0:T(8,128)}, f32[128,8,128]{2,1,0:T(8,128)}, f32[6,8192]{1,0:T(8,128)}) custom-call(bf16[128,4096]{1,0:T(8,128)(2,1)} %collective-permute-done.3.refs_0_, ...), custom_call_target="tpu_custom_call", output_to_operand_aliasing={{0}: (10, {}), {1}: (11, {}), {2}: (12, {}), {3}: (13, {}),... | custom-call | bytes 54000000 | tf_op jit(solution)/shard_map/forward/pallas_call | solution.py:73
  153.5 17.8 %all_to_all.20.states_ref = f32[128,8,128]{2,1,0:T(8,128)} all-to-all(f32[128,8,128]{2,1,0:T(8,128)} %get-tuple-element.66.refs_2_), channel_id=1, replica_groups=mesh['ctx'=8,'ch'=16] {'ctx','ch'}, dimensions={0} | all-to-all | bytes 1048576 | tf_op jit(solution)/shard_map/all_to_all | solution.py:518
  173.4 4.0 %all-to-all-start.3 = ((f32[128,8,128]{2,1,0:T(8,128)}), f32[128,8,128]{2,1,0:T(8,128)S(1)}, u32[]{:S(2)}, u32[]{:S(2)}) async-start(f32[128,8,128]{2,1,0:T(8,128)} %scan_forward.1), calls=%async_computation.3 | async-start | bytes 1048576 | tf_op jit(solution)/shard_map/all_to_all | solution.py:518
  177.4 7.9 %collective-permute-start.5 = (f32[6,8192]{1,0:T(8,128)S(1)}, f32[6,8192]{1,0:T(8,128)S(1)}, u32[]{:S(2)}, u32[]{:S(2)}) collective-permute-start(f32[6,8192]{1,0:T(8,128)S(1)} %copy-done.12), channel_id=1, source_target_pairs={{1,0},{2,1},{3,2},{4,3},{5,4},{6,5},{7,6},{8,7},{9,8},{10,9},{11,1... | collective-permute-start | bytes 589832 | tf_op jit(solution)/shard_map/ppermute | solution.py:514
  190.4 3.8 %collective-permute-done.7.refs_2_ = f32[1,8192]{1,0:T(1,128)S(1)} collective-permute-done((f32[1,8192]{1,0:T(1,128)S(1)}, f32[1,8192]{1,0:T(1,128)S(1)}, u32[]{:S(2)}, u32[]{:S(2)}) %collective-permute-start.7) | collective-permute-done | bytes 32800 | tf_op jit(solution)/shard_map/ppermute | solution.py:514
  195.3 9.7 %medium_back.2 = (bf16[128,8192]{1,0:T(8,128)(2,1)}, bf16[128,8192]{1,0:T(8,128)(2,1)}, bf16[128,8192]{1,0:T(8,128)(2,1)}) custom-call(bf16[128,4096]{1,0:T(8,128)(2,1)} %get-tuple-element.85.refs_0_, bf16[128,4096]{1,0:T(8,128)(2,1)} %copy-done.9, f32[1,8192]{1,0:T(1,128)} %copy-done.14, bf16[128,8192]{1,0:T(8,128)(2,1)} %refs_3_.13, ...), custom_call_target="tpu_custom_call" | custom-call | bytes 30600000 | tf_op jit(solution)/shard_map/medium_back/pallas_call | solution.py:73
  206.0 9.8 %medium_back.3 = (bf16[128,8192]{1,0:T(8,128)(2,1)}, bf16[128,8192]{1,0:T(8,128)(2,1)}, bf16[128,8192]{1,0:T(8,128)(2,1)}) custom-call(bf16[128,4096]{1,0:T(8,128)(2,1)} %get-tuple-element.79.refs_0_, bf16[128,4096]{1,0:T(8,128)(2,1)} %copy-done.10, f32[1,8192]{1,0:T(1,128)} %copy-done.14, ...), custom_call_target="tpu_custom_call", output_to_operand_aliasing={{0}: (13, {}), {1}: (14, {}), {2}: (15, {})} | custom-call | bytes 30600000 | tf_op jit(solution)/shard_map/medium_back/pallas_call | solution.py:73
  216.6 14.0 %long_forward.1 = (bf16[128,8192]{1,0:T(8,128)(2,1)}, bf16[128,8192]{1,0:T(8,128)(2,1)}, bf16[128,8192]{1,0:T(8,128)(2,1)}) custom-call(f32[128,8192]{1,0:T(8,128)} %get-tuple-element.65.refs_0_, f32[128,8,128]{2,1,0:T(8,128)} %copy-done.8, f32[128,8,128]{2,1,0:T(8,128)} %get-tuple-element.66.refs_2_, bf16[128,8192]{1,0:T(8,128)(2,1)} %refs_3_.11, ...), custom_call_target="tpu_custom_call" | custom-call | bytes 50400000 | tf_op jit(solution)/shard_map/long_forward/pallas_call | solution.py:73
  (67 shorter events, 29.7 us)
Async XLA Ops:
  0.6 7.8 %copy-start.18 = (f32[512,16]{0,1:T(8,128)S(1)}, f32[512,16]{0,1:T(8,128)}, u32[]{:S(2)}) copy-start(f32[512,16]{0,1:T(8,128)} %param.22) | copy-start | bytes 98308
  4.3 13.8 %collective-permute-start = (bf16[16,8192]{1,0:T(8,128)(2,1)}, bf16[16,8192]{1,0:T(8,128)(2,1)S(1)}, u32[]{:S(2)}, u32[]{:S(2)}) collective-permute-start(bf16[16,8192]{1,0:T(8,128)(2,1)} %get-tuple-element.50), channel_id=1, source_target_pairs={{0,1},{1,2},{2,3},{3,4},{4,5},{5,6},{6,7},{7,8},{8,9},{9,10},{10,1... | collective-permute-start | bytes 786440 | tf_op jit(solution)/shard_map/ppermute | solution.py:514
  18.8 18.1 %copy-start.19 = (bf16[16,8192]{1,0:T(8,128)(2,1)S(1)}, bf16[16,8192]{1,0:T(8,128)(2,1)}, u32[]{:S(2)}) copy-start(bf16[16,8192]{1,0:T(8,128)(2,1)} %get-tuple-element.53) | copy-start | bytes 786436
  18.8 25.9 %copy-start.20 = (bf16[8,8192]{1,0:T(8,128)(2,1)S(1)}, bf16[8,8192]{1,0:T(8,128)(2,1)}, u32[]{:S(2)}) copy-start(bf16[8,8192]{1,0:T(8,128)(2,1)} %get-tuple-element.54) | copy-start | bytes 393220
  29.0 25.6 %all-to-all-start = ((f32[128,8,128]{2,1,0:T(8,128)}), f32[128,8,128]{2,1,0:T(8,128)S(1)}, u32[]{:S(2)}, u32[]{:S(2)}) async-start(f32[128,8,128]{2,1,0:T(8,128)} %get-tuple-element.52), calls=%async_computation | async-start | bytes 1048576 | tf_op jit(solution)/shard_map/all_to_all | solution.py:518
  36.9 17.6 %collective-permute-start.1 = (bf16[16,8192]{1,0:T(8,128)(2,1)S(1)}, bf16[16,8192]{1,0:T(8,128)(2,1)S(1)}, u32[]{:S(2)}, u32[]{:S(2)}) collective-permute-start(bf16[16,8192]{1,0:T(8,128)(2,1)S(1)} %copy-done.19), channel_id=1, source_target_pairs={{1,0},{2,1},{3,2},{4,3},{5,4},{6,5},{7,6},{8,7},{9,8},{10,9},{11,1... | collective-permute-start | bytes 786440 | tf_op jit(solution)/shard_map/ppermute | solution.py:514
  44.7 9.9 %collective-permute-start.2 = (bf16[8,8192]{1,0:T(8,128)(2,1)S(1)}, bf16[8,8192]{1,0:T(8,128)(2,1)S(1)}, u32[]{:S(2)}, u32[]{:S(2)}) collective-permute-start(bf16[8,8192]{1,0:T(8,128)(2,1)S(1)} %copy-done.20), channel_id=1, source_target_pairs={{0,2},{1,3},{2,4},{3,5},{4,6},{5,7},{6,8},{7,9},{8,10},{9,11},{10,... | collective-permute-start | bytes 393224 | tf_op jit(solution)/shard_map/ppermute | solution.py:514
  54.6 20.4 %copy-start.11 = (bf16[8,8192]{1,0:T(8,128)(2,1)}, bf16[8,8192]{1,0:T(8,128)(2,1)S(1)}, u32[]{:S(2)}) copy-start(bf16[8,8192]{1,0:T(8,128)(2,1)S(1)} %collective-permute-done.2.refs_1_) | copy-start | bytes 393220
  54.6 15.9 %copy-start.1 = (bf16[16,8192]{1,0:T(8,128)(2,1)}, bf16[16,8192]{1,0:T(8,128)(2,1)S(1)}, u32[]{:S(2)}) copy-start(bf16[16,8192]{1,0:T(8,128)(2,1)S(1)} %collective-permute-done.1.refs_6_) | copy-start | bytes 786436
  57.5 22.6 %all-to-all-start.1 = ((f32[128,8,128]{2,1,0:T(8,128)}), f32[128,8,128]{2,1,0:T(8,128)S(1)}, u32[]{:S(2)}, u32[]{:S(2)}) async-start(f32[128,8,128]{2,1,0:T(8,128)} %scan_back.1), calls=%async_computation.1 | async-start | bytes 1048576 | tf_op jit(solution)/shard_map/all_to_all | solution.py:518
  70.4 11.9 %copy-start.3 = (bf16[128,4096]{1,0:T(8,128)(2,1)S(1)}, bf16[128,4096]{1,0:T(8,128)(2,1)}, u32[]{:S(2)}) copy-start(bf16[128,4096]{1,0:T(8,128)(2,1)} %product_one.2.refs_2_) | copy-start | bytes 3145732
  70.4 14.1 %copy-start.5 = (f32[512,16]{1,0:T(8,128)S(1)}, f32[512,16]{1,0:T(8,128)}, u32[]{:S(2)}) copy-start(f32[512,16]{1,0:T(8,128)} %copy.36.residue) | copy-start | bytes 98308
  80.1 16.4 %copy-start.2 = (f32[128,8,128]{2,1,0:T(8,128)}, f32[128,8,128]{2,1,0:T(8,128)S(1)}, u32[]{:S(2)}) copy-start(f32[128,8,128]{2,1,0:T(8,128)S(1)} %all-to-all-done.1.refs_1_) | copy-start | bytes 1572868
  80.1 41.3 %collective-permute-start.4 = (bf16[128,4096]{1,0:T(8,128)(2,1)}, bf16[128,4096]{1,0:T(8,128)(2,1)}, u32[]{:S(2)}, u32[]{:S(2)}) collective-permute-start(bf16[128,4096]{1,0:T(8,128)(2,1)} %product_one.3.refs_2_), channel_id=1, source_target_pairs={{0,1},{1,2},{2,3},{3,4},{4,5},{5,6},{6,7},{7,8},{8,9},{9,10},{10,1... | collective-permute-start | bytes 3145736 | tf_op jit(solution)/shard_map/ppermute | solution.py:514
  82.4 55.0 %collective-permute-start.3 = (bf16[128,4096]{1,0:T(8,128)(2,1)S(1)}, bf16[128,4096]{1,0:T(8,128)(2,1)}, u32[]{:S(2)}, u32[]{:S(2)}) collective-permute-start(bf16[128,4096]{1,0:T(8,128)(2,1)S(1)} %copy-done.3), channel_id=1, source_target_pairs={{0,1},{1,2},{2,3},{3,4},{4,5},{5,6},{6,7},{7,8},{8,9},{9,10},{10,1... | collective-permute-start | bytes 3145736 | tf_op jit(solution)/shard_map/ppermute | solution.py:514
  103.7 90.5 %collective-permute-start.9 = (bf16[128,4096]{1,0:T(8,128)(2,1)}, bf16[128,4096]{1,0:T(8,128)(2,1)S(1)}, u32[]{:S(2)}, u32[]{:S(2)}) collective-permute-start(bf16[128,4096]{1,0:T(8,128)(2,1)} %get-tuple-element.85.refs_0_), channel_id=1, source_target_pairs={{1,0},{2,1},{3,2},{4,3},{5,4},{6,5},{7,6},{8,7},{9,8},{10,9},{11,1... | collective-permute-start | bytes 3145736 | tf_op jit(solution)/shard_map/ppermute | solution.py:514
  117.8 87.2 %collective-permute-start.6 = (bf16[128,4096]{1,0:T(8,128)(2,1)}, bf16[128,4096]{1,0:T(8,128)(2,1)S(1)}, u32[]{:S(2)}, u32[]{:S(2)}) collective-permute-start(bf16[128,4096]{1,0:T(8,128)(2,1)} %get-tuple-element.79.refs_0_), channel_id=1, source_target_pairs={{1,0},{2,1},{3,2},{4,3},{5,4},{6,5},{7,6},{8,7},{9,8},{10,9},{11,1... | collective-permute-start | bytes 3145736 | tf_op jit(solution)/shard_map/ppermute | solution.py:514
  153.5 24.0 %copy-start.12 = (f32[6,8192]{1,0:T(8,128)S(1)}, f32[6,8192]{1,0:T(8,128)}, u32[]{:S(2)}) copy-start(f32[6,8192]{1,0:T(8,128)} %get-tuple-element.67) | copy-start | bytes 589828
  153.5 31.8 %copy-start.15 = (f32[2,8192]{1,0:T(2,128)S(1)}, f32[2,8192]{1,0:T(2,128)}, u32[]{:S(2)}) copy-start(f32[2,8192]{1,0:T(2,128)} %get-tuple-element.82) | copy-start | bytes 196612
  153.5 34.5 %copy-start.17 = (f32[1,8192]{1,0:T(1,128)S(1)}, f32[1,8192]{1,0:T(1,128)}, u32[]{:S(2)}) copy-start(f32[1,8192]{1,0:T(1,128)} %get-tuple-element.80) | copy-start | bytes 98308
  173.4 42.4 %all-to-all-start.3 = ((f32[128,8,128]{2,1,0:T(8,128)}), f32[128,8,128]{2,1,0:T(8,128)S(1)}, u32[]{:S(2)}, u32[]{:S(2)}) async-start(f32[128,8,128]{2,1,0:T(8,128)} %scan_forward.1), calls=%async_computation.3 | async-start | bytes 1048576 | tf_op jit(solution)/shard_map/all_to_all | solution.py:518
  177.4 16.8 %collective-permute-start.5 = (f32[6,8192]{1,0:T(8,128)S(1)}, f32[6,8192]{1,0:T(8,128)S(1)}, u32[]{:S(2)}, u32[]{:S(2)}) collective-permute-start(f32[6,8192]{1,0:T(8,128)S(1)} %copy-done.12), channel_id=1, source_target_pairs={{1,0},{2,1},{3,2},{4,3},{5,4},{6,5},{7,6},{8,7},{9,8},{10,9},{11,1... | collective-permute-start | bytes 589832 | tf_op jit(solution)/shard_map/ppermute | solution.py:514
  185.3 8.9 %collective-permute-start.8 = (f32[2,8192]{1,0:T(2,128)S(1)}, f32[2,8192]{1,0:T(2,128)S(1)}, u32[]{:S(2)}, u32[]{:S(2)}) collective-permute-start(f32[2,8192]{1,0:T(2,128)S(1)} %copy-done.15), channel_id=1, source_target_pairs={{1,0},{2,1},{3,2},{4,3},{5,4},{6,5},{7,6},{8,7},{9,8},{10,9},{11,1... | collective-permute-start | bytes 196616 | tf_op jit(solution)/shard_map/ppermute | solution.py:514
  188.0 6.2 %collective-permute-start.7 = (f32[1,8192]{1,0:T(1,128)S(1)}, f32[1,8192]{1,0:T(1,128)S(1)}, u32[]{:S(2)}, u32[]{:S(2)}) collective-permute-start(f32[1,8192]{1,0:T(1,128)S(1)} %copy-done.17), channel_id=1, source_target_pairs={{2,0},{3,1},{4,2},{5,3},{6,4},{7,5},{8,6},{9,7},{10,8},{11,9},{12,... | collective-permute-start | bytes 98312 | tf_op jit(solution)/shard_map/ppermute | solution.py:514
  (10 other events, 16.0 us)

commit v3 on v2

--- a/solution.py
+++ b/solution.py
@@ -29,10 +29,15 @@
     )
 
 
-def lane_call(body, name, channels, ins, outs, scratch, us, part=(0, 1), into=None, width=1024, unroll=2):
+def hint(start, of):
+    return start if isinstance(start, int) else pl.multiple_of(start, of)
+
+
+def lane_call(body, name, channels, ins, outs, scratch, us, part=(0, 1), into=None, width=1024, unroll=8):
     span = channels // part[1]
     width = min(width, span)
     tiles = width // LANES
+    unroll = min(unroll, tiles)
     blocks = span // width
     into = into or {}
 
@@ -47,9 +52,9 @@
 
     def view(ref, kind, t):
         if kind == "r":
-            return ref.at[:, pl.ds(pl.multiple_of(t * LANES, LANES), LANES)]
+            return ref.at[:, pl.ds(hint(t * LANES, LANES), LANES)]
         if kind == "g":
-            return ref.at[pl.ds(pl.multiple_of(t * TILE_GROUPS, TILE_GROUPS), TILE_GROUPS), :]
+            return ref.at[pl.ds(hint(t * TILE_GROUPS, TILE_GROUPS), TILE_GROUPS), :]
         return ref.at[pl.ds(2 * t, 2)]
 
     kinds = [kind for _, kind in ins] + [kind for _, _, kind in outs]
@@ -61,14 +66,17 @@
 
         def step(k, unused):
             for u in range(unroll):
-                t = k * unroll + u
+                t = u if unroll == tiles else k * unroll + u
                 body(
                     *[view(ref, kind, t) for ref, kind in zip(arrays, kinds)],
                     *[ref.at[u] for ref in extra],
                 )
             return unused
 
-        lax.fori_loop(0, tiles // unroll, step, 0)
+        if unroll == tiles:
+            step(0, 0)
+        else:
+            lax.fori_loop(0, tiles // unroll, step, 0)
 
     return pl.pallas_call(
         kernel,
@@ -162,31 +170,33 @@
     return signal * (1.0 - odd).astype(signal.dtype), signal * odd.astype(signal.dtype)
 
 
-def long_product(base_ref, signal, tables, backward):
+def long_product(base_ref, signal, backward):
     base = base_ref[...]
     row, lane = iota((STRIP, LANES), 0), iota((STRIP, LANES), 1)
     first = 0 if backward else STRIP - LANES
     keep = lane >= row if backward else lane + first <= row
-    for g in range(TILE_GROUPS):
-        p, half = g // 2, g % 2
-        table = jnp.where(keep, circulant(base, g, STRIP, -first), 0.0).astype(BF16)
-        tables[p * STRIP : (p + 1) * STRIP, half * LANES : (half + 1) * LANES] = table
+    tables = [
+        jnp.where(keep, circulant(base, g, STRIP, -first), 0.0).astype(BF16)
+        for g in range(TILE_GROUPS)
+    ]
+    left = jnp.concatenate(
+        [jnp.concatenate(tables[0::2], 0), jnp.concatenate(tables[1::2], 0)], 1
+    )
     even, odd = split_groups(signal)
     right = jnp.concatenate([windows(even, first, LANES), windows(odd, first, LANES)], 0)
-    return pick(jnp.dot(tables[...], right, preferred_element_type=F32), STRIP, TILE_GROUPS // 2)
-
-
-def medium_product(base_ref, pair, tables, backward):
+    return pick(jnp.dot(left, right, preferred_element_type=F32), STRIP, TILE_GROUPS // 2)
+
+
+def medium_product(base_ref, pair, backward):
     base = base_ref[...]
     row, lane = iota((STRIP, LANES), 0), iota((STRIP, LANES), 1)
-    for g in range(TILE_GROUPS):
-        whole = circulant(base, g, STRIP)
-        keep = lane >= row if backward else lane > row
-        rows = slice(g * STRIP, (g + 1) * STRIP)
-        tables[rows, 0:LANES] = jnp.where(keep, whole, 0.0).astype(BF16)
-        tables[rows, LANES:] = jnp.where(keep, 0.0, whole).astype(BF16)
-    products = jnp.dot(tables[...], windows(pair, 0, 2 * LANES), preferred_element_type=F32)
-    return pick(products, STRIP, TILE_GROUPS)
+    keep = lane >= row if backward else lane > row
+    wholes = [circulant(base, g, STRIP) for g in range(TILE_GROUPS)]
+    first = [jnp.where(keep, whole, 0.0).astype(BF16) for whole in wholes]
+    second = [jnp.where(keep, 0.0, whole).astype(BF16) for whole in wholes]
+    left = jnp.concatenate([jnp.concatenate(first, 0), jnp.concatenate(second, 0)], 1)
+    products = jnp.dot(left, windows(pair, 0, 2 * LANES), preferred_element_type=F32)
+    return pick(products, STRIP, TILE_GROUPS), first
 
 
 def on_channels(base, column):
@@ -326,9 +336,9 @@
     cotangent[...] = rounded
 
 
-def long_back_near_body(cotangent, table, base, near, tables):
+def long_back_near_body(cotangent, table, base, near):
     signal = cotangent[...]
-    product = long_product(base, signal, tables, True)
+    product = long_product(base, signal, True)
     near[...] = product + table[SKIP : SKIP + 1, :] * signal.astype(F32)
 
 
@@ -374,21 +384,23 @@
 
 
 def forward_body(
-    before, before_kv, signal, query, li_key, prev, table, base_ref, base_long, rate,
-    conv_one, value_two, near, state, head, ext_q, ext_k, ext_m, tables, tables_edge, tables_long,
+    before, before_kv, signal, query, li_key, prev, mixed_head, table, base_ref, base_long, rate,
+    conv_one, value_two, near, state, head, ext_q, ext_k, ext_m,
 ):
     weights = table[...]
     earlier = before[...]
     pair = jnp.concatenate([earlier, signal[...]], 0)
-    conv = medium_product(base_ref, pair, tables, False)
+    conv, _ = medium_product(base_ref, pair, False)
     base = base_ref[...]
     row, lane = iota((16, LANES), 0), iota((16, LANES), 1)
-    for g in range(TILE_GROUPS):
-        whole = circulant(base, g, 16, ROWS - 16)
-        tables_edge[g * 16 : (g + 1) * 16, :] = jnp.where(
-            lane <= row + (ROWS - 16), whole, 0.0
-        ).astype(BF16)
-    edge = pick(jnp.dot(tables_edge[...], earlier, preferred_element_type=F32), 16, TILE_GROUPS)
+    left = jnp.concatenate(
+        [
+            jnp.where(lane <= row + (ROWS - 16), circulant(base, g, 16, ROWS - 16), 0.0).astype(BF16)
+            for g in range(TILE_GROUPS)
+        ],
+        0,
+    )
+    edge = pick(jnp.dot(left, earlier, preferred_element_type=F32), 16, TILE_GROUPS)
     raw = before_kv[...].astype(F32)
     w_k, w_v = taps(weights, MR_K), taps(weights, MR_V)
     key_last = w_k[0] * raw[3:4] + w_k[1] * raw[2:3] + w_k[2] * raw[1:2]
@@ -416,17 +428,18 @@
     conv_one[...] = conv.astype(BF16)
     value_two[...] = value.astype(BF16)
     near[...] = (
-        long_product(base_long, rounded, tables_long, False) + weights[SKIP : SKIP + 1] * product
+        long_product(base_long, rounded, False) + weights[SKIP : SKIP + 1] * product
     )
     head[0:2, :] = product[0:2]
     head[2:4, :] = value[0:2]
     head[4:6, :] = conv[0:2]
+    head[6:8, :] = mixed_head[...]
 
 
 def long_body(
     near, start, end, li_query, upstream, prev, following, next_head, grad_two, grad_two_after,
-    value_two, table, rate, residue, base_back,
-    out, grad_li_query, grad_li_key, ext_q, ext_g, ext_k,
+    value_two, mixed_grad, conv_one, table, rate, residue, base_back,
+    out, grad_li_query, grad_li_key, grad_mr_query, ext_q, ext_g, ext_k, ext_m,
 ):
     weights = table[...]
     distance = (iota((ROWS + 16, LANES), 0) + 1).astype(F32)
@@ -452,20 +465,20 @@
     fill(ext_k, grad_two[...].astype(F32) * value_two[...].astype(F32))
     ext_k[8 + ROWS : 10 + ROWS, :] = grad_two_after[...] * next_head[2:4, :]
     grad_li_key[...] = short_backward(ext_k, taps(weights, LI_K)).astype(BF16)
+    fill(ext_m, mixed_grad[...].astype(F32) * conv_one[...].astype(F32))
+    ext_m[8 + ROWS : 10 + ROWS, :] = next_head[6:8, :] * next_head[4:6, :]
+    grad_mr_query[...] = short_backward(ext_m, taps(weights, MR_Q)).astype(BF16)
 
 
 def medium_back_body(
-    conv_grad, after, after_next, key, value, prev, following, mixed_grad, mixed_after,
-    conv_one, next_head, table, base_ref,
-    grad_query, grad_key, grad_value, ext_k, ext_v, ext_gk, ext_gv, ext_q, tables,
+    conv_grad, after, after_next, key, value, prev, following, table, base_ref,
+    grad_key, grad_value, ext_k, ext_v, ext_gk, ext_gv,
 ):
     weights = table[...]
     later = after[...]
     pair = jnp.concatenate([conv_grad[...], later], 0)
-    grad = medium_product(base_ref, pair, tables, True)
-    left = jnp.concatenate(
-        [tables[g * STRIP : g * STRIP + 16, 0:LANES] for g in range(TILE_GROUPS)], 0
-    )
+    grad, first_half = medium_product(base_ref, pair, True)
+    left = jnp.concatenate([part[0:16] for part in first_half], 0)
     edge = pick(jnp.dot(left, later, preferred_element_type=F32), 16, TILE_GROUPS)
     far = on_channels(base_ref[...], MR_TAPS - 1) * after_next[...].astype(BF16).astype(F32)
     past = edge[0:8] + jnp.where(iota((8, LANES), 0) == 1, far, 0.0)
@@ -479,9 +492,6 @@
     fill(ext_gv, grad * keys_one[0:ROWS], None, past * keys_one[ROWS:])
     grad_key[...] = short_backward(ext_gk, taps(weights, MR_K)).astype(BF16)
     grad_value[...] = short_backward(ext_gv, taps(weights, MR_V)).astype(BF16)
-    fill(ext_q, mixed_grad[...].astype(F32) * conv_one[...].astype(F32))
-    ext_q[8 + ROWS : 10 + ROWS, :] = mixed_after[...] * next_head[4:6, :]
-    grad_query[...] = short_backward(ext_q, taps(weights, MR_Q)).astype(BF16)
 
 
 def scan_states(states, rates, backward):
@@ -554,33 +564,29 @@
     )
     my_rates = jnp.repeat(my_rates.T, GROUP, axis=1)
 
-    tables_long = ((TILE_GROUPS // 2 * STRIP, 2 * LANES), BF16)
-    tables_medium = ((TILE_GROUPS * STRIP, 2 * LANES), BF16)
-    tables_edge = ((TILE_GROUPS * 16, LANES), BF16)
-
     cotangent, state_back = lane_call(
         upstream_body, "upstream", channels,
         [(li_query, "r"), (upstream, "r"), (prev, "r"), (table, "r"), (rate, "r")],
         [full, state_out], [EXT], 7,
     )
-    gathered_back = after(exchanged(state_back), following, before_kv)
+    gathered_back = exchanged(state_back)
+    (near_back,) = lane_call(
+        long_back_near_body, "long_back_near", channels,
+        [(cotangent, "r"), (table, "r"), (long_turned, "g")],
+        [full32], [], 6, unroll=4,
+    )
+    gathered_back = after(gathered_back, following, before_kv, near_back)
     signal_one = [
         lane_call(
             product_one_body, "product_one", channels,
             [(mr_key, "r"), (mr_value, "r"), (prev, "r"), (table, "r")],
-            [half], [EXT, EXT], 4, part,
+            [half], [EXT, EXT], 3, part,
         )[0]
         for part in halves
     ]
-    (near_back,) = lane_call(
-        long_back_near_body, "long_back_near", channels,
-        [(cotangent, "r"), (table, "r"), (long_turned, "g")],
-        [full32], [tables_long], 6,
-    )
     closing = exchanged(scan_states(gathered_back, my_rates, True))
     before_one = [sent(after(signal, closing), 1) for signal in signal_one]
 
-    outs = [full, few(2), full, few(2), few(1), half]
     into = {}
     conv_grad = []
     for part in halves:
@@ -588,13 +594,13 @@
             long_back_body, "long_back", channels,
             [(near_back, "r"), (closing, "s"), (li_query, "r"), (li_key, "r"), (mr_query, "r"),
              (prev, "r"), (following, "r"), (table, "r"), (rate, "r"), (residue, "r")],
-            outs, [EXT, EXT, EXT, EXT], 6.5, part, into,
+            [full, few(2), full, few(2), few(1), half],
+            [EXT, EXT, EXT, EXT], 6, part, into, unroll=4,
         )
         conv_grad.append(got[5])
         into = dict(enumerate(got[:5]))
     grad_two, grad_two_after, mixed_grad, mixed_head, conv_head, _ = got
     after_one = [sent(signal, -1) for signal in conv_grad]
-    mixed_after = sent(mixed_head, -1)
     after_next = sent(conv_head, -2)
 
     into = {}
@@ -602,34 +608,38 @@
         got = lane_call(
             forward_body, "forward", channels,
             [(before_one[n], "r"), (before_kv, "r"), (signal_one[n], "r"), (mr_query, "r"),
-             (li_key, "r"), (prev, "r"), (table, "r"), (medium, "g"), (long, "g"), (rate, "r")],
-            [full, full, full32, state_out, few(6)],
-            [EXT, EXT, EXT, tables_medium, tables_edge, tables_long], 15, part, into,
+             (li_key, "r"), (prev, "r"), (mixed_head, "r"), (table, "r"), (medium, "g"),
+             (long, "g"), (rate, "r")],
+            [full, full, full32, state_out, few(8)],
+            [EXT, EXT, EXT], 14, part, into, unroll=4,
         )
         into = dict(enumerate(got))
     conv_one, value_two, near, state, head = got
     next_head = sent(head, -1)
-    start = exchanged(scan_states(exchanged(state), my_rates, False))
-
-    output, grad_li_query, grad_li_key = lane_call(
+
+    def medium_back(n, into):
+        return lane_call(
+            medium_back_body, "medium_back", channels,
+            [(conv_grad[n], "r"), (after_one[n], "r"), (after_next, "r"), (mr_key, "r"),
+             (mr_value, "r"), (prev, "r"), (following, "r"), (table, "r"), (medium_turned, "g")],
+            [full, full], [EXT, EXT, EXT, EXT], 8, halves[n], into, unroll=4,
+        )
+
+    gathered = exchanged(state)
+    got = medium_back(0, {})
+    gathered = after(gathered, next_head, after_next, *got)
+    start = exchanged(scan_states(gathered, my_rates, False))
+    grad_mr_key, grad_mr_value = medium_back(1, dict(enumerate(got)))
+    start = after(start, grad_mr_key)
+
+    output, grad_li_query, grad_li_key, grad_mr_query = lane_call(
         long_body, "long_forward", channels,
         [(near, "r"), (start, "s"), (state, "s"), (li_query, "r"), (upstream, "r"), (prev, "r"),
          (following, "r"), (next_head, "r"), (grad_two, "r"), (grad_two_after, "r"),
-         (value_two, "r"), (table, "r"), (rate, "r"), (residue, "r"), (long_turned, "g")],
-        [full, full, full], [EXT, EXT, EXT], 14,
-    )
-    into = {}
-    for n, part in enumerate(halves):
-        got = lane_call(
-            medium_back_body, "medium_back", channels,
-            [(conv_grad[n], "r"), (after_one[n], "r"), (after_next, "r"), (mr_key, "r"),
-             (mr_value, "r"), (prev, "r"), (following, "r"), (mixed_grad, "r"),
-             (mixed_after, "r"), (conv_one, "r"), (next_head, "r"), (table, "r"),
-             (medium_turned, "g")],
-            [full, full, full], [EXT, EXT, EXT, EXT, EXT, tables_medium], 8.5, part, into,
-        )
-        into = dict(enumerate(got))
-    grad_mr_query, grad_mr_key, grad_mr_value = got
+         (value_two, "r"), (mixed_grad, "r"), (conv_one, "r"), (table, "r"), (rate, "r"),
+         (residue, "r"), (long_turned, "g")],
+        [full, full, full, full], [EXT, EXT, EXT, EXT], 14, unroll=4,
+    )
     return (output, grad_mr_query, grad_mr_key, grad_mr_value, grad_li_query, grad_li_key)
 
 

time: 233 us -> 222 us (0.953)
  blocking collectives: 17.8 us -> 0 us
  starting transfers between devices: 61.7 us -> 77.4 us
  Pallas kernels: 123 us -> 111 us
  waiting for transfers between devices: 18.9 us -> 22 us
    all_to_all x3 -> x4, starting transfers between devices: 20.4 us -> 38.6 us  [exchanged(): return lax.all_to_all(array, AXES, split_axis=0, concat_axis=0, tiled=True)]
    all_to_all x1 -> x0, blocking collectives: 17.8 us -> none  [exchanged(): return lax.all_to_all(array, AXES, split_axis=0, concat_axis=0, tiled=True)]
    pallas_call x11, Pallas kernels: 110 us -> 98.3 us  [lane_call(): pl.pallas_call(kernel, name=name, grid=(blocks,), in_specs=[spec(a.shape,...]
    all_to_all x3 -> x4, waiting for transfers between devices: 5.13 us -> 15.3 us  [exchanged(): return lax.all_to_all(array, AXES, split_axis=0, concat_axis=0, tiled=True)]
    ppermute x10 -> x9, waiting for transfers between devices: 13.7 us -> 6.69 us  [sent(): return lax.ppermute(array, AXES, pairs)]
    ppermute x10 -> x9, starting transfers between devices: 41.3 us -> 38.8 us  [sent(): return lax.ppermute(array, AXES, pairs)]
    unnamed x44 -> x38, local copies, waits for them, and re-layouts: 5.38 us -> 6.16 us
  transfers between devices with their start and end apart: 13 -> 13, of which waited for: 4 -> 4; matrix products, arithmetic and copies ran while one was open for 1% -> 2% of each run, Pallas kernels for 41% -> 37%
where the time goes in v3:
time: 222 us; the launch traced here: 220 us
  Pallas kernels  111 us (50%)
  starting transfers between devices  77.4 us (35%)
  waiting for transfers between devices  22 us (10%)
  local copies, waits for them, and re-layouts  8.52 us (4%)
    pallas_call x11, Pallas kernels, lane_call(): pl.pallas_call(kernel, name=name, grid=(blocks,), in_specs=[spec(a.shape,...  98.3 us
    ppermute x9, starting transfers between devices, sent(): return lax.ppermute(array, AXES, pairs)  38.8 us
    all_to_all x4, starting transfers between devices, exchanged(): return lax.all_to_all(array, AXES, split_axis=0, concat_axis=0, tiled=True)  38.6 us
    all_to_all x4, waiting for transfers between devices, exchanged(): return lax.all_to_all(array, AXES, split_axis=0, concat_axis=0, tiled=True)  15.3 us
    ppermute x9, waiting for transfers between devices, sent(): return lax.ppermute(array, AXES, pairs)  6.69 us
    unnamed x38, local copies, waits for them, and re-layouts  6.16 us
    pallas_call x1, Pallas kernels, make_tables(): pl.pallas_call(kernel, name='tables', grid=(groups // block,), in_specs=[...  5.1 us
  transfers between devices with their start and end apart: 13, of which 4 were waited for; matrix products, arithmetic and copies ran while one was open for 2% of the time, Pallas kernels for 37%

profile of v3, /device:TPU:1, one launch (start us, length us, event | category | flops | bytes accessed | tf_op | source)
XLA Modules:
  0.0 220.1 jit_solution(2885356892406320404)
XLA Ops:
  0.7 3.6 %edges.1 = (bf16[16,8192]{1,0:T(8,128)(2,1)}, bf16[16,8192]{1,0:T(8,128)(2,1)}, bf16[8,8192]{1,0:T(8,128)(2,1)}) custom-call(bf16[128,8192]{1,0:T(8,128)(2,1)} %refs_3_.10, bf16[128,8192]{1,0:T(8,128)(2,1)} %refs_3_.12, bf16[128,8192]{1,0:T(8,128)(2,1)} %refs_4_.12, bf16[128,8192]{1,0:T(8,128)(2,1)} %refs_3_.13, bf16[128,8192]{1,0:T(8,128)(2,1)} %refs_4_.10, ...), custom_call_target="tpu_custom_call" | custom-call | bytes 12600000 | tf_op jit(solution)/shard_map/edges/pallas_call | solution.py:260
  4.3 4.0 %collective-permute-start = (bf16[16,8192]{1,0:T(8,128)(2,1)}, bf16[16,8192]{1,0:T(8,128)(2,1)S(1)}, u32[]{:S(2)}, u32[]{:S(2)}) collective-permute-start(bf16[16,8192]{1,0:T(8,128)(2,1)} %get-tuple-element.51), channel_id=1, source_target_pairs={{0,1},{1,2},{2,3},{3,4},{4,5},{5,6},{6,7},{7,8},{8,9},{9,10},{10,1... | collective-permute-start | bytes 786440 | tf_op jit(solution)/shard_map/ppermute | solution.py:524
  10.1 5.1 %tables.1 = (f32[24,8192]{1,0:T(8,128)}, f32[512,128]{1,0:T(8,128)}, f32[512,128]{1,0:T(8,128)}, f32[512,128]{1,0:T(8,128)}, f32[512,128]{1,0:T(8,128)}) custom-call(bf16[3,3,8192]{2,1,0:T(4,128)(2,1)} %mr.1, bf16[3,3,8192]{2,1,0:T(4,128)(2,1)} %li.1, f32[1,8192]{1,0:T(1,128)} %bitcast.3, bf16[128,512]{1,0:T(8,128)(2,1)} %filters.1, f32[512,16]{1,0:T(8,128)} %copy-done.4, ...), custom_call_target="tpu_custom_call" | custom-call | bytes 18000000 | tf_op jit(solution)/shard_map/tables/pallas_call | solution.py:303
  18.8 7.7 %upstream.1 = (bf16[128,8192]{1,0:T(8,128)(2,1)}, f32[128,8,128]{2,1,0:T(8,128)}) custom-call(bf16[128,8192]{1,0:T(8,128)(2,1)} %refs_3_.13, bf16[128,8192]{1,0:T(8,128)(2,1)} %refs_4_.13, bf16[16,8192]{1,0:T(8,128)(2,1)} %copy-done, f32[24,8192]{1,0:T(8,128)} %get-tuple-element.52.refs_3_.refs_1_.refs_7_.refs_13_, ...), custom_call_target="tpu_custom_call" | custom-call | bytes 25200000 | tf_op jit(solution)/shard_map/upstream/pallas_call | solution.py:81
  26.4 7.9 %all-to-all-start = ((f32[128,8,128]{2,1,0:T(8,128)}), f32[128,8,128]{2,1,0:T(8,128)S(1)}, u32[]{:S(2)}, u32[]{:S(2)}) async-start(f32[128,8,128]{2,1,0:T(8,128)} %get-tuple-element.53), calls=%async_computation | async-start | bytes 1048576 | tf_op jit(solution)/shard_map/all_to_all | solution.py:528
  34.3 7.7 %collective-permute-start.1 = (bf16[16,8192]{1,0:T(8,128)(2,1)S(1)}, bf16[16,8192]{1,0:T(8,128)(2,1)S(1)}, u32[]{:S(2)}, u32[]{:S(2)}) collective-permute-start(bf16[16,8192]{1,0:T(8,128)(2,1)S(1)} %copy-done.16), channel_id=1, source_target_pairs={{1,0},{2,1},{3,2},{4,3},{5,4},{6,5},{7,6},{8,7},{9,8},{10,9},{11,1... | collective-permute-start | bytes 786440 | tf_op jit(solution)/shard_map/ppermute | solution.py:524
  44.9 9.2 %long_back_near.1.refs_0_ = f32[128,8192]{1,0:T(8,128)} custom-call(bf16[128,8192]{1,0:T(8,128)(2,1)} %get-tuple-element.56.refs_0_, f32[24,8192]{1,0:T(8,128)} %get-tuple-element.52.refs_3_.refs_1_.refs_7_.refs_13_, f32[512,128]{1,0:T(8,128)} %get-tuple-element.57.refs_2_.refs_16_), custom_call_target="tpu_custom_call" | custom-call | bytes 21600000 | tf_op jit(solution)/shard_map/long_back_near/pallas_call | solution.py:81
  57.1 9.7 %all-to-all-start.1 = ((f32[128,8,128]{2,1,0:T(8,128)}), f32[128,8,128]{2,1,0:T(8,128)S(1)}, u32[]{:S(2)}, u32[]{:S(2)}) async-start(f32[128,8,128]{2,1,0:T(8,128)} %scan_back.1), calls=%async_computation.1 | async-start | bytes 1048576 | tf_op jit(solution)/shard_map/all_to_all | solution.py:528
  66.8 4.3 %product_one.3.refs_2_ = bf16[128,4096]{1,0:T(8,128)(2,1)} custom-call(bf16[128,8192]{1,0:T(8,128)(2,1)} %refs_3_.12, bf16[128,8192]{1,0:T(8,128)(2,1)} %refs_4_.12, bf16[16,8192]{1,0:T(8,128)(2,1)} %copy-done, f32[24,8192]{1,0:T(8,128)} %get-tuple-element.52.refs_3_.refs_1_.refs_7_.refs_13_), custom_call_target="tpu_custom_call" | custom-call | bytes 10800000 | tf_op jit(solution)/shard_map/product_one/pallas_call | solution.py:81
  71.1 9.8 %all-to-all-done.1.refs_1_ = f32[128,8,128]{2,1,0:T(8,128)S(1)} async-done(((f32[128,8,128]{2,1,0:T(8,128)}), f32[128,8,128]{2,1,0:T(8,128)S(1)}, u32[]{:S(2)}, u32[]{:S(2)}) %all-to-all-start.1) | async-done | bytes 524320 | tf_op jit(solution)/shard_map/all_to_all | solution.py:528
  83.1 4.3 %product_one.2.refs_2_ = bf16[128,4096]{1,0:T(8,128)(2,1)} custom-call(bf16[128,8192]{1,0:T(8,128)(2,1)} %refs_3_.12, bf16[128,8192]{1,0:T(8,128)(2,1)} %refs_4_.12, bf16[16,8192]{1,0:T(8,128)(2,1)} %copy-done, f32[24,8192]{1,0:T(8,128)} %get-tuple-element.52.refs_3_.refs_1_.refs_7_.refs_13_), custom_call_target="tpu_custom_call" | custom-call | bytes 10800000 | tf_op jit(solution)/shard_map/product_one/pallas_call | solution.py:81
  90.4 6.7 %long_back.2 = (bf16[128,8192]{1,0:T(8,128)(2,1)}, f32[2,8192]{1,0:T(2,128)}, bf16[128,8192]{1,0:T(8,128)(2,1)}, f32[2,8192]{1,0:T(2,128)}, f32[1,8192]{1,0:T(1,128)}, /*index=5*/bf16[128,4096]{1,0:T(8,128)(2,1)}) custom-call(f32[128,8192]{1,0:T(8,128)} %long_back_near.1.refs_0_, f32[128,8,128]{2,1,0:T(8,128)} %copy-done.2, bf16[128,8192]{1,0:T(8,128)(2,1)} %refs_3_.13, ...), custom_call_target="tpu_custom_call" | custom-call | bytes 21600000 | tf_op jit(solution)/shard_map/long_back/pallas_call | solution.py:81
  97.0 6.8 %collective-permute-start.7 = (bf16[128,4096]{1,0:T(8,128)(2,1)}, bf16[128,4096]{1,0:T(8,128)(2,1)S(1)}, u32[]{:S(2)}, u32[]{:S(2)}) collective-permute-start(bf16[128,4096]{1,0:T(8,128)(2,1)} %get-tuple-element.78.refs_0_), channel_id=1, source_target_pairs={{1,0},{2,1},{3,2},{4,3},{5,4},{6,5},{7,6},{8,7},{9,8},{10,9},{11,1... | collective-permute-start | bytes 3145736 | tf_op jit(solution)/shard_map/ppermute | solution.py:524
  103.8 6.7 %long_back.3 = (bf16[128,8192]{1,0:T(8,128)(2,1)}, f32[2,8192]{1,0:T(2,128)}, bf16[128,8192]{1,0:T(8,128)(2,1)}, f32[2,8192]{1,0:T(2,128)}, f32[1,8192]{1,0:T(1,128)}, /*index=5*/bf16[128,4096]{1,0:T(8,128)(2,1)}) custom-call(f32[128,8192]{1,0:T(8,128)} %long_back_near.1.refs_0_, ...), custom_call_target="tpu_custom_call", output_to_operand_aliasing={{0}: (10, {}), {1}: (11, {}), {2}: (12, {}), {3}: (13, {}),... | custom-call | bytes 21600000 | tf_op jit(solution)/shard_map/long_back/pallas_call | solution.py:81
  114.1 14.3 %forward.2 = (bf16[128,8192]{1,0:T(8,128)(2,1)}, bf16[128,8192]{1,0:T(8,128)(2,1)}, f32[128,8192]{1,0:T(8,128)}, f32[128,8,128]{2,1,0:T(8,128)}, f32[8,8192]{1,0:T(8,128)}) custom-call(bf16[128,4096]{1,0:T(8,128)(2,1)} %collective-permute-done.4.refs_0_, bf16[8,8192]{1,0:T(8,128)(2,1)} %copy-done.10, bf16[128,4096]{1,0:T(8,128)(2,1)} %product_one.3.refs_2_, ...), custom_call_target="tpu_custom_call" | custom-call | bytes 50400000 | tf_op jit(solution)/shard_map/forward/pallas_call | solution.py:81
  128.4 14.3 %forward.3 = (bf16[128,8192]{1,0:T(8,128)(2,1)}, bf16[128,8192]{1,0:T(8,128)(2,1)}, f32[128,8192]{1,0:T(8,128)}, f32[128,8,128]{2,1,0:T(8,128)}, f32[8,8192]{1,0:T(8,128)}) custom-call(bf16[128,4096]{1,0:T(8,128)(2,1)} %collective-permute-done.3.refs_0_, ...), custom_call_target="tpu_custom_call", output_to_operand_aliasing={{0}: (11, {}), {1}: (12, {}), {2}: (13, {}), {3}: (14, {}),... | custom-call | bytes 50400000 | tf_op jit(solution)/shard_map/forward/pallas_call | solution.py:81
  142.8 11.2 %all-to-all-start.2 = ((f32[128,8,128]{2,1,0:T(8,128)}), f32[128,8,128]{2,1,0:T(8,128)S(1)}, u32[]{:S(2)}, u32[]{:S(2)}) async-start(f32[128,8,128]{2,1,0:T(8,128)} %get-tuple-element.75.refs_2_), calls=%async_computation.2 | async-start | bytes 1048576 | tf_op jit(solution)/shard_map/all_to_all | solution.py:528
  154.0 7.7 %collective-permute-start.5 = (f32[8,8192]{1,0:T(8,128)}, f32[8,8192]{1,0:T(8,128)S(1)}, u32[]{:S(2)}, u32[]{:S(2)}) collective-permute-start(f32[8,8192]{1,0:T(8,128)} %get-tuple-element.76), channel_id=1, source_target_pairs={{1,0},{2,1},{3,2},{4,3},{5,4},{6,5},{7,6},{8,7},{9,8},{10,9},{11,1... | collective-permute-start | bytes 786440 | tf_op jit(solution)/shard_map/ppermute | solution.py:524
  164.4 3.8 %collective-permute-done.6.refs_2_ = f32[1,8192]{1,0:T(1,128)S(1)} collective-permute-done((f32[1,8192]{1,0:T(1,128)S(1)}, f32[1,8192]{1,0:T(1,128)S(1)}, u32[]{:S(2)}, u32[]{:S(2)}) %collective-permute-start.6) | collective-permute-done | bytes 32800 | tf_op jit(solution)/shard_map/ppermute | solution.py:524
  169.2 7.6 %medium_back.2 = (bf16[128,8192]{1,0:T(8,128)(2,1)}, bf16[128,8192]{1,0:T(8,128)(2,1)}) custom-call(bf16[128,4096]{1,0:T(8,128)(2,1)} %get-tuple-element.78.refs_0_, bf16[128,4096]{1,0:T(8,128)(2,1)} %copy-done.9, f32[1,8192]{1,0:T(1,128)} %copy-done.12, bf16[128,8192]{1,0:T(8,128)(2,1)} %refs_3_.12, bf16[128,8192]{1,0:T(8,128)(2,1)} %refs_4_.12, ...), custom_call_target="tpu_custom_call" | custom-call | bytes 28800000 | tf_op jit(solution)/shard_map/medium_back/pallas_call | solution.py:81
  179.7 9.8 %all-to-all-start.3 = ((f32[128,8,128]{2,1,0:T(8,128)}), f32[128,8,128]{2,1,0:T(8,128)S(1)}, u32[]{:S(2)}, u32[]{:S(2)}) async-start(f32[128,8,128]{2,1,0:T(8,128)} %scan_forward.1), calls=%async_computation.3 | async-start | bytes 1048576 | tf_op jit(solution)/shard_map/all_to_all | solution.py:528
  190.5 7.6 %medium_back.3 = (bf16[128,8192]{1,0:T(8,128)(2,1)}, bf16[128,8192]{1,0:T(8,128)(2,1)}) custom-call(bf16[128,4096]{1,0:T(8,128)(2,1)} %get-tuple-element.83.refs_0_, bf16[128,4096]{1,0:T(8,128)(2,1)} %copy-done.8, f32[1,8192]{1,0:T(1,128)} %copy-done.12, bf16[128,8192]{1,0:T(8,128)(2,1)} %refs_3_.12, ...), custom_call_target="tpu_custom_call", output_to_operand_aliasing={{0}: (9, {}), {1}: (10, {})} | custom-call | bytes 28800000 | tf_op jit(solution)/shard_map/medium_back/pallas_call | solution.py:81
  198.1 5.5 %all-to-all-done.3.refs_1_ = f32[128,8,128]{2,1,0:T(8,128)S(1)} async-done(((f32[128,8,128]{2,1,0:T(8,128)}), f32[128,8,128]{2,1,0:T(8,128)S(1)}, u32[]{:S(2)}, u32[]{:S(2)}) %all-to-all-start.3) | async-done | bytes 524320 | tf_op jit(solution)/shard_map/all_to_all | solution.py:528
  204.4 15.6 %long_forward.1 = (bf16[128,8192]{1,0:T(8,128)(2,1)}, bf16[128,8192]{1,0:T(8,128)(2,1)}, bf16[128,8192]{1,0:T(8,128)(2,1)}, bf16[128,8192]{1,0:T(8,128)(2,1)}) custom-call(f32[128,8192]{1,0:T(8,128)} %get-tuple-element.74.refs_0_, f32[128,8,128]{2,1,0:T(8,128)} %copy-done.5, f32[128,8,128]{2,1,0:T(8,128)} %get-tuple-element.75.refs_2_, ...), custom_call_target="tpu_custom_call" | custom-call | bytes 50400000 | tf_op jit(solution)/shard_map/long_forward/pallas_call | solution.py:81
  (60 shorter events, 28.1 us)
Async XLA Ops:
  0.6 7.7 %copy-start.13 = (f32[512,16]{0,1:T(8,128)S(1)}, f32[512,16]{0,1:T(8,128)}, u32[]{:S(2)}) copy-start(f32[512,16]{0,1:T(8,128)} %param.21) | copy-start | bytes 98308
  0.6 7.8 %copy-start.15 = (f32[512,16]{0,1:T(8,128)S(1)}, f32[512,16]{0,1:T(8,128)}, u32[]{:S(2)}) copy-start(f32[512,16]{0,1:T(8,128)} %param.22) | copy-start | bytes 98308
  4.3 13.8 %collective-permute-start = (bf16[16,8192]{1,0:T(8,128)(2,1)}, bf16[16,8192]{1,0:T(8,128)(2,1)S(1)}, u32[]{:S(2)}, u32[]{:S(2)}) collective-permute-start(bf16[16,8192]{1,0:T(8,128)(2,1)} %get-tuple-element.51), channel_id=1, source_target_pairs={{0,1},{1,2},{2,3},{3,4},{4,5},{5,6},{6,7},{7,8},{8,9},{9,10},{10,1... | collective-permute-start | bytes 786440 | tf_op jit(solution)/shard_map/ppermute | solution.py:524
  8.5 1.6 copy-start.4
  18.8 15.6 %copy-start.16 = (bf16[16,8192]{1,0:T(8,128)(2,1)S(1)}, bf16[16,8192]{1,0:T(8,128)(2,1)}, u32[]{:S(2)}) copy-start(bf16[16,8192]{1,0:T(8,128)(2,1)} %get-tuple-element.54) | copy-start | bytes 786436
  18.8 23.3 %copy-start.17 = (bf16[8,8192]{1,0:T(8,128)(2,1)S(1)}, bf16[8,8192]{1,0:T(8,128)(2,1)}, u32[]{:S(2)}) copy-start(bf16[8,8192]{1,0:T(8,128)(2,1)} %get-tuple-element.55) | copy-start | bytes 393220
  26.4 27.7 %all-to-all-start = ((f32[128,8,128]{2,1,0:T(8,128)}), f32[128,8,128]{2,1,0:T(8,128)S(1)}, u32[]{:S(2)}, u32[]{:S(2)}) async-start(f32[128,8,128]{2,1,0:T(8,128)} %get-tuple-element.53), calls=%async_computation | async-start | bytes 1048576 | tf_op jit(solution)/shard_map/all_to_all | solution.py:528
  34.3 19.8 %collective-permute-start.1 = (bf16[16,8192]{1,0:T(8,128)(2,1)S(1)}, bf16[16,8192]{1,0:T(8,128)(2,1)S(1)}, u32[]{:S(2)}, u32[]{:S(2)}) collective-permute-start(bf16[16,8192]{1,0:T(8,128)(2,1)S(1)} %copy-done.16), channel_id=1, source_target_pairs={{1,0},{2,1},{3,2},{4,3},{5,4},{6,5},{7,6},{8,7},{9,8},{10,9},{11,1... | collective-permute-start | bytes 786440 | tf_op jit(solution)/shard_map/ppermute | solution.py:524
  42.1 12.0 %collective-permute-start.2 = (bf16[8,8192]{1,0:T(8,128)(2,1)S(1)}, bf16[8,8192]{1,0:T(8,128)(2,1)S(1)}, u32[]{:S(2)}, u32[]{:S(2)}) collective-permute-start(bf16[8,8192]{1,0:T(8,128)(2,1)S(1)} %copy-done.17), channel_id=1, source_target_pairs={{0,2},{1,3},{2,4},{3,5},{4,6},{5,7},{6,8},{7,9},{8,10},{9,11},{10,... | collective-permute-start | bytes 393224 | tf_op jit(solution)/shard_map/ppermute | solution.py:524
  54.1 33.4 %copy-start.10 = (bf16[8,8192]{1,0:T(8,128)(2,1)}, bf16[8,8192]{1,0:T(8,128)(2,1)S(1)}, u32[]{:S(2)}) copy-start(bf16[8,8192]{1,0:T(8,128)(2,1)S(1)} %collective-permute-done.2.refs_1_) | copy-start | bytes 393220
  54.1 17.0 %copy-start.1 = (bf16[16,8192]{1,0:T(8,128)(2,1)}, bf16[16,8192]{1,0:T(8,128)(2,1)S(1)}, u32[]{:S(2)}) copy-start(bf16[16,8192]{1,0:T(8,128)(2,1)S(1)} %collective-permute-done.1.refs_6_) | copy-start | bytes 786436
  57.1 23.8 %all-to-all-start.1 = ((f32[128,8,128]{2,1,0:T(8,128)}), f32[128,8,128]{2,1,0:T(8,128)S(1)}, u32[]{:S(2)}, u32[]{:S(2)}) async-start(f32[128,8,128]{2,1,0:T(8,128)} %scan_back.1), calls=%async_computation.1 | async-start | bytes 1048576 | tf_op jit(solution)/shard_map/all_to_all | solution.py:528
  71.1 18.5 %copy-start.3 = (f32[512,16]{1,0:T(8,128)S(1)}, f32[512,16]{1,0:T(8,128)}, u32[]{:S(2)}) copy-start(f32[512,16]{1,0:T(8,128)} %copy.35.residue) | copy-start | bytes 98308
  80.9 6.6 %copy-start.2 = (f32[128,8,128]{2,1,0:T(8,128)}, f32[128,8,128]{2,1,0:T(8,128)S(1)}, u32[]{:S(2)}) copy-start(f32[128,8,128]{2,1,0:T(8,128)S(1)} %all-to-all-done.1.refs_1_) | copy-start | bytes 1572868
  80.9 33.2 %collective-permute-start.4 = (bf16[128,4096]{1,0:T(8,128)(2,1)}, bf16[128,4096]{1,0:T(8,128)(2,1)}, u32[]{:S(2)}, u32[]{:S(2)}) collective-permute-start(bf16[128,4096]{1,0:T(8,128)(2,1)} %product_one.3.refs_2_), channel_id=1, source_target_pairs={{0,1},{1,2},{2,3},{3,4},{4,5},{5,6},{6,7},{7,8},{8,9},{9,10},{10,1... | collective-permute-start | bytes 3145736 | tf_op jit(solution)/shard_map/ppermute | solution.py:524
  87.4 40.9 %collective-permute-start.3 = (bf16[128,4096]{1,0:T(8,128)(2,1)}, bf16[128,4096]{1,0:T(8,128)(2,1)}, u32[]{:S(2)}, u32[]{:S(2)}) collective-permute-start(bf16[128,4096]{1,0:T(8,128)(2,1)} %product_one.2.refs_2_), channel_id=1, source_target_pairs={{0,1},{1,2},{2,3},{3,4},{4,5},{5,6},{6,7},{7,8},{8,9},{9,10},{10,1... | collective-permute-start | bytes 3145736 | tf_op jit(solution)/shard_map/ppermute | solution.py:524
  97.0 71.2 %collective-permute-start.7 = (bf16[128,4096]{1,0:T(8,128)(2,1)}, bf16[128,4096]{1,0:T(8,128)(2,1)S(1)}, u32[]{:S(2)}, u32[]{:S(2)}) collective-permute-start(bf16[128,4096]{1,0:T(8,128)(2,1)} %get-tuple-element.78.refs_0_), channel_id=1, source_target_pairs={{1,0},{2,1},{3,2},{4,3},{5,4},{6,5},{7,6},{8,7},{9,8},{10,9},{11,1... | collective-permute-start | bytes 3145736 | tf_op jit(solution)/shard_map/ppermute | solution.py:524
  110.5 79.0 %collective-permute-start.8 = (bf16[128,4096]{1,0:T(8,128)(2,1)}, bf16[128,4096]{1,0:T(8,128)(2,1)S(1)}, u32[]{:S(2)}, u32[]{:S(2)}) collective-permute-start(bf16[128,4096]{1,0:T(8,128)(2,1)} %get-tuple-element.83.refs_0_), channel_id=1, source_target_pairs={{1,0},{2,1},{3,2},{4,3},{5,4},{6,5},{7,6},{8,7},{9,8},{10,9},{11,1... | collective-permute-start | bytes 3145736 | tf_op jit(solution)/shard_map/ppermute | solution.py:524
  128.4 33.3 %copy-start.14 = (f32[1,8192]{1,0:T(1,128)S(1)}, f32[1,8192]{1,0:T(1,128)}, u32[]{:S(2)}) copy-start(f32[1,8192]{1,0:T(1,128)} %get-tuple-element.77) | copy-start | bytes 98308
  142.8 34.0 %all-to-all-start.2 = ((f32[128,8,128]{2,1,0:T(8,128)}), f32[128,8,128]{2,1,0:T(8,128)S(1)}, u32[]{:S(2)}, u32[]{:S(2)}) async-start(f32[128,8,128]{2,1,0:T(8,128)} %get-tuple-element.75.refs_2_), calls=%async_computation.2 | async-start | bytes 1048576 | tf_op jit(solution)/shard_map/all_to_all | solution.py:528
  154.0 22.8 %collective-permute-start.5 = (f32[8,8192]{1,0:T(8,128)}, f32[8,8192]{1,0:T(8,128)S(1)}, u32[]{:S(2)}, u32[]{:S(2)}) collective-permute-start(f32[8,8192]{1,0:T(8,128)} %get-tuple-element.76), channel_id=1, source_target_pairs={{1,0},{2,1},{3,2},{4,3},{5,4},{6,5},{7,6},{8,7},{9,8},{10,9},{11,1... | collective-permute-start | bytes 786440 | tf_op jit(solution)/shard_map/ppermute | solution.py:524
  161.7 6.5 %collective-permute-start.6 = (f32[1,8192]{1,0:T(1,128)S(1)}, f32[1,8192]{1,0:T(1,128)S(1)}, u32[]{:S(2)}, u32[]{:S(2)}) collective-permute-start(f32[1,8192]{1,0:T(1,128)S(1)} %copy-done.14), channel_id=1, source_target_pairs={{2,0},{3,1},{4,2},{5,3},{6,4},{7,5},{8,6},{9,7},{10,8},{11,9},{12,... | collective-permute-start | bytes 98312 | tf_op jit(solution)/shard_map/ppermute | solution.py:524
  176.8 21.3 %copy-start.11 = (f32[8,8192]{1,0:T(8,128)}, f32[8,8192]{1,0:T(8,128)S(1)}, u32[]{:S(2)}) copy-start(f32[8,8192]{1,0:T(8,128)S(1)} %collective-permute-done.5.refs_7_) | copy-start | bytes 786436
  179.7 23.9 %all-to-all-start.3 = ((f32[128,8,128]{2,1,0:T(8,128)}), f32[128,8,128]{2,1,0:T(8,128)S(1)}, u32[]{:S(2)}, u32[]{:S(2)}) async-start(f32[128,8,128]{2,1,0:T(8,128)} %scan_forward.1), calls=%async_computation.3 | async-start | bytes 1048576 | tf_op jit(solution)/shard_map/all_to_all | solution.py:528
  (7 other events, 5.8 us)

commit v4 on v3

--- a/solution.py
+++ b/solution.py
@@ -11,8 +11,8 @@
 MODES = 16
 ROWS = 128
 LANES = 128
-STRIP = 32
-STRIPS = ROWS // STRIP
+STRIP_FORWARD = 32
+STRIP_BACK = 64
 TILE_GROUPS = LANES // GROUP
 AXES = ("ctx", "ch")
 BF16 = jnp.bfloat16
@@ -33,7 +33,7 @@
     return start if isinstance(start, int) else pl.multiple_of(start, of)
 
 
-def lane_call(body, name, channels, ins, outs, scratch, us, part=(0, 1), into=None, width=1024, unroll=8):
+def lane_call(body, name, channels, ins, outs, scratch, us, part=(0, 1), into=None, width=1024, unroll=8, whole=False):
     span = channels // part[1]
     width = min(width, span)
     tiles = width // LANES
@@ -42,8 +42,8 @@
     into = into or {}
 
     def spec(shape, kind):
-        whole = {"r": shape[-1], "g": shape[0] * GROUP, "s": shape[0] * (LANES // 2)}[kind] == channels
-        first = part[0] * blocks if whole else 0
+        held = {"r": shape[-1], "g": shape[0] * GROUP, "s": shape[0] * (LANES // 2)}[kind]
+        first = part[0] * blocks if held == channels else 0
         if kind == "r":
             return pl.BlockSpec((shape[0], width), lambda i: (0, first + i))
         if kind == "g":
@@ -63,6 +63,10 @@
     def kernel(*refs):
         arrays = refs[:count_in] + refs[count_in + len(into) : count_in + len(into) + count_out]
         extra = refs[count_in + len(into) + count_out :]
+
+        if whole:
+            body(*arrays, *extra)
+            return
 
         def step(k, unused):
             for u in range(unroll):
@@ -86,7 +90,9 @@
         + [pl.BlockSpec(memory_space=pl.ANY)] * len(into),
         out_specs=[spec(shape, kind) for shape, _, kind in outs],
         out_shape=[jax.ShapeDtypeStruct(shape, dtype) for shape, dtype, _ in outs],
-        scratch_shapes=[pltpu.VMEM((unroll, *shape), dtype) for shape, dtype in scratch],
+        scratch_shapes=[
+            pltpu.VMEM(shape if whole else (unroll, *shape), dtype) for shape, dtype in scratch
+        ],
         input_output_aliases={count_in + n: at for n, at in enumerate(into)},
         compiler_params=pltpu.CompilerParams(vmem_limit_bytes=VMEM_LIMIT),
         cost_estimate=cost(us),
@@ -150,11 +156,11 @@
     return jnp.concatenate(picked, 0)
 
 
-def windows(signal, first, length):
+def windows(signal, strip, first, length):
     count = signal.shape[0]
     parts = []
-    for q in range(STRIPS):
-        low, high = STRIP * q + first, STRIP * q + first + length
+    for q in range(ROWS // strip):
+        low, high = strip * q + first, strip * q + first + length
         inside = signal[max(low, 0) : min(high, count)]
         pieces = [inside]
         if low < 0:
@@ -171,32 +177,36 @@
 
 
 def long_product(base_ref, signal, backward):
+    strip = STRIP_BACK if backward else STRIP_FORWARD
     base = base_ref[...]
-    row, lane = iota((STRIP, LANES), 0), iota((STRIP, LANES), 1)
-    first = 0 if backward else STRIP - LANES
+    row, lane = iota((strip, LANES), 0), iota((strip, LANES), 1)
+    first = 0 if backward else strip - LANES
     keep = lane >= row if backward else lane + first <= row
     tables = [
-        jnp.where(keep, circulant(base, g, STRIP, -first), 0.0).astype(BF16)
+        jnp.where(keep, circulant(base, g, strip, -first), 0.0).astype(BF16)
         for g in range(TILE_GROUPS)
     ]
     left = jnp.concatenate(
         [jnp.concatenate(tables[0::2], 0), jnp.concatenate(tables[1::2], 0)], 1
     )
     even, odd = split_groups(signal)
-    right = jnp.concatenate([windows(even, first, LANES), windows(odd, first, LANES)], 0)
-    return pick(jnp.dot(left, right, preferred_element_type=F32), STRIP, TILE_GROUPS // 2)
+    right = jnp.concatenate(
+        [windows(even, strip, first, LANES), windows(odd, strip, first, LANES)], 0
+    )
+    return pick(jnp.dot(left, right, preferred_element_type=F32), strip, TILE_GROUPS // 2)
 
 
 def medium_product(base_ref, pair, backward):
+    strip = STRIP_BACK if backward else STRIP_FORWARD
     base = base_ref[...]
-    row, lane = iota((STRIP, LANES), 0), iota((STRIP, LANES), 1)
+    row, lane = iota((strip, LANES), 0), iota((strip, LANES), 1)
     keep = lane >= row if backward else lane > row
-    wholes = [circulant(base, g, STRIP) for g in range(TILE_GROUPS)]
+    wholes = [circulant(base, g, strip) for g in range(TILE_GROUPS)]
     first = [jnp.where(keep, whole, 0.0).astype(BF16) for whole in wholes]
     second = [jnp.where(keep, 0.0, whole).astype(BF16) for whole in wholes]
     left = jnp.concatenate([jnp.concatenate(first, 0), jnp.concatenate(second, 0)], 1)
-    products = jnp.dot(left, windows(pair, 0, 2 * LANES), preferred_element_type=F32)
-    return pick(products, STRIP, TILE_GROUPS), first
+    products = jnp.dot(left, windows(pair, strip, 0, 2 * LANES), preferred_element_type=F32)
+    return pick(products, strip, TILE_GROUPS), first
 
 
 def on_channels(base, column):
@@ -315,17 +325,76 @@
     )(mr_short, li_short, li_skip, mr_filter, li_rate, li_residue)
 
 
-def product_one_body(key, value, prev, table, out, ext_k, ext_v):
+PITCH = ROWS + 16
+
+
+def product_one_rows(key, value, prev, following, table, keys_one, value_one, beyond, out, *scratch):
+    rows_k, rows_v, weights, out_k, out_v, out_p = scratch
+    tiles = key.shape[1] // LANES
+    at = [slice(t * LANES, (t + 1) * LANES) for t in range(tiles)]
+    for t in range(tiles):
+        weights[t * TABLE_ROWS : (t + 1) * TABLE_ROWS, :] = table[:, at[t]]
+        before, _ = margins_before(prev.at[:, at[t]])
+        after_a, after_b = margins_after(following.at[:, at[t]])
+        start = t * PITCH
+        rows_k[start : start + 8, :] = turned(before, 4)
+        rows_v[start : start + 8, :] = before
+        rows_k[start + 8 : start + 8 + ROWS, :] = key[:, at[t]].astype(F32)
+        rows_v[start + 8 : start + 8 + ROWS, :] = value[:, at[t]].astype(F32)
+        rows_k[start + 8 + ROWS : start + PITCH, :] = turned(after_a, 2)
+        rows_v[start + 8 + ROWS : start + PITCH, :] = after_b
+
+    def row(ref, r, pitch=PITCH):
+        return ref[pl.ds(r, tiles, stride=pitch), :]
+
+    w_k = [row(weights, MR_K + j, TABLE_ROWS) for j in range(SHORT)]
+    w_v = [row(weights, MR_V + j, TABLE_ROWS) for j in range(SHORT)]
+    last_k, last_v = [row(rows_k, 7), row(rows_k, 6)], [row(rows_v, 7), row(rows_v, 6)]
+    for r in range(ROWS + 2):
+        now_k, now_v = row(rows_k, 8 + r), row(rows_v, 8 + r)
+        k = w_k[0] * now_k + w_k[1] * last_k[0] + w_k[2] * last_k[1]
+        v = w_v[0] * now_v + w_v[1] * last_v[0] + w_v[2] * last_v[1]
+        last_k, last_v = [now_k, last_k[0]], [now_v, last_v[0]]
+        out_k[pl.ds(r, tiles, stride=PITCH), :] = k
+        out_v[pl.ds(r, tiles, stride=PITCH), :] = v
+        if r < ROWS:
+            out_p[pl.ds(r, tiles, stride=PITCH), :] = k * v
+    for t in range(tiles):
+        start = t * PITCH
+        keys_one[:, at[t]] = out_k[start : start + ROWS, :].astype(BF16)
+        value_one[:, at[t]] = out_v[start : start + ROWS, :].astype(BF16)
+        out[:, at[t]] = out_p[start : start + ROWS, :].astype(BF16)
+        beyond[0:2, at[t]] = out_k[start + ROWS : start + ROWS + 2, :]
+        beyond[2:4, at[t]] = out_v[start + ROWS : start + ROWS + 2, :]
+
+
+def rolled_forward(signal, prev8, weights):
+    total = weights[0] * signal
+    first = iota((8, LANES), 0)
+    for by in (1, 2):
+        moved = turned(signal, by)
+        top = jnp.where(first < by, turned(prev8, by), moved[0:8])
+        rest = [moved[8:]] if signal.shape[0] > 8 else []
+        total += weights[by] * jnp.concatenate([top, *rest], 0)
+    return total
+
+
+def product_one_body(key, value, prev, following, table, keys_one, value_one, beyond, out):
     weights = table[...]
-    margin, _ = margins_before(prev)
-    fill(ext_k, key[...].astype(F32), turned(margin, 4))
-    fill(ext_v, value[...].astype(F32), margin)
-    keys_one = short_forward(ext_k, taps(weights, MR_K))
-    value_one = short_forward(ext_v, taps(weights, MR_V))
-    out[...] = (keys_one * value_one).astype(BF16)
-
-
-def upstream_body(li_query, upstream, prev, table, rate, cotangent, state, ext):
+    before, _ = margins_before(prev)
+    after_a, after_b = margins_after(following)
+    w_k, w_v = taps(weights, MR_K), taps(weights, MR_V)
+    signal_k, signal_v = key[...].astype(F32), value[...].astype(F32)
+    k = rolled_forward(signal_k, turned(before, 4), w_k)
+    v = rolled_forward(signal_v, before, w_v)
+    keys_one[...] = k.astype(BF16)
+    value_one[...] = v.astype(BF16)
+    out[...] = (k * v).astype(BF16)
+    beyond[0:2, :] = rolled_forward(turned(after_a, 2), signal_k[ROWS - 8 :], w_k)[0:2]
+    beyond[2:4, :] = rolled_forward(after_b, signal_v[ROWS - 8 :], w_v)[0:2]
+
+
+def upstream_body(li_query, upstream, prev, table, rate, query_two_out, cotangent, state, ext):
     weights = table[...]
     _, margin = margins_before(prev)
     fill(ext, li_query[...].astype(F32), turned(margin, 2))
@@ -334,6 +403,7 @@
     position = iota((ROWS, LANES), 0).astype(F32)
     store_state(state, absorb(jnp.exp(-rate[...] * position), rounded))
     cotangent[...] = rounded
+    query_two_out[...] = query_two.astype(BF16)
 
 
 def long_back_near_body(cotangent, table, base, near):
@@ -344,15 +414,16 @@
 
 def long_back_body(
     near, closing, li_query, li_key, query, prev, following, table, rate, residue,
-    grad_two, grad_two_after, mixed_grad, mixed_head, out_head, out,
+    grad_two, grad_two_after, mixed_grad, mixed_head, out_head, query_one, keys_two_out, out,
     ext_q, ext_k, ext_g, ext_o,
 ):
     weights = table[...]
     _, before = margins_before(prev)
     after, _ = margins_after(following)
-    fill(ext_q, li_query[...].astype(F32), None, after)
+    base = 8 + ROWS
+    ext_q[base - 16 : base, :] = li_query[ROWS - 16 :, :].astype(F32)
+    ext_q[base:, :] = after
     w = taps(weights, LI_Q)
-    base = 8 + ROWS
     query_after = (
         w[0] * ext_q[base : base + 8, :]
         + w[1] * ext_q[base - 1 : base + 7, :]
@@ -376,7 +447,10 @@
     fill(ext_g, own * keys_two[0:ROWS], None, past * keys_two[ROWS:])
     mixed = short_backward(ext_g, taps(weights, LI_V))
     fill(ext_o, query[...].astype(F32), turned(before, 4))
-    conv_grad = mixed * short_forward(ext_o, taps(weights, MR_Q))
+    queries = short_forward(ext_o, taps(weights, MR_Q))
+    conv_grad = mixed * queries
+    query_one[...] = queries.astype(BF16)
+    keys_two_out[...] = keys_two[0:ROWS].astype(BF16)
     mixed_grad[...] = mixed.astype(BF16)
     mixed_head[...] = mixed[0:2]
     out[...] = conv_grad.astype(BF16)
@@ -384,8 +458,8 @@
 
 
 def forward_body(
-    before, before_kv, signal, query, li_key, prev, mixed_head, table, base_ref, base_long, rate,
-    conv_one, value_two, near, state, head, ext_q, ext_k, ext_m,
+    before, before_kv, signal, query_one, keys_two, prev, mixed_head, table, base_ref, base_long,
+    rate, conv_one, value_two, near, state, head, ext_m,
 ):
     weights = table[...]
     earlier = before[...]
@@ -408,20 +482,16 @@
     far = on_channels(base, 1) * (key_last * value_last).astype(BF16).astype(F32)
     conv_before = edge[8:16] + jnp.where(iota((8, LANES), 0) == 6, far, 0.0)
     _, margin = margins_before(prev)
-    fill(ext_q, query[...].astype(F32), turned(margin, 4))
     w = taps(weights, MR_Q)
-    query_one = short_forward(ext_q, w)
     query_before = w[0] * margin[0:8] + w[1] * turned(margin, 1) + w[2] * turned(margin, 2)
     mixed_before = turned(query_before, 4) * conv_before
     fill(
         ext_m,
-        (query_one * conv).astype(BF16).astype(F32),
+        (query_one[...].astype(F32) * conv).astype(BF16).astype(F32),
         mixed_before.astype(BF16).astype(F32),
     )
     value = short_forward(ext_m, taps(weights, LI_V))
-    fill(ext_k, li_key[...].astype(F32), margin)
-    keys_two = short_forward(ext_k, taps(weights, LI_K))
-    product = keys_two * value
+    product = keys_two[...].astype(F32) * value
     rounded = product.astype(BF16)
     position = (ROWS - 1 - iota((ROWS, LANES), 0)).astype(F32)
     store_state(state, absorb(jnp.exp(-rate[...] * position), rounded))
@@ -436,20 +506,29 @@
     head[6:8, :] = mixed_head[...]
 
 
+def late_body(
+    grad_two, grad_two_after, value_two, mixed_grad, conv_one, next_head, table,
+    grad_li_key, grad_mr_query, ext_k, ext_m,
+):
+    weights = table[...]
+    fill(ext_k, grad_two[...].astype(F32) * value_two[...].astype(F32))
+    ext_k[8 + ROWS : 10 + ROWS, :] = grad_two_after[...] * next_head[2:4, :]
+    grad_li_key[...] = short_backward(ext_k, taps(weights, LI_K)).astype(BF16)
+    fill(ext_m, mixed_grad[...].astype(F32) * conv_one[...].astype(F32))
+    ext_m[8 + ROWS : 10 + ROWS, :] = next_head[6:8, :] * next_head[4:6, :]
+    grad_mr_query[...] = short_backward(ext_m, taps(weights, MR_Q)).astype(BF16)
+
+
 def long_body(
-    near, start, end, li_query, upstream, prev, following, next_head, grad_two, grad_two_after,
-    value_two, mixed_grad, conv_one, table, rate, residue, base_back,
-    out, grad_li_query, grad_li_key, grad_mr_query, ext_q, ext_g, ext_k, ext_m,
+    near, start, end, query_two, upstream, following, next_head, table, rate, residue, base_back,
+    out, grad_li_query, ext_g,
 ):
     weights = table[...]
     distance = (iota((ROWS + 16, LANES), 0) + 1).astype(F32)
     emit = (residue[...] * jnp.exp(-rate[...] * distance)).astype(BF16)
     emitted = jnp.dot(emit, spread(load_state(start)), preferred_element_type=F32)
     conv = near[...] + emitted[0:ROWS]
-    _, margin = margins_before(prev)
-    fill(ext_q, li_query[...].astype(F32), turned(margin, 2))
-    query_two = short_forward(ext_q, taps(weights, LI_Q))
-    out[...] = (query_two * conv).astype(BF16)
+    out[...] = (query_two[...].astype(F32) * conv).astype(BF16)
     ended = jnp.dot(emit[0:16], spread(load_state(end)), preferred_element_type=F32)
     impulse = base_back[...]
     at_once = on_channels(impulse, 0) + weights[SKIP : SKIP + 1]
@@ -462,17 +541,11 @@
     ext_g[8 + ROWS : 9 + ROWS, :] = after[4:5] * past_first
     ext_g[9 + ROWS : 10 + ROWS, :] = after[5:6] * past_second
     grad_li_query[...] = short_backward(ext_g, taps(weights, LI_Q)).astype(BF16)
-    fill(ext_k, grad_two[...].astype(F32) * value_two[...].astype(F32))
-    ext_k[8 + ROWS : 10 + ROWS, :] = grad_two_after[...] * next_head[2:4, :]
-    grad_li_key[...] = short_backward(ext_k, taps(weights, LI_K)).astype(BF16)
-    fill(ext_m, mixed_grad[...].astype(F32) * conv_one[...].astype(F32))
-    ext_m[8 + ROWS : 10 + ROWS, :] = next_head[6:8, :] * next_head[4:6, :]
-    grad_mr_query[...] = short_backward(ext_m, taps(weights, MR_Q)).astype(BF16)
 
 
 def medium_back_body(
-    conv_grad, after, after_next, key, value, prev, following, table, base_ref,
-    grad_key, grad_value, ext_k, ext_v, ext_gk, ext_gv,
+    conv_grad, after, after_next, keys_one, value_one, beyond, table, base_ref,
+    grad_key, grad_value, ext_gk, ext_gv,
 ):
     weights = table[...]
     later = after[...]
@@ -482,40 +555,62 @@
     edge = pick(jnp.dot(left, later, preferred_element_type=F32), 16, TILE_GROUPS)
     far = on_channels(base_ref[...], MR_TAPS - 1) * after_next[...].astype(BF16).astype(F32)
     past = edge[0:8] + jnp.where(iota((8, LANES), 0) == 1, far, 0.0)
-    before, _ = margins_before(prev)
-    next_a, next_b = margins_after(following)
-    fill(ext_k, key[...].astype(F32), turned(before, 4), turned(next_a, 2))
-    fill(ext_v, value[...].astype(F32), before, next_b)
-    keys_one = short_forward(ext_k, taps(weights, MR_K), ROWS + 8)
-    value_one = short_forward(ext_v, taps(weights, MR_V), ROWS + 8)
-    fill(ext_gk, grad * value_one[0:ROWS], None, past * value_one[ROWS:])
-    fill(ext_gv, grad * keys_one[0:ROWS], None, past * keys_one[ROWS:])
+    fill(ext_gk, grad * value_one[...].astype(F32))
+    fill(ext_gv, grad * keys_one[...].astype(F32))
+    ext_gk[8 + ROWS : 10 + ROWS, :] = past[0:2] * beyond[2:4, :]
+    ext_gv[8 + ROWS : 10 + ROWS, :] = past[0:2] * beyond[0:2, :]
     grad_key[...] = short_backward(ext_gk, taps(weights, MR_K)).astype(BF16)
     grad_value[...] = short_backward(ext_gv, taps(weights, MR_V)).astype(BF16)
 
 
-def scan_states(states, rates, backward):
+def state_total(states, rates, copies, backward):
     count = states.shape[0]
 
     def kernel(states_ref, rates_ref, out_ref):
         decay = jnp.exp(rates_ref[...] * (-float(ROWS)))
-
-        def step(k, carried):
+        total = jnp.zeros(rates.shape, F32)
+        for k in range(count):
+            total = decay * total + states_ref[count - 1 - k if backward else k]
+        for n in range(copies):
+            out_ref[n] = total
+
+    whole = pl.BlockSpec(memory_space=pltpu.VMEM)
+    return pl.pallas_call(
+        kernel,
+        name="total_back" if backward else "total_forward",
+        out_shape=jax.ShapeDtypeStruct((copies, *rates.shape), F32),
+        in_specs=[whole, whole],
+        out_specs=whole,
+        cost_estimate=cost(2),
+    )(states, rates)
+
+
+def state_carries(states, totals, rates, place, backward):
+    count, segments = states.shape[0], totals.shape[0]
+
+    def kernel(place_ref, states_ref, totals_ref, rates_ref, out_ref):
+        mine = place_ref[0]
+        decay = jnp.exp(rates_ref[...] * (-float(ROWS)))
+        segment_decay = jnp.exp(rates_ref[...] * (-float(ROWS * count)))
+        carried = jnp.zeros(rates.shape, F32)
+        for k in range(segments):
+            n = segments - 1 - k if backward else k
+            passed = n > mine if backward else n < mine
+            carried = jnp.where(passed, segment_decay * carried + totals_ref[n], carried)
+        for k in range(count):
             b = count - 1 - k if backward else k
             out_ref[b] = carried
-            return decay * carried + states_ref[b]
-
-        lax.fori_loop(0, count, step, jnp.zeros((8, LANES), F32), unroll=8)
-
-    out_shape = jax.ShapeDtypeStruct(states.shape, F32)
+            carried = decay * carried + states_ref[b]
+
+    whole = pl.BlockSpec(memory_space=pltpu.VMEM)
     return pl.pallas_call(
         kernel,
-        name="scan_back" if backward else "scan_forward",
-        out_shape=out_shape,
-        in_specs=[pl.BlockSpec(memory_space=pltpu.VMEM)] * 2,
-        out_specs=pl.BlockSpec(memory_space=pltpu.VMEM),
+        name="carry_back" if backward else "carry_forward",
+        out_shape=jax.ShapeDtypeStruct(states.shape, F32),
+        in_specs=[pl.BlockSpec(memory_space=pltpu.SMEM), whole, whole, whole],
+        out_specs=whole,
         cost_estimate=cost(2),
-    )(states, rates)
+    )(place, states, totals, rates)
 
 
 def sent(array, by):
@@ -524,8 +619,8 @@
     return lax.ppermute(array, AXES, pairs)
 
 
-def exchanged(array):
-    return lax.all_to_all(array, AXES, split_axis=0, concat_axis=0, tiled=True)
+def exchanged(array, axis):
+    return lax.all_to_all(array, axis, split_axis=0, concat_axis=0, tiled=True)
 
 
 def after(array, *others):
@@ -558,33 +653,49 @@
     )
     rate = li_rate.reshape(1, channels)
     residue = li_residue.reshape(1, channels)
-    me = lax.axis_index(AXES)
-    my_rates = lax.dynamic_slice(
-        li_rate, ((me // 2) * TILE_GROUPS, (me % 2) * 8), (TILE_GROUPS, 8)
-    )
-    my_rates = jnp.repeat(my_rates.T, GROUP, axis=1)
-
-    cotangent, state_back = lane_call(
-        upstream_body, "upstream", channels,
-        [(li_query, "r"), (upstream, "r"), (prev, "r"), (table, "r"), (rate, "r")],
-        [full, state_out], [EXT], 7,
-    )
-    gathered_back = exchanged(state_back)
+    peers = lax.axis_size("ch")
+    share = 2 * tiles // peers
+    segments = lax.axis_size("ctx")
+    place = lax.axis_index("ctx").reshape(1)
+    my_groups = share // 2 * TILE_GROUPS
+    my_rates = lax.dynamic_slice_in_dim(li_rate, lax.axis_index("ch") * my_groups, my_groups, 0)
+    my_rates = my_rates.reshape(share // 2, TILE_GROUPS, 2, 8).transpose(0, 2, 3, 1)
+    my_rates = jnp.repeat(my_rates, GROUP, axis=3).reshape(share, 8, LANES)
+
+    def to_scan(state):
+        return exchanged(state, "ch").reshape(peers, share, 8, LANES)
+
+    cotangent_inputs = [(li_query, "r"), (upstream, "r"), (prev, "r"), (table, "r"), (rate, "r")]
+    query_two, cotangent, state_back = lane_call(
+        upstream_body, "upstream", channels, cotangent_inputs,
+        [full, full, state_out], [EXT], 7,
+    )
+    gathered_back = to_scan(state_back)
     (near_back,) = lane_call(
         long_back_near_body, "long_back_near", channels,
         [(cotangent, "r"), (table, "r"), (long_turned, "g")],
-        [full32], [], 6, unroll=4,
+        [full32], [], 8, unroll=4,
     )
     gathered_back = after(gathered_back, following, before_kv, near_back)
-    signal_one = [
-        lane_call(
-            product_one_body, "product_one", channels,
-            [(mr_key, "r"), (mr_value, "r"), (prev, "r"), (table, "r")],
-            [half], [EXT, EXT], 3, part,
-        )[0]
-        for part in halves
-    ]
-    closing = exchanged(scan_states(gathered_back, my_rates, True))
+    totals_back = exchanged(state_total(gathered_back, my_rates, segments, True), "ctx")
+
+    into = {}
+    signal_one = []
+    for n, part in enumerate(halves):
+        tall = (8 * PITCH, LANES), F32
+        got = lane_call(
+            product_one_body if n else product_one_rows, "product_one", channels,
+            [(mr_key, "r"), (mr_value, "r"), (prev, "r"), (following, "r"), (table, "r")],
+            [full, full, few(4), half],
+            [] if n else [tall, tall, ((8 * TABLE_ROWS, LANES), F32), tall, tall, tall],
+            4, part, into, whole=n == 0,
+        )
+        signal_one.append(got[3])
+        into = dict(enumerate(got[:3]))
+    keys_one, value_one, beyond_one = got[:3]
+    totals_back = after(totals_back, signal_one[0])
+    carries = state_carries(gathered_back, totals_back, my_rates, place, True)
+    closing = exchanged(carries.reshape(2 * tiles, 8, LANES), "ch")
     before_one = [sent(after(signal, closing), 1) for signal in signal_one]
 
     into = {}
@@ -594,12 +705,12 @@
             long_back_body, "long_back", channels,
             [(near_back, "r"), (closing, "s"), (li_query, "r"), (li_key, "r"), (mr_query, "r"),
              (prev, "r"), (following, "r"), (table, "r"), (rate, "r"), (residue, "r")],
-            [full, few(2), full, few(2), few(1), half],
+            [full, few(2), full, few(2), few(1), full, full, half],
             [EXT, EXT, EXT, EXT], 6, part, into, unroll=4,
         )
-        conv_grad.append(got[5])
-        into = dict(enumerate(got[:5]))
-    grad_two, grad_two_after, mixed_grad, mixed_head, conv_head, _ = got
+        conv_grad.append(got[7])
+        into = dict(enumerate(got[:7]))
+    grad_two, grad_two_after, mixed_grad, mixed_head, conv_head, query_one, keys_two, _ = got
     after_one = [sent(signal, -1) for signal in conv_grad]
     after_next = sent(conv_head, -2)
 
@@ -607,11 +718,11 @@
     for n, part in enumerate(halves):
         got = lane_call(
             forward_body, "forward", channels,
-            [(before_one[n], "r"), (before_kv, "r"), (signal_one[n], "r"), (mr_query, "r"),
-             (li_key, "r"), (prev, "r"), (mixed_head, "r"), (table, "r"), (medium, "g"),
+            [(before_one[n], "r"), (before_kv, "r"), (signal_one[n], "r"), (query_one, "r"),
+             (keys_two, "r"), (prev, "r"), (mixed_head, "r"), (table, "r"), (medium, "g"),
              (long, "g"), (rate, "r")],
             [full, full, full32, state_out, few(8)],
-            [EXT, EXT, EXT], 14, part, into, unroll=4,
+            [EXT], 13, part, into, unroll=4,
         )
         into = dict(enumerate(got))
     conv_one, value_two, near, state, head = got
@@ -620,25 +731,32 @@
     def medium_back(n, into):
         return lane_call(
             medium_back_body, "medium_back", channels,
-            [(conv_grad[n], "r"), (after_one[n], "r"), (after_next, "r"), (mr_key, "r"),
-             (mr_value, "r"), (prev, "r"), (following, "r"), (table, "r"), (medium_turned, "g")],
-            [full, full], [EXT, EXT, EXT, EXT], 8, halves[n], into, unroll=4,
+            [(conv_grad[n], "r"), (after_one[n], "r"), (after_next, "r"), (keys_one, "r"),
+             (value_one, "r"), (beyond_one, "r"), (table, "r"), (medium_turned, "g")],
+            [full, full], [EXT, EXT], 7, halves[n], into, unroll=4,
         )
 
-    gathered = exchanged(state)
+    gathered = to_scan(state)
     got = medium_back(0, {})
     gathered = after(gathered, next_head, after_next, *got)
-    start = exchanged(scan_states(gathered, my_rates, False))
+    totals = exchanged(state_total(gathered, my_rates, segments, False), "ctx")
     grad_mr_key, grad_mr_value = medium_back(1, dict(enumerate(got)))
-    start = after(start, grad_mr_key)
-
-    output, grad_li_query, grad_li_key, grad_mr_query = lane_call(
+    totals = after(totals, grad_mr_key)
+    carries = state_carries(gathered, totals, my_rates, place, False)
+    start = exchanged(carries.reshape(2 * tiles, 8, LANES), "ch")
+    grad_li_key, grad_mr_query = lane_call(
+        late_body, "late", channels,
+        [(grad_two, "r"), (grad_two_after, "r"), (value_two, "r"), (mixed_grad, "r"),
+         (conv_one, "r"), (next_head, "r"), (table, "r")],
+        [full, full], [EXT, EXT], 6,
+    )
+    start = after(start, grad_li_key)
+    output, grad_li_query = lane_call(
         long_body, "long_forward", channels,
-        [(near, "r"), (start, "s"), (state, "s"), (li_query, "r"), (upstream, "r"), (prev, "r"),
-         (following, "r"), (next_head, "r"), (grad_two, "r"), (grad_two_after, "r"),
-         (value_two, "r"), (mixed_grad, "r"), (conv_one, "r"), (table, "r"), (rate, "r"),
-         (residue, "r"), (long_turned, "g")],
-        [full, full, full, full], [EXT, EXT, EXT, EXT], 14, unroll=4,
+        [(near, "r"), (start, "s"), (state, "s"), (query_two, "r"), (upstream, "r"),
+         (following, "r"), (next_head, "r"), (table, "r"), (rate, "r"), (residue, "r"),
+         (long_turned, "g")],
+        [full, full], [EXT], 9,
     )
     return (output, grad_mr_query, grad_mr_key, grad_mr_value, grad_li_query, grad_li_key)
 

time: 222 us -> 230 us (1.036)
  blocking collectives: 0 us -> 17.4 us
  waiting for transfers between devices: 22 us -> 8.41 us
  Pallas kernels: 111 us -> 121 us
  starting transfers between devices: 77.4 us -> 69.2 us
    all_to_all x0 -> x1, blocking collectives: none -> 17.4 us  [exchanged(): return lax.all_to_all(array, axis, split_axis=0, concat_axis=0, tiled=True)]
    all_to_all x4 -> x5, waiting for transfers between devices: 15.3 us -> 2.15 us  [exchanged(): return lax.all_to_all(array, axis, split_axis=0, concat_axis=0, tiled=True)]
    all_to_all x4 -> x5, starting transfers between devices: 38.6 us -> 29.1 us  [exchanged(): return lax.all_to_all(array, axis, split_axis=0, concat_axis=0, tiled=True)]
    pallas_call x11 -> x12, Pallas kernels: 98.3 us -> 105 us  [lane_call(): pl.pallas_call(kernel, name=name, grid=(blocks,), in_specs=[spec(a.shape,...]
    pallas_call x2 -> x4, Pallas kernels: 4.22 us -> 7.61 us  [the longest x2 4 us: state_carries(): pl.pallas_call(kernel, name='carry_back' if backward else 'carry_forward'...]
    unnamed x38 -> x42, local copies, waits for them, and re-layouts: 6.16 us -> 7.58 us
  transfers between devices with their start and end apart: 13 -> 14, of which waited for: 4 -> 4; matrix products, arithmetic and copies ran while one was open for 2% -> 2% of each run, Pallas kernels for 37% -> 41%
where the time goes in v4:
time: 230 us; the launch traced here: 227 us
  Pallas kernels  121 us (53%)
  starting transfers between devices  69.2 us (30%)
  blocking collectives  17.4 us (8%)
  local copies, waits for them, and re-layouts  10.1 us (4%)
  waiting for transfers between devices  8.41 us (4%)
    pallas_call x12, Pallas kernels, lane_call(): pl.pallas_call(kernel, name=name, grid=(blocks,), in_specs=[spec(a.shape,...  105 us
    ppermute x9, starting transfers between devices, sent(): return lax.ppermute(array, AXES, pairs)  40.1 us
    all_to_all x5, starting transfers between devices, exchanged(): return lax.all_to_all(array, axis, split_axis=0, concat_axis=0, tiled=True)  29.1 us
    all_to_all x1, blocking collectives, exchanged(): return lax.all_to_all(array, axis, split_axis=0, concat_axis=0, tiled=True)  17.4 us
    unnamed x42, local copies, waits for them, and re-layouts  7.58 us
    ppermute x9, waiting for transfers between devices, sent(): return lax.ppermute(array, AXES, pairs)  6.26 us
    pallas_call x1, Pallas kernels, make_tables(): pl.pallas_call(kernel, name='tables', grid=(groups // block,), in_specs=[...  5.12 us
  transfers between devices with their start and end apart: 14, of which 4 were waited for; matrix products, arithmetic and copies ran while one was open for 2% of the time, Pallas kernels for 41%

profile of v4, /device:TPU:1, one launch (start us, length us, event | category | flops | bytes accessed | tf_op | source)
XLA Modules:
  0.0 227.5 jit_solution(8758244584609869955)
XLA Ops:
  0.7 3.6 %edges.1 = (bf16[16,8192]{1,0:T(8,128)(2,1)}, bf16[16,8192]{1,0:T(8,128)(2,1)}, bf16[8,8192]{1,0:T(8,128)(2,1)}) custom-call(bf16[128,8192]{1,0:T(8,128)(2,1)} %refs_4_.4, bf16[128,8192]{1,0:T(8,128)(2,1)} %refs_0_.4, bf16[128,8192]{1,0:T(8,128)(2,1)} %refs_1_.4, bf16[128,8192]{1,0:T(8,128)(2,1)} %refs_2_.3, bf16[128,8192]{1,0:T(8,128)(2,1)} %refs_3_.3, ...), custom_call_target="tpu_custom_call" | custom-call | bytes 12600000 | tf_op jit(solution)/shard_map/edges/pallas_call | solution.py:270
  4.3 4.0 %collective-permute-start = (bf16[16,8192]{1,0:T(8,128)(2,1)}, bf16[16,8192]{1,0:T(8,128)(2,1)S(1)}, u32[]{:S(2)}, u32[]{:S(2)}) collective-permute-start(bf16[16,8192]{1,0:T(8,128)(2,1)} %get-tuple-element.66), channel_id=1, source_target_pairs={{0,1},{1,2},{2,3},{3,4},{4,5},{5,6},{6,7},{7,8},{8,9},{9,10},{10,1... | collective-permute-start | bytes 786440 | tf_op jit(solution)/shard_map/ppermute | solution.py:619
  10.1 5.1 %tables.1 = (f32[24,8192]{1,0:T(8,128)}, f32[512,128]{1,0:T(8,128)}, f32[512,128]{1,0:T(8,128)}, f32[512,128]{1,0:T(8,128)}, f32[512,128]{1,0:T(8,128)}) custom-call(bf16[3,3,8192]{2,1,0:T(4,128)(2,1)} %mr.1, bf16[3,3,8192]{2,1,0:T(4,128)(2,1)} %li.1, f32[1,8192]{1,0:T(1,128)} %bitcast.18, bf16[128,512]{1,0:T(8,128)(2,1)} %filters.1, f32[512,16]{1,0:T(8,128)} %copy-done.5, ...), custom_call_target="tpu_custom_call" | custom-call | bytes 18000000 | tf_op jit(solution)/shard_map/tables/pallas_call | solution.py:313
  18.8 7.9 %upstream.1 = (bf16[128,8192]{1,0:T(8,128)(2,1)}, bf16[128,8192]{1,0:T(8,128)(2,1)}, f32[128,8,128]{2,1,0:T(8,128)}) custom-call(bf16[128,8192]{1,0:T(8,128)(2,1)} %refs_2_.3, bf16[128,8192]{1,0:T(8,128)(2,1)} %refs_4_.5, bf16[16,8192]{1,0:T(8,128)(2,1)} %copy-done, f32[24,8192]{1,0:T(8,128)} %get-tuple-element.68.refs_4_.refs_3_.refs_1_.refs_7_.refs_6_, ...), custom_call_target="tpu_custom_call" | custom-call | bytes 25200000 | tf_op jit(solution)/shard_map/upstream/pallas_call | solution.py:85
  26.6 4.6 %all-to-all-start = ((f32[128,8,128]{2,1,0:T(8,128)}), f32[128,8,128]{2,1,0:T(8,128)S(1)}, u32[]{:S(2)}, u32[]{:S(2)}) async-start(f32[128,8,128]{2,1,0:T(8,128)} %get-tuple-element.73), calls=%async_computation | async-start | bytes 1048576 | tf_op jit(solution)/shard_map/all_to_all | solution.py:623
  31.3 8.1 %collective-permute-start.1 = (bf16[16,8192]{1,0:T(8,128)(2,1)S(1)}, bf16[16,8192]{1,0:T(8,128)(2,1)S(1)}, u32[]{:S(2)}, u32[]{:S(2)}) collective-permute-start(bf16[16,8192]{1,0:T(8,128)(2,1)S(1)} %copy-done.18), channel_id=1, source_target_pairs={{1,0},{2,1},{3,2},{4,3},{5,4},{6,5},{7,6},{8,7},{9,8},{10,9},{11,1... | collective-permute-start | bytes 786440 | tf_op jit(solution)/shard_map/ppermute | solution.py:619
  42.4 9.2 %long_back_near.1.refs_0_ = f32[128,8192]{1,0:T(8,128)} custom-call(bf16[128,8192]{1,0:T(8,128)(2,1)} %get-tuple-element.75.refs_0_, f32[24,8192]{1,0:T(8,128)} %get-tuple-element.68.refs_4_.refs_3_.refs_1_.refs_7_.refs_6_, f32[512,128]{1,0:T(8,128)} %get-tuple-element.76.refs_2_.refs_10_), custom_call_target="tpu_custom_call" | custom-call | bytes 28800000 | tf_op jit(solution)/shard_map/long_back_near/pallas_call | solution.py:85
  54.2 4.4 %all-to-all-start.1 = ((f32[8,8,8,128]{3,2,1,0:T(8,128)}), f32[8,8,8,128]{3,2,1,0:T(8,128)S(1)}, u32[]{:S(2)}, u32[]{:S(2)}) async-start(f32[8,8,8,128]{3,2,1,0:T(8,128)} %total_back.1), calls=%async_computation.1 | async-start | bytes 524288 | tf_op jit(solution)/shard_map/all_to_all | solution.py:623
  58.6 6.2 %product_one.2 = (bf16[128,8192]{1,0:T(8,128)(2,1)}, bf16[128,8192]{1,0:T(8,128)(2,1)}, f32[4,8192]{1,0:T(4,128)}, bf16[128,4096]{1,0:T(8,128)(2,1)}) custom-call(bf16[128,8192]{1,0:T(8,128)(2,1)} %refs_0_.4, bf16[128,8192]{1,0:T(8,128)(2,1)} %refs_1_.4, bf16[16,8192]{1,0:T(8,128)(2,1)} %copy-done, bf16[16,8192]{1,0:T(8,128)(2,1)} %copy-done.1, ...), custom_call_target="tpu_custom_call" | custom-call | bytes 14400000 | tf_op jit(solution)/shard_map/product_one/pallas_call | solution.py:85
  67.8 17.4 %all_to_all.30.refs_1_ = f32[128,8,128]{2,1,0:T(8,128)} all-to-all(f32[128,8,128]{2,1,0:T(8,128)} %bitcast.16), channel_id=1, replica_groups=mesh['ctx'=8,'ch'=16] {'ch'}, dimensions={0} | all-to-all | bytes 1048576 | tf_op jit(solution)/shard_map/all_to_all | solution.py:623
  87.6 4.8 %product_one.3 = (bf16[128,8192]{1,0:T(8,128)(2,1)}, bf16[128,8192]{1,0:T(8,128)(2,1)}, f32[4,8192]{1,0:T(4,128)}, bf16[128,4096]{1,0:T(8,128)(2,1)}) custom-call(bf16[128,8192]{1,0:T(8,128)(2,1)} %refs_0_.4, bf16[128,8192]{1,0:T(8,128)(2,1)} %refs_1_.4, bf16[16,8192]{1,0:T(8,128)(2,1)} %copy-done, ...), custom_call_target="tpu_custom_call", output_to_operand_aliasing={{0}: (5, {}), {1}: (6, {}), {2}: (7, {})} | custom-call | bytes 14400000 | tf_op jit(solution)/shard_map/product_one/pallas_call | solution.py:85
  95.1 7.4 %long_back.2 = (bf16[128,8192]{1,0:T(8,128)(2,1)}, f32[2,8192]{1,0:T(2,128)}, bf16[128,8192]{1,0:T(8,128)(2,1)}, f32[2,8192]{1,0:T(2,128)}, f32[1,8192]{1,0:T(1,...) custom-call(f32[128,8192]{1,0:T(8,128)} %long_back_near.1.refs_0_, ...), custom_call_target="tpu_custom_call" | custom-call | bytes 21600000 | tf_op jit(solution)/shard_map/long_back/pallas_call | solution.py:85
  102.5 7.0 %collective-permute-start.7 = (bf16[128,4096]{1,0:T(8,128)(2,1)}, bf16[128,4096]{1,0:T(8,128)(2,1)S(1)}, u32[]{:S(2)}, u32[]{:S(2)}) collective-permute-start(bf16[128,4096]{1,0:T(8,128)(2,1)} %get-tuple-element.103.refs_0_), channel_id=1, source_target_pairs={{1,0},{2,1},{3,2},{4,3},{5,4},{6,5},{7,6},{8,7},{9,8},{10,9},{11,1... | collective-permute-start | bytes 3145736 | tf_op jit(solution)/shard_map/ppermute | solution.py:619
  109.4 7.4 %long_back.3 = (bf16[128,8192]{1,0:T(8,128)(2,1)}, f32[2,8192]{1,0:T(2,128)}, bf16[128,8192]{1,0:T(8,128)(2,1)}, f32[2,8192]{1,0:T(2,128)}, f32[1,8192]{1,0:T(1,...) custom-call(f32[128,8192]{1,0:T(8,128)} %long_back_near.1.refs_0_, ...), custom_call_target="tpu_custom_call", output_to_operand_aliasing={{0}: (10, {}), {1}: (11, {}), {2}: (12, {}), {3}: (13, {}),... | custom-call | bytes 21600000 | tf_op jit(solution)/shard_map/long_back/pallas_call | solution.py:85
  120.5 14.1 %forward.2 = (bf16[128,8192]{1,0:T(8,128)(2,1)}, bf16[128,8192]{1,0:T(8,128)(2,1)}, f32[128,8192]{1,0:T(8,128)}, f32[128,8,128]{2,1,0:T(8,128)}, f32[8,8192]{1,0:T(8,128)}) custom-call(bf16[128,4096]{1,0:T(8,128)(2,1)} %collective-permute-done.4.refs_0_, bf16[8,8192]{1,0:T(8,128)(2,1)} %copy-done.13, bf16[128,4096]{1,0:T(8,128)(2,1)} %get-tuple-element.93.refs_2_, ...), custom_call_target="tpu_custom_call" | custom-call | bytes 46800000 | tf_op jit(solution)/shard_map/forward/pallas_call | solution.py:85
  134.5 14.1 %forward.3 = (bf16[128,8192]{1,0:T(8,128)(2,1)}, bf16[128,8192]{1,0:T(8,128)(2,1)}, f32[128,8192]{1,0:T(8,128)}, f32[128,8,128]{2,1,0:T(8,128)}, f32[8,8192]{1,0:T(8,128)}) custom-call(bf16[128,4096]{1,0:T(8,128)(2,1)} %collective-permute-done.3.refs_0_, ...), custom_call_target="tpu_custom_call", output_to_operand_aliasing={{0}: (11, {}), {1}: (12, {}), {2}: (13, {}), {3}: (14, {}),... | custom-call | bytes 46800000 | tf_op jit(solution)/shard_map/forward/pallas_call | solution.py:85
  148.6 3.6 %all-to-all-start.3 = ((f32[128,8,128]{2,1,0:T(8,128)}), f32[128,8,128]{2,1,0:T(8,128)S(1)}, u32[]{:S(2)}, u32[]{:S(2)}) async-start(f32[128,8,128]{2,1,0:T(8,128)} %get-tuple-element.100.refs_2_), calls=%async_computation.3 | async-start | bytes 1048576 | tf_op jit(solution)/shard_map/all_to_all | solution.py:623
  152.2 8.6 %collective-permute-start.5 = (f32[8,8192]{1,0:T(8,128)}, f32[8,8192]{1,0:T(8,128)S(1)}, u32[]{:S(2)}, u32[]{:S(2)}) collective-permute-start(f32[8,8192]{1,0:T(8,128)} %get-tuple-element.101), channel_id=1, source_target_pairs={{1,0},{2,1},{3,2},{4,3},{5,4},{6,5},{7,6},{8,7},{9,8},{10,9},{11,1... | collective-permute-start | bytes 786440 | tf_op jit(solution)/shard_map/ppermute | solution.py:619
  168.0 7.5 %medium_back.2 = (bf16[128,8192]{1,0:T(8,128)(2,1)}, bf16[128,8192]{1,0:T(8,128)(2,1)}) custom-call(bf16[128,4096]{1,0:T(8,128)(2,1)} %get-tuple-element.103.refs_0_, bf16[128,4096]{1,0:T(8,128)(2,1)} %copy-done.8, f32[1,8192]{1,0:T(1,128)} %copy-done.14, bf16[128,8192]{1,0:T(8,128)(2,1)} %get-tuple-element.104.refs_3_, ...), custom_call_target="tpu_custom_call" | custom-call | bytes 25200000 | tf_op jit(solution)/shard_map/medium_back/pallas_call | solution.py:85
  178.1 11.0 %all-to-all-start.4 = ((f32[8,8,8,128]{3,2,1,0:T(8,128)}), f32[8,8,8,128]{3,2,1,0:T(8,128)S(1)}, u32[]{:S(2)}, u32[]{:S(2)}) async-start(f32[8,8,8,128]{3,2,1,0:T(8,128)} %total_forward.1), calls=%async_computation.4 | async-start | bytes 524288 | tf_op jit(solution)/shard_map/all_to_all | solution.py:623
  190.2 7.5 %medium_back.3 = (bf16[128,8192]{1,0:T(8,128)(2,1)}, bf16[128,8192]{1,0:T(8,128)(2,1)}) custom-call(bf16[128,4096]{1,0:T(8,128)(2,1)} %get-tuple-element.111.refs_0_, bf16[128,4096]{1,0:T(8,128)(2,1)} %copy-done.7, f32[1,8192]{1,0:T(1,128)} %copy-done.14, ...), custom_call_target="tpu_custom_call", output_to_operand_aliasing={{0}: (8, {}), {1}: (9, {})} | custom-call | bytes 25200000 | tf_op jit(solution)/shard_map/medium_back/pallas_call | solution.py:85
  200.4 5.5 %all-to-all-start.5 = ((f32[128,8,128]{2,1,0:T(8,128)}), f32[128,8,128]{2,1,0:T(8,128)S(1)}, u32[]{:S(2)}, u32[]{:S(2)}) async-start(f32[128,8,128]{2,1,0:T(8,128)} %bitcast.15), calls=%async_computation.5 | async-start | bytes 1048576 | tf_op jit(solution)/shard_map/all_to_all | solution.py:623
  205.9 9.2 %late.1 = (bf16[128,8192]{1,0:T(8,128)(2,1)}, bf16[128,8192]{1,0:T(8,128)(2,1)}) custom-call(bf16[128,8192]{1,0:T(8,128)(2,1)} %get-tuple-element.114.refs_0_, f32[2,8192]{1,0:T(2,128)} %get-tuple-element.115.refs_1_, bf16[128,8192]{1,0:T(8,128)(2,1)} %get-tuple-element.116.refs_2_, bf16[128,8192]{1,0:T(8,128)(2,1)} %get-tuple-element.117.refs_3_, ...), custom_call_target="tpu_custom_call" | custom-call | bytes 21600000 | tf_op jit(solution)/shard_map/late/pallas_call | solution.py:85
  217.8 9.7 %long_forward.1 = (bf16[128,8192]{1,0:T(8,128)(2,1)}, bf16[128,8192]{1,0:T(8,128)(2,1)}) custom-call(f32[128,8192]{1,0:T(8,128)} %get-tuple-element.99.refs_0_, f32[128,8,128]{2,1,0:T(8,128)} %copy-done.6, f32[128,8,128]{2,1,0:T(8,128)} %get-tuple-element.100.refs_2_, bf16[128,8192]{1,0:T(8,128)(2,1)} %get-tuple-element.121.refs_3_, ...), custom_call_target="tpu_custom_call" | custom-call | bytes 32400000 | tf_op jit(solution)/shard_map/long_forward/pallas_call | solution.py:85
  (72 shorter events, 38.6 us)
Async XLA Ops:
  0.6 7.7 %copy-start.15 = (f32[512,16]{0,1:T(8,128)S(1)}, f32[512,16]{0,1:T(8,128)}, u32[]{:S(2)}) copy-start(f32[512,16]{0,1:T(8,128)} %param.21) | copy-start | bytes 98308
  0.6 7.8 %copy-start.17 = (f32[512,16]{0,1:T(8,128)S(1)}, f32[512,16]{0,1:T(8,128)}, u32[]{:S(2)}) copy-start(f32[512,16]{0,1:T(8,128)} %param.22) | copy-start | bytes 98308
  4.3 13.8 %collective-permute-start = (bf16[16,8192]{1,0:T(8,128)(2,1)}, bf16[16,8192]{1,0:T(8,128)(2,1)S(1)}, u32[]{:S(2)}, u32[]{:S(2)}) collective-permute-start(bf16[16,8192]{1,0:T(8,128)(2,1)} %get-tuple-element.66), channel_id=1, source_target_pairs={{0,1},{1,2},{2,3},{3,4},{4,5},{5,6},{6,7},{7,8},{8,9},{9,10},{10,1... | collective-permute-start | bytes 786440 | tf_op jit(solution)/shard_map/ppermute | solution.py:619
  18.8 12.5 %copy-start.18 = (bf16[16,8192]{1,0:T(8,128)(2,1)S(1)}, bf16[16,8192]{1,0:T(8,128)(2,1)}, u32[]{:S(2)}) copy-start(bf16[16,8192]{1,0:T(8,128)(2,1)} %get-tuple-element.67) | copy-start | bytes 786436
  18.8 20.6 %copy-start.19 = (bf16[8,8192]{1,0:T(8,128)(2,1)S(1)}, bf16[8,8192]{1,0:T(8,128)(2,1)}, u32[]{:S(2)}) copy-start(bf16[8,8192]{1,0:T(8,128)(2,1)} %get-tuple-element.74) | copy-start | bytes 393220
  26.6 24.9 %all-to-all-start = ((f32[128,8,128]{2,1,0:T(8,128)}), f32[128,8,128]{2,1,0:T(8,128)S(1)}, u32[]{:S(2)}, u32[]{:S(2)}) async-start(f32[128,8,128]{2,1,0:T(8,128)} %get-tuple-element.73), calls=%async_computation | async-start | bytes 1048576 | tf_op jit(solution)/shard_map/all_to_all | solution.py:623
  31.3 20.3 %collective-permute-start.1 = (bf16[16,8192]{1,0:T(8,128)(2,1)S(1)}, bf16[16,8192]{1,0:T(8,128)(2,1)S(1)}, u32[]{:S(2)}, u32[]{:S(2)}) collective-permute-start(bf16[16,8192]{1,0:T(8,128)(2,1)S(1)} %copy-done.18), channel_id=1, source_target_pairs={{1,0},{2,1},{3,2},{4,3},{5,4},{6,5},{7,6},{8,7},{9,8},{10,9},{11,1... | collective-permute-start | bytes 786440 | tf_op jit(solution)/shard_map/ppermute | solution.py:619
  39.4 12.2 %collective-permute-start.2 = (bf16[8,8192]{1,0:T(8,128)(2,1)S(1)}, bf16[8,8192]{1,0:T(8,128)(2,1)S(1)}, u32[]{:S(2)}, u32[]{:S(2)}) collective-permute-start(bf16[8,8192]{1,0:T(8,128)(2,1)S(1)} %copy-done.19), channel_id=1, source_target_pairs={{0,2},{1,3},{2,4},{3,5},{4,6},{5,7},{6,8},{7,9},{8,10},{9,11},{10,... | collective-permute-start | bytes 393224 | tf_op jit(solution)/shard_map/ppermute | solution.py:619
  51.5 40.8 %copy-start.13 = (bf16[8,8192]{1,0:T(8,128)(2,1)}, bf16[8,8192]{1,0:T(8,128)(2,1)S(1)}, u32[]{:S(2)}) copy-start(bf16[8,8192]{1,0:T(8,128)(2,1)S(1)} %collective-permute-done.2.refs_1_) | copy-start | bytes 393220
  51.6 7.1 %copy-start.1 = (bf16[16,8192]{1,0:T(8,128)(2,1)}, bf16[16,8192]{1,0:T(8,128)(2,1)S(1)}, u32[]{:S(2)}) copy-start(bf16[16,8192]{1,0:T(8,128)(2,1)S(1)} %collective-permute-done.1.refs_3_.refs_6_.refs_5_) | copy-start | bytes 786436
  54.2 10.9 %all-to-all-start.1 = ((f32[8,8,8,128]{3,2,1,0:T(8,128)}), f32[8,8,8,128]{3,2,1,0:T(8,128)S(1)}, u32[]{:S(2)}, u32[]{:S(2)}) async-start(f32[8,8,8,128]{3,2,1,0:T(8,128)} %total_back.1), calls=%async_computation.1 | async-start | bytes 524288 | tf_op jit(solution)/shard_map/all_to_all | solution.py:623
  64.9 20.4 %copy-start.12 = (bf16[128,4096]{1,0:T(8,128)(2,1)S(1)}, bf16[128,4096]{1,0:T(8,128)(2,1)}, u32[]{:S(2)}) copy-start(bf16[128,4096]{1,0:T(8,128)(2,1)} %get-tuple-element.93.refs_2_) | copy-start | bytes 3145732
  85.3 35.2 %collective-permute-start.4 = (bf16[128,4096]{1,0:T(8,128)(2,1)S(1)}, bf16[128,4096]{1,0:T(8,128)(2,1)}, u32[]{:S(2)}, u32[]{:S(2)}) collective-permute-start(bf16[128,4096]{1,0:T(8,128)(2,1)S(1)} %copy-done.12), channel_id=1, source_target_pairs={{0,1},{1,2},{2,3},{3,4},{4,5},{5,6},{6,7},{7,8},{8,9},{9,10},{10,1... | collective-permute-start | bytes 3145736 | tf_op jit(solution)/shard_map/ppermute | solution.py:619
  87.6 6.7 %copy-start.4 = (f32[512,16]{1,0:T(8,128)S(1)}, f32[512,16]{1,0:T(8,128)}, u32[]{:S(2)}) copy-start(f32[512,16]{1,0:T(8,128)} %copy.40.residue) | copy-start | bytes 98308
  92.4 42.1 %collective-permute-start.3 = (bf16[128,4096]{1,0:T(8,128)(2,1)}, bf16[128,4096]{1,0:T(8,128)(2,1)}, u32[]{:S(2)}, u32[]{:S(2)}) collective-permute-start(bf16[128,4096]{1,0:T(8,128)(2,1)} %get-tuple-element.80.refs_2_), channel_id=1, source_target_pairs={{0,1},{1,2},{2,3},{3,4},{4,5},{5,6},{6,7},{7,8},{8,9},{9,10},{10,1... | collective-permute-start | bytes 3145736 | tf_op jit(solution)/shard_map/ppermute | solution.py:619
  102.5 64.5 %collective-permute-start.7 = (bf16[128,4096]{1,0:T(8,128)(2,1)}, bf16[128,4096]{1,0:T(8,128)(2,1)S(1)}, u32[]{:S(2)}, u32[]{:S(2)}) collective-permute-start(bf16[128,4096]{1,0:T(8,128)(2,1)} %get-tuple-element.103.refs_0_), channel_id=1, source_target_pairs={{1,0},{2,1},{3,2},{4,3},{5,4},{6,5},{7,6},{8,7},{9,8},{10,9},{11,1... | collective-permute-start | bytes 3145736 | tf_op jit(solution)/shard_map/ppermute | solution.py:619
  116.9 72.3 %collective-permute-start.8 = (bf16[128,4096]{1,0:T(8,128)(2,1)}, bf16[128,4096]{1,0:T(8,128)(2,1)S(1)}, u32[]{:S(2)}, u32[]{:S(2)}) collective-permute-start(bf16[128,4096]{1,0:T(8,128)(2,1)} %get-tuple-element.111.refs_0_), channel_id=1, source_target_pairs={{1,0},{2,1},{3,2},{4,3},{5,4},{6,5},{7,6},{8,7},{9,8},{10,9},{11,1... | collective-permute-start | bytes 3145736 | tf_op jit(solution)/shard_map/ppermute | solution.py:619
  134.5 26.3 %copy-start.16 = (f32[1,8192]{1,0:T(1,128)S(1)}, f32[1,8192]{1,0:T(1,128)}, u32[]{:S(2)}) copy-start(f32[1,8192]{1,0:T(1,128)} %get-tuple-element.102) | copy-start | bytes 98308
  148.6 26.9 %all-to-all-start.3 = ((f32[128,8,128]{2,1,0:T(8,128)}), f32[128,8,128]{2,1,0:T(8,128)S(1)}, u32[]{:S(2)}, u32[]{:S(2)}) async-start(f32[128,8,128]{2,1,0:T(8,128)} %get-tuple-element.100.refs_2_), calls=%async_computation.3 | async-start | bytes 1048576 | tf_op jit(solution)/shard_map/all_to_all | solution.py:623
  152.2 23.3 %collective-permute-start.5 = (f32[8,8192]{1,0:T(8,128)}, f32[8,8192]{1,0:T(8,128)S(1)}, u32[]{:S(2)}, u32[]{:S(2)}) collective-permute-start(f32[8,8192]{1,0:T(8,128)} %get-tuple-element.101), channel_id=1, source_target_pairs={{1,0},{2,1},{3,2},{4,3},{5,4},{6,5},{7,6},{8,7},{9,8},{10,9},{11,1... | collective-permute-start | bytes 786440 | tf_op jit(solution)/shard_map/ppermute | solution.py:619
  160.8 6.2 %collective-permute-start.6 = (f32[1,8192]{1,0:T(1,128)S(1)}, f32[1,8192]{1,0:T(1,128)S(1)}, u32[]{:S(2)}, u32[]{:S(2)}) collective-permute-start(f32[1,8192]{1,0:T(1,128)S(1)} %copy-done.16), channel_id=1, source_target_pairs={{2,0},{3,1},{4,2},{5,3},{6,4},{7,5},{8,6},{9,7},{10,8},{11,9},{12,... | collective-permute-start | bytes 98312 | tf_op jit(solution)/shard_map/ppermute | solution.py:619
  175.5 22.2 %copy-start.9 = (f32[8,8192]{1,0:T(8,128)}, f32[8,8192]{1,0:T(8,128)S(1)}, u32[]{:S(2)}) copy-start(f32[8,8192]{1,0:T(8,128)S(1)} %collective-permute-done.5.refs_5_.refs_6_) | copy-start | bytes 786436
  178.1 19.6 %all-to-all-start.4 = ((f32[8,8,8,128]{3,2,1,0:T(8,128)}), f32[8,8,8,128]{3,2,1,0:T(8,128)S(1)}, u32[]{:S(2)}, u32[]{:S(2)}) async-start(f32[8,8,8,128]{3,2,1,0:T(8,128)} %total_forward.1), calls=%async_computation.4 | async-start | bytes 524288 | tf_op jit(solution)/shard_map/all_to_all | solution.py:623
  200.4 16.6 %all-to-all-start.5 = ((f32[128,8,128]{2,1,0:T(8,128)}), f32[128,8,128]{2,1,0:T(8,128)S(1)}, u32[]{:S(2)}, u32[]{:S(2)}) async-start(f32[128,8,128]{2,1,0:T(8,128)} %bitcast.15), calls=%async_computation.5 | async-start | bytes 1048576 | tf_op jit(solution)/shard_map/all_to_all | solution.py:623
  (10 other events, 8.8 us)

commit v5 on v3

v5 whole, which is shorter than its diff:
```python
import jax
import jax.numpy as jnp
from jax import lax
from jax.experimental import pallas as pl
from jax.experimental.pallas import tpu as pltpu
from jax.sharding import PartitionSpec as P

GROUP = 16
SHORT = 3
MR_TAPS = 128
MODES = 16
ROWS = 128
LANES = 128
STRIP_FORWARD = 32
STRIP_BACK = 64
TILE_GROUPS = LANES // GROUP
AXES = ("ctx", "ch")
BF16 = jnp.bfloat16
F32 = jnp.float32
VMEM_LIMIT = 56 * 1024 * 1024

MR_Q, MR_K, MR_V, LI_Q, LI_K, LI_V, SKIP = 0, 3, 6, 9, 12, 15, 18
TABLE_ROWS = 24


def cost(microseconds):
    return pl.CostEstimate(
        flops=0, bytes_accessed=int(microseconds * 3.6e6), transcendentals=0
    )


def hint(start, of):
    return start if isinstance(start, int) else pl.multiple_of(start, of)


def lane_call(body, name, channels, ins, outs, us, part=(0, 1), into=None, width=1024, unroll=8):
    span = channels // part[1]
    width = min(width, span)
    tiles = width // LANES
    unroll = min(unroll, tiles)
    blocks = span // width
    into = into or {}

    def spec(shape, kind):
        held = {"r": shape[-1], "g": shape[0] * GROUP, "s": shape[0] * (LANES // 2)}[kind]
        first = part[0] * blocks if held == channels else 0
        if kind == "r":
            return pl.BlockSpec((shape[0], width), lambda i: (0, first + i))
        if kind == "g":
            return pl.BlockSpec((width // GROUP, shape[1]), lambda i: (first + i, 0))
        return pl.BlockSpec((2 * tiles, 8, LANES), lambda i: (first + i, 0, 0))

    def view(ref, kind, t):
        if kind == "r":
            return ref.at[:, pl.ds(hint(t * LANES, LANES), LANES)]
        if kind == "g":
            return ref.at[pl.ds(hint(t * TILE_GROUPS, TILE_GROUPS), TILE_GROUPS), :]
        return ref.at[pl.ds(2 * t, 2)]

    kinds = [kind for _, kind in ins] + [kind for _, _, kind in outs]
    count_in, count_out = len(ins), len(outs)

    def kernel(*refs):
        arrays = refs[:count_in] + refs[count_in + len(into) : count_in + len(into) + count_out]

        def step(k, unused):
            running = []
            for u in range(unroll):
                t = u if unroll == tiles else k * unroll + u
                running.append(body(*[view(ref, kind, t) for ref, kind in zip(arrays, kinds)]))
            while running:
                running = [tile for tile in running if next(tile, False)]
            return unused

        if unroll == tiles:
            step(0, 0)
        else:
            lax.fori_loop(0, tiles // unroll, step, 0)

    return pl.pallas_call(
        kernel,
        name=name,
        grid=(blocks,),
        in_specs=[spec(a.shape, kind) for a, kind in ins]
        + [pl.BlockSpec(memory_space=pl.ANY)] * len(into),
        out_specs=[spec(shape, kind) for shape, _, kind in outs],
        out_shape=[jax.ShapeDtypeStruct(shape, dtype) for shape, dtype, _ in outs],
        input_output_aliases={count_in + n: at for n, at in enumerate(into)},
        compiler_params=pltpu.CompilerParams(vmem_limit_bytes=VMEM_LIMIT),
        cost_estimate=cost(us),
    )(*[a for a, _ in ins], *into.values())


def turned(x, by):
    return pltpu.roll(x, by, 0) if by else x


def taps(table, first):
    return [table[first + j : first + j + 1, :] for j in range(SHORT)]


def short_forward(signal, weights, prev8):
    total = weights[0] * signal
    first = iota((8, LANES), 0)
    for by in (1, 2):
        moved = turned(signal, by)
        top = jnp.where(first < by, turned(prev8, by), moved[0:8])
        rest = [moved[8:]] if signal.shape[0] > 8 else []
        total += weights[by] * jnp.concatenate([top, *rest], 0)
    return total


def short_backward(signal, weights, next8):
    total = weights[0] * signal
    rows = signal.shape[0]
    last = iota((8, LANES), 0)
    for by in (1, 2):
        moved = turned(signal, rows - by)
        bottom = jnp.where(last >= 8 - by, turned(next8, 8 - by), moved[rows - 8 :])
        total += weights[by] * jnp.concatenate([moved[: rows - 8], bottom], 0)
    return total


def two_rows(first, second):
    at = iota((8, LANES), 0)
    return jnp.where(at == 0, first, jnp.where(at == 1, second, 0.0))


def iota(shape, dim):
    return lax.broadcasted_iota(jnp.int32, shape, dim)


def circulant(base, g, rows, shift=0):
    row = jnp.broadcast_to(base[g : g + 1, :], (rows, LANES))
    return pltpu.roll(row, shift, 1, stride=1, stride_axis=0)


def pick(products, rows, count):
    columns = LANES // count
    owner = iota((rows, LANES), 1) // columns
    picked = []
    for q in range(products.shape[1] // LANES):
        at = slice(q * LANES, (q + 1) * LANES)
        total = products[0:rows, at]
        for p in range(1, count):
            total = jnp.where(owner == p, products[p * rows : (p + 1) * rows, at], total)
        picked.append(total)
    return jnp.concatenate(picked, 0)


def windows(signal, strip, first, length):
    count = signal.shape[0]
    parts = []
    for q in range(ROWS // strip):
        low, high = strip * q + first, strip * q + first + length
        inside = signal[max(low, 0) : min(high, count)]
        pieces = [inside]
        if low < 0:
            pieces.insert(0, jnp.zeros((-low, LANES), signal.dtype))
        if high > count:
            pieces.append(jnp.zeros((high - count, LANES), signal.dtype))
        parts.append(jnp.concatenate(pieces, 0) if len(pieces) > 1 else inside)
    return jnp.concatenate(parts, 1)


def split_groups(signal):
    odd = ((iota(signal.shape, 1) // GROUP) % 2).astype(F32)
    return signal * (1.0 - odd).astype(signal.dtype), signal * odd.astype(signal.dtype)


def long_tables(base_ref, backward):
    strip = STRIP_BACK if backward else STRIP_FORWARD
    base = base_ref[...]
    row, lane = iota((strip, LANES), 0), iota((strip, LANES), 1)
    first = 0 if backward else strip - LANES
    keep = lane >= row if backward else lane + first <= row
    tables = [
        jnp.where(keep, circulant(base, g, strip, -first), 0.0).astype(BF16)
        for g in range(TILE_GROUPS)
    ]
    return jnp.concatenate(
        [jnp.concatenate(tables[0::2], 0), jnp.concatenate(tables[1::2], 0)], 1
    )


def long_windows(signal, backward):
    strip = STRIP_BACK if backward else STRIP_FORWARD
    first = 0 if backward else strip - LANES
    even, odd = split_groups(signal)
    return jnp.concatenate(
        [windows(even, strip, first, LANES), windows(odd, strip, first, LANES)], 0
    )


def medium_tables(base, backward):
    strip = STRIP_BACK if backward else STRIP_FORWARD
    row, lane = iota((strip, LANES), 0), iota((strip, LANES), 1)
    keep = lane >= row if backward else lane > row
    wholes = [circulant(base, g, strip) for g in range(TILE_GROUPS)]
    first = [jnp.where(keep, whole, 0.0).astype(BF16) for whole in wholes]
    second = [jnp.where(keep, 0.0, whole).astype(BF16) for whole in wholes]
    return jnp.concatenate([jnp.concatenate(first, 0), jnp.concatenate(second, 0)], 1), first


def on_channels(base, column):
    own = iota((TILE_GROUPS, LANES), 0) == iota((TILE_GROUPS, LANES), 1) // GROUP
    return jnp.where(own, base[:, column : column + 1], 0.0).sum(0, keepdims=True)


def own_group():
    return (iota((LANES, LANES), 0) // MODES == iota((LANES, LANES), 1) // GROUP).astype(F32)


def spread(state):
    return (jnp.concatenate([state] * TILE_GROUPS, 0) * own_group()).astype(BF16)


def absorb(powers, signal):
    every = lax.dot_general(
        powers.astype(BF16), signal, (((0,), (0,)), ((), ())), preferred_element_type=F32
    )
    return (every * own_group()).reshape(TILE_GROUPS, MODES, LANES).sum(0)


def store_state(ref, state):
    ref[...] = state.reshape(2, 8, LANES).astype(ref.dtype)


def load_state(ref):
    return ref[...].astype(F32).reshape(MODES, LANES)


def margins_before(ref):
    rows = ref[...].astype(F32)
    return rows[0:8], rows[8:16]


def margins_after(ref):
    rows = ref[...].astype(F32)
    return rows[0:8], rows[8:16]


def edges(mr_query, mr_key, mr_value, li_query, li_key, upstream):
    channels = mr_query.shape[1]
    width = min(2048, channels)

    def kernel(q_end, k_end, v_end, lq_end, lk_end, lq, lk, g, k, v, last, first, last_kv, a, b):
        a[0:4, :] = k_end[...].astype(F32)[12:16]
        a[4:8, :] = v_end[...].astype(F32)[12:16]
        a[8:12, :] = q_end[...].astype(F32)[12:16]
        a[12:14, :] = lq_end[...].astype(F32)[14:16]
        a[14:16, :] = lk_end[...].astype(F32)[14:16]
        for n, ref in enumerate((lq, lk, g, k, v)):
            b[2 * n : 2 * n + 2, :] = ref[...].astype(F32)[0:2]
        b[10:16, :] = jnp.zeros((6, width), F32)
        last[...] = a[...].astype(BF16)
        first[...] = b[...].astype(BF16)
        last_kv[...] = a[0:8, :].astype(BF16)

    low = pl.BlockSpec((16, width), lambda i: (ROWS // 16 - 1, i))
    high = pl.BlockSpec((16, width), lambda i: (0, i))
    small = jax.ShapeDtypeStruct((16, channels), BF16)
    return pl.pallas_call(
        kernel,
        name="edges",
        grid=(channels // width,),
        in_specs=[low] * 5 + [high] * 5,
        out_specs=[high, high, pl.BlockSpec((8, width), lambda i: (0, i))],
        out_shape=[small, small, jax.ShapeDtypeStruct((8, channels), BF16)],
        scratch_shapes=[pltpu.VMEM((16, width), F32)] * 2,
        compiler_params=pltpu.CompilerParams(vmem_limit_bytes=VMEM_LIMIT),
        cost_estimate=cost(3.5),
    )(mr_query, mr_key, mr_value, li_query, li_key, li_query, li_key, upstream, mr_key, mr_value)


def make_tables(mr_short, li_short, li_skip, mr_filter, li_rate, li_residue):
    groups = mr_filter.shape[1]
    channels = groups * GROUP
    block = min(128, groups)
    width = block * GROUP

    def kernel(mr, li, skip, filters, rate, residue, table, medium, medium_back, long, long_back):
        for n in range(3):
            table[3 * n : 3 * n + 3, :] = mr[n].astype(F32)
            table[9 + 3 * n : 12 + 3 * n, :] = li[n].astype(F32)
        table[SKIP : SKIP + 1, :] = skip[...]
        table[SKIP + 1 :, :] = jnp.zeros((TABLE_ROWS - SKIP - 1, width), F32)
        row, lane = iota((LANES, LANES), 0), iota((LANES, LANES), 1)
        same = (row == lane).astype(F32).astype(BF16)
        turn = (row == (LANES - lane) % LANES).astype(F32).astype(BF16)
        by_rows = (((0,), (0,)), ((), ()))
        medium[...] = lax.dot_general(filters[...], turn, by_rows, preferred_element_type=F32)
        medium_back[...] = lax.dot_general(filters[...], same, by_rows, preferred_element_type=F32)
        position = iota((block, LANES), 1).astype(F32)
        impulse = jnp.zeros((block, LANES), F32)
        for n in range(MODES):
            impulse += residue[:, n : n + 1] * jnp.exp(-rate[:, n : n + 1] * position)
        long_back[...] = impulse
        long[...] = jnp.dot(impulse.astype(BF16), turn, preferred_element_type=F32)

    shorts = pl.BlockSpec((3, 3, width), lambda i: (0, 0, i))
    modes = pl.BlockSpec((block, MODES), lambda i: (i, 0))
    by_tap = pl.BlockSpec((block, LANES), lambda i: (i, 0))
    shapes = [jax.ShapeDtypeStruct((TABLE_ROWS, channels), F32)]
    shapes += [jax.ShapeDtypeStruct((groups, LANES), F32)] * 4
    return pl.pallas_call(
        kernel,
        name="tables",
        grid=(groups // block,),
        in_specs=[
            shorts, shorts, pl.BlockSpec((1, width), lambda i: (0, i)),
            pl.BlockSpec((MR_TAPS, block), lambda i: (0, i)), modes, modes,
        ],
        out_specs=[pl.BlockSpec((TABLE_ROWS, width), lambda i: (0, i))] + [by_tap] * 4,
        out_shape=shapes,
        compiler_params=pltpu.CompilerParams(vmem_limit_bytes=VMEM_LIMIT),
        cost_estimate=cost(5),
    )(mr_short, li_short, li_skip, mr_filter, li_rate, li_residue)


def product_one_body(key, value, prev, following, table, keys_one, value_one, beyond, out):
    weights = table[...]
    before, _ = margins_before(prev)
    after_a, after_b = margins_after(following)
    w_k, w_v = taps(weights, MR_K), taps(weights, MR_V)
    signal_k, signal_v = key[...].astype(F32), value[...].astype(F32)
    yield True
    k = short_forward(signal_k, w_k, turned(before, 4))
    v = short_forward(signal_v, w_v, before)
    yield True
    keys_one[...] = k.astype(BF16)
    value_one[...] = v.astype(BF16)
    out[...] = (k * v).astype(BF16)
    beyond[0:2, :] = short_forward(turned(after_a, 2), w_k, signal_k[ROWS - 8 :])[0:2]
    beyond[2:4, :] = short_forward(after_b, w_v, signal_v[ROWS - 8 :])[0:2]


def upstream_body(li_query, upstream, prev, table, rate, query_two_out, cotangent, state):
    weights = table[...]
    _, margin = margins_before(prev)
    signal, given, decay = li_query[...].astype(F32), upstream[...].astype(F32), rate[...]
    yield True
    powers = jnp.exp(-decay * iota((ROWS, LANES), 0).astype(F32))
    query_two = short_forward(signal, taps(weights, LI_Q), turned(margin, 2))
    rounded = (given * query_two).astype(BF16)
    yield True
    absorbed = absorb(powers, rounded)
    yield True
    store_state(state, absorbed)
    cotangent[...] = rounded
    query_two_out[...] = query_two.astype(BF16)


def long_back_near_body(cotangent, table, base, near):
    signal = cotangent[...]
    skip = table[SKIP : SKIP + 1, :]
    left, right = long_tables(base, True), long_windows(signal, True)
    yield True
    products = jnp.dot(left, right, preferred_element_type=F32)
    yield True
    near[...] = pick(products, STRIP_BACK, TILE_GROUPS // 2) + skip * signal.astype(F32)


def long_back_body(
    near_ref, closing, li_query, li_key, query, prev, following, table, rate, residue,
    grad_two, grad_two_after, mixed_grad, mixed_head, out_head, out,
):
    weights = table[...]
    _, before = margins_before(prev)
    after, _ = margins_after(following)
    near, state = near_ref[...], load_state(closing)
    key, queries = li_key[...].astype(F32), query[...].astype(F32)
    query_end = li_query[ROWS - 16 :, :].astype(F32)[8:16]
    distance = (ROWS - iota((ROWS + 16, LANES), 0)).astype(F32)
    emit = (residue[...] * jnp.exp(-rate[...] * distance)).astype(BF16)
    cot_after = turned(after, 4) * short_forward(after, taps(weights, LI_Q), query_end)
    yield True
    emitted = jnp.dot(emit, spread(state), preferred_element_type=F32)
    later = jnp.dot(emit[ROWS:], spread(state - cot_after[0:1]), preferred_element_type=F32)
    yield True
    skip = weights[SKIP : SKIP + 1]
    own = near + emitted[0:ROWS]
    at_row = iota((8, LANES), 0)
    past = jnp.where(at_row == 0, emitted[ROWS : ROWS + 8], later[0:8]) + skip * cot_after
    past = jnp.where(at_row < 2, past, 0.0)
    w_k = taps(weights, LI_K)
    keys_two = short_forward(key, w_k, before)
    keys_after = short_forward(turned(after, 6), w_k, key[ROWS - 8 :])
    mixed = short_backward(own * keys_two, taps(weights, LI_V), past * keys_after)
    queries = short_forward(queries, taps(weights, MR_Q), turned(before, 4))
    conv_grad = mixed * queries
    yield True
    grad_two[...] = own.astype(BF16)
    grad_two_after[...] = past[0:2]
    mixed_grad[...] = mixed.astype(BF16)
    mixed_head[...] = mixed[0:2]
    out[...] = conv_grad.astype(BF16)
    out_head[...] = conv_grad[0:1]


def forward_body(
    before, before_kv, signal, query, key, prev, table, base_ref, base_long,
    rate, conv_one, value_two, near, state, state_sent, head,
):
    weights = table[...]
    earlier = before[...]
    pair = jnp.concatenate([earlier, signal[...]], 0)
    queries, keys = query[...].astype(F32), key[...].astype(F32)
    _, margin = margins_before(prev)
    raw = before_kv[...].astype(F32)
    base = base_ref[...]
    left, _ = medium_tables(base, False)
    row, lane = iota((16, LANES), 0), iota((16, LANES), 1)
    left_edge = jnp.concatenate(
        [
            jnp.where(lane <= row + (ROWS - 16), circulant(base, g, 16, ROWS - 16), 0.0).astype(BF16)
            for g in range(TILE_GROUPS)
        ],
        0,
    )
    yield True
    products = jnp.dot(
        left, windows(pair, STRIP_FORWARD, 0, 2 * LANES), preferred_element_type=F32
    )
    products_edge = jnp.dot(left_edge, earlier, preferred_element_type=F32)
    yield True
    query_one = short_forward(queries, taps(weights, MR_Q), turned(margin, 4))
    keys_two = short_forward(keys, taps(weights, LI_K), margin)
    conv = pick(products, STRIP_FORWARD, TILE_GROUPS)
    edge = pick(products_edge, 16, TILE_GROUPS)
    w_k, w_v = taps(weights, MR_K), taps(weights, MR_V)
    key_last = w_k[0] * raw[3:4] + w_k[1] * raw[2:3] + w_k[2] * raw[1:2]
    value_last = w_v[0] * raw[7:8] + w_v[1] * raw[6:7] + w_v[2] * raw[5:6]
    far = on_channels(base, 1) * (key_last * value_last).astype(BF16).astype(F32)
    conv_before = edge[8:16] + jnp.where(iota((8, LANES), 0) == 6, far, 0.0)
    w = taps(weights, MR_Q)
    query_before = w[0] * margin + w[1] * turned(margin, 1) + w[2] * turned(margin, 2)
    mixed_before = turned(query_before, 4) * conv_before
    mixed = (query_one * conv).astype(BF16).astype(F32)
    value = short_forward(mixed, taps(weights, LI_V), mixed_before.astype(BF16).astype(F32))
    product = keys_two * value
    rounded = product.astype(BF16)
    yield True
    left, right = long_tables(base_long, False), long_windows(rounded, False)
    powers = jnp.exp(-rate[...] * (ROWS - 1 - iota((ROWS, LANES), 0)).astype(F32))
    yield True
    products = jnp.dot(left, right, preferred_element_type=F32)
    absorbed = absorb(powers, rounded)
    yield True
    store_state(state, absorbed)
    store_state(state_sent, absorbed)
    conv_one[...] = conv.astype(BF16)
    value_two[...] = value.astype(BF16)
    near[...] = (
        pick(products, STRIP_FORWARD, TILE_GROUPS // 2) + weights[SKIP : SKIP + 1] * product
    )
    head[0:2, :] = product[0:2]
    head[2:4, :] = value[0:2]
    head[4:6, :] = conv[0:2]


def late_body(
    grad_two, grad_two_after, value_two, mixed_grad, mixed_after, conv_one, next_head, table,
    grad_li_key, grad_mr_query,
):
    weights = table[...]
    head = next_head[...]
    past_two, past_mixed = grad_two_after[...], mixed_after[...]
    key_grad = grad_two[...].astype(F32) * value_two[...].astype(F32)
    query_grad = mixed_grad[...].astype(F32) * conv_one[...].astype(F32)
    key_past = two_rows(past_two[0:1] * head[2:3], past_two[1:2] * head[3:4])
    query_past = two_rows(past_mixed[0:1] * head[4:5], past_mixed[1:2] * head[5:6])
    yield True
    first = short_backward(key_grad, taps(weights, LI_K), key_past)
    second = short_backward(query_grad, taps(weights, MR_Q), query_past)
    yield True
    grad_li_key[...] = first.astype(BF16)
    grad_mr_query[...] = second.astype(BF16)


def long_body(
    near_ref, start, end, query_two, upstream, following, next_head, table, rate, residue, base_back,
    out, grad_li_query,
):
    weights = table[...]
    near, queries, given = near_ref[...], query_two[...].astype(F32), upstream[...].astype(F32)
    distance = (iota((ROWS + 16, LANES), 0) + 1).astype(F32)
    emit = (residue[...] * jnp.exp(-rate[...] * distance)).astype(BF16)
    started, ending = spread(load_state(start)), spread(load_state(end))
    head = next_head[...]
    impulse = base_back[...]
    after, _ = margins_after(following)
    yield True
    emitted = jnp.dot(emit, started, preferred_element_type=F32)
    ended = jnp.dot(emit[0:16], ending, preferred_element_type=F32)
    yield True
    conv = near + emitted[0:ROWS]
    at_once = on_channels(impulse, 0) + weights[SKIP : SKIP + 1]
    first, second = head[0:1], head[1:2]
    past = emitted[ROWS : ROWS + 8] + ended[0:8]
    past_first = past[0:1] + at_once * first
    past_second = past[1:2] + on_channels(impulse, 1) * first + at_once * second
    grad_past = two_rows(after[4:5] * past_first, after[5:6] * past_second)
    grad = short_backward(given * conv, taps(weights, LI_Q), grad_past)
    yield True
    out[...] = (queries * conv).astype(BF16)
    grad_li_query[...] = grad.astype(BF16)


def medium_back_body(
    conv_grad, after, after_next, keys_one, value_one, beyond, table, base_ref,
    grad_key, grad_value,
):
    weights = table[...]
    later = after[...]
    pair = jnp.concatenate([conv_grad[...], later], 0)
    keys, values = keys_one[...].astype(F32), value_one[...].astype(F32)
    past_kv = beyond[...]
    base = base_ref[...]
    left, first_half = medium_tables(base, True)
    far = on_channels(base, MR_TAPS - 1) * after_next[...].astype(BF16).astype(F32)
    yield True
    products = jnp.dot(left, windows(pair, STRIP_BACK, 0, 2 * LANES), preferred_element_type=F32)
    left_edge = jnp.concatenate([part[0:16] for part in first_half], 0)
    products_edge = jnp.dot(left_edge, later, preferred_element_type=F32)
    yield True
    grad = pick(products, STRIP_BACK, TILE_GROUPS)
    edge = pick(products_edge, 16, TILE_GROUPS)
    past_first, past_second = edge[0:1], edge[1:2] + far
    key_past = two_rows(past_first * past_kv[2:3], past_second * past_kv[3:4])
    value_past = two_rows(past_first * past_kv[0:1], past_second * past_kv[1:2])
    key_grad = short_backward(grad * values, taps(weights, MR_K), key_past)
    value_grad = short_backward(grad * keys, taps(weights, MR_V), value_past)
    yield True
    grad_key[...] = key_grad.astype(BF16)
    grad_value[...] = value_grad.astype(BF16)


def scan_states(states, rates, backward):
    count = states.shape[0]

    def kernel(states_ref, rates_ref, out_ref):
        decay = jnp.exp(rates_ref[...] * (-float(ROWS)))
        carried = jnp.zeros((8, LANES), F32)
        for k in range(count):
            b = count - 1 - k if backward else k
            out_ref[b] = carried.astype(BF16)
            carried = decay * carried + states_ref[b].astype(F32)

    return pl.pallas_call(
        kernel,
        name="scan_back" if backward else "scan_forward",
        out_shape=jax.ShapeDtypeStruct(states.shape, BF16),
        in_specs=[pl.BlockSpec(memory_space=pltpu.VMEM)] * 2,
        out_specs=pl.BlockSpec(memory_space=pltpu.VMEM),
        cost_estimate=cost(2),
    )(states, rates)


def sent(array, by):
    size = lax.axis_size(AXES)
    pairs = [(i, i + by) for i in range(size) if 0 <= i + by < size]
    return lax.ppermute(array, AXES, pairs)


def exchanged(array):
    return lax.all_to_all(array, AXES, split_axis=0, concat_axis=0, tiled=True)


def after(array, *others):
    return lax.optimization_barrier((array, *others))[0]


def per_device(
    mr_query, mr_key, mr_value, li_query, li_key, upstream,
    mr_short, li_short, mr_filter, li_rate, li_residue, li_skip,
):
    channels = mr_query.shape[1]
    tiles = channels // LANES
    assert mr_query.shape[0] == ROWS and lax.axis_size(AXES) == 2 * tiles
    rows = (ROWS, channels)
    full, full32 = (rows, BF16, "r"), (rows, F32, "r")
    half = ((ROWS, channels // 2), BF16, "r")
    state_out = ((2 * tiles, 8, LANES), F32, "s")
    state_sent = ((2 * tiles, 8, LANES), BF16, "s")
    halves = ((0, 2), (1, 2))

    def few(n):
        return ((n, channels), F32, "r")

    last_rows, first_rows, last_kv = edges(mr_query, mr_key, mr_value, li_query, li_key, upstream)
    prev = sent(last_rows, 1)
    following = sent(first_rows, -1)
    before_kv = sent(last_kv, 2)

    table, medium, medium_turned, long, long_turned = make_tables(
        mr_short, li_short, li_skip[None, :], mr_filter, li_rate, li_residue
    )
    rate = li_rate.reshape(1, channels)
    residue = li_residue.reshape(1, channels)
    me = lax.axis_index(AXES)
    my_rates = lax.dynamic_slice(
        li_rate, ((me // 2) * TILE_GROUPS, (me % 2) * 8), (TILE_GROUPS, 8)
    )
    my_rates = jnp.repeat(my_rates.T, GROUP, axis=1)

    key_in = after(mr_key, before_kv, following)
    into = {}
    signal_one = []
    for n, part in enumerate(halves):
        got = lane_call(
            product_one_body, "product_one", channels,
            [(key_in, "r"), (mr_value, "r"), (prev, "r"), (following, "r"), (table, "r")],
            [full, full, few(4), half], 4, part, into,
        )
        signal_one.append(got[3])
        into = dict(enumerate(got[:3]))
    keys_one, value_one, beyond_one = got[:3]
    before_one = [sent(signal, 1) for signal in signal_one]

    query_two, cotangent, state_back = lane_call(
        upstream_body, "upstream", channels,
        [(after(li_query, *signal_one), "r"), (upstream, "r"), (prev, "r"), (table, "r"),
         (rate, "r")],
        [full, full, state_sent], 7,
    )
    gathered_back = exchanged(state_back)
    (near_back,) = lane_call(
        long_back_near_body, "long_back_near", channels,
        [(cotangent, "r"), (table, "r"), (long_turned, "g")],
        [full32], 8, unroll=4,
    )

    def forward(n, into):
        return lane_call(
            forward_body, "forward", channels,
            [(before_one[n], "r"), (before_kv, "r"), (signal_one[n], "r"), (mr_query, "r"),
             (li_key, "r"), (prev, "r"), (table, "r"), (medium, "g"), (long, "g"), (rate, "r")],
            [full, full, full32, state_out, state_sent, few(6)],
            13, halves[n], into, unroll=2,
        )

    got_forward = forward(0, {})
    gathered_back = after(gathered_back, near_back, got_forward[0])
    closing = exchanged(scan_states(gathered_back, my_rates, True))
    conv_one, value_two, near, state, state_outgoing, head = forward(
        1, dict(enumerate(got_forward))
    )
    next_head = sent(head, -1)
    gathered = exchanged(state_outgoing)

    into = {}
    conv_grad = []
    near_later = after(near_back, conv_one)
    for part in halves:
        got = lane_call(
            long_back_body, "long_back", channels,
            [(near_later, "r"), (closing, "s"), (li_query, "r"), (li_key, "r"), (mr_query, "r"),
             (prev, "r"), (following, "r"), (table, "r"), (rate, "r"), (residue, "r")],
            [full, few(2), full, few(2), few(1), half],
            6, part, into, unroll=4,
        )
        conv_grad.append(got[5])
        into = dict(enumerate(got[:5]))
    grad_two, grad_two_after, mixed_grad, mixed_head, conv_head, _ = got
    after_one = [sent(after(signal, next_head), -1) for signal in conv_grad]
    after_next = sent(conv_head, -2)
    mixed_after = sent(mixed_head, -1)

    gathered = after(gathered, next_head)
    start = exchanged(scan_states(gathered, my_rates, False))
    grad_li_key, grad_mr_query = lane_call(
        late_body, "late", channels,
        [(grad_two, "r"), (grad_two_after, "r"), (value_two, "r"), (mixed_grad, "r"),
         (mixed_after, "r"), (conv_one, "r"), (next_head, "r"), (table, "r")],
        [full, full], 6,
    )

    def medium_back(n, into):
        return lane_call(
            medium_back_body, "medium_back", channels,
            [(conv_grad[n], "r"), (after_one[n], "r"), (after_next, "r"), (keys_one, "r"),
             (value_one, "r"), (beyond_one, "r"), (table, "r"), (medium_turned, "g")],
            [full, full], 7, halves[n], into, unroll=4,
        )

    got = medium_back(0, {})
    start = after(start, grad_li_key, *got)
    output, grad_li_query = lane_call(
        long_body, "long_forward", channels,
        [(near, "r"), (start, "s"), (state, "s"), (query_two, "r"), (upstream, "r"),
         (following, "r"), (next_head, "r"), (table, "r"), (rate, "r"), (residue, "r"),
         (long_turned, "g")],
        [full, full], 9, unroll=4,
    )
    grad_mr_key, grad_mr_value = medium_back(1, dict(enumerate(got)))
    return (output, grad_mr_query, grad_mr_key, grad_mr_value, grad_li_query, grad_li_key)


def solution(mesh):
    split = P(("ctx", "ch"), None)
    return jax.shard_map(
        per_device,
        mesh=mesh,
        in_specs=(split,) * 6 + (P(),) * 6,
        out_specs=(split,) * 6,
        check_vma=False,
    )
```

time: 222 us -> 247 us (1.11)
  blocking collectives: 0 us -> 39.3 us
  waiting for transfers between devices: 22 us -> 1.99 us
  Pallas kernels: 111 us -> 115 us
    all_to_all x0 -> x1, blocking collectives: none -> 39.3 us  [exchanged(): return lax.all_to_all(array, AXES, split_axis=0, concat_axis=0, tiled=True)]
    all_to_all x4 -> x3, waiting for transfers between devices: 15.3 us -> 0.06 us  [exchanged(): return lax.all_to_all(array, AXES, split_axis=0, concat_axis=0, tiled=True)]
    ppermute x9 -> x10, waiting for transfers between devices: 6.69 us -> 1.94 us  [sent(): return lax.ppermute(array, AXES, pairs)]
    all_to_all x4 -> x3, starting transfers between devices: 38.6 us -> 34.1 us  [exchanged(): return lax.all_to_all(array, AXES, split_axis=0, concat_axis=0, tiled=True)]
    ppermute x9 -> x10, starting transfers between devices: 38.8 us -> 42.9 us  [sent(): return lax.ppermute(array, AXES, pairs)]
    pallas_call x11 -> x12, Pallas kernels: 98.3 us -> 102 us  [lane_call(): pl.pallas_call(kernel, name=name, grid=(blocks,), in_specs=[spec(a.shape,...]
  transfers between devices with their start and end apart: 13 -> 13, of which waited for: 4 -> 3; matrix products, arithmetic and copies ran while one was open for 2% -> 2% of each run, Pallas kernels for 37% -> 36%
where the time goes in v5:
time: 247 us; the launch traced here: 245 us
  Pallas kernels  115 us (47%)
  starting transfers between devices  76.9 us (31%)
  blocking collectives  39.3 us (16%)
  local copies, waits for them, and re-layouts  10.8 us (4%)
    pallas_call x12, Pallas kernels, lane_call(): pl.pallas_call(kernel, name=name, grid=(blocks,), in_specs=[spec(a.shape,...  102 us
    ppermute x10, starting transfers between devices, sent(): return lax.ppermute(array, AXES, pairs)  42.9 us
    all_to_all x1, blocking collectives, exchanged(): return lax.all_to_all(array, AXES, split_axis=0, concat_axis=0, tiled=True)  39.3 us
    all_to_all x3, starting transfers between devices, exchanged(): return lax.all_to_all(array, AXES, split_axis=0, concat_axis=0, tiled=True)  34.1 us
    unnamed x38, local copies, waits for them, and re-layouts  8.45 us
    pallas_call x1, Pallas kernels, make_tables(): pl.pallas_call(kernel, name='tables', grid=(groups // block,), in_specs=[...  5.13 us
  transfers between devices with their start and end apart: 13, of which 3 were waited for; matrix products, arithmetic and copies ran while one was open for 2% of the time, Pallas kernels for 36%

profile of v5, /device:TPU:1, one launch (start us, length us, event | category | flops | bytes accessed | tf_op | source)
XLA Modules:
  0.0 244.7 jit_solution(684542849281393857)
XLA Ops:
  0.7 3.6 %edges.1 = (bf16[16,8192]{1,0:T(8,128)(2,1)}, bf16[16,8192]{1,0:T(8,128)(2,1)}, bf16[8,8192]{1,0:T(8,128)(2,1)}) custom-call(bf16[128,8192]{1,0:T(8,128)(2,1)} %refs_4_.8, bf16[128,8192]{1,0:T(8,128)(2,1)} %refs_0_.1, bf16[128,8192]{1,0:T(8,128)(2,1)} %refs_1_.4, bf16[128,8192]{1,0:T(8,128)(2,1)} %refs_2_.3, bf16[128,8192]{1,0:T(8,128)(2,1)} %refs_3_.7, ...), custom_call_target="tpu_custom_call" | custom-call | bytes 12600000 | tf_op jit(solution)/shard_map/edges/pallas_call | solution.py:263
  4.3 9.5 %collective-permute-start.1 = (bf16[16,8192]{1,0:T(8,128)(2,1)}, bf16[16,8192]{1,0:T(8,128)(2,1)S(1)}, u32[]{:S(2)}, u32[]{:S(2)}) collective-permute-start(bf16[16,8192]{1,0:T(8,128)(2,1)} %get-tuple-element.66), channel_id=1, source_target_pairs={{1,0},{2,1},{3,2},{4,3},{5,4},{6,5},{7,6},{8,7},{9,8},{10,9},{11,1... | collective-permute-start | bytes 786440 | tf_op jit(solution)/shard_map/ppermute | solution.py:563
  19.4 5.1 %tables.1 = (f32[24,8192]{1,0:T(8,128)}, f32[512,128]{1,0:T(8,128)}, f32[512,128]{1,0:T(8,128)}, f32[512,128]{1,0:T(8,128)}, f32[512,128]{1,0:T(8,128)}) custom-call(bf16[3,3,8192]{2,1,0:T(4,128)(2,1)} %mr.1, bf16[3,3,8192]{2,1,0:T(4,128)(2,1)} %li.1, f32[1,8192]{1,0:T(1,128)} %bitcast.3, bf16[128,512]{1,0:T(8,128)(2,1)} %filters.1, f32[512,16]{1,0:T(8,128)} %copy.38.rate, ...), custom_call_target="tpu_custom_call" | custom-call | bytes 18000000 | tf_op jit(solution)/shard_map/tables/pallas_call | solution.py:306
  27.2 4.7 %product_one.2 = (bf16[128,8192]{1,0:T(8,128)(2,1)}, bf16[128,8192]{1,0:T(8,128)(2,1)}, f32[4,8192]{1,0:T(4,128)}, bf16[128,4096]{1,0:T(8,128)(2,1)}) custom-call(bf16[128,8192]{1,0:T(8,128)(2,1)} %refs_0_.1, bf16[128,8192]{1,0:T(8,128)(2,1)} %refs_1_.4, bf16[16,8192]{1,0:T(8,128)(2,1)} %copy-done, bf16[16,8192]{1,0:T(8,128)(2,1)} %copy-done.1, ...), custom_call_target="tpu_custom_call" | custom-call | bytes 14400000 | tf_op jit(solution)/shard_map/product_one/pallas_call | solution.py:80
  33.8 4.8 %product_one.3 = (bf16[128,8192]{1,0:T(8,128)(2,1)}, bf16[128,8192]{1,0:T(8,128)(2,1)}, f32[4,8192]{1,0:T(4,128)}, bf16[128,4096]{1,0:T(8,128)(2,1)}) custom-call(bf16[128,8192]{1,0:T(8,128)(2,1)} %refs_0_.1, bf16[128,8192]{1,0:T(8,128)(2,1)} %refs_1_.4, bf16[16,8192]{1,0:T(8,128)(2,1)} %copy-done, ...), custom_call_target="tpu_custom_call", output_to_operand_aliasing={{0}: (5, {}), {1}: (6, {}), {2}: (7, {})} | custom-call | bytes 14400000 | tf_op jit(solution)/shard_map/product_one/pallas_call | solution.py:80
  41.3 7.9 %upstream.1 = (bf16[128,8192]{1,0:T(8,128)(2,1)}, bf16[128,8192]{1,0:T(8,128)(2,1)}, bf16[128,8,128]{2,1,0:T(8,128)(2,1)}) custom-call(bf16[128,8192]{1,0:T(8,128)(2,1)} %refs_2_.3, bf16[128,8192]{1,0:T(8,128)(2,1)} %refs_4_.9, bf16[16,8192]{1,0:T(8,128)(2,1)} %copy-done, f32[24,8192]{1,0:T(8,128)} %get-tuple-element.69.refs_4_.refs_6_.refs_3_.refs_1_.refs_7_, ...), custom_call_target="tpu_custom_call" | custom-call | bytes 25200000 | tf_op jit(solution)/shard_map/upstream/pallas_call | solution.py:80
  49.2 14.4 %all-to-all-start.2 = ((bf16[128,8,128]{2,1,0:T(8,128)(2,1)}), bf16[128,8,128]{2,1,0:T(8,128)(2,1)S(1)}, u32[]{:S(2)}, u32[]{:S(2)}) async-start(bf16[128,8,128]{2,1,0:T(8,128)(2,1)} %get-tuple-element.92), calls=%async_computation.2 | async-start | bytes 524288 | tf_op jit(solution)/shard_map/all_to_all | solution.py:567
  64.4 9.2 %long_back_near.1.refs_0_ = f32[128,8192]{1,0:T(8,128)} custom-call(bf16[128,8192]{1,0:T(8,128)(2,1)} %get-tuple-element.88.refs_0_, f32[24,8192]{1,0:T(8,128)} %get-tuple-element.69.refs_4_.refs_6_.refs_3_.refs_1_.refs_7_, f32[512,128]{1,0:T(8,128)} %get-tuple-element.89.refs_2_.refs_10_), custom_call_target="tpu_custom_call" | custom-call | bytes 28800000 | tf_op jit(solution)/shard_map/long_back_near/pallas_call | solution.py:80
  74.6 13.1 %forward.2 = (bf16[128,8192]{1,0:T(8,128)(2,1)}, bf16[128,8192]{1,0:T(8,128)(2,1)}, f32[128,8192]{1,0:T(8,128)}, f32[128,8,128]{2,1,0:T(8,128)}, bf16[128,8,128]{2,1,0:T(8,128)(2,1)}, /*index=5*/f32[6,8192]{1,0:T(8,128)}) custom-call(bf16[128,4096]{1,0:T(8,128)(2,1)} %copy-done.7, bf16[8,8192]{1,0:T(8,128)(2,1)} %copy-done.13, ...), custom_call_target="tpu_custom_call" | custom-call | bytes 46800000 | tf_op jit(solution)/shard_map/forward/pallas_call | solution.py:80
  88.4 1.9 scan_back.1
  90.4 9.8 %all-to-all-start.3 = ((bf16[128,8,128]{2,1,0:T(8,128)(2,1)}), bf16[128,8,128]{2,1,0:T(8,128)(2,1)S(1)}, u32[]{:S(2)}, u32[]{:S(2)}) async-start(bf16[128,8,128]{2,1,0:T(8,128)(2,1)} %scan_back.1), calls=%async_computation.3 | async-start | bytes 524288 | tf_op jit(solution)/shard_map/all_to_all | solution.py:567
  101.1 13.1 %forward.3 = (bf16[128,8192]{1,0:T(8,128)(2,1)}, bf16[128,8192]{1,0:T(8,128)(2,1)}, f32[128,8192]{1,0:T(8,128)}, f32[128,8,128]{2,1,0:T(8,128)}, bf16[128,8,128]{2,1,0:T(8,128)(2,1)}, /*index=5*/f32[6,8192]{1,0:T(8,128)}) custom-call(bf16[128,4096]{1,0:T(8,128)(2,1)} %copy-done.6, ...), custom_call_target="tpu_custom_call", output_to_operand_aliasing={{0}: (10, {}), {1}: (11, {}), {2}: (12, {}), {3}: (13, {}),... | custom-call | bytes 46800000 | tf_op jit(solution)/shard_map/forward/pallas_call | solution.py:80
  114.2 7.7 %collective-permute-start.5 = (f32[6,8192]{1,0:T(8,128)}, f32[6,8192]{1,0:T(8,128)S(1)}, u32[]{:S(2)}, u32[]{:S(2)}) collective-permute-start(f32[6,8192]{1,0:T(8,128)} %get-tuple-element.85), channel_id=1, source_target_pairs={{1,0},{2,1},{3,2},{4,3},{5,4},{6,5},{7,6},{8,7},{9,8},{10,9},{11,1... | collective-permute-start | bytes 589832 | tf_op jit(solution)/shard_map/ppermute | solution.py:563
  123.4 7.0 %long_back.2 = (bf16[128,8192]{1,0:T(8,128)(2,1)}, f32[2,8192]{1,0:T(2,128)}, bf16[128,8192]{1,0:T(8,128)(2,1)}, f32[2,8192]{1,0:T(2,128)}, f32[1,8192]{1,0:T(1,128)}, /*index=5*/bf16[128,4096]{1,0:T(8,128)(2,1)}) custom-call(f32[128,8192]{1,0:T(8,128)} %long_back_near.1.refs_0_, bf16[128,8,128]{2,1,0:T(8,128)(2,1)} %copy-done.2, bf16[128,8192]{1,0:T(8,128)(2,1)} %refs_2_.3, ...), custom_call_target="tpu_custom_call" | custom-call | bytes 21600000 | tf_op jit(solution)/shard_map/long_back/pallas_call | solution.py:80
  130.4 5.5 %collective-permute-start.7 = (bf16[128,4096]{1,0:T(8,128)(2,1)}, bf16[128,4096]{1,0:T(8,128)(2,1)S(1)}, u32[]{:S(2)}, u32[]{:S(2)}) collective-permute-start(bf16[128,4096]{1,0:T(8,128)(2,1)} %get-tuple-element.106.refs_0_), channel_id=1, source_target_pairs={{1,0},{2,1},{3,2},{4,3},{5,4},{6,5},{7,6},{8,7},{9,8},{10,9},{11,1... | collective-permute-start | bytes 3145736 | tf_op jit(solution)/shard_map/ppermute | solution.py:563
  136.0 7.1 %long_back.3 = (bf16[128,8192]{1,0:T(8,128)(2,1)}, f32[2,8192]{1,0:T(2,128)}, bf16[128,8192]{1,0:T(8,128)(2,1)}, f32[2,8192]{1,0:T(2,128)}, f32[1,8192]{1,0:T(1,128)}, /*index=5*/bf16[128,4096]{1,0:T(8,128)(2,1)}) custom-call(f32[128,8192]{1,0:T(8,128)} %long_back_near.1.refs_0_, ...), custom_call_target="tpu_custom_call", output_to_operand_aliasing={{0}: (10, {}), {1}: (11, {}), {2}: (12, {}), {3}: (13, {}),... | custom-call | bytes 21600000 | tf_op jit(solution)/shard_map/long_back/pallas_call | solution.py:80
  145.0 39.3 %all_to_all.20.states_ref = bf16[128,8,128]{2,1,0:T(8,128)(2,1)} all-to-all(bf16[128,8,128]{2,1,0:T(8,128)(2,1)S(1)} %copy-done.5), channel_id=1, replica_groups=mesh['ctx'=8,'ch'=16] {'ctx','ch'}, dimensions={0} | all-to-all | bytes 524288 | tf_op jit(solution)/shard_map/all_to_all | solution.py:567
  186.2 9.9 %all-to-all-start.1 = ((bf16[128,8,128]{2,1,0:T(8,128)(2,1)}), bf16[128,8,128]{2,1,0:T(8,128)(2,1)S(1)}, u32[]{:S(2)}, u32[]{:S(2)}) async-start(bf16[128,8,128]{2,1,0:T(8,128)(2,1)} %scan_forward.1), calls=%async_computation.1 | async-start | bytes 524288 | tf_op jit(solution)/shard_map/all_to_all | solution.py:567
  196.1 7.7 %collective-permute-start.6 = (f32[2,8192]{1,0:T(2,128)}, f32[2,8192]{1,0:T(2,128)S(1)}, u32[]{:S(2)}, u32[]{:S(2)}) collective-permute-start(f32[2,8192]{1,0:T(2,128)} %get-tuple-element.103), channel_id=1, source_target_pairs={{1,0},{2,1},{3,2},{4,3},{5,4},{6,5},{7,6},{8,7},{9,8},{10,9},{11,1... | collective-permute-start | bytes 196616 | tf_op jit(solution)/shard_map/ppermute | solution.py:563
  203.8 2.8 %collective-permute-start.8 = (f32[1,8192]{1,0:T(1,128)}, f32[1,8192]{1,0:T(1,128)S(1)}, u32[]{:S(2)}, u32[]{:S(2)}) collective-permute-start(f32[1,8192]{1,0:T(1,128)} %get-tuple-element.107), channel_id=1, source_target_pairs={{2,0},{3,1},{4,2},{5,3},{6,4},{7,5},{8,6},{9,7},{10,8},{11,9},{12,... | collective-permute-start | bytes 98312 | tf_op jit(solution)/shard_map/ppermute | solution.py:563
  207.3 9.2 %late.1 = (bf16[128,8192]{1,0:T(8,128)(2,1)}, bf16[128,8192]{1,0:T(8,128)(2,1)}) custom-call(bf16[128,8192]{1,0:T(8,128)(2,1)} %get-tuple-element.99.refs_0_, f32[2,8192]{1,0:T(2,128)} %get-tuple-element.100.refs_1_, bf16[128,8192]{1,0:T(8,128)(2,1)} %get-tuple-element.101.refs_2_, bf16[128,8192]{1,0:T(8,128)(2,1)} %get-tuple-element.102.refs_3_, ...), custom_call_target="tpu_custom_call" | custom-call | bytes 21600000 | tf_op jit(solution)/shard_map/late/pallas_call | solution.py:80
  217.5 7.7 %medium_back.2 = (bf16[128,8192]{1,0:T(8,128)(2,1)}, bf16[128,8192]{1,0:T(8,128)(2,1)}) custom-call(bf16[128,4096]{1,0:T(8,128)(2,1)} %get-tuple-element.106.refs_0_, bf16[128,4096]{1,0:T(8,128)(2,1)} %copy-done.8, f32[1,8192]{1,0:T(1,128)} %copy-done.14, bf16[128,8192]{1,0:T(8,128)(2,1)} %get-tuple-element.108.refs_3_, ...), custom_call_target="tpu_custom_call" | custom-call | bytes 25200000 | tf_op jit(solution)/shard_map/medium_back/pallas_call | solution.py:80
  226.3 7.8 %medium_back.3 = (bf16[128,8192]{1,0:T(8,128)(2,1)}, bf16[128,8192]{1,0:T(8,128)(2,1)}) custom-call(bf16[128,4096]{1,0:T(8,128)(2,1)} %get-tuple-element.120.refs_0_, bf16[128,4096]{1,0:T(8,128)(2,1)} %copy-done.9, f32[1,8192]{1,0:T(1,128)} %copy-done.14, ...), custom_call_target="tpu_custom_call", output_to_operand_aliasing={{0}: (8, {}), {1}: (9, {})} | custom-call | bytes 25200000 | tf_op jit(solution)/shard_map/medium_back/pallas_call | solution.py:80
  234.1 10.5 %long_forward.1 = (bf16[128,8192]{1,0:T(8,128)(2,1)}, bf16[128,8192]{1,0:T(8,128)(2,1)}) custom-call(f32[128,8192]{1,0:T(8,128)} %get-tuple-element.83.refs_0_, bf16[128,8,128]{2,1,0:T(8,128)(2,1)} %copy-done.12, f32[128,8,128]{2,1,0:T(8,128)} %get-tuple-element.115.refs_2_, bf16[128,8192]{1,0:T(8,128)(2,1)} %get-tuple-element.116.refs_3_, ...), custom_call_target="tpu_custom_call" | custom-call | bytes 32400000 | tf_op jit(solution)/shard_map/long_forward/pallas_call | solution.py:80
  (62 shorter events, 24.3 us)
Async XLA Ops:
  0.6 17.0 %copy-start.17 = (f32[512,16]{0,1:T(8,128)S(1)}, f32[512,16]{0,1:T(8,128)}, u32[]{:S(2)}) copy-start(f32[512,16]{0,1:T(8,128)} %param.22) | copy-start | bytes 98308
  0.6 17.9 %copy-start.16 = (f32[512,16]{0,1:T(8,128)S(1)}, f32[512,16]{0,1:T(8,128)}, u32[]{:S(2)}) copy-start(f32[512,16]{0,1:T(8,128)} %param.21) | copy-start | bytes 98308
  4.3 21.7 %collective-permute-start.1 = (bf16[16,8192]{1,0:T(8,128)(2,1)}, bf16[16,8192]{1,0:T(8,128)(2,1)S(1)}, u32[]{:S(2)}, u32[]{:S(2)}) collective-permute-start(bf16[16,8192]{1,0:T(8,128)(2,1)} %get-tuple-element.66), channel_id=1, source_target_pairs={{1,0},{2,1},{3,2},{4,3},{5,4},{6,5},{7,6},{8,7},{9,8},{10,9},{11,1... | collective-permute-start | bytes 786440 | tf_op jit(solution)/shard_map/ppermute | solution.py:563
  13.8 12.6 %collective-permute-start.2 = (bf16[16,8192]{1,0:T(8,128)(2,1)}, bf16[16,8192]{1,0:T(8,128)(2,1)S(1)}, u32[]{:S(2)}, u32[]{:S(2)}) collective-permute-start(bf16[16,8192]{1,0:T(8,128)(2,1)} %get-tuple-element.68), channel_id=1, source_target_pairs={{0,1},{1,2},{2,3},{3,4},{4,5},{5,6},{6,7},{7,8},{8,9},{9,10},{10,1... | collective-permute-start | bytes 786440 | tf_op jit(solution)/shard_map/ppermute | solution.py:563
  15.7 10.2 %collective-permute-start = (bf16[8,8192]{1,0:T(8,128)(2,1)}, bf16[8,8192]{1,0:T(8,128)(2,1)S(1)}, u32[]{:S(2)}, u32[]{:S(2)}) collective-permute-start(bf16[8,8192]{1,0:T(8,128)(2,1)} %get-tuple-element.65), channel_id=1, source_target_pairs={{0,2},{1,3},{2,4},{3,5},{4,6},{5,7},{6,8},{7,9},{8,10},{9,11},{10,... | collective-permute-start | bytes 393224 | tf_op jit(solution)/shard_map/ppermute | solution.py:563
  26.0 12.7 %copy-start.13 = (bf16[8,8192]{1,0:T(8,128)(2,1)}, bf16[8,8192]{1,0:T(8,128)(2,1)S(1)}, u32[]{:S(2)}) copy-start(bf16[8,8192]{1,0:T(8,128)(2,1)S(1)} %collective-permute-done.refs_1_) | copy-start | bytes 393220
  31.9 41.7 %collective-permute-start.4 = (bf16[128,4096]{1,0:T(8,128)(2,1)}, bf16[128,4096]{1,0:T(8,128)(2,1)S(1)}, u32[]{:S(2)}, u32[]{:S(2)}) collective-permute-start(bf16[128,4096]{1,0:T(8,128)(2,1)} %get-tuple-element.76.refs_2_), channel_id=1, source_target_pairs={{0,1},{1,2},{2,3},{3,4},{4,5},{5,6},{6,7},{7,8},{8,9},{9,10},{10,1... | collective-permute-start | bytes 3145736 | tf_op jit(solution)/shard_map/ppermute | solution.py:563
  33.8 6.7 %copy-start.4 = (f32[512,16]{1,0:T(8,128)S(1)}, f32[512,16]{1,0:T(8,128)}, u32[]{:S(2)}) copy-start(f32[512,16]{1,0:T(8,128)} %copy.38.rate) | copy-start | bytes 98308
  38.6 61.5 %collective-permute-start.3 = (bf16[128,4096]{1,0:T(8,128)(2,1)}, bf16[128,4096]{1,0:T(8,128)(2,1)S(1)}, u32[]{:S(2)}, u32[]{:S(2)}) collective-permute-start(bf16[128,4096]{1,0:T(8,128)(2,1)} %get-tuple-element.73.refs_2_), channel_id=1, source_target_pairs={{0,1},{1,2},{2,3},{3,4},{4,5},{5,6},{6,7},{7,8},{8,9},{9,10},{10,1... | collective-permute-start | bytes 3145736 | tf_op jit(solution)/shard_map/ppermute | solution.py:563
  49.2 38.6 %all-to-all-start.2 = ((bf16[128,8,128]{2,1,0:T(8,128)(2,1)}), bf16[128,8,128]{2,1,0:T(8,128)(2,1)S(1)}, u32[]{:S(2)}, u32[]{:S(2)}) async-start(bf16[128,8,128]{2,1,0:T(8,128)(2,1)} %get-tuple-element.92), calls=%async_computation.2 | async-start | bytes 524288 | tf_op jit(solution)/shard_map/all_to_all | solution.py:567
  90.4 32.3 %all-to-all-start.3 = ((bf16[128,8,128]{2,1,0:T(8,128)(2,1)}), bf16[128,8,128]{2,1,0:T(8,128)(2,1)S(1)}, u32[]{:S(2)}, u32[]{:S(2)}) async-start(bf16[128,8,128]{2,1,0:T(8,128)(2,1)} %scan_back.1), calls=%async_computation.3 | async-start | bytes 524288 | tf_op jit(solution)/shard_map/all_to_all | solution.py:567
  100.2 1.0 copy-start.6
  101.1 20.8 %copy-start.3 = (f32[512,16]{1,0:T(8,128)S(1)}, f32[512,16]{1,0:T(8,128)}, u32[]{:S(2)}) copy-start(f32[512,16]{1,0:T(8,128)} %copy.39.residue) | copy-start | bytes 98308
  114.2 16.2 %collective-permute-start.5 = (f32[6,8192]{1,0:T(8,128)}, f32[6,8192]{1,0:T(8,128)S(1)}, u32[]{:S(2)}, u32[]{:S(2)}) collective-permute-start(f32[6,8192]{1,0:T(8,128)} %get-tuple-element.85), channel_id=1, source_target_pairs={{1,0},{2,1},{3,2},{4,3},{5,4},{6,5},{7,6},{8,7},{9,8},{10,9},{11,1... | collective-permute-start | bytes 589832 | tf_op jit(solution)/shard_map/ppermute | solution.py:563
  130.4 12.6 %copy-start.11 = (f32[6,8192]{1,0:T(8,128)}, f32[6,8192]{1,0:T(8,128)S(1)}, u32[]{:S(2)}) copy-start(f32[6,8192]{1,0:T(8,128)S(1)} %collective-permute-done.5.refs_6_) | copy-start | bytes 589828
  130.4 86.1 %collective-permute-start.7 = (bf16[128,4096]{1,0:T(8,128)(2,1)}, bf16[128,4096]{1,0:T(8,128)(2,1)S(1)}, u32[]{:S(2)}, u32[]{:S(2)}) collective-permute-start(bf16[128,4096]{1,0:T(8,128)(2,1)} %get-tuple-element.106.refs_0_), channel_id=1, source_target_pairs={{1,0},{2,1},{3,2},{4,3},{5,4},{6,5},{7,6},{8,7},{9,8},{10,9},{11,1... | collective-permute-start | bytes 3145736 | tf_op jit(solution)/shard_map/ppermute | solution.py:563
  135.9 9.0 %copy-start.5 = (bf16[128,8,128]{2,1,0:T(8,128)(2,1)S(1)}, bf16[128,8,128]{2,1,0:T(8,128)(2,1)}, u32[]{:S(2)}) copy-start(bf16[128,8,128]{2,1,0:T(8,128)(2,1)} %get-tuple-element.84) | copy-start | bytes 786436
  143.0 82.2 %collective-permute-start.9 = (bf16[128,4096]{1,0:T(8,128)(2,1)}, bf16[128,4096]{1,0:T(8,128)(2,1)S(1)}, u32[]{:S(2)}, u32[]{:S(2)}) collective-permute-start(bf16[128,4096]{1,0:T(8,128)(2,1)} %get-tuple-element.120.refs_0_), channel_id=1, source_target_pairs={{1,0},{2,1},{3,2},{4,3},{5,4},{6,5},{7,6},{8,7},{9,8},{10,9},{11,1... | collective-permute-start | bytes 3145736 | tf_op jit(solution)/shard_map/ppermute | solution.py:563
  186.2 39.0 %all-to-all-start.1 = ((bf16[128,8,128]{2,1,0:T(8,128)(2,1)}), bf16[128,8,128]{2,1,0:T(8,128)(2,1)S(1)}, u32[]{:S(2)}, u32[]{:S(2)}) async-start(bf16[128,8,128]{2,1,0:T(8,128)(2,1)} %scan_forward.1), calls=%async_computation.1 | async-start | bytes 524288 | tf_op jit(solution)/shard_map/all_to_all | solution.py:567
  196.1 10.6 %collective-permute-start.6 = (f32[2,8192]{1,0:T(2,128)}, f32[2,8192]{1,0:T(2,128)S(1)}, u32[]{:S(2)}, u32[]{:S(2)}) collective-permute-start(f32[2,8192]{1,0:T(2,128)} %get-tuple-element.103), channel_id=1, source_target_pairs={{1,0},{2,1},{3,2},{4,3},{5,4},{6,5},{7,6},{8,7},{9,8},{10,9},{11,1... | collective-permute-start | bytes 196616 | tf_op jit(solution)/shard_map/ppermute | solution.py:563
  203.8 12.7 %collective-permute-start.8 = (f32[1,8192]{1,0:T(1,128)}, f32[1,8192]{1,0:T(1,128)S(1)}, u32[]{:S(2)}, u32[]{:S(2)}) collective-permute-start(f32[1,8192]{1,0:T(1,128)} %get-tuple-element.107), channel_id=1, source_target_pairs={{2,0},{3,1},{4,2},{5,3},{6,4},{7,5},{8,6},{9,7},{10,8},{11,9},{12,... | collective-permute-start | bytes 98312 | tf_op jit(solution)/shard_map/ppermute | solution.py:563
  216.5 1.0 copy-start.8
  225.3 8.8 %copy-start.12 = (bf16[128,8,128]{2,1,0:T(8,128)(2,1)}, bf16[128,8,128]{2,1,0:T(8,128)(2,1)S(1)}, u32[]{:S(2)}) copy-start(bf16[128,8,128]{2,1,0:T(8,128)(2,1)S(1)} %all-to-all-done.1.refs_1_) | copy-start | bytes 786436
  225.3 1.0 copy-start.9
  (7 other events, 5.1 us)

commit v6 on v5

--- a/solution.py
+++ b/solution.py
@@ -33,58 +33,90 @@
     return start if isinstance(start, int) else pl.multiple_of(start, of)
 
 
-def lane_call(body, name, channels, ins, outs, us, part=(0, 1), into=None, width=1024, unroll=8):
+def lane_call(body, name, channels, ins, outs, us, part=(0, 1), into=None, width=1024, unroll=4):
     span = channels // part[1]
     width = min(width, span)
     tiles = width // LANES
     unroll = min(unroll, tiles)
     blocks = span // width
     into = into or {}
-
-    def spec(shape, kind):
-        held = {"r": shape[-1], "g": shape[0] * GROUP, "s": shape[0] * (LANES // 2)}[kind]
-        first = part[0] * blocks if held == channels else 0
+    kinds = [kind for _, kind in ins] + [kind for _, _, kind in outs]
+    shapes = [a.shape for a, _ in ins] + [shape for shape, _, _ in outs]
+    dtypes = [a.dtype for a, _ in ins] + [dtype for _, dtype, _ in outs]
+    count, count_in, count_into = len(kinds), len(ins), len(into)
+
+    def channels_of(shape, kind):
+        return {"r": shape[-1], "g": shape[0] * GROUP, "s": shape[0] * (LANES // 2)}[kind]
+
+    def cut(ref, kind, start, size):
         if kind == "r":
-            return pl.BlockSpec((shape[0], width), lambda i: (0, first + i))
+            return ref.at[:, pl.ds(hint(start, LANES), size)]
         if kind == "g":
-            return pl.BlockSpec((width // GROUP, shape[1]), lambda i: (first + i, 0))
-        return pl.BlockSpec((2 * tiles, 8, LANES), lambda i: (first + i, 0, 0))
-
-    def view(ref, kind, t):
+            return ref.at[pl.ds(hint(start // GROUP, TILE_GROUPS), size // GROUP), :]
+        return ref.at[pl.ds(start // (LANES // 2), size // (LANES // 2))]
+
+    def kept(shape, kind):
         if kind == "r":
-            return ref.at[:, pl.ds(hint(t * LANES, LANES), LANES)]
-        if kind == "g":
-            return ref.at[pl.ds(hint(t * TILE_GROUPS, TILE_GROUPS), TILE_GROUPS), :]
-        return ref.at[pl.ds(2 * t, 2)]
-
-    kinds = [kind for _, kind in ins] + [kind for _, _, kind in outs]
-    count_in, count_out = len(ins), len(outs)
+            return (shape[0], span)
+        return (span // GROUP, shape[1]) if kind == "g" else (span // (LANES // 2), *shape[1:])
+
+    first = [
+        part[0] * span if channels_of(shape, kind) == channels else 0
+        for shape, kind in zip(shapes, kinds)
+    ]
 
     def kernel(*refs):
-        arrays = refs[:count_in] + refs[count_in + len(into) : count_in + len(into) + count_out]
-
-        def step(k, unused):
-            running = []
-            for u in range(unroll):
-                t = u if unroll == tiles else k * unroll + u
-                running.append(body(*[view(ref, kind, t) for ref, kind in zip(arrays, kinds)]))
-            while running:
-                running = [tile for tile in running if next(tile, False)]
+        far = refs[:count_in] + refs[count_in + count_into : count + count_into]
+        held = refs[count + count_into : -1]
+        arrived = refs[-1]
+
+        def copy(n, b):
+            outside = cut(far[n], kinds[n], first[n] + b * width, width)
+            inside = cut(held[n], kinds[n], b * width, width)
+            if n < count_in:
+                return pltpu.make_async_copy(outside, inside, arrived.at[n, b])
+            return pltpu.make_async_copy(inside, outside, arrived.at[n, b])
+
+        for b in range(blocks):
+            for n in range(count_in):
+                copy(n, b).start()
+
+        def block(b, unused):
+            for n in range(count_in):
+                copy(n, b).wait()
+
+            def step(k, unused):
+                running = []
+                for u in range(unroll):
+                    start = b * width + (k * unroll + u) * LANES
+                    running.append(
+                        body(*[cut(ref, kind, start, LANES) for ref, kind in zip(held, kinds)])
+                    )
+                while running:
+                    running = [tile for tile in running if next(tile, False)]
+                return unused
+
+            lax.fori_loop(0, tiles // unroll, step, 0)
+            for n in range(count_in, count):
+                copy(n, b).start()
             return unused
 
-        if unroll == tiles:
-            step(0, 0)
-        else:
-            lax.fori_loop(0, tiles // unroll, step, 0)
-
+        lax.fori_loop(0, blocks, block, 0)
+        for b in range(blocks):
+            for n in range(count_in, count):
+                copy(n, b).wait()
+
+    anywhere = pl.BlockSpec(memory_space=pl.ANY)
     return pl.pallas_call(
         kernel,
         name=name,
-        grid=(blocks,),
-        in_specs=[spec(a.shape, kind) for a, kind in ins]
-        + [pl.BlockSpec(memory_space=pl.ANY)] * len(into),
-        out_specs=[spec(shape, kind) for shape, _, kind in outs],
+        in_specs=[anywhere] * (count_in + count_into),
+        out_specs=[anywhere] * len(outs),
         out_shape=[jax.ShapeDtypeStruct(shape, dtype) for shape, dtype, _ in outs],
+        scratch_shapes=[
+            *[pltpu.VMEM(kept(*which), dtype) for *which, dtype in zip(shapes, kinds, dtypes)],
+            pltpu.SemaphoreType.DMA((count, blocks)),
+        ],
         input_output_aliases={count_in + n: at for n, at in enumerate(into)},
         compiler_params=pltpu.CompilerParams(vmem_limit_bytes=VMEM_LIMIT),
         cost_estimate=cost(us),
@@ -242,9 +274,9 @@
 
 def edges(mr_query, mr_key, mr_value, li_query, li_key, upstream):
     channels = mr_query.shape[1]
-    width = min(2048, channels)
-
-    def kernel(q_end, k_end, v_end, lq_end, lk_end, lq, lk, g, k, v, last, first, last_kv, a, b):
+    width = channels
+
+    def kernel(q_end, k_end, v_end, lq_end, lk_end, lq, lk, g, k, v, last, first, a, b):
         a[0:4, :] = k_end[...].astype(F32)[12:16]
         a[4:8, :] = v_end[...].astype(F32)[12:16]
         a[8:12, :] = q_end[...].astype(F32)[12:16]
@@ -255,7 +287,6 @@
         b[10:16, :] = jnp.zeros((6, width), F32)
         last[...] = a[...].astype(BF16)
         first[...] = b[...].astype(BF16)
-        last_kv[...] = a[0:8, :].astype(BF16)
 
     low = pl.BlockSpec((16, width), lambda i: (ROWS // 16 - 1, i))
     high = pl.BlockSpec((16, width), lambda i: (0, i))
@@ -265,8 +296,8 @@
         name="edges",
         grid=(channels // width,),
         in_specs=[low] * 5 + [high] * 5,
-        out_specs=[high, high, pl.BlockSpec((8, width), lambda i: (0, i))],
-        out_shape=[small, small, jax.ShapeDtypeStruct((8, channels), BF16)],
+        out_specs=[high, high],
+        out_shape=[small, small],
         scratch_shapes=[pltpu.VMEM((16, width), F32)] * 2,
         compiler_params=pltpu.CompilerParams(vmem_limit_bytes=VMEM_LIMIT),
         cost_estimate=cost(3.5),
@@ -318,24 +349,19 @@
     )(mr_short, li_short, li_skip, mr_filter, li_rate, li_residue)
 
 
-def product_one_body(key, value, prev, following, table, keys_one, value_one, beyond, out):
+def product_one_body(key, value, prev, table, out):
     weights = table[...]
     before, _ = margins_before(prev)
-    after_a, after_b = margins_after(following)
     w_k, w_v = taps(weights, MR_K), taps(weights, MR_V)
     signal_k, signal_v = key[...].astype(F32), value[...].astype(F32)
     yield True
     k = short_forward(signal_k, w_k, turned(before, 4))
     v = short_forward(signal_v, w_v, before)
     yield True
-    keys_one[...] = k.astype(BF16)
-    value_one[...] = v.astype(BF16)
     out[...] = (k * v).astype(BF16)
-    beyond[0:2, :] = short_forward(turned(after_a, 2), w_k, signal_k[ROWS - 8 :])[0:2]
-    beyond[2:4, :] = short_forward(after_b, w_v, signal_v[ROWS - 8 :])[0:2]
-
-
-def upstream_body(li_query, upstream, prev, table, rate, query_two_out, cotangent, state):
+
+
+def upstream_body(li_query, upstream, prev, table, rate, cotangent, state):
     weights = table[...]
     _, margin = margins_before(prev)
     signal, given, decay = li_query[...].astype(F32), upstream[...].astype(F32), rate[...]
@@ -348,7 +374,6 @@
     yield True
     store_state(state, absorbed)
     cotangent[...] = rounded
-    query_two_out[...] = query_two.astype(BF16)
 
 
 def long_back_near_body(cotangent, table, base, near):
@@ -358,7 +383,8 @@
     yield True
     products = jnp.dot(left, right, preferred_element_type=F32)
     yield True
-    near[...] = pick(products, STRIP_BACK, TILE_GROUPS // 2) + skip * signal.astype(F32)
+    product = pick(products, STRIP_BACK, TILE_GROUPS // 2) + skip * signal.astype(F32)
+    near[...] = product.astype(BF16)
 
 
 def long_back_body(
@@ -368,7 +394,7 @@
     weights = table[...]
     _, before = margins_before(prev)
     after, _ = margins_after(following)
-    near, state = near_ref[...], load_state(closing)
+    near, state = near_ref[...].astype(F32), load_state(closing)
     key, queries = li_key[...].astype(F32), query[...].astype(F32)
     query_end = li_query[ROWS - 16 :, :].astype(F32)[8:16]
     distance = (ROWS - iota((ROWS + 16, LANES), 0)).astype(F32)
@@ -400,14 +426,14 @@
 
 def forward_body(
     before, before_kv, signal, query, key, prev, table, base_ref, base_long,
-    rate, conv_one, value_two, near, state, state_sent, head,
+    rate, conv_one, value_two, near, state, head,
 ):
     weights = table[...]
     earlier = before[...]
     pair = jnp.concatenate([earlier, signal[...]], 0)
     queries, keys = query[...].astype(F32), key[...].astype(F32)
     _, margin = margins_before(prev)
-    raw = before_kv[...].astype(F32)
+    raw, _ = margins_before(before_kv)
     base = base_ref[...]
     left, _ = medium_tables(base, False)
     row, lane = iota((16, LANES), 0), iota((16, LANES), 1)
@@ -448,12 +474,10 @@
     absorbed = absorb(powers, rounded)
     yield True
     store_state(state, absorbed)
-    store_state(state_sent, absorbed)
     conv_one[...] = conv.astype(BF16)
     value_two[...] = value.astype(BF16)
-    near[...] = (
-        pick(products, STRIP_FORWARD, TILE_GROUPS // 2) + weights[SKIP : SKIP + 1] * product
-    )
+    own = pick(products, STRIP_FORWARD, TILE_GROUPS // 2) + weights[SKIP : SKIP + 1] * product
+    near[...] = own.astype(BF16)
     head[0:2, :] = product[0:2]
     head[2:4, :] = value[0:2]
     head[4:6, :] = conv[0:2]
@@ -479,22 +503,25 @@
 
 
 def long_body(
-    near_ref, start, end, query_two, upstream, following, next_head, table, rate, residue, base_back,
+    near_ref, start, end, li_query, upstream, prev, following, next_head, table, rate, residue,
+    base_back,
     out, grad_li_query,
 ):
     weights = table[...]
-    near, queries, given = near_ref[...], query_two[...].astype(F32), upstream[...].astype(F32)
+    near, queries, given = (ref[...].astype(F32) for ref in (near_ref, li_query, upstream))
     distance = (iota((ROWS + 16, LANES), 0) + 1).astype(F32)
     emit = (residue[...] * jnp.exp(-rate[...] * distance)).astype(BF16)
     started, ending = spread(load_state(start)), spread(load_state(end))
     head = next_head[...]
     impulse = base_back[...]
     after, _ = margins_after(following)
+    _, margin = margins_before(prev)
     yield True
     emitted = jnp.dot(emit, started, preferred_element_type=F32)
     ended = jnp.dot(emit[0:16], ending, preferred_element_type=F32)
     yield True
     conv = near + emitted[0:ROWS]
+    queries = short_forward(queries, taps(weights, LI_Q), turned(margin, 2))
     at_once = on_channels(impulse, 0) + weights[SKIP : SKIP + 1]
     first, second = head[0:1], head[1:2]
     past = emitted[ROWS : ROWS + 8] + ended[0:8]
@@ -508,14 +535,15 @@
 
 
 def medium_back_body(
-    conv_grad, after, after_next, keys_one, value_one, beyond, table, base_ref,
+    conv_grad, after, after_next, key, value, prev, following, table, base_ref,
     grad_key, grad_value,
 ):
     weights = table[...]
     later = after[...]
     pair = jnp.concatenate([conv_grad[...], later], 0)
-    keys, values = keys_one[...].astype(F32), value_one[...].astype(F32)
-    past_kv = beyond[...]
+    keys, values = key[...].astype(F32), value[...].astype(F32)
+    before, _ = margins_before(prev)
+    next_keys, next_values = margins_after(following)
     base = base_ref[...]
     left, first_half = medium_tables(base, True)
     far = on_channels(base, MR_TAPS - 1) * after_next[...].astype(BF16).astype(F32)
@@ -527,8 +555,13 @@
     grad = pick(products, STRIP_BACK, TILE_GROUPS)
     edge = pick(products_edge, 16, TILE_GROUPS)
     past_first, past_second = edge[0:1], edge[1:2] + far
-    key_past = two_rows(past_first * past_kv[2:3], past_second * past_kv[3:4])
-    value_past = two_rows(past_first * past_kv[0:1], past_second * past_kv[1:2])
+    w_k, w_v = taps(weights, MR_K), taps(weights, MR_V)
+    keys_past = short_forward(turned(next_keys, 2), w_k, keys[ROWS - 8 :])
+    values_past = short_forward(next_values, w_v, values[ROWS - 8 :])
+    keys = short_forward(keys, w_k, turned(before, 4))
+    values = short_forward(values, w_v, before)
+    key_past = two_rows(past_first * values_past[0:1], past_second * values_past[1:2])
+    value_past = two_rows(past_first * keys_past[0:1], past_second * keys_past[1:2])
     key_grad = short_backward(grad * values, taps(weights, MR_K), key_past)
     value_grad = short_backward(grad * keys, taps(weights, MR_V), value_past)
     yield True
@@ -544,13 +577,13 @@
         carried = jnp.zeros((8, LANES), F32)
         for k in range(count):
             b = count - 1 - k if backward else k
-            out_ref[b] = carried.astype(BF16)
-            carried = decay * carried + states_ref[b].astype(F32)
+            out_ref[b] = carried
+            carried = decay * carried + states_ref[b]
 
     return pl.pallas_call(
         kernel,
         name="scan_back" if backward else "scan_forward",
-        out_shape=jax.ShapeDtypeStruct(states.shape, BF16),
+        out_shape=jax.ShapeDtypeStruct(states.shape, F32),
         in_specs=[pl.BlockSpec(memory_space=pltpu.VMEM)] * 2,
         out_specs=pl.BlockSpec(memory_space=pltpu.VMEM),
         cost_estimate=cost(2),
@@ -579,19 +612,18 @@
     tiles = channels // LANES
     assert mr_query.shape[0] == ROWS and lax.axis_size(AXES) == 2 * tiles
     rows = (ROWS, channels)
-    full, full32 = (rows, BF16, "r"), (rows, F32, "r")
+    full = (rows, BF16, "r")
     half = ((ROWS, channels // 2), BF16, "r")
     state_out = ((2 * tiles, 8, LANES), F32, "s")
-    state_sent = ((2 * tiles, 8, LANES), BF16, "s")
     halves = ((0, 2), (1, 2))
 
     def few(n):
         return ((n, channels), F32, "r")
 
-    last_rows, first_rows, last_kv = edges(mr_query, mr_key, mr_value, li_query, li_key, upstream)
+    last_rows, first_rows = edges(mr_query, mr_key, mr_value, li_query, li_key, upstream)
     prev = sent(last_rows, 1)
     following = sent(first_rows, -1)
-    before_kv = sent(last_kv, 2)
+    before_kv = sent(last_rows, 2)
 
     table, medium, medium_turned, long, long_turned = make_tables(
         mr_short, li_short, li_skip[None, :], mr_filter, li_rate, li_residue
@@ -604,96 +636,89 @@
     )
     my_rates = jnp.repeat(my_rates.T, GROUP, axis=1)
 
-    key_in = after(mr_key, before_kv, following)
-    into = {}
-    signal_one = []
-    for n, part in enumerate(halves):
-        got = lane_call(
-            product_one_body, "product_one", channels,
-            [(key_in, "r"), (mr_value, "r"), (prev, "r"), (following, "r"), (table, "r")],
-            [full, full, few(4), half], 4, part, into,
-        )
-        signal_one.append(got[3])
-        into = dict(enumerate(got[:3]))
-    keys_one, value_one, beyond_one = got[:3]
-    before_one = [sent(signal, 1) for signal in signal_one]
-
-    query_two, cotangent, state_back = lane_call(
+    cotangent, state_back = lane_call(
         upstream_body, "upstream", channels,
-        [(after(li_query, *signal_one), "r"), (upstream, "r"), (prev, "r"), (table, "r"),
-         (rate, "r")],
-        [full, full, state_sent], 7,
+        [(li_query, "r"), (upstream, "r"), (prev, "r"), (table, "r"), (rate, "r")],
+        [full, state_out], 5,
     )
     gathered_back = exchanged(state_back)
     (near_back,) = lane_call(
         long_back_near_body, "long_back_near", channels,
         [(cotangent, "r"), (table, "r"), (long_turned, "g")],
-        [full32], 8, unroll=4,
-    )
-
-    def forward(n, into):
-        return lane_call(
-            forward_body, "forward", channels,
-            [(before_one[n], "r"), (before_kv, "r"), (signal_one[n], "r"), (mr_query, "r"),
-             (li_key, "r"), (prev, "r"), (table, "r"), (medium, "g"), (long, "g"), (rate, "r")],
-            [full, full, full32, state_out, state_sent, few(6)],
-            13, halves[n], into, unroll=2,
-        )
-
-    got_forward = forward(0, {})
-    gathered_back = after(gathered_back, near_back, got_forward[0])
-    closing = exchanged(scan_states(gathered_back, my_rates, True))
-    conv_one, value_two, near, state, state_outgoing, head = forward(
-        1, dict(enumerate(got_forward))
-    )
-    next_head = sent(head, -1)
-    gathered = exchanged(state_outgoing)
+        [full], 6,
+    )
+    gathered_back = after(gathered_back, following, before_kv, near_back)
+    carries_back = scan_states(gathered_back, my_rates, True)
+    closing = exchanged(carries_back)
+
+    key_in = after(mr_key, carries_back)
+    signal_one = [
+        lane_call(
+            product_one_body, "product_one", channels,
+            [(key_in, "r"), (mr_value, "r"), (prev, "r"), (table, "r")],
+            [half], 3, part,
+        )[0]
+        for part in halves
+    ]
+    before_one = [sent(signal, 1) for signal in signal_one]
 
     into = {}
     conv_grad = []
-    near_later = after(near_back, conv_one)
     for part in halves:
         got = lane_call(
             long_back_body, "long_back", channels,
-            [(near_later, "r"), (closing, "s"), (li_query, "r"), (li_key, "r"), (mr_query, "r"),
+            [(near_back, "r"), (closing, "s"), (li_query, "r"), (li_key, "r"), (mr_query, "r"),
              (prev, "r"), (following, "r"), (table, "r"), (rate, "r"), (residue, "r")],
             [full, few(2), full, few(2), few(1), half],
-            6, part, into, unroll=4,
+            5, part, into,
         )
         conv_grad.append(got[5])
         into = dict(enumerate(got[:5]))
     grad_two, grad_two_after, mixed_grad, mixed_head, conv_head, _ = got
-    after_one = [sent(after(signal, next_head), -1) for signal in conv_grad]
+    after_one = [sent(signal, -1) for signal in conv_grad]
     after_next = sent(conv_head, -2)
     mixed_after = sent(mixed_head, -1)
 
-    gathered = after(gathered, next_head)
+    into = {}
+    for n, part in enumerate(halves):
+        got = lane_call(
+            forward_body, "forward", channels,
+            [(before_one[n], "r"), (before_kv, "r"), (signal_one[n], "r"), (mr_query, "r"),
+             (li_key, "r"), (prev, "r"), (table, "r"), (medium, "g"), (long, "g"), (rate, "r")],
+            [full, full, full, state_out, few(6)],
+            12, part, into, unroll=2,
+        )
+        into = dict(enumerate(got))
+    conv_one, value_two, near, state, head = got
+    next_head = sent(head, -1)
+    gathered = exchanged(state)
+
+    def medium_back(n, into):
+        return lane_call(
+            medium_back_body, "medium_back", channels,
+            [(conv_grad[n], "r"), (after_one[n], "r"), (after_next, "r"), (mr_key, "r"),
+             (mr_value, "r"), (prev, "r"), (following, "r"), (table, "r"), (medium_turned, "g")],
+            [full, full], 6, halves[n], into,
+        )
+
+    got = medium_back(0, {})
+    gathered = after(gathered, next_head, after_next, *got)
     start = exchanged(scan_states(gathered, my_rates, False))
+    grad_mr_key, grad_mr_value = medium_back(1, dict(enumerate(got)))
     grad_li_key, grad_mr_query = lane_call(
         late_body, "late", channels,
         [(grad_two, "r"), (grad_two_after, "r"), (value_two, "r"), (mixed_grad, "r"),
          (mixed_after, "r"), (conv_one, "r"), (next_head, "r"), (table, "r")],
-        [full, full], 6,
-    )
-
-    def medium_back(n, into):
-        return lane_call(
-            medium_back_body, "medium_back", channels,
-            [(conv_grad[n], "r"), (after_one[n], "r"), (after_next, "r"), (keys_one, "r"),
-             (value_one, "r"), (beyond_one, "r"), (table, "r"), (medium_turned, "g")],
-            [full, full], 7, halves[n], into, unroll=4,
-        )
-
-    got = medium_back(0, {})
-    start = after(start, grad_li_key, *got)
+        [full, full], 5,
+    )
+    start = after(start, grad_li_key, grad_mr_key)
     output, grad_li_query = lane_call(
         long_body, "long_forward", channels,
-        [(near, "r"), (start, "s"), (state, "s"), (query_two, "r"), (upstream, "r"),
-         (following, "r"), (next_head, "r"), (table, "r"), (rate, "r"), (residue, "r"),
+        [(near, "r"), (start, "s"), (state, "s"), (li_query, "r"), (upstream, "r"),
+         (prev, "r"), (following, "r"), (next_head, "r"), (table, "r"), (rate, "r"), (residue, "r"),
          (long_turned, "g")],
-        [full, full], 9, unroll=4,
-    )
-    grad_mr_key, grad_mr_value = medium_back(1, dict(enumerate(got)))
+        [full, full], 7,
+    )
     return (output, grad_mr_query, grad_mr_key, grad_mr_value, grad_li_query, grad_li_key)
 
 

time: 247 us -> 252 us (1.020)
  waiting for transfers between devices: 1.99 us -> 47.7 us
  blocking collectives: 39.3 us -> 0 us
  starting transfers between devices: 76.9 us -> 79.5 us
    all_to_all x1 -> x0, blocking collectives: 39.3 us -> none  [exchanged(): return lax.all_to_all(array, AXES, split_axis=0, concat_axis=0, tiled=True)]
    all_to_all x3 -> x4, waiting for transfers between devices: 0.06 us -> 38.6 us  [exchanged(): return lax.all_to_all(array, AXES, split_axis=0, concat_axis=0, tiled=True)]
    ppermute x10, waiting for transfers between devices: 1.94 us -> 9.11 us  [sent(): return lax.ppermute(array, AXES, pairs)]
    all_to_all x3 -> x4, starting transfers between devices: 34.1 us -> 36.1 us  [exchanged(): return lax.all_to_all(array, AXES, split_axis=0, concat_axis=0, tiled=True)]
    unnamed x38 -> x42, local copies, waits for them, and re-layouts: 8.45 us -> 7.48 us
  transfers between devices with their start and end apart: 13 -> 14, of which waited for: 3 -> 5; matrix products, arithmetic and copies ran while one was open for 2% -> 1% of each run, Pallas kernels for 36% -> 35%
where the time goes in v6:
time: 252 us; the launch traced here: 251 us
  Pallas kernels  113 us (45%)
  starting transfers between devices  79.5 us (32%)
  waiting for transfers between devices  47.7 us (19%)
  local copies, waits for them, and re-layouts  9.83 us (4%)
    pallas_call x12, Pallas kernels, lane_call(): pl.pallas_call(kernel, name=name, in_specs=[anywhere] * (count_in + count...  100 us
    ppermute x10, starting transfers between devices, sent(): return lax.ppermute(array, AXES, pairs)  43.3 us
    all_to_all x4, waiting for transfers between devices, exchanged(): return lax.all_to_all(array, AXES, split_axis=0, concat_axis=0, tiled=True)  38.6 us
    all_to_all x4, starting transfers between devices, exchanged(): return lax.all_to_all(array, AXES, split_axis=0, concat_axis=0, tiled=True)  36.1 us
    ppermute x10, waiting for transfers between devices, sent(): return lax.ppermute(array, AXES, pairs)  9.11 us
    unnamed x42, local copies, waits for them, and re-layouts  7.48 us
    pallas_call x1, Pallas kernels, make_tables(): pl.pallas_call(kernel, name='tables', grid=(groups // block,), in_specs=[...  5.14 us
  transfers between devices with their start and end apart: 14, of which 5 were waited for; matrix products, arithmetic and copies ran while one was open for 1% of the time, Pallas kernels for 35%

profile of v6, /device:TPU:1, one launch (start us, length us, event | category | flops | bytes accessed | tf_op | source)
XLA Modules:
  0.0 250.8 jit_solution(4832343526785969918)
XLA Ops:
  3.3 4.0 %collective-permute-start = (bf16[16,8192]{1,0:T(8,128)(2,1)}, bf16[16,8192]{1,0:T(8,128)(2,1)S(1)}, u32[]{:S(2)}, u32[]{:S(2)}) collective-permute-start(bf16[16,8192]{1,0:T(8,128)(2,1)} %get-tuple-element.49), channel_id=1, source_target_pairs={{0,1},{1,2},{2,3},{3,4},{4,5},{5,6},{6,7},{7,8},{8,9},{9,10},{10,1... | collective-permute-start | bytes 786440 | tf_op jit(solution)/shard_map/ppermute | solution.py:596
  9.1 5.1 %tables.1 = (f32[24,8192]{1,0:T(8,128)}, f32[512,128]{1,0:T(8,128)}, f32[512,128]{1,0:T(8,128)}, f32[512,128]{1,0:T(8,128)}, f32[512,128]{1,0:T(8,128)}) custom-call(bf16[3,3,8192]{2,1,0:T(4,128)(2,1)} %mr.1, bf16[3,3,8192]{2,1,0:T(4,128)(2,1)} %li.1, f32[1,8192]{1,0:T(1,128)} %bitcast.3, bf16[128,512]{1,0:T(8,128)(2,1)} %filters.1, f32[512,16]{1,0:T(8,128)} %copy-done.4, ...), custom_call_target="tpu_custom_call" | custom-call | bytes 18000000 | tf_op jit(solution)/shard_map/tables/pallas_call | solution.py:337
  17.8 7.3 %upstream.1 = (bf16[128,8192]{1,0:T(8,128)(2,1)}, f32[128,8,128]{2,1,0:T(8,128)}) custom-call(bf16[128,8192]{1,0:T(8,128)(2,1)} %refs_3_.13, bf16[128,8192]{1,0:T(8,128)(2,1)} %refs_4_.13, bf16[16,8192]{1,0:T(8,128)(2,1)} %copy-done, f32[24,8192]{1,0:T(8,128)} %get-tuple-element.50.refs_3_.refs_1_.refs_6_.refs_7_.refs_8_, ...), custom_call_target="tpu_custom_call" | custom-call | bytes 18000000 | tf_op jit(solution)/shard_map/upstream/pallas_call | solution.py:110
  25.1 7.9 %all-to-all-start = ((f32[128,8,128]{2,1,0:T(8,128)}), f32[128,8,128]{2,1,0:T(8,128)S(1)}, u32[]{:S(2)}, u32[]{:S(2)}) async-start(f32[128,8,128]{2,1,0:T(8,128)} %get-tuple-element.51), calls=%async_computation | async-start | bytes 1048576 | tf_op jit(solution)/shard_map/all_to_all | solution.py:600
  33.0 7.7 %collective-permute-start.1 = (bf16[16,8192]{1,0:T(8,128)(2,1)S(1)}, bf16[16,8192]{1,0:T(8,128)(2,1)S(1)}, u32[]{:S(2)}, u32[]{:S(2)}) collective-permute-start(bf16[16,8192]{1,0:T(8,128)(2,1)S(1)} %copy-done.19), channel_id=1, source_target_pairs={{1,0},{2,1},{3,2},{4,3},{5,4},{6,5},{7,6},{8,7},{9,8},{10,9},{11,1... | collective-permute-start | bytes 786440 | tf_op jit(solution)/shard_map/ppermute | solution.py:596
  43.6 8.0 %long_back_near.1.refs_0_ = bf16[128,8192]{1,0:T(8,128)(2,1)} custom-call(bf16[128,8192]{1,0:T(8,128)(2,1)} %get-tuple-element.53.refs_0_, f32[24,8192]{1,0:T(8,128)} %get-tuple-element.50.refs_3_.refs_1_.refs_6_.refs_7_.refs_8_, f32[512,128]{1,0:T(8,128)} %get-tuple-element.54.refs_2_.refs_11_), custom_call_target="tpu_custom_call" | custom-call | bytes 21600000 | tf_op jit(solution)/shard_map/long_back_near/pallas_call | solution.py:110
  55.8 3.9 %product_one.3.refs_2_ = bf16[128,4096]{1,0:T(8,128)(2,1)} custom-call(bf16[128,8192]{1,0:T(8,128)(2,1)} %refs_3_.12, bf16[128,8192]{1,0:T(8,128)(2,1)} %refs_4_.12, bf16[16,8192]{1,0:T(8,128)(2,1)} %copy-done, f32[24,8192]{1,0:T(8,128)} %get-tuple-element.50.refs_3_.refs_1_.refs_6_.refs_7_.refs_8_), custom_call_target="tpu_custom_call" | custom-call | bytes 10800000 | tf_op jit(solution)/shard_map/product_one/pallas_call | solution.py:110
  63.1 4.0 %product_one.2.refs_2_ = bf16[128,4096]{1,0:T(8,128)(2,1)} custom-call(bf16[128,8192]{1,0:T(8,128)(2,1)} %refs_3_.12, bf16[128,8192]{1,0:T(8,128)(2,1)} %refs_4_.12, bf16[16,8192]{1,0:T(8,128)(2,1)} %copy-done, f32[24,8192]{1,0:T(8,128)} %get-tuple-element.50.refs_3_.refs_1_.refs_6_.refs_7_.refs_8_), custom_call_target="tpu_custom_call" | custom-call | bytes 10800000 | tf_op jit(solution)/shard_map/product_one/pallas_call | solution.py:110
  69.0 11.0 %all-to-all-start.2 = ((f32[128,8,128]{2,1,0:T(8,128)}), f32[128,8,128]{2,1,0:T(8,128)S(1)}, u32[]{:S(2)}, u32[]{:S(2)}) async-start(f32[128,8,128]{2,1,0:T(8,128)} %scan_back.1), calls=%async_computation.2 | async-start | bytes 1048576 | tf_op jit(solution)/shard_map/all_to_all | solution.py:600
  80.7 38.5 %all-to-all-done.2.refs_1_ = f32[128,8,128]{2,1,0:T(8,128)S(1)} async-done(((f32[128,8,128]{2,1,0:T(8,128)}), f32[128,8,128]{2,1,0:T(8,128)S(1)}, u32[]{:S(2)}, u32[]{:S(2)}) %all-to-all-start.2) | async-done | bytes 524320 | tf_op jit(solution)/shard_map/all_to_all | solution.py:600
  120.1 6.8 %long_back.2 = (bf16[128,8192]{1,0:T(8,128)(2,1)}, f32[2,8192]{1,0:T(2,128)}, bf16[128,8192]{1,0:T(8,128)(2,1)}, f32[2,8192]{1,0:T(2,128)}, f32[1,8192]{1,0:T(1,128)}, /*index=5*/bf16[128,4096]{1,0:T(8,128)(2,1)}) custom-call(bf16[128,8192]{1,0:T(8,128)(2,1)} %long_back_near.1.refs_0_, f32[128,8,128]{2,1,0:T(8,128)} %copy-done.2, ...), custom_call_target="tpu_custom_call" | custom-call | bytes 18000000 | tf_op jit(solution)/shard_map/long_back/pallas_call | solution.py:110
  129.7 6.9 %long_back.3 = (bf16[128,8192]{1,0:T(8,128)(2,1)}, f32[2,8192]{1,0:T(2,128)}, bf16[128,8192]{1,0:T(8,128)(2,1)}, f32[2,8192]{1,0:T(2,128)}, f32[1,8192]{1,0:T(1,128)}, /*index=5*/bf16[128,4096]{1,0:T(8,128)(2,1)}) custom-call(bf16[128,8192]{1,0:T(8,128)(2,1)} %long_back_near.1.refs_0_,, ...), custom_call_target="tpu_custom_call", output_to_operand_aliasing={{0}: (10, {}), {1}: (11, {}), {2}: (12, {}), {3}: (13, {}),... | custom-call | bytes 18000000 | tf_op jit(solution)/shard_map/long_back/pallas_call | solution.py:110
  136.6 3.4 %collective-permute-start.9 = (bf16[128,4096]{1,0:T(8,128)(2,1)}, bf16[128,4096]{1,0:T(8,128)(2,1)S(1)}, u32[]{:S(2)}, u32[]{:S(2)}) collective-permute-start(bf16[128,4096]{1,0:T(8,128)(2,1)} %get-tuple-element.85.refs_0_), channel_id=1, source_target_pairs={{1,0},{2,1},{3,2},{4,3},{5,4},{6,5},{7,6},{8,7},{9,8},{10,9},{11,1... | collective-permute-start | bytes 3145736 | tf_op jit(solution)/shard_map/ppermute | solution.py:596
  140.1 13.6 %forward.2 = (bf16[128,8192]{1,0:T(8,128)(2,1)}, bf16[128,8192]{1,0:T(8,128)(2,1)}, bf16[128,8192]{1,0:T(8,128)(2,1)}, f32[128,8,128]{2,1,0:T(8,128)}, f32[6,8192]{1,0:T(8,128)}) custom-call(bf16[128,4096]{1,0:T(8,128)(2,1)} %collective-permute-done.4.refs_0_, bf16[16,8192]{1,0:T(8,128)(2,1)} %copy-done.11, bf16[128,4096]{1,0:T(8,128)(2,1)} %product_one.3.refs_2_, ...), custom_call_target="tpu_custom_call" | custom-call | bytes 43200000 | tf_op jit(solution)/shard_map/forward/pallas_call | solution.py:110
  153.7 13.6 %forward.3 = (bf16[128,8192]{1,0:T(8,128)(2,1)}, bf16[128,8192]{1,0:T(8,128)(2,1)}, bf16[128,8192]{1,0:T(8,128)(2,1)}, f32[128,8,128]{2,1,0:T(8,128)}, f32[6,8192]{1,0:T(8,128)}) custom-call(bf16[128,4096]{1,0:T(8,128)(2,1)} %collective-permute-done.3.refs_0_, ...), custom_call_target="tpu_custom_call", output_to_operand_aliasing={{0}: (10, {}), {1}: (11, {}), {2}: (12, {}), {3}: (13, {}),... | custom-call | bytes 43200000 | tf_op jit(solution)/shard_map/forward/pallas_call | solution.py:110
  167.3 7.5 %all-to-all-start.1 = ((f32[128,8,128]{2,1,0:T(8,128)}), f32[128,8,128]{2,1,0:T(8,128)S(1)}, u32[]{:S(2)}, u32[]{:S(2)}) async-start(f32[128,8,128]{2,1,0:T(8,128)} %get-tuple-element.65.refs_2_), calls=%async_computation.1 | async-start | bytes 1048576 | tf_op jit(solution)/shard_map/all_to_all | solution.py:600
  174.8 7.7 %collective-permute-start.5 = (f32[6,8192]{1,0:T(8,128)}, f32[6,8192]{1,0:T(8,128)S(1)}, u32[]{:S(2)}, u32[]{:S(2)}) collective-permute-start(f32[6,8192]{1,0:T(8,128)} %get-tuple-element.66), channel_id=1, source_target_pairs={{1,0},{2,1},{3,2},{4,3},{5,4},{6,5},{7,6},{8,7},{9,8},{10,9},{11,1... | collective-permute-start | bytes 589832 | tf_op jit(solution)/shard_map/ppermute | solution.py:596
  185.2 3.8 %collective-permute-done.6.refs_2_ = f32[1,8192]{1,0:T(1,128)S(1)} collective-permute-done((f32[1,8192]{1,0:T(1,128)S(1)}, f32[1,8192]{1,0:T(1,128)S(1)}, u32[]{:S(2)}, u32[]{:S(2)}) %collective-permute-start.6) | collective-permute-done | bytes 32800 | tf_op jit(solution)/shard_map/ppermute | solution.py:596
  190.0 9.4 %medium_back.2 = (bf16[128,8192]{1,0:T(8,128)(2,1)}, bf16[128,8192]{1,0:T(8,128)(2,1)}) custom-call(bf16[128,4096]{1,0:T(8,128)(2,1)} %get-tuple-element.73.refs_0_, bf16[128,4096]{1,0:T(8,128)(2,1)} %copy-done.9, f32[1,8192]{1,0:T(1,128)} %copy-done.12, bf16[128,8192]{1,0:T(8,128)(2,1)} %refs_3_.12, bf16[128,8192]{1,0:T(8,128)(2,1)} %refs_4_.12, ...), custom_call_target="tpu_custom_call" | custom-call | bytes 21600000 | tf_op jit(solution)/shard_map/medium_back/pallas_call | solution.py:110
  202.4 9.8 %all-to-all-start.3 = ((f32[128,8,128]{2,1,0:T(8,128)}), f32[128,8,128]{2,1,0:T(8,128)S(1)}, u32[]{:S(2)}, u32[]{:S(2)}) async-start(f32[128,8,128]{2,1,0:T(8,128)} %scan_forward.1), calls=%async_computation.3 | async-start | bytes 1048576 | tf_op jit(solution)/shard_map/all_to_all | solution.py:600
  212.2 7.9 %collective-permute-start.8 = (f32[2,8192]{1,0:T(2,128)S(1)}, f32[2,8192]{1,0:T(2,128)S(1)}, u32[]{:S(2)}, u32[]{:S(2)}) collective-permute-start(f32[2,8192]{1,0:T(2,128)S(1)} %copy-done.13), channel_id=1, source_target_pairs={{1,0},{2,1},{3,2},{4,3},{5,4},{6,5},{7,6},{8,7},{9,8},{10,9},{11,1... | collective-permute-start | bytes 196616 | tf_op jit(solution)/shard_map/ppermute | solution.py:596
  221.9 8.0 %late.1 = (bf16[128,8192]{1,0:T(8,128)(2,1)}, bf16[128,8192]{1,0:T(8,128)(2,1)}) custom-call(bf16[128,8192]{1,0:T(8,128)(2,1)} %get-tuple-element.78.refs_0_, f32[2,8192]{1,0:T(2,128)} %get-tuple-element.79.refs_1_, bf16[128,8192]{1,0:T(8,128)(2,1)} %get-tuple-element.80.refs_2_, bf16[128,8192]{1,0:T(8,128)(2,1)} %get-tuple-element.81.refs_3_, ...), custom_call_target="tpu_custom_call" | custom-call | bytes 18000000 | tf_op jit(solution)/shard_map/late/pallas_call | solution.py:110
  230.9 9.4 %medium_back.3 = (bf16[128,8192]{1,0:T(8,128)(2,1)}, bf16[128,8192]{1,0:T(8,128)(2,1)}) custom-call(bf16[128,4096]{1,0:T(8,128)(2,1)} %get-tuple-element.85.refs_0_, bf16[128,4096]{1,0:T(8,128)(2,1)} %copy-done.8, f32[1,8192]{1,0:T(1,128)} %copy-done.12, bf16[128,8192]{1,0:T(8,128)(2,1)} %refs_3_.12, ...), custom_call_target="tpu_custom_call", output_to_operand_aliasing={{0}: (9, {}), {1}: (10, {})} | custom-call | bytes 21600000 | tf_op jit(solution)/shard_map/medium_back/pallas_call | solution.py:110
  241.2 9.5 %long_forward.1 = (bf16[128,8192]{1,0:T(8,128)(2,1)}, bf16[128,8192]{1,0:T(8,128)(2,1)}) custom-call(bf16[128,8192]{1,0:T(8,128)(2,1)} %get-tuple-element.64.refs_0_, f32[128,8,128]{2,1,0:T(8,128)} %copy-done.5, f32[128,8,128]{2,1,0:T(8,128)} %get-tuple-element.65.refs_2_, bf16[128,8192]{1,0:T(8,128)(2,1)} %refs_3_.13, bf16[128,8192]{1,0:T(8,128)(2,1)} %refs_4_.13, ...), custom_call_target="tpu_custom_call" | custom-call | bytes 25200000 | tf_op jit(solution)/shard_map/long_forward/pallas_call | solution.py:110
  (67 shorter events, 34.7 us)
Async XLA Ops:
  0.6 6.7 %copy-start.17 = (f32[512,16]{0,1:T(8,128)S(1)}, f32[512,16]{0,1:T(8,128)}, u32[]{:S(2)}) copy-start(f32[512,16]{0,1:T(8,128)} %param.22) | copy-start | bytes 98308
  0.6 7.6 %copy-start.15 = (f32[512,16]{0,1:T(8,128)S(1)}, f32[512,16]{0,1:T(8,128)}, u32[]{:S(2)}) copy-start(f32[512,16]{0,1:T(8,128)} %param.21) | copy-start | bytes 98308
  3.3 13.8 %collective-permute-start = (bf16[16,8192]{1,0:T(8,128)(2,1)}, bf16[16,8192]{1,0:T(8,128)(2,1)S(1)}, u32[]{:S(2)}, u32[]{:S(2)}) collective-permute-start(bf16[16,8192]{1,0:T(8,128)(2,1)} %get-tuple-element.49), channel_id=1, source_target_pairs={{0,1},{1,2},{2,3},{3,4},{4,5},{5,6},{6,7},{7,8},{8,9},{9,10},{10,1... | collective-permute-start | bytes 786440 | tf_op jit(solution)/shard_map/ppermute | solution.py:596
  17.8 15.2 %copy-start.19 = (bf16[16,8192]{1,0:T(8,128)(2,1)S(1)}, bf16[16,8192]{1,0:T(8,128)(2,1)}, u32[]{:S(2)}) copy-start(bf16[16,8192]{1,0:T(8,128)(2,1)} %get-tuple-element.52) | copy-start | bytes 786436
  17.8 23.0 %copy-start.18 = (bf16[16,8192]{1,0:T(8,128)(2,1)S(1)}, bf16[16,8192]{1,0:T(8,128)(2,1)}, u32[]{:S(2)}) copy-start(bf16[16,8192]{1,0:T(8,128)(2,1)} %get-tuple-element.49) | copy-start | bytes 786436
  25.1 27.7 %all-to-all-start = ((f32[128,8,128]{2,1,0:T(8,128)}), f32[128,8,128]{2,1,0:T(8,128)S(1)}, u32[]{:S(2)}, u32[]{:S(2)}) async-start(f32[128,8,128]{2,1,0:T(8,128)} %get-tuple-element.51), calls=%async_computation | async-start | bytes 1048576 | tf_op jit(solution)/shard_map/all_to_all | solution.py:600
  33.0 19.8 %collective-permute-start.1 = (bf16[16,8192]{1,0:T(8,128)(2,1)S(1)}, bf16[16,8192]{1,0:T(8,128)(2,1)S(1)}, u32[]{:S(2)}, u32[]{:S(2)}) collective-permute-start(bf16[16,8192]{1,0:T(8,128)(2,1)S(1)} %copy-done.19), channel_id=1, source_target_pairs={{1,0},{2,1},{3,2},{4,3},{5,4},{6,5},{7,6},{8,7},{9,8},{10,9},{11,1... | collective-permute-start | bytes 786440 | tf_op jit(solution)/shard_map/ppermute | solution.py:596
  40.8 12.1 %collective-permute-start.2 = (bf16[16,8192]{1,0:T(8,128)(2,1)S(1)}, bf16[16,8192]{1,0:T(8,128)(2,1)S(1)}, u32[]{:S(2)}, u32[]{:S(2)}) collective-permute-start(bf16[16,8192]{1,0:T(8,128)(2,1)S(1)} %copy-done.18), channel_id=1, source_target_pairs={{0,2},{1,3},{2,4},{3,5},{4,6},{5,7},{6,8},{7,9},{8,10},{9,11},{10,... | collective-permute-start | bytes 786440 | tf_op jit(solution)/shard_map/ppermute | solution.py:596
  52.8 6.9 %copy-start.1 = (bf16[16,8192]{1,0:T(8,128)(2,1)}, bf16[16,8192]{1,0:T(8,128)(2,1)S(1)}, u32[]{:S(2)}) copy-start(bf16[16,8192]{1,0:T(8,128)(2,1)S(1)} %collective-permute-done.1.refs_6_) | copy-start | bytes 786436
  52.9 14.2 %copy-start.11 = (bf16[16,8192]{1,0:T(8,128)(2,1)}, bf16[16,8192]{1,0:T(8,128)(2,1)S(1)}, u32[]{:S(2)}) copy-start(bf16[16,8192]{1,0:T(8,128)(2,1)S(1)} %collective-permute-done.2.refs_1_) | copy-start | bytes 786436
  59.8 20.2 %copy-start.3 = (f32[512,16]{1,0:T(8,128)S(1)}, f32[512,16]{1,0:T(8,128)}, u32[]{:S(2)}) copy-start(f32[512,16]{1,0:T(8,128)} %copy.35.residue) | copy-start | bytes 98308
  59.8 80.3 %collective-permute-start.4 = (bf16[128,4096]{1,0:T(8,128)(2,1)}, bf16[128,4096]{1,0:T(8,128)(2,1)}, u32[]{:S(2)}, u32[]{:S(2)}) collective-permute-start(bf16[128,4096]{1,0:T(8,128)(2,1)} %product_one.3.refs_2_), channel_id=1, source_target_pairs={{0,1},{1,2},{2,3},{3,4},{4,5},{5,6},{6,7},{7,8},{8,9},{9,10},{10,1... | collective-permute-start | bytes 3145736 | tf_op jit(solution)/shard_map/ppermute | solution.py:596
  67.0 86.6 %collective-permute-start.3 = (bf16[128,4096]{1,0:T(8,128)(2,1)}, bf16[128,4096]{1,0:T(8,128)(2,1)}, u32[]{:S(2)}, u32[]{:S(2)}) collective-permute-start(bf16[128,4096]{1,0:T(8,128)(2,1)} %product_one.2.refs_2_), channel_id=1, source_target_pairs={{0,1},{1,2},{2,3},{3,4},{4,5},{5,6},{6,7},{7,8},{8,9},{9,10},{10,1... | collective-permute-start | bytes 3145736 | tf_op jit(solution)/shard_map/ppermute | solution.py:596
  69.0 50.3 %all-to-all-start.2 = ((f32[128,8,128]{2,1,0:T(8,128)}), f32[128,8,128]{2,1,0:T(8,128)S(1)}, u32[]{:S(2)}, u32[]{:S(2)}) async-start(f32[128,8,128]{2,1,0:T(8,128)} %scan_back.1), calls=%async_computation.2 | async-start | bytes 1048576 | tf_op jit(solution)/shard_map/all_to_all | solution.py:600
  126.9 62.1 %collective-permute-start.7 = (bf16[128,4096]{1,0:T(8,128)(2,1)}, bf16[128,4096]{1,0:T(8,128)(2,1)S(1)}, u32[]{:S(2)}, u32[]{:S(2)}) collective-permute-start(bf16[128,4096]{1,0:T(8,128)(2,1)} %get-tuple-element.73.refs_0_), channel_id=1, source_target_pairs={{1,0},{2,1},{3,2},{4,3},{5,4},{6,5},{7,6},{8,7},{9,8},{10,9},{11,1... | collective-permute-start | bytes 3145736 | tf_op jit(solution)/shard_map/ppermute | solution.py:596
  136.6 93.3 %collective-permute-start.9 = (bf16[128,4096]{1,0:T(8,128)(2,1)}, bf16[128,4096]{1,0:T(8,128)(2,1)S(1)}, u32[]{:S(2)}, u32[]{:S(2)}) collective-permute-start(bf16[128,4096]{1,0:T(8,128)(2,1)} %get-tuple-element.85.refs_0_), channel_id=1, source_target_pairs={{1,0},{2,1},{3,2},{4,3},{5,4},{6,5},{7,6},{8,7},{9,8},{10,9},{11,1... | collective-permute-start | bytes 3145736 | tf_op jit(solution)/shard_map/ppermute | solution.py:596
  153.6 28.9 %copy-start.16 = (f32[1,8192]{1,0:T(1,128)S(1)}, f32[1,8192]{1,0:T(1,128)}, u32[]{:S(2)}) copy-start(f32[1,8192]{1,0:T(1,128)} %get-tuple-element.72) | copy-start | bytes 98308
  167.3 32.1 %all-to-all-start.1 = ((f32[128,8,128]{2,1,0:T(8,128)}), f32[128,8,128]{2,1,0:T(8,128)S(1)}, u32[]{:S(2)}, u32[]{:S(2)}) async-start(f32[128,8,128]{2,1,0:T(8,128)} %get-tuple-element.65.refs_2_), calls=%async_computation.1 | async-start | bytes 1048576 | tf_op jit(solution)/shard_map/all_to_all | solution.py:600
  174.8 24.6 %collective-permute-start.5 = (f32[6,8192]{1,0:T(8,128)}, f32[6,8192]{1,0:T(8,128)S(1)}, u32[]{:S(2)}, u32[]{:S(2)}) collective-permute-start(f32[6,8192]{1,0:T(8,128)} %get-tuple-element.66), channel_id=1, source_target_pairs={{1,0},{2,1},{3,2},{4,3},{5,4},{6,5},{7,6},{8,7},{9,8},{10,9},{11,1... | collective-permute-start | bytes 589832 | tf_op jit(solution)/shard_map/ppermute | solution.py:596
  182.5 6.5 %collective-permute-start.6 = (f32[1,8192]{1,0:T(1,128)S(1)}, f32[1,8192]{1,0:T(1,128)S(1)}, u32[]{:S(2)}, u32[]{:S(2)}) collective-permute-start(f32[1,8192]{1,0:T(1,128)S(1)} %copy-done.16), channel_id=1, source_target_pairs={{2,0},{3,1},{4,2},{5,3},{6,4},{7,5},{8,6},{9,7},{10,8},{11,9},{12,... | collective-permute-start | bytes 98312 | tf_op jit(solution)/shard_map/ppermute | solution.py:596
  199.4 12.8 %copy-start.13 = (f32[2,8192]{1,0:T(2,128)S(1)}, f32[2,8192]{1,0:T(2,128)}, u32[]{:S(2)}) copy-start(f32[2,8192]{1,0:T(2,128)} %get-tuple-element.82) | copy-start | bytes 196612
  199.4 21.9 %copy-start.10 = (f32[6,8192]{1,0:T(8,128)}, f32[6,8192]{1,0:T(8,128)S(1)}, u32[]{:S(2)}) copy-start(f32[6,8192]{1,0:T(8,128)S(1)} %collective-permute-done.5.refs_6_.refs_7_) | copy-start | bytes 589828
  202.4 38.0 %all-to-all-start.3 = ((f32[128,8,128]{2,1,0:T(8,128)}), f32[128,8,128]{2,1,0:T(8,128)S(1)}, u32[]{:S(2)}, u32[]{:S(2)}) async-start(f32[128,8,128]{2,1,0:T(8,128)} %scan_forward.1), calls=%async_computation.3 | async-start | bytes 1048576 | tf_op jit(solution)/shard_map/all_to_all | solution.py:600
  212.2 9.1 %collective-permute-start.8 = (f32[2,8192]{1,0:T(2,128)S(1)}, f32[2,8192]{1,0:T(2,128)S(1)}, u32[]{:S(2)}, u32[]{:S(2)}) collective-permute-start(f32[2,8192]{1,0:T(2,128)S(1)} %copy-done.13), channel_id=1, source_target_pairs={{1,0},{2,1},{3,2},{4,3},{5,4},{6,5},{7,6},{8,7},{9,8},{10,9},{11,1... | collective-permute-start | bytes 196616 | tf_op jit(solution)/shard_map/ppermute | solution.py:596
  (10 other events, 7.9 us)

commit v7 on v6

--- a/solution.py
+++ b/solution.py
@@ -12,7 +12,7 @@
 ROWS = 128
 LANES = 128
 STRIP_FORWARD = 32
-STRIP_BACK = 64
+STRIP_BACK = 32
 TILE_GROUPS = LANES // GROUP
 AXES = ("ctx", "ch")
 BF16 = jnp.bfloat16
@@ -33,7 +33,7 @@
     return start if isinstance(start, int) else pl.multiple_of(start, of)
 
 
-def lane_call(body, name, channels, ins, outs, us, part=(0, 1), into=None, width=1024, unroll=4):
+def lane_call(body, name, channels, ins, outs, us, part=(0, 1), into=None, width=1024, unroll=4, exts=0):
     span = channels // part[1]
     width = min(width, span)
     tiles = width // LANES
@@ -67,8 +67,8 @@
 
     def kernel(*refs):
         far = refs[:count_in] + refs[count_in + count_into : count + count_into]
-        held = refs[count + count_into : -1]
-        arrived = refs[-1]
+        held = refs[count + count_into : 2 * count + count_into]
+        arrived, *extra = refs[2 * count + count_into :]
 
         def copy(n, b):
             outside = cut(far[n], kinds[n], first[n] + b * width, width)
@@ -90,7 +90,10 @@
                 for u in range(unroll):
                     start = b * width + (k * unroll + u) * LANES
                     running.append(
-                        body(*[cut(ref, kind, start, LANES) for ref, kind in zip(held, kinds)])
+                        body(
+                            *[cut(ref, kind, start, LANES) for ref, kind in zip(held, kinds)],
+                            *[ref.at[u, n] for ref in extra for n in range(exts)],
+                        )
                     )
                 while running:
                     running = [tile for tile in running if next(tile, False)]
@@ -116,6 +119,7 @@
         scratch_shapes=[
             *[pltpu.VMEM(kept(*which), dtype) for *which, dtype in zip(shapes, kinds, dtypes)],
             pltpu.SemaphoreType.DMA((count, blocks)),
+            *([pltpu.VMEM((unroll, exts, ROWS + 16, LANES), F32)] if exts else []),
         ],
         input_output_aliases={count_in + n: at for n, at in enumerate(into)},
         compiler_params=pltpu.CompilerParams(vmem_limit_bytes=VMEM_LIMIT),
@@ -151,6 +155,19 @@
         bottom = jnp.where(last >= 8 - by, turned(next8, 8 - by), moved[rows - 8 :])
         total += weights[by] * jnp.concatenate([moved[: rows - 8], bottom], 0)
     return total
+
+
+def filled(ext, signal, prev8=None, next8=None):
+    ext[8 : 8 + ROWS, :] = signal
+    if prev8 is not None:
+        ext[0:8, :] = prev8
+    if next8 is not None:
+        ext[8 + ROWS :, :] = next8
+
+
+def shifted_sum(ext, weights, way, rows=ROWS):
+    parts = [w * ext[8 + way * j : 8 + way * j + rows, :] for j, w in enumerate(weights)]
+    return parts[0] + parts[1] + parts[2]
 
 
 def two_rows(first, second):
@@ -358,7 +375,10 @@
     k = short_forward(signal_k, w_k, turned(before, 4))
     v = short_forward(signal_v, w_v, before)
     yield True
-    out[...] = (k * v).astype(BF16)
+    out[0:ROWS, :] = (k * v).astype(BF16)
+    key_last = w_k[0] * before[3:4] + w_k[1] * before[2:3] + w_k[2] * before[1:2]
+    value_last = w_v[0] * before[7:8] + w_v[1] * before[6:7] + w_v[2] * before[5:6]
+    out[ROWS:, :] = jnp.broadcast_to(key_last * value_last, (16, LANES)).astype(BF16)
 
 
 def upstream_body(li_query, upstream, prev, table, rate, cotangent, state):
@@ -425,15 +445,15 @@
 
 
 def forward_body(
-    before, before_kv, signal, query, key, prev, table, base_ref, base_long,
+    before, signal, query, key, prev, table, base_ref, base_long,
     rate, conv_one, value_two, near, state, head,
 ):
     weights = table[...]
-    earlier = before[...]
-    pair = jnp.concatenate([earlier, signal[...]], 0)
+    earlier = before[0:ROWS, :]
+    pair = jnp.concatenate([earlier, signal[0:ROWS, :]], 0)
+    before_last = before[ROWS:, :].astype(F32)[0:1]
     queries, keys = query[...].astype(F32), key[...].astype(F32)
     _, margin = margins_before(prev)
-    raw, _ = margins_before(before_kv)
     base = base_ref[...]
     left, _ = medium_tables(base, False)
     row, lane = iota((16, LANES), 0), iota((16, LANES), 1)
@@ -454,10 +474,7 @@
     keys_two = short_forward(keys, taps(weights, LI_K), margin)
     conv = pick(products, STRIP_FORWARD, TILE_GROUPS)
     edge = pick(products_edge, 16, TILE_GROUPS)
-    w_k, w_v = taps(weights, MR_K), taps(weights, MR_V)
-    key_last = w_k[0] * raw[3:4] + w_k[1] * raw[2:3] + w_k[2] * raw[1:2]
-    value_last = w_v[0] * raw[7:8] + w_v[1] * raw[6:7] + w_v[2] * raw[5:6]
-    far = on_channels(base, 1) * (key_last * value_last).astype(BF16).astype(F32)
+    far = on_channels(base, 1) * before_last
     conv_before = edge[8:16] + jnp.where(iota((8, LANES), 0) == 6, far, 0.0)
     w = taps(weights, MR_Q)
     query_before = w[0] * margin + w[1] * turned(margin, 1) + w[2] * turned(margin, 2)
@@ -536,7 +553,7 @@
 
 def medium_back_body(
     conv_grad, after, after_next, key, value, prev, following, table, base_ref,
-    grad_key, grad_value,
+    grad_key, grad_value, ext_k, ext_v, ext_gk, ext_gv,
 ):
     weights = table[...]
     later = after[...]
@@ -547,26 +564,23 @@
     base = base_ref[...]
     left, first_half = medium_tables(base, True)
     far = on_channels(base, MR_TAPS - 1) * after_next[...].astype(BF16).astype(F32)
+    filled(ext_k, keys, turned(before, 4), turned(next_keys, 2))
+    filled(ext_v, values, before, next_values)
     yield True
     products = jnp.dot(left, windows(pair, STRIP_BACK, 0, 2 * LANES), preferred_element_type=F32)
     left_edge = jnp.concatenate([part[0:16] for part in first_half], 0)
     products_edge = jnp.dot(left_edge, later, preferred_element_type=F32)
+    keys = shifted_sum(ext_k, taps(weights, MR_K), -1, ROWS + 8)
+    values = shifted_sum(ext_v, taps(weights, MR_V), -1, ROWS + 8)
     yield True
     grad = pick(products, STRIP_BACK, TILE_GROUPS)
     edge = pick(products_edge, 16, TILE_GROUPS)
-    past_first, past_second = edge[0:1], edge[1:2] + far
-    w_k, w_v = taps(weights, MR_K), taps(weights, MR_V)
-    keys_past = short_forward(turned(next_keys, 2), w_k, keys[ROWS - 8 :])
-    values_past = short_forward(next_values, w_v, values[ROWS - 8 :])
-    keys = short_forward(keys, w_k, turned(before, 4))
-    values = short_forward(values, w_v, before)
-    key_past = two_rows(past_first * values_past[0:1], past_second * values_past[1:2])
-    value_past = two_rows(past_first * keys_past[0:1], past_second * keys_past[1:2])
-    key_grad = short_backward(grad * values, taps(weights, MR_K), key_past)
-    value_grad = short_backward(grad * keys, taps(weights, MR_V), value_past)
-    yield True
-    grad_key[...] = key_grad.astype(BF16)
-    grad_value[...] = value_grad.astype(BF16)
+    past = two_rows(edge[0:1], edge[1:2] + far)
+    filled(ext_gk, grad * values[0:ROWS], None, past * values[ROWS:])
+    filled(ext_gv, grad * keys[0:ROWS], None, past * keys[ROWS:])
+    yield True
+    grad_key[...] = shifted_sum(ext_gk, taps(weights, MR_K), 1).astype(BF16)
+    grad_value[...] = shifted_sum(ext_gv, taps(weights, MR_V), 1).astype(BF16)
 
 
 def scan_states(states, rates, backward):
@@ -614,6 +628,7 @@
     rows = (ROWS, channels)
     full = (rows, BF16, "r")
     half = ((ROWS, channels // 2), BF16, "r")
+    halo = ((ROWS + 16, channels // 2), BF16, "r")
     state_out = ((2 * tiles, 8, LANES), F32, "s")
     halves = ((0, 2), (1, 2))
 
@@ -623,7 +638,6 @@
     last_rows, first_rows = edges(mr_query, mr_key, mr_value, li_query, li_key, upstream)
     prev = sent(last_rows, 1)
     following = sent(first_rows, -1)
-    before_kv = sent(last_rows, 2)
 
     table, medium, medium_turned, long, long_turned = make_tables(
         mr_short, li_short, li_skip[None, :], mr_filter, li_rate, li_residue
@@ -636,9 +650,19 @@
     )
     my_rates = jnp.repeat(my_rates.T, GROUP, axis=1)
 
+    signal_one = [
+        lane_call(
+            product_one_body, "product_one", channels,
+            [(mr_key, "r"), (mr_value, "r"), (prev, "r"), (table, "r")],
+            [halo], 3, part,
+        )[0]
+        for part in halves
+    ]
+    before_one = [sent(signal, 1) for signal in signal_one]
     cotangent, state_back = lane_call(
         upstream_body, "upstream", channels,
-        [(li_query, "r"), (upstream, "r"), (prev, "r"), (table, "r"), (rate, "r")],
+        [(after(li_query, *signal_one), "r"), (upstream, "r"), (prev, "r"), (table, "r"),
+         (rate, "r")],
         [full, state_out], 5,
     )
     gathered_back = exchanged(state_back)
@@ -647,27 +671,30 @@
         [(cotangent, "r"), (table, "r"), (long_turned, "g")],
         [full], 6,
     )
-    gathered_back = after(gathered_back, following, before_kv, near_back)
-    carries_back = scan_states(gathered_back, my_rates, True)
-    closing = exchanged(carries_back)
-
-    key_in = after(mr_key, carries_back)
-    signal_one = [
-        lane_call(
-            product_one_body, "product_one", channels,
-            [(key_in, "r"), (mr_value, "r"), (prev, "r"), (table, "r")],
-            [half], 3, part,
-        )[0]
-        for part in halves
-    ]
-    before_one = [sent(signal, 1) for signal in signal_one]
+
+    def forward(n, into):
+        return lane_call(
+            forward_body, "forward", channels,
+            [(before_one[n], "r"), (signal_one[n], "r"), (mr_query, "r"), (li_key, "r"),
+             (prev, "r"), (table, "r"), (medium, "g"), (long, "g"), (rate, "r")],
+            [full, full, full, state_out, few(6)],
+            12, halves[n], into, unroll=2,
+        )
+
+    got = forward(0, {})
+    gathered_back = after(gathered_back, following, near_back, got[0])
+    closing = exchanged(scan_states(gathered_back, my_rates, True))
+    conv_one, value_two, near, state, head = forward(1, dict(enumerate(got)))
+    next_head = sent(head, -1)
+    gathered = exchanged(state)
 
     into = {}
     conv_grad = []
+    near_later = after(near_back, conv_one)
     for part in halves:
         got = lane_call(
             long_back_body, "long_back", channels,
-            [(near_back, "r"), (closing, "s"), (li_query, "r"), (li_key, "r"), (mr_query, "r"),
+            [(near_later, "r"), (closing, "s"), (li_query, "r"), (li_key, "r"), (mr_query, "r"),
              (prev, "r"), (following, "r"), (table, "r"), (rate, "r"), (residue, "r")],
             [full, few(2), full, few(2), few(1), half],
             5, part, into,
@@ -675,43 +702,29 @@
         conv_grad.append(got[5])
         into = dict(enumerate(got[:5]))
     grad_two, grad_two_after, mixed_grad, mixed_head, conv_head, _ = got
-    after_one = [sent(signal, -1) for signal in conv_grad]
     after_next = sent(conv_head, -2)
     mixed_after = sent(mixed_head, -1)
 
-    into = {}
-    for n, part in enumerate(halves):
-        got = lane_call(
-            forward_body, "forward", channels,
-            [(before_one[n], "r"), (before_kv, "r"), (signal_one[n], "r"), (mr_query, "r"),
-             (li_key, "r"), (prev, "r"), (table, "r"), (medium, "g"), (long, "g"), (rate, "r")],
-            [full, full, full, state_out, few(6)],
-            12, part, into, unroll=2,
-        )
-        into = dict(enumerate(got))
-    conv_one, value_two, near, state, head = got
-    next_head = sent(head, -1)
-    gathered = exchanged(state)
+    gathered = after(gathered, next_head, conv_head)
+    after_one = [sent(after(conv_grad[0], gathered), -1)]
+    start = exchanged(scan_states(gathered, my_rates, False))
+    after_one.append(sent(after(conv_grad[1], start), -1))
 
     def medium_back(n, into):
         return lane_call(
             medium_back_body, "medium_back", channels,
             [(conv_grad[n], "r"), (after_one[n], "r"), (after_next, "r"), (mr_key, "r"),
              (mr_value, "r"), (prev, "r"), (following, "r"), (table, "r"), (medium_turned, "g")],
-            [full, full], 6, halves[n], into,
+            [full, full], 6, halves[n], into, exts=4,
         )
 
     got = medium_back(0, {})
-    gathered = after(gathered, next_head, after_next, *got)
-    start = exchanged(scan_states(gathered, my_rates, False))
-    grad_mr_key, grad_mr_value = medium_back(1, dict(enumerate(got)))
     grad_li_key, grad_mr_query = lane_call(
         late_body, "late", channels,
         [(grad_two, "r"), (grad_two_after, "r"), (value_two, "r"), (mixed_grad, "r"),
          (mixed_after, "r"), (conv_one, "r"), (next_head, "r"), (table, "r")],
         [full, full], 5,
     )
-    start = after(start, grad_li_key, grad_mr_key)
     output, grad_li_query = lane_call(
         long_body, "long_forward", channels,
         [(near, "r"), (start, "s"), (state, "s"), (li_query, "r"), (upstream, "r"),
@@ -719,6 +732,7 @@
          (long_turned, "g")],
         [full, full], 7,
     )
+    grad_mr_key, grad_mr_value = medium_back(1, dict(enumerate(got)))
     return (output, grad_mr_query, grad_mr_key, grad_mr_value, grad_li_query, grad_li_key)
 
 

time: 252 us -> 241 us (0.956)
  starting transfers between devices: 79.5 us -> 73.1 us
  Pallas kernels: 113 us -> 109 us
    all_to_all x4, waiting for transfers between devices: 38.6 us -> 11.9 us  [exchanged(): return lax.all_to_all(array, AXES, split_axis=0, concat_axis=0, tiled=True)]
    ppermute x10 -> x9, waiting for transfers between devices: 9.11 us -> 34.6 us  [sent(): return lax.ppermute(array, AXES, pairs)]
    all_to_all x4, starting transfers between devices: 36.1 us -> 32 us  [exchanged(): return lax.all_to_all(array, AXES, split_axis=0, concat_axis=0, tiled=True)]
    pallas_call x12, Pallas kernels: 100 us -> 96.7 us  [lane_call(): pl.pallas_call(kernel, name=name, in_specs=[anywhere] * (count_in + count...]
    ppermute x10 -> x9, starting transfers between devices: 43.3 us -> 41.2 us  [sent(): return lax.ppermute(array, AXES, pairs)]
    unnamed x42 -> x40, local copies, waits for them, and re-layouts: 7.48 us -> 8.25 us
  transfers between devices with their start and end apart: 14 -> 13, of which waited for: 5 -> 4; matrix products, arithmetic and copies ran while one was open for 1% -> 2% of each run, Pallas kernels for 35% -> 38%
where the time goes in v7:
time: 241 us; the launch traced here: 240 us
  Pallas kernels  109 us (45%)
  starting transfers between devices  73.1 us (30%)
  waiting for transfers between devices  46.5 us (19%)
  local copies, waits for them, and re-layouts  10.6 us (4%)
    pallas_call x12, Pallas kernels, lane_call(): pl.pallas_call(kernel, name=name, in_specs=[anywhere] * (count_in + count...  96.7 us
    ppermute x9, starting transfers between devices, sent(): return lax.ppermute(array, AXES, pairs)  41.2 us
    ppermute x9, waiting for transfers between devices, sent(): return lax.ppermute(array, AXES, pairs)  34.6 us
    all_to_all x4, starting transfers between devices, exchanged(): return lax.all_to_all(array, AXES, split_axis=0, concat_axis=0, tiled=True)  32 us
    all_to_all x4, waiting for transfers between devices, exchanged(): return lax.all_to_all(array, AXES, split_axis=0, concat_axis=0, tiled=True)  11.9 us
    unnamed x40, local copies, waits for them, and re-layouts  8.25 us
    pallas_call x1, Pallas kernels, make_tables(): pl.pallas_call(kernel, name='tables', grid=(groups // block,), in_specs=[...  5.13 us
  transfers between devices with their start and end apart: 13, of which 4 were waited for; matrix products, arithmetic and copies ran while one was open for 2% of the time, Pallas kernels for 38%

profile of v7, /device:TPU:1, one launch (start us, length us, event | category | flops | bytes accessed | tf_op | source)
XLA Modules:
  0.0 240.3 jit_solution(2348278982957691517)
XLA Ops:
  9.1 5.1 %tables.1 = (f32[24,8192]{1,0:T(8,128)}, f32[512,128]{1,0:T(8,128)}, f32[512,128]{1,0:T(8,128)}, f32[512,128]{1,0:T(8,128)}, f32[512,128]{1,0:T(8,128)}) custom-call(bf16[3,3,8192]{2,1,0:T(4,128)(2,1)} %mr.1, bf16[3,3,8192]{2,1,0:T(4,128)(2,1)} %li.1, f32[1,8192]{1,0:T(1,128)} %bitcast.3, bf16[128,512]{1,0:T(8,128)(2,1)} %filters.1, f32[512,16]{1,0:T(8,128)} %copy.34.rate, ...), custom_call_target="tpu_custom_call" | custom-call | bytes 18000000 | tf_op jit(solution)/shard_map/tables/pallas_call | solution.py:354
  17.8 4.1 %product_one.3.refs_1_ = bf16[144,4096]{1,0:T(8,128)(2,1)} custom-call(bf16[128,8192]{1,0:T(8,128)(2,1)} %refs_3_.13, bf16[128,8192]{1,0:T(8,128)(2,1)} %refs_4_.9, bf16[16,8192]{1,0:T(8,128)(2,1)} %copy-done, f32[24,8192]{1,0:T(8,128)} %get-tuple-element.52.refs_3_.refs_5_.refs_1_.refs_7_.refs_8_), custom_call_target="tpu_custom_call" | custom-call | bytes 10800000 | tf_op jit(solution)/shard_map/product_one/pallas_call | solution.py:113
  24.0 4.1 %product_one.2.refs_1_ = bf16[144,4096]{1,0:T(8,128)(2,1)} custom-call(bf16[128,8192]{1,0:T(8,128)(2,1)} %refs_3_.13, bf16[128,8192]{1,0:T(8,128)(2,1)} %refs_4_.9, bf16[16,8192]{1,0:T(8,128)(2,1)} %copy-done, f32[24,8192]{1,0:T(8,128)} %get-tuple-element.52.refs_3_.refs_5_.refs_1_.refs_7_.refs_8_), custom_call_target="tpu_custom_call" | custom-call | bytes 10800000 | tf_op jit(solution)/shard_map/product_one/pallas_call | solution.py:113
  30.8 7.3 %upstream.1 = (bf16[128,8192]{1,0:T(8,128)(2,1)}, f32[128,8,128]{2,1,0:T(8,128)}) custom-call(bf16[128,8192]{1,0:T(8,128)(2,1)} %refs_3_.11, bf16[128,8192]{1,0:T(8,128)(2,1)} %refs_4_.7, bf16[16,8192]{1,0:T(8,128)(2,1)} %copy-done, f32[24,8192]{1,0:T(8,128)} %get-tuple-element.52.refs_3_.refs_5_.refs_1_.refs_7_.refs_8_, ...), custom_call_target="tpu_custom_call" | custom-call | bytes 18000000 | tf_op jit(solution)/shard_map/upstream/pallas_call | solution.py:113
  38.1 12.4 %all-to-all-start.1 = ((f32[128,8,128]{2,1,0:T(8,128)}), f32[128,8,128]{2,1,0:T(8,128)S(1)}, u32[]{:S(2)}, u32[]{:S(2)}) async-start(f32[128,8,128]{2,1,0:T(8,128)} %get-tuple-element.68), calls=%async_computation.1 | async-start | bytes 1048576 | tf_op jit(solution)/shard_map/all_to_all | solution.py:614
  50.5 7.7 %collective-permute-start.4 = (bf16[16,8192]{1,0:T(8,128)(2,1)S(1)}, bf16[16,8192]{1,0:T(8,128)(2,1)S(1)}, u32[]{:S(2)}, u32[]{:S(2)}) collective-permute-start(bf16[16,8192]{1,0:T(8,128)(2,1)S(1)} %copy-done.18), channel_id=1, source_target_pairs={{1,0},{2,1},{3,2},{4,3},{5,4},{6,5},{7,6},{8,7},{9,8},{10,9},{11,1... | collective-permute-start | bytes 786440 | tf_op jit(solution)/shard_map/ppermute | solution.py:610
  59.1 7.9 %long_back_near.1.refs_0_ = bf16[128,8192]{1,0:T(8,128)(2,1)} custom-call(bf16[128,8192]{1,0:T(8,128)(2,1)} %get-tuple-element.64.refs_0_, f32[24,8192]{1,0:T(8,128)} %get-tuple-element.52.refs_3_.refs_5_.refs_1_.refs_7_.refs_8_, f32[512,128]{1,0:T(8,128)} %get-tuple-element.65.refs_2_.refs_11_), custom_call_target="tpu_custom_call" | custom-call | bytes 21600000 | tf_op jit(solution)/shard_map/long_back_near/pallas_call | solution.py:113
  68.1 13.2 %forward.2 = (bf16[128,8192]{1,0:T(8,128)(2,1)}, bf16[128,8192]{1,0:T(8,128)(2,1)}, bf16[128,8192]{1,0:T(8,128)(2,1)}, f32[128,8,128]{2,1,0:T(8,128)}, f32[6,8192]{1,0:T(8,128)}) custom-call(bf16[144,4096]{1,0:T(8,128)(2,1)} %copy-done.8, bf16[144,4096]{1,0:T(8,128)(2,1)} %product_one.3.refs_1_, bf16[128,8192]{1,0:T(8,128)(2,1)} %refs_4_.6, ...), custom_call_target="tpu_custom_call" | custom-call | bytes 43200000 | tf_op jit(solution)/shard_map/forward/pallas_call | solution.py:113
  81.3 5.6 %all-to-all-done.1.states_ref = f32[128,8,128]{2,1,0:T(8,128)S(1)} async-done(((f32[128,8,128]{2,1,0:T(8,128)}), f32[128,8,128]{2,1,0:T(8,128)S(1)}, u32[]{:S(2)}, u32[]{:S(2)}) %all-to-all-start.1) | async-done | bytes 524320 | tf_op jit(solution)/shard_map/all_to_all | solution.py:614
  89.8 5.3 %all-to-all-start.2 = ((f32[128,8,128]{2,1,0:T(8,128)}), f32[128,8,128]{2,1,0:T(8,128)S(1)}, u32[]{:S(2)}, u32[]{:S(2)}) async-start(f32[128,8,128]{2,1,0:T(8,128)} %scan_back.1), calls=%async_computation.2 | async-start | bytes 1048576 | tf_op jit(solution)/shard_map/all_to_all | solution.py:614
  96.2 13.2 %forward.3 = (bf16[128,8192]{1,0:T(8,128)(2,1)}, bf16[128,8192]{1,0:T(8,128)(2,1)}, bf16[128,8192]{1,0:T(8,128)(2,1)}, f32[128,8,128]{2,1,0:T(8,128)}, f32[6,8192]{1,0:T(8,128)}) custom-call(bf16[144,4096]{1,0:T(8,128)(2,1)} %copy-done.9, ...), custom_call_target="tpu_custom_call", output_to_operand_aliasing={{0}: (9, {}), {1}: (10, {}), {2}: (11, {}), {3}: (12, {}), ... | custom-call | bytes 43200000 | tf_op jit(solution)/shard_map/forward/pallas_call | solution.py:113
  109.5 9.8 %all-to-all-start = ((f32[128,8,128]{2,1,0:T(8,128)}), f32[128,8,128]{2,1,0:T(8,128)S(1)}, u32[]{:S(2)}, u32[]{:S(2)}) async-start(f32[128,8,128]{2,1,0:T(8,128)} %get-tuple-element.61.refs_2_), calls=%async_computation | async-start | bytes 1048576 | tf_op jit(solution)/shard_map/all_to_all | solution.py:614
  119.2 7.7 %collective-permute-start.3 = (f32[6,8192]{1,0:T(8,128)}, f32[6,8192]{1,0:T(8,128)S(1)}, u32[]{:S(2)}, u32[]{:S(2)}) collective-permute-start(f32[6,8192]{1,0:T(8,128)} %get-tuple-element.62), channel_id=1, source_target_pairs={{1,0},{2,1},{3,2},{4,3},{5,4},{6,5},{7,6},{8,7},{9,8},{10,9},{11,1... | collective-permute-start | bytes 589832 | tf_op jit(solution)/shard_map/ppermute | solution.py:610
  127.7 6.8 %long_back.2 = (bf16[128,8192]{1,0:T(8,128)(2,1)}, f32[2,8192]{1,0:T(2,128)}, bf16[128,8192]{1,0:T(8,128)(2,1)}, f32[2,8192]{1,0:T(2,128)}, f32[1,8192]{1,0:T(1,128)}, /*index=5*/bf16[128,4096]{1,0:T(8,128)(2,1)}) custom-call(bf16[128,8192]{1,0:T(8,128)(2,1)} %long_back_near.1.refs_0_, f32[128,8,128]{2,1,0:T(8,128)} %copy-done.2, ...), custom_call_target="tpu_custom_call" | custom-call | bytes 18000000 | tf_op jit(solution)/shard_map/long_back/pallas_call | solution.py:113
  134.6 6.9 %long_back.3 = (bf16[128,8192]{1,0:T(8,128)(2,1)}, f32[2,8192]{1,0:T(2,128)}, bf16[128,8192]{1,0:T(8,128)(2,1)}, f32[2,8192]{1,0:T(2,128)}, f32[1,8192]{1,0:T(1,128)}, /*index=5*/bf16[128,4096]{1,0:T(8,128)(2,1)}) custom-call(bf16[128,8192]{1,0:T(8,128)(2,1)} %long_back_near.1.refs_0_,, ...), custom_call_target="tpu_custom_call", output_to_operand_aliasing={{0}: (10, {}), {1}: (11, {}), {2}: (12, {}), {3}: (13, {}),... | custom-call | bytes 18000000 | tf_op jit(solution)/shard_map/long_back/pallas_call | solution.py:113
  144.5 4.5 %all-to-all-start.3 = ((f32[128,8,128]{2,1,0:T(8,128)}), f32[128,8,128]{2,1,0:T(8,128)S(1)}, u32[]{:S(2)}, u32[]{:S(2)}) async-start(f32[128,8,128]{2,1,0:T(8,128)} %scan_forward.1), calls=%async_computation.3 | async-start | bytes 1048576 | tf_op jit(solution)/shard_map/all_to_all | solution.py:614
  149.0 7.7 %collective-permute-start.8 = (bf16[128,4096]{1,0:T(8,128)(2,1)S(1)}, bf16[128,4096]{1,0:T(8,128)(2,1)}, u32[]{:S(2)}, u32[]{:S(2)}) collective-permute-start(bf16[128,4096]{1,0:T(8,128)(2,1)S(1)} %copy-done.11), channel_id=1, source_target_pairs={{1,0},{2,1},{3,2},{4,3},{5,4},{6,5},{7,6},{8,7},{9,8},{10,9},{11,1... | collective-permute-start | bytes 3145736 | tf_op jit(solution)/shard_map/ppermute | solution.py:610
  156.7 6.3 %all-to-all-done.3.refs_1_ = f32[128,8,128]{2,1,0:T(8,128)S(1)} async-done(((f32[128,8,128]{2,1,0:T(8,128)}), f32[128,8,128]{2,1,0:T(8,128)S(1)}, u32[]{:S(2)}, u32[]{:S(2)}) %all-to-all-start.3) | async-done | bytes 524320 | tf_op jit(solution)/shard_map/all_to_all | solution.py:614
  169.0 4.2 %collective-permute-start.7 = (f32[1,8192]{1,0:T(1,128)}, f32[1,8192]{1,0:T(1,128)S(1)}, u32[]{:S(2)}, u32[]{:S(2)}) collective-permute-start(f32[1,8192]{1,0:T(1,128)} %get-tuple-element.76), channel_id=1, source_target_pairs={{2,0},{3,1},{4,2},{5,3},{6,4},{7,5},{8,6},{9,7},{10,8},{11,9},{12,... | collective-permute-start | bytes 98312 | tf_op jit(solution)/shard_map/ppermute | solution.py:610
  173.1 31.6 %collective-permute-done.5.refs_4_ = f32[2,8192]{1,0:T(2,128)S(1)} collective-permute-done((f32[2,8192]{1,0:T(2,128)}, f32[2,8192]{1,0:T(2,128)S(1)}, u32[]{:S(2)}, u32[]{:S(2)}) %collective-permute-start.5) | collective-permute-done | bytes 65568 | tf_op jit(solution)/shard_map/ppermute | solution.py:610
  205.4 8.0 %late.1 = (bf16[128,8192]{1,0:T(8,128)(2,1)}, bf16[128,8192]{1,0:T(8,128)(2,1)}) custom-call(bf16[128,8192]{1,0:T(8,128)(2,1)} %get-tuple-element.79.refs_0_, f32[2,8192]{1,0:T(2,128)} %get-tuple-element.80.refs_1_, bf16[128,8192]{1,0:T(8,128)(2,1)} %get-tuple-element.81.refs_2_, bf16[128,8192]{1,0:T(8,128)(2,1)} %get-tuple-element.82.refs_3_, ...), custom_call_target="tpu_custom_call" | custom-call | bytes 18000000 | tf_op jit(solution)/shard_map/late/pallas_call | solution.py:113
  213.4 9.5 %long_forward.1 = (bf16[128,8192]{1,0:T(8,128)(2,1)}, bf16[128,8192]{1,0:T(8,128)(2,1)}) custom-call(bf16[128,8192]{1,0:T(8,128)(2,1)} %get-tuple-element.60.refs_0_, f32[128,8,128]{2,1,0:T(8,128)} %copy-done.5, f32[128,8,128]{2,1,0:T(8,128)} %get-tuple-element.61.refs_2_, bf16[128,8192]{1,0:T(8,128)(2,1)} %refs_3_.11, bf16[128,8192]{1,0:T(8,128)(2,1)} %refs_4_.7, ...), custom_call_target="tpu_custom_call" | custom-call | bytes 25200000 | tf_op jit(solution)/shard_map/long_forward/pallas_call | solution.py:113
  223.5 7.8 %medium_back.2 = (bf16[128,8192]{1,0:T(8,128)(2,1)}, bf16[128,8192]{1,0:T(8,128)(2,1)}) custom-call(bf16[128,4096]{1,0:T(8,128)(2,1)} %get-tuple-element.89.refs_0_, bf16[128,4096]{1,0:T(8,128)(2,1)} %collective-permute-done.8.refs_1_, f32[1,8192]{1,0:T(1,128)} %copy-done.14, bf16[128,8192]{1,0:T(8,128)(2,1)} %refs_3_.13, bf16[128,8192]{1,0:T(8,128)(2,1)} %refs_4_.9, ...), custom_call_target="tpu_custom_call" | custom-call | bytes 21600000 | tf_op jit(solution)/shard_map/medium_back/pallas_call | solution.py:113
  232.3 7.8 %medium_back.3 = (bf16[128,8192]{1,0:T(8,128)(2,1)}, bf16[128,8192]{1,0:T(8,128)(2,1)}) custom-call(bf16[128,4096]{1,0:T(8,128)(2,1)} %get-tuple-element.86.refs_0_, bf16[128,4096]{1,0:T(8,128)(2,1)} %copy-done.12, f32[1,8192]{1,0:T(1,128)} %copy-done.14, bf16[128,8192]{1,0:T(8,128)(2,1)} %refs_3_.13, ...), custom_call_target="tpu_custom_call", output_to_operand_aliasing={{0}: (9, {}), {1}: (10, {})} | custom-call | bytes 21600000 | tf_op jit(solution)/shard_map/medium_back/pallas_call | solution.py:113
  (63 shorter events, 34.4 us)
Async XLA Ops:
  0.6 6.7 %copy-start.17 = (f32[512,16]{0,1:T(8,128)S(1)}, f32[512,16]{0,1:T(8,128)}, u32[]{:S(2)}) copy-start(f32[512,16]{0,1:T(8,128)} %param.22) | copy-start | bytes 98308
  0.6 7.6 %copy-start.16 = (f32[512,16]{0,1:T(8,128)S(1)}, f32[512,16]{0,1:T(8,128)}, u32[]{:S(2)}) copy-start(f32[512,16]{0,1:T(8,128)} %param.21) | copy-start | bytes 98308
  3.3 13.8 %collective-permute-start = (bf16[16,8192]{1,0:T(8,128)(2,1)}, bf16[16,8192]{1,0:T(8,128)(2,1)S(1)}, u32[]{:S(2)}, u32[]{:S(2)}) collective-permute-start(bf16[16,8192]{1,0:T(8,128)(2,1)} %get-tuple-element.51), channel_id=1, source_target_pairs={{0,1},{1,2},{2,3},{3,4},{4,5},{5,6},{6,7},{7,8},{8,9},{9,10},{10,1... | collective-permute-start | bytes 786440 | tf_op jit(solution)/shard_map/ppermute | solution.py:610
  21.9 8.1 %copy-start.4 = (f32[512,16]{1,0:T(8,128)S(1)}, f32[512,16]{1,0:T(8,128)}, u32[]{:S(2)}) copy-start(f32[512,16]{1,0:T(8,128)} %copy.34.rate) | copy-start | bytes 98308
  21.9 45.1 %collective-permute-start.2 = (bf16[144,4096]{1,0:T(8,128)(2,1)}, bf16[144,4096]{1,0:T(8,128)(2,1)S(1)}, u32[]{:S(2)}, u32[]{:S(2)}) collective-permute-start(bf16[144,4096]{1,0:T(8,128)(2,1)} %product_one.3.refs_1_), channel_id=1, source_target_pairs={{0,1},{1,2},{2,3},{3,4},{4,5},{5,6},{6,7},{7,8},{8,9},{9,10},{10,1... | collective-permute-start | bytes 3538952 | tf_op jit(solution)/shard_map/ppermute | solution.py:610
  28.1 67.0 %collective-permute-start.1 = (bf16[144,4096]{1,0:T(8,128)(2,1)}, bf16[144,4096]{1,0:T(8,128)(2,1)S(1)}, u32[]{:S(2)}, u32[]{:S(2)}) collective-permute-start(bf16[144,4096]{1,0:T(8,128)(2,1)} %product_one.2.refs_1_), channel_id=1, source_target_pairs={{0,1},{1,2},{2,3},{3,4},{4,5},{5,6},{6,7},{7,8},{8,9},{9,10},{10,1... | collective-permute-start | bytes 3538952 | tf_op jit(solution)/shard_map/ppermute | solution.py:610
  30.8 19.7 %copy-start.18 = (bf16[16,8192]{1,0:T(8,128)(2,1)S(1)}, bf16[16,8192]{1,0:T(8,128)(2,1)}, u32[]{:S(2)}) copy-start(bf16[16,8192]{1,0:T(8,128)(2,1)} %get-tuple-element.69) | copy-start | bytes 786436
  38.1 48.8 %all-to-all-start.1 = ((f32[128,8,128]{2,1,0:T(8,128)}), f32[128,8,128]{2,1,0:T(8,128)S(1)}, u32[]{:S(2)}, u32[]{:S(2)}) async-start(f32[128,8,128]{2,1,0:T(8,128)} %get-tuple-element.68), calls=%async_computation.1 | async-start | bytes 1048576 | tf_op jit(solution)/shard_map/all_to_all | solution.py:614
  50.5 30.8 %collective-permute-start.4 = (bf16[16,8192]{1,0:T(8,128)(2,1)S(1)}, bf16[16,8192]{1,0:T(8,128)(2,1)S(1)}, u32[]{:S(2)}, u32[]{:S(2)}) collective-permute-start(bf16[16,8192]{1,0:T(8,128)(2,1)S(1)} %copy-done.18), channel_id=1, source_target_pairs={{1,0},{2,1},{3,2},{4,3},{5,4},{6,5},{7,6},{8,7},{9,8},{10,9},{11,1... | collective-permute-start | bytes 786440 | tf_op jit(solution)/shard_map/ppermute | solution.py:610
  81.3 28.1 %copy-start.1 = (bf16[16,8192]{1,0:T(8,128)(2,1)}, bf16[16,8192]{1,0:T(8,128)(2,1)S(1)}, u32[]{:S(2)}) copy-start(bf16[16,8192]{1,0:T(8,128)(2,1)S(1)} %collective-permute-done.4.refs_6_) | copy-start | bytes 786436
  89.8 19.6 %all-to-all-start.2 = ((f32[128,8,128]{2,1,0:T(8,128)}), f32[128,8,128]{2,1,0:T(8,128)S(1)}, u32[]{:S(2)}, u32[]{:S(2)}) async-start(f32[128,8,128]{2,1,0:T(8,128)} %scan_back.1), calls=%async_computation.2 | async-start | bytes 1048576 | tf_op jit(solution)/shard_map/all_to_all | solution.py:614
  96.2 30.8 %copy-start.3 = (f32[512,16]{1,0:T(8,128)S(1)}, f32[512,16]{1,0:T(8,128)}, u32[]{:S(2)}) copy-start(f32[512,16]{1,0:T(8,128)} %copy.35.residue) | copy-start | bytes 98308
  109.4 18.3 %copy-start.2 = (f32[128,8,128]{2,1,0:T(8,128)}, f32[128,8,128]{2,1,0:T(8,128)S(1)}, u32[]{:S(2)}) copy-start(f32[128,8,128]{2,1,0:T(8,128)S(1)} %all-to-all-done.2.refs_1_) | copy-start | bytes 1572868
  109.5 32.0 %all-to-all-start = ((f32[128,8,128]{2,1,0:T(8,128)}), f32[128,8,128]{2,1,0:T(8,128)S(1)}, u32[]{:S(2)}, u32[]{:S(2)}) async-start(f32[128,8,128]{2,1,0:T(8,128)} %get-tuple-element.61.refs_2_), calls=%async_computation | async-start | bytes 1048576 | tf_op jit(solution)/shard_map/all_to_all | solution.py:614
  119.2 22.2 %collective-permute-start.3 = (f32[6,8192]{1,0:T(8,128)}, f32[6,8192]{1,0:T(8,128)S(1)}, u32[]{:S(2)}, u32[]{:S(2)}) collective-permute-start(f32[6,8192]{1,0:T(8,128)} %get-tuple-element.62), channel_id=1, source_target_pairs={{1,0},{2,1},{3,2},{4,3},{5,4},{6,5},{7,6},{8,7},{9,8},{10,9},{11,1... | collective-permute-start | bytes 589832 | tf_op jit(solution)/shard_map/ppermute | solution.py:610
  141.5 7.5 %copy-start.11 = (bf16[128,4096]{1,0:T(8,128)(2,1)S(1)}, bf16[128,4096]{1,0:T(8,128)(2,1)}, u32[]{:S(2)}) copy-start(bf16[128,4096]{1,0:T(8,128)(2,1)} %get-tuple-element.89.refs_0_) | copy-start | bytes 3145732
  141.5 21.6 %copy-start.10 = (bf16[128,4096]{1,0:T(8,128)(2,1)S(1)}, bf16[128,4096]{1,0:T(8,128)(2,1)}, u32[]{:S(2)}) copy-start(bf16[128,4096]{1,0:T(8,128)(2,1)} %get-tuple-element.86.refs_0_) | copy-start | bytes 3145732
  141.5 3.0 %copy-start.13 = (f32[6,8192]{1,0:T(8,128)}, f32[6,8192]{1,0:T(8,128)S(1)}, u32[]{:S(2)}) copy-start(f32[6,8192]{1,0:T(8,128)S(1)} %collective-permute-done.3.refs_7_.refs_6_) | copy-start | bytes 589828
  144.5 18.6 %all-to-all-start.3 = ((f32[128,8,128]{2,1,0:T(8,128)}), f32[128,8,128]{2,1,0:T(8,128)S(1)}, u32[]{:S(2)}, u32[]{:S(2)}) async-start(f32[128,8,128]{2,1,0:T(8,128)} %scan_forward.1), calls=%async_computation.3 | async-start | bytes 1048576 | tf_op jit(solution)/shard_map/all_to_all | solution.py:614
  149.0 73.9 %collective-permute-start.8 = (bf16[128,4096]{1,0:T(8,128)(2,1)S(1)}, bf16[128,4096]{1,0:T(8,128)(2,1)}, u32[]{:S(2)}, u32[]{:S(2)}) collective-permute-start(bf16[128,4096]{1,0:T(8,128)(2,1)S(1)} %copy-done.11), channel_id=1, source_target_pairs={{1,0},{2,1},{3,2},{4,3},{5,4},{6,5},{7,6},{8,7},{9,8},{10,9},{11,1... | collective-permute-start | bytes 3145736 | tf_op jit(solution)/shard_map/ppermute | solution.py:610
  163.1 50.4 %copy-start.5 = (f32[128,8,128]{2,1,0:T(8,128)}, f32[128,8,128]{2,1,0:T(8,128)S(1)}, u32[]{:S(2)}) copy-start(f32[128,8,128]{2,1,0:T(8,128)S(1)} %all-to-all-done.3.refs_1_) | copy-start | bytes 1572868
  163.1 68.2 %collective-permute-start.6 = (bf16[128,4096]{1,0:T(8,128)(2,1)S(1)}, bf16[128,4096]{1,0:T(8,128)(2,1)S(1)}, u32[]{:S(2)}, u32[]{:S(2)}) collective-permute-start(bf16[128,4096]{1,0:T(8,128)(2,1)S(1)} %copy-done.10), channel_id=1, source_target_pairs={{1,0},{2,1},{3,2},{4,3},{5,4},{6,5},{7,6},{8,7},{9,8},{10,9},{11,1... | collective-permute-start | bytes 3145736 | tf_op jit(solution)/shard_map/ppermute | solution.py:610
  166.7 38.0 %collective-permute-start.5 = (f32[2,8192]{1,0:T(2,128)}, f32[2,8192]{1,0:T(2,128)S(1)}, u32[]{:S(2)}, u32[]{:S(2)}) collective-permute-start(f32[2,8192]{1,0:T(2,128)} %get-tuple-element.83), channel_id=1, source_target_pairs={{1,0},{2,1},{3,2},{4,3},{5,4},{6,5},{7,6},{8,7},{9,8},{10,9},{11,1... | collective-permute-start | bytes 196616 | tf_op jit(solution)/shard_map/ppermute | solution.py:610
  169.0 54.0 %collective-permute-start.7 = (f32[1,8192]{1,0:T(1,128)}, f32[1,8192]{1,0:T(1,128)S(1)}, u32[]{:S(2)}, u32[]{:S(2)}) collective-permute-start(f32[1,8192]{1,0:T(1,128)} %get-tuple-element.76), channel_id=1, source_target_pairs={{2,0},{3,1},{4,2},{5,3},{6,4},{7,5},{8,6},{9,7},{10,8},{11,9},{12,... | collective-permute-start | bytes 98312 | tf_op jit(solution)/shard_map/ppermute | solution.py:610
  (8 other events, 6.6 us)

commit v8 on v7

--- a/solution.py
+++ b/solution.py
@@ -1,3 +1,5 @@
+import math
+
 import jax
 import jax.numpy as jnp
 from jax import lax
@@ -33,11 +35,12 @@
     return start if isinstance(start, int) else pl.multiple_of(start, of)
 
 
-def lane_call(body, name, channels, ins, outs, us, part=(0, 1), into=None, width=1024, unroll=4, exts=0):
-    span = channels // part[1]
+def lane_call(body, name, channels, ins, outs, us, part=None, into=None, width=1024, unroll=4, exts=0):
+    begin, end = part or (0, channels)
+    span = end - begin
     width = min(width, span)
     tiles = width // LANES
-    unroll = min(unroll, tiles)
+    unroll = math.gcd(unroll, tiles)
     blocks = span // width
     into = into or {}
     kinds = [kind for _, kind in ins] + [kind for _, _, kind in outs]
@@ -61,7 +64,7 @@
         return (span // GROUP, shape[1]) if kind == "g" else (span // (LANES // 2), *shape[1:])
 
     first = [
-        part[0] * span if channels_of(shape, kind) == channels else 0
+        begin if channels_of(shape, kind) == channels else 0
         for shape, kind in zip(shapes, kinds)
     ]
 
@@ -627,10 +630,13 @@
     assert mr_query.shape[0] == ROWS and lax.axis_size(AXES) == 2 * tiles
     rows = (ROWS, channels)
     full = (rows, BF16, "r")
-    half = ((ROWS, channels // 2), BF16, "r")
-    halo = ((ROWS + 16, channels // 2), BF16, "r")
     state_out = ((2 * tiles, 8, LANES), F32, "s")
-    halves = ((0, 2), (1, 2))
+    cut = tiles * 3 // 4 * LANES
+    parts = ((0, cut), (cut, channels))
+
+    def own(n, part):
+        return ((n, part[1] - part[0]), BF16, "r")
+
 
     def few(n):
         return ((n, channels), F32, "r")
@@ -654,9 +660,9 @@
         lane_call(
             product_one_body, "product_one", channels,
             [(mr_key, "r"), (mr_value, "r"), (prev, "r"), (table, "r")],
-            [halo], 3, part,
+            [own(ROWS + 16, part)], 3, part,
         )[0]
-        for part in halves
+        for part in parts
     ]
     before_one = [sent(signal, 1) for signal in signal_one]
     cotangent, state_back = lane_call(
@@ -678,7 +684,7 @@
             [(before_one[n], "r"), (signal_one[n], "r"), (mr_query, "r"), (li_key, "r"),
              (prev, "r"), (table, "r"), (medium, "g"), (long, "g"), (rate, "r")],
             [full, full, full, state_out, few(6)],
-            12, halves[n], into, unroll=2,
+            12, parts[n], into, unroll=2,
         )
 
     got = forward(0, {})
@@ -686,17 +692,18 @@
     closing = exchanged(scan_states(gathered_back, my_rates, True))
     conv_one, value_two, near, state, head = forward(1, dict(enumerate(got)))
     next_head = sent(head, -1)
-    gathered = exchanged(state)
+    gathered = after(exchanged(state), next_head)
 
     into = {}
     conv_grad = []
     near_later = after(near_back, conv_one)
-    for part in halves:
+    for part in parts:
+        near_later = after(near_later, gathered) if into else near_later
         got = lane_call(
             long_back_body, "long_back", channels,
             [(near_later, "r"), (closing, "s"), (li_query, "r"), (li_key, "r"), (mr_query, "r"),
              (prev, "r"), (following, "r"), (table, "r"), (rate, "r"), (residue, "r")],
-            [full, few(2), full, few(2), few(1), half],
+            [full, few(2), full, few(2), few(1), own(ROWS, part)],
             5, part, into,
         )
         conv_grad.append(got[5])
@@ -705,8 +712,8 @@
     after_next = sent(conv_head, -2)
     mixed_after = sent(mixed_head, -1)
 
-    gathered = after(gathered, next_head, conv_head)
-    after_one = [sent(after(conv_grad[0], gathered), -1)]
+    gathered = after(gathered, conv_head)
+    after_one = [sent(after(conv_grad[0], gathered, after_next, mixed_after), -1)]
     start = exchanged(scan_states(gathered, my_rates, False))
     after_one.append(sent(after(conv_grad[1], start), -1))
 
@@ -715,16 +722,16 @@
             medium_back_body, "medium_back", channels,
             [(conv_grad[n], "r"), (after_one[n], "r"), (after_next, "r"), (mr_key, "r"),
              (mr_value, "r"), (prev, "r"), (following, "r"), (table, "r"), (medium_turned, "g")],
-            [full, full], 6, halves[n], into, exts=4,
+            [full, full], 6, parts[n], into, exts=4,
         )
 
-    got = medium_back(0, {})
     grad_li_key, grad_mr_query = lane_call(
         late_body, "late", channels,
         [(grad_two, "r"), (grad_two_after, "r"), (value_two, "r"), (mixed_grad, "r"),
          (mixed_after, "r"), (conv_one, "r"), (next_head, "r"), (table, "r")],
         [full, full], 5,
     )
+    start = after(start, grad_li_key)
     output, grad_li_query = lane_call(
         long_body, "long_forward", channels,
         [(near, "r"), (start, "s"), (state, "s"), (li_query, "r"), (upstream, "r"),
@@ -732,6 +739,8 @@
          (long_turned, "g")],
         [full, full], 7,
     )
+    conv_grad[0] = after(conv_grad[0], grad_li_query)
+    got = medium_back(0, {})
     grad_mr_key, grad_mr_value = medium_back(1, dict(enumerate(got)))
     return (output, grad_mr_query, grad_mr_key, grad_mr_value, grad_li_query, grad_li_key)
 

time: 241 us -> 264 us (1.095)
  blocking collectives: 0 us -> 38.4 us
  waiting for transfers between devices: 46.5 us -> 25.9 us
  starting transfers between devices: 73.1 us -> 79.1 us
    all_to_all x0 -> x1, blocking collectives: none -> 38.4 us  [exchanged(): return lax.all_to_all(array, AXES, split_axis=0, concat_axis=0, tiled=True)]
    ppermute x9, waiting for transfers between devices: 34.6 us -> 14.7 us  [sent(): return lax.ppermute(array, AXES, pairs)]
    ppermute x9, starting transfers between devices: 41.2 us -> 45.9 us  [sent(): return lax.ppermute(array, AXES, pairs)]
    all_to_all x4 -> x3, starting transfers between devices: 32 us -> 33.2 us  [exchanged(): return lax.all_to_all(array, AXES, split_axis=0, concat_axis=0, tiled=True)]
    all_to_all x4 -> x3, waiting for transfers between devices: 11.9 us -> 11.1 us  [exchanged(): return lax.all_to_all(array, AXES, split_axis=0, concat_axis=0, tiled=True)]
  transfers between devices with their start and end apart: 13 -> 12, of which waited for: 4 -> 5; matrix products, arithmetic and copies ran while one was open for 2% -> 2% of each run, Pallas kernels for 38% -> 28%
where the time goes in v8:
time: 264 us; the launch traced here: 263 us
  Pallas kernels  109 us (41%)
  starting transfers between devices  79.1 us (30%)
  blocking collectives  38.4 us (15%)
  waiting for transfers between devices  25.9 us (10%)
  local copies, waits for them, and re-layouts  9.64 us (4%)
    pallas_call x12, Pallas kernels, lane_call(): pl.pallas_call(kernel, name=name, in_specs=[anywhere] * (count_in + count...  96.6 us
    ppermute x9, starting transfers between devices, sent(): return lax.ppermute(array, AXES, pairs)  45.9 us
    all_to_all x1, blocking collectives, exchanged(): return lax.all_to_all(array, AXES, split_axis=0, concat_axis=0, tiled=True)  38.4 us
    all_to_all x3, starting transfers between devices, exchanged(): return lax.all_to_all(array, AXES, split_axis=0, concat_axis=0, tiled=True)  33.2 us
    ppermute x9, waiting for transfers between devices, sent(): return lax.ppermute(array, AXES, pairs)  14.7 us
    all_to_all x3, waiting for transfers between devices, exchanged(): return lax.all_to_all(array, AXES, split_axis=0, concat_axis=0, tiled=True)  11.1 us
    unnamed x40, local copies, waits for them, and re-layouts  7.29 us
  transfers between devices with their start and end apart: 12, of which 5 were waited for; matrix products, arithmetic and copies ran while one was open for 2% of the time, Pallas kernels for 28%

profile of v8, /device:TPU:1, one launch (start us, length us, event | category | flops | bytes accessed | tf_op | source)
XLA Modules:
  0.0 262.9 jit_solution(2290476385495636995)
XLA Ops:
  3.3 4.0 %collective-permute-start = (bf16[16,8192]{1,0:T(8,128)(2,1)}, bf16[16,8192]{1,0:T(8,128)(2,1)S(1)}, u32[]{:S(2)}, u32[]{:S(2)}) collective-permute-start(bf16[16,8192]{1,0:T(8,128)(2,1)} %get-tuple-element.55), channel_id=1, source_target_pairs={{0,1},{1,2},{2,3},{3,4},{4,5},{5,6},{6,7},{7,8},{8,9},{9,10},{10,1... | collective-permute-start | bytes 786440 | tf_op jit(solution)/shard_map/ppermute | solution.py:613
  9.0 5.1 %tables.1 = (f32[24,8192]{1,0:T(8,128)}, f32[512,128]{1,0:T(8,128)}, f32[512,128]{1,0:T(8,128)}, f32[512,128]{1,0:T(8,128)}, f32[512,128]{1,0:T(8,128)}) custom-call(bf16[3,3,8192]{2,1,0:T(4,128)(2,1)} %mr.1, bf16[3,3,8192]{2,1,0:T(4,128)(2,1)} %li.1, f32[1,8192]{1,0:T(1,128)} %bitcast.3, bf16[128,512]{1,0:T(8,128)(2,1)} %filters.1, f32[512,16]{1,0:T(8,128)} %copy.34.rate, ...), custom_call_target="tpu_custom_call" | custom-call | bytes 18000000 | tf_op jit(solution)/shard_map/tables/pallas_call | solution.py:357
  17.8 5.3 %product_one.3.refs_1_ = bf16[144,6144]{1,0:T(8,128)(2,1)} custom-call(bf16[128,8192]{1,0:T(8,128)(2,1)} %refs_3_.13, bf16[128,8192]{1,0:T(8,128)(2,1)} %refs_4_.9, bf16[16,8192]{1,0:T(8,128)(2,1)} %copy-done, f32[24,8192]{1,0:T(8,128)} %get-tuple-element.56.refs_3_.refs_5_.refs_1_.refs_7_.refs_8_), custom_call_target="tpu_custom_call" | custom-call | bytes 10800000 | tf_op jit(solution)/shard_map/product_one/pallas_call | solution.py:116
  30.8 7.3 %upstream.1 = (bf16[128,8192]{1,0:T(8,128)(2,1)}, f32[128,8,128]{2,1,0:T(8,128)}) custom-call(bf16[128,8192]{1,0:T(8,128)(2,1)} %refs_3_.11, bf16[128,8192]{1,0:T(8,128)(2,1)} %refs_4_.7, bf16[16,8192]{1,0:T(8,128)(2,1)} %copy-done, f32[24,8192]{1,0:T(8,128)} %get-tuple-element.56.refs_3_.refs_5_.refs_1_.refs_7_.refs_8_, ...), custom_call_target="tpu_custom_call" | custom-call | bytes 18000000 | tf_op jit(solution)/shard_map/upstream/pallas_call | solution.py:116
  38.1 12.4 %all-to-all-start.1 = ((f32[128,8,128]{2,1,0:T(8,128)}), f32[128,8,128]{2,1,0:T(8,128)S(1)}, u32[]{:S(2)}, u32[]{:S(2)}) async-start(f32[128,8,128]{2,1,0:T(8,128)} %get-tuple-element.74), calls=%async_computation.1 | async-start | bytes 1048576 | tf_op jit(solution)/shard_map/all_to_all | solution.py:617
  50.5 7.7 %collective-permute-start.4 = (bf16[16,8192]{1,0:T(8,128)(2,1)S(1)}, bf16[16,8192]{1,0:T(8,128)(2,1)S(1)}, u32[]{:S(2)}, u32[]{:S(2)}) collective-permute-start(bf16[16,8192]{1,0:T(8,128)(2,1)S(1)} %copy-done.18), channel_id=1, source_target_pairs={{1,0},{2,1},{3,2},{4,3},{5,4},{6,5},{7,6},{8,7},{9,8},{10,9},{11,1... | collective-permute-start | bytes 786440 | tf_op jit(solution)/shard_map/ppermute | solution.py:613
  58.2 8.0 %long_back_near.1.refs_0_ = bf16[128,8192]{1,0:T(8,128)(2,1)} custom-call(bf16[128,8192]{1,0:T(8,128)(2,1)} %get-tuple-element.69.refs_0_, f32[24,8192]{1,0:T(8,128)} %get-tuple-element.56.refs_3_.refs_5_.refs_1_.refs_7_.refs_8_, f32[512,128]{1,0:T(8,128)} %get-tuple-element.70.refs_2_.refs_11_), custom_call_target="tpu_custom_call" | custom-call | bytes 21600000 | tf_op jit(solution)/shard_map/long_back_near/pallas_call | solution.py:116
  69.3 18.8 %forward.2 = (bf16[128,8192]{1,0:T(8,128)(2,1)}, bf16[128,8192]{1,0:T(8,128)(2,1)}, bf16[128,8192]{1,0:T(8,128)(2,1)}, f32[128,8,128]{2,1,0:T(8,128)}, f32[6,8192]{1,0:T(8,128)}) custom-call(bf16[144,6144]{1,0:T(8,128)(2,1)} %copy-done.7, bf16[144,6144]{1,0:T(8,128)(2,1)} %product_one.3.refs_1_, bf16[128,8192]{1,0:T(8,128)(2,1)} %refs_4_.6, ...), custom_call_target="tpu_custom_call" | custom-call | bytes 43200000 | tf_op jit(solution)/shard_map/forward/pallas_call | solution.py:116
  89.0 7.6 %forward.3 = (bf16[128,8192]{1,0:T(8,128)(2,1)}, bf16[128,8192]{1,0:T(8,128)(2,1)}, bf16[128,8192]{1,0:T(8,128)(2,1)}, f32[128,8,128]{2,1,0:T(8,128)}, f32[6,8192]{1,0:T(8,128)}) custom-call(bf16[144,2048]{1,0:T(8,128)(2,1)} %copy-done.11, ...), custom_call_target="tpu_custom_call", output_to_operand_aliasing={{0}: (9, {}), {1}: (10, {}), {2}: (11, {}), {3}: (12, {}), ... | custom-call | bytes 43200000 | tf_op jit(solution)/shard_map/forward/pallas_call | solution.py:116
  96.6 16.8 %all-to-all-start = ((f32[128,8,128]{2,1,0:T(8,128)}), f32[128,8,128]{2,1,0:T(8,128)S(1)}, u32[]{:S(2)}, u32[]{:S(2)}) async-start(f32[128,8,128]{2,1,0:T(8,128)} %get-tuple-element.65.refs_2_), calls=%async_computation | async-start | bytes 1048576 | tf_op jit(solution)/shard_map/all_to_all | solution.py:617
  116.4 11.1 %all-to-all-done.states_ref = f32[128,8,128]{2,1,0:T(8,128)S(1)} async-done(((f32[128,8,128]{2,1,0:T(8,128)}), f32[128,8,128]{2,1,0:T(8,128)S(1)}, u32[]{:S(2)}, u32[]{:S(2)}) %all-to-all-start) | async-done | bytes 524320 | tf_op jit(solution)/shard_map/all_to_all | solution.py:617
  131.5 7.9 %collective-permute-start.3 = (f32[6,8192]{1,0:T(8,128)S(1)}, f32[6,8192]{1,0:T(8,128)S(1)}, u32[]{:S(2)}, u32[]{:S(2)}) collective-permute-start(f32[6,8192]{1,0:T(8,128)S(1)} %copy-done.13), channel_id=1, source_target_pairs={{1,0},{2,1},{3,2},{4,3},{5,4},{6,5},{7,6},{8,7},{9,8},{10,9},{11,1... | collective-permute-start | bytes 589832 | tf_op jit(solution)/shard_map/ppermute | solution.py:613
  140.2 5.7 %collective-permute-done.3.refs_6_.refs_7_ = f32[6,8192]{1,0:T(8,128)S(1)} collective-permute-done((f32[6,8192]{1,0:T(8,128)S(1)}, f32[6,8192]{1,0:T(8,128)S(1)}, u32[]{:S(2)}, u32[]{:S(2)}) %collective-permute-start.3) | collective-permute-done | bytes 196640 | tf_op jit(solution)/shard_map/ppermute | solution.py:613
  146.7 9.1 %long_back.2 = (bf16[128,8192]{1,0:T(8,128)(2,1)}, f32[2,8192]{1,0:T(2,128)}, bf16[128,8192]{1,0:T(8,128)(2,1)}, f32[2,8192]{1,0:T(2,128)}, f32[1,8192]{1,0:T(1,128)}, /*index=5*/bf16[128,6144]{1,0:T(8,128)(2,1)}) custom-call(bf16[128,8192]{1,0:T(8,128)(2,1)} %long_back_near.1.refs_0_, f32[128,8,128]{2,1,0:T(8,128)} %copy-done.2, ...), custom_call_target="tpu_custom_call" | custom-call | bytes 18000000 | tf_op jit(solution)/shard_map/long_back/pallas_call | solution.py:116
  155.8 4.6 %long_back.3 = (bf16[128,8192]{1,0:T(8,128)(2,1)}, f32[2,8192]{1,0:T(2,128)}, bf16[128,8192]{1,0:T(8,128)(2,1)}, f32[2,8192]{1,0:T(2,128)}, f32[1,8192]{1,0:T(1,128)}, /*index=5*/bf16[128,2048]{1,0:T(8,128)(2,1)}) custom-call(bf16[128,8192]{1,0:T(8,128)(2,1)} %long_back_near.1.refs_0_,, ...), custom_call_target="tpu_custom_call", output_to_operand_aliasing={{0}: (10, {}), {1}: (11, {}), {2}: (12, {}), {3}: (13, {}),... | custom-call | bytes 18000000 | tf_op jit(solution)/shard_map/long_back/pallas_call | solution.py:116
  160.4 7.8 %collective-permute-start.5 = (f32[2,8192]{1,0:T(2,128)}, f32[2,8192]{1,0:T(2,128)S(1)}, u32[]{:S(2)}, u32[]{:S(2)}) collective-permute-start(f32[2,8192]{1,0:T(2,128)} %get-tuple-element.88), channel_id=1, source_target_pairs={{1,0},{2,1},{3,2},{4,3},{5,4},{6,5},{7,6},{8,7},{9,8},{10,9},{11,1... | collective-permute-start | bytes 196616 | tf_op jit(solution)/shard_map/ppermute | solution.py:613
  170.3 4.2 %collective-permute-done.7.refs_2_ = f32[1,8192]{1,0:T(1,128)S(1)} collective-permute-done((f32[1,8192]{1,0:T(1,128)}, f32[1,8192]{1,0:T(1,128)S(1)}, u32[]{:S(2)}, u32[]{:S(2)}) %collective-permute-start.7) | collective-permute-done | bytes 32800 | tf_op jit(solution)/shard_map/ppermute | solution.py:613
  174.6 4.6 %collective-permute-start.8 = (bf16[128,6144]{1,0:T(8,128)(2,1)S(1)}, bf16[128,6144]{1,0:T(8,128)(2,1)S(1)}, u32[]{:S(2)}, u32[]{:S(2)}) collective-permute-start(bf16[128,6144]{1,0:T(8,128)(2,1)S(1)} %copy-done.8), channel_id=1, source_target_pairs={{1,0},{2,1},{3,2},{4,3},{5,4},{6,5},{7,6},{8,7},{9,8},{10,9},{11,1... | collective-permute-start | bytes 4718600 | tf_op jit(solution)/shard_map/ppermute | solution.py:613
  181.3 38.4 %all_to_all.20.refs_1_ = f32[128,8,128]{2,1,0:T(8,128)} all-to-all(f32[128,8,128]{2,1,0:T(8,128)} %scan_forward.1), channel_id=1, replica_groups=mesh['ctx'=8,'ch'=16] {'ctx','ch'}, dimensions={0} | all-to-all | bytes 1048576 | tf_op jit(solution)/shard_map/all_to_all | solution.py:617
  219.7 7.9 %collective-permute-start.6 = (bf16[128,2048]{1,0:T(8,128)(2,1)}, bf16[128,2048]{1,0:T(8,128)(2,1)S(1)}, u32[]{:S(2)}, u32[]{:S(2)}) collective-permute-start(bf16[128,2048]{1,0:T(8,128)(2,1)} %get-tuple-element.94.refs_0_), channel_id=1, source_target_pairs={{1,0},{2,1},{3,2},{4,3},{5,4},{6,5},{7,6},{8,7},{9,8},{10,9},{11,1... | collective-permute-start | bytes 1572872 | tf_op jit(solution)/shard_map/ppermute | solution.py:613
  227.6 8.0 %late.1 = (bf16[128,8192]{1,0:T(8,128)(2,1)}, bf16[128,8192]{1,0:T(8,128)(2,1)}) custom-call(bf16[128,8192]{1,0:T(8,128)(2,1)} %get-tuple-element.84.refs_0_, f32[2,8192]{1,0:T(2,128)} %get-tuple-element.85.refs_1_, bf16[128,8192]{1,0:T(8,128)(2,1)} %get-tuple-element.86.refs_2_, bf16[128,8192]{1,0:T(8,128)(2,1)} %get-tuple-element.87.refs_3_, ...), custom_call_target="tpu_custom_call" | custom-call | bytes 18000000 | tf_op jit(solution)/shard_map/late/pallas_call | solution.py:116
  235.7 9.5 %long_forward.1 = (bf16[128,8192]{1,0:T(8,128)(2,1)}, bf16[128,8192]{1,0:T(8,128)(2,1)}) custom-call(bf16[128,8192]{1,0:T(8,128)(2,1)} %get-tuple-element.64.refs_0_, f32[128,8,128]{2,1,0:T(8,128)} %all_to_all.20.refs_1_, f32[128,8,128]{2,1,0:T(8,128)} %get-tuple-element.65.refs_2_, bf16[128,8192]{1,0:T(8,128)(2,1)} %refs_3_.11, bf16[128,8192]{1,0:T(8,128)(2,1)} %refs_4_.7, ...), custom_call_target="tpu_custom_call" | custom-call | bytes 25200000 | tf_op jit(solution)/shard_map/long_forward/pallas_call | solution.py:116
  246.3 10.7 %medium_back.2 = (bf16[128,8192]{1,0:T(8,128)(2,1)}, bf16[128,8192]{1,0:T(8,128)(2,1)}) custom-call(bf16[128,6144]{1,0:T(8,128)(2,1)} %get-tuple-element.99.refs_0_, bf16[128,6144]{1,0:T(8,128)(2,1)} %copy-done.9, f32[1,8192]{1,0:T(1,128)} %copy-done.14, bf16[128,8192]{1,0:T(8,128)(2,1)} %refs_3_.13, bf16[128,8192]{1,0:T(8,128)(2,1)} %refs_4_.9, ...), custom_call_target="tpu_custom_call" | custom-call | bytes 21600000 | tf_op jit(solution)/shard_map/medium_back/pallas_call | solution.py:116
  257.8 4.9 %medium_back.3 = (bf16[128,8192]{1,0:T(8,128)(2,1)}, bf16[128,8192]{1,0:T(8,128)(2,1)}) custom-call(bf16[128,2048]{1,0:T(8,128)(2,1)} %get-tuple-element.94.refs_0_, bf16[128,2048]{1,0:T(8,128)(2,1)} %copy-done.12, f32[1,8192]{1,0:T(1,128)} %copy-done.14, bf16[128,8192]{1,0:T(8,128)(2,1)} %refs_3_.13, ...), custom_call_target="tpu_custom_call", output_to_operand_aliasing={{0}: (9, {}), {1}: (10, {})} | custom-call | bytes 21600000 | tf_op jit(solution)/shard_map/medium_back/pallas_call | solution.py:116
  (62 shorter events, 34.4 us)
Async XLA Ops:
  0.6 7.6 %copy-start.16 = (f32[512,16]{0,1:T(8,128)S(1)}, f32[512,16]{0,1:T(8,128)}, u32[]{:S(2)}) copy-start(f32[512,16]{0,1:T(8,128)} %param.21) | copy-start | bytes 98308
  3.3 13.8 %collective-permute-start = (bf16[16,8192]{1,0:T(8,128)(2,1)}, bf16[16,8192]{1,0:T(8,128)(2,1)S(1)}, u32[]{:S(2)}, u32[]{:S(2)}) collective-permute-start(bf16[16,8192]{1,0:T(8,128)(2,1)} %get-tuple-element.55), channel_id=1, source_target_pairs={{0,1},{1,2},{2,3},{3,4},{4,5},{5,6},{6,7},{7,8},{8,9},{9,10},{10,1... | collective-permute-start | bytes 786440 | tf_op jit(solution)/shard_map/ppermute | solution.py:613
  23.1 7.0 %copy-start.4 = (f32[512,16]{1,0:T(8,128)S(1)}, f32[512,16]{1,0:T(8,128)}, u32[]{:S(2)}) copy-start(f32[512,16]{1,0:T(8,128)} %copy.34.rate) | copy-start | bytes 98308
  23.1 45.0 %collective-permute-start.2 = (bf16[144,6144]{1,0:T(8,128)(2,1)}, bf16[144,6144]{1,0:T(8,128)(2,1)S(1)}, u32[]{:S(2)}, u32[]{:S(2)}) collective-permute-start(bf16[144,6144]{1,0:T(8,128)(2,1)} %product_one.3.refs_1_), channel_id=1, source_target_pairs={{0,1},{1,2},{2,3},{3,4},{4,5},{5,6},{6,7},{7,8},{8,9},{9,10},{10,1... | collective-permute-start | bytes 5308424 | tf_op jit(solution)/shard_map/ppermute | solution.py:613
  28.1 60.0 %collective-permute-start.1 = (bf16[144,2048]{1,0:T(8,128)(2,1)}, bf16[144,2048]{1,0:T(8,128)(2,1)S(1)}, u32[]{:S(2)}, u32[]{:S(2)}) collective-permute-start(bf16[144,2048]{1,0:T(8,128)(2,1)} %product_one.2.refs_1_), channel_id=1, source_target_pairs={{0,1},{1,2},{2,3},{3,4},{4,5},{5,6},{6,7},{7,8},{8,9},{9,10},{10,1... | collective-permute-start | bytes 1769480 | tf_op jit(solution)/shard_map/ppermute | solution.py:613
  30.8 19.7 %copy-start.18 = (bf16[16,8192]{1,0:T(8,128)(2,1)S(1)}, bf16[16,8192]{1,0:T(8,128)(2,1)}, u32[]{:S(2)}) copy-start(bf16[16,8192]{1,0:T(8,128)(2,1)} %get-tuple-element.75) | copy-start | bytes 786436
  38.1 50.0 %all-to-all-start.1 = ((f32[128,8,128]{2,1,0:T(8,128)}), f32[128,8,128]{2,1,0:T(8,128)S(1)}, u32[]{:S(2)}, u32[]{:S(2)}) async-start(f32[128,8,128]{2,1,0:T(8,128)} %get-tuple-element.74), calls=%async_computation.1 | async-start | bytes 1048576 | tf_op jit(solution)/shard_map/all_to_all | solution.py:617
  50.5 37.6 %collective-permute-start.4 = (bf16[16,8192]{1,0:T(8,128)(2,1)S(1)}, bf16[16,8192]{1,0:T(8,128)(2,1)S(1)}, u32[]{:S(2)}, u32[]{:S(2)}) collective-permute-start(bf16[16,8192]{1,0:T(8,128)(2,1)S(1)} %copy-done.18), channel_id=1, source_target_pairs={{1,0},{2,1},{3,2},{4,3},{5,4},{6,5},{7,6},{8,7},{9,8},{10,9},{11,1... | collective-permute-start | bytes 786440 | tf_op jit(solution)/shard_map/ppermute | solution.py:613
  88.1 8.5 %copy-start.1 = (bf16[16,8192]{1,0:T(8,128)(2,1)}, bf16[16,8192]{1,0:T(8,128)(2,1)S(1)}, u32[]{:S(2)}) copy-start(bf16[16,8192]{1,0:T(8,128)(2,1)S(1)} %collective-permute-done.4.refs_6_) | copy-start | bytes 786436
  88.1 8.5 %copy-start.6 = (f32[128,8,128]{2,1,0:T(8,128)}, f32[128,8,128]{2,1,0:T(8,128)S(1)}, u32[]{:S(2)}) copy-start(f32[128,8,128]{2,1,0:T(8,128)S(1)} %all-to-all-done.1.states_ref) | copy-start | bytes 1572868
  96.6 34.9 %copy-start.13 = (f32[6,8192]{1,0:T(8,128)S(1)}, f32[6,8192]{1,0:T(8,128)}, u32[]{:S(2)}) copy-start(f32[6,8192]{1,0:T(8,128)} %get-tuple-element.66) | copy-start | bytes 589828
  96.6 42.8 %copy-start.3 = (f32[512,16]{1,0:T(8,128)S(1)}, f32[512,16]{1,0:T(8,128)}, u32[]{:S(2)}) copy-start(f32[512,16]{1,0:T(8,128)} %copy.35.residue) | copy-start | bytes 98308
  96.6 30.9 %all-to-all-start = ((f32[128,8,128]{2,1,0:T(8,128)}), f32[128,8,128]{2,1,0:T(8,128)S(1)}, u32[]{:S(2)}, u32[]{:S(2)}) async-start(f32[128,8,128]{2,1,0:T(8,128)} %get-tuple-element.65.refs_2_), calls=%async_computation | async-start | bytes 1048576 | tf_op jit(solution)/shard_map/all_to_all | solution.py:617
  127.5 28.3 %copy-start.5 = (f32[128,8,128]{2,1,0:T(8,128)}, f32[128,8,128]{2,1,0:T(8,128)S(1)}, u32[]{:S(2)}) copy-start(f32[128,8,128]{2,1,0:T(8,128)S(1)} %all-to-all-done.states_ref) | copy-start | bytes 1572868
  127.5 18.4 %all-to-all-start.2 = ((f32[128,8,128]{2,1,0:T(8,128)}), f32[128,8,128]{2,1,0:T(8,128)S(1)}, u32[]{:S(2)}, u32[]{:S(2)}) async-start(f32[128,8,128]{2,1,0:T(8,128)} %scan_back.1), calls=%async_computation.2 | async-start | bytes 1048576 | tf_op jit(solution)/shard_map/all_to_all | solution.py:617
  131.5 14.3 %collective-permute-start.3 = (f32[6,8192]{1,0:T(8,128)S(1)}, f32[6,8192]{1,0:T(8,128)S(1)}, u32[]{:S(2)}, u32[]{:S(2)}) collective-permute-start(f32[6,8192]{1,0:T(8,128)S(1)} %copy-done.13), channel_id=1, source_target_pairs={{1,0},{2,1},{3,2},{4,3},{5,4},{6,5},{7,6},{8,7},{9,8},{10,9},{11,1... | collective-permute-start | bytes 589832 | tf_op jit(solution)/shard_map/ppermute | solution.py:613
  145.9 14.5 %copy-start.10 = (f32[6,8192]{1,0:T(8,128)}, f32[6,8192]{1,0:T(8,128)S(1)}, u32[]{:S(2)}) copy-start(f32[6,8192]{1,0:T(8,128)S(1)} %collective-permute-done.3.refs_6_.refs_7_) | copy-start | bytes 589828
  155.8 18.8 %copy-start.8 = (bf16[128,6144]{1,0:T(8,128)(2,1)S(1)}, bf16[128,6144]{1,0:T(8,128)(2,1)}, u32[]{:S(2)}) copy-start(bf16[128,6144]{1,0:T(8,128)(2,1)} %get-tuple-element.99.refs_0_) | copy-start | bytes 4718596
  160.4 14.2 %collective-permute-start.5 = (f32[2,8192]{1,0:T(2,128)}, f32[2,8192]{1,0:T(2,128)S(1)}, u32[]{:S(2)}, u32[]{:S(2)}) collective-permute-start(f32[2,8192]{1,0:T(2,128)} %get-tuple-element.88), channel_id=1, source_target_pairs={{1,0},{2,1},{3,2},{4,3},{5,4},{6,5},{7,6},{8,7},{9,8},{10,9},{11,1... | collective-permute-start | bytes 196616 | tf_op jit(solution)/shard_map/ppermute | solution.py:613
  168.2 6.4 %collective-permute-start.7 = (f32[1,8192]{1,0:T(1,128)}, f32[1,8192]{1,0:T(1,128)S(1)}, u32[]{:S(2)}, u32[]{:S(2)}) collective-permute-start(f32[1,8192]{1,0:T(1,128)} %get-tuple-element.82), channel_id=1, source_target_pairs={{2,0},{3,1},{4,2},{5,3},{6,4},{7,5},{8,6},{9,7},{10,8},{11,9},{12,... | collective-permute-start | bytes 98312 | tf_op jit(solution)/shard_map/ppermute | solution.py:613
  174.6 61.1 %copy-start.14 = (f32[1,8192]{1,0:T(1,128)}, f32[1,8192]{1,0:T(1,128)S(1)}, u32[]{:S(2)}) copy-start(f32[1,8192]{1,0:T(1,128)S(1)} %collective-permute-done.7.refs_2_) | copy-start | bytes 98308
  174.6 53.0 %copy-start.15 = (f32[2,8192]{1,0:T(2,128)}, f32[2,8192]{1,0:T(2,128)S(1)}, u32[]{:S(2)}) copy-start(f32[2,8192]{1,0:T(2,128)S(1)} %collective-permute-done.5.refs_4_) | copy-start | bytes 196612
  174.6 70.6 %collective-permute-start.8 = (bf16[128,6144]{1,0:T(8,128)(2,1)S(1)}, bf16[128,6144]{1,0:T(8,128)(2,1)S(1)}, u32[]{:S(2)}, u32[]{:S(2)}) collective-permute-start(bf16[128,6144]{1,0:T(8,128)(2,1)S(1)} %copy-done.8), channel_id=1, source_target_pairs={{1,0},{2,1},{3,2},{4,3},{5,4},{6,5},{7,6},{8,7},{9,8},{10,9},{11,1... | collective-permute-start | bytes 4718600 | tf_op jit(solution)/shard_map/ppermute | solution.py:613
  219.7 37.3 %collective-permute-start.6 = (bf16[128,2048]{1,0:T(8,128)(2,1)}, bf16[128,2048]{1,0:T(8,128)(2,1)S(1)}, u32[]{:S(2)}, u32[]{:S(2)}) collective-permute-start(bf16[128,2048]{1,0:T(8,128)(2,1)} %get-tuple-element.94.refs_0_), channel_id=1, source_target_pairs={{1,0},{2,1},{3,2},{4,3},{5,4},{6,5},{7,6},{8,7},{9,8},{10,9},{11,1... | collective-permute-start | bytes 1572872 | tf_op jit(solution)/shard_map/ppermute | solution.py:613
  (7 other events, 12.3 us)
